TPU v7x, 32 devices: a whole 2x2x4 slice. The times are simulated.
32 devices in a mesh: seq: 4 (over y, x), fsdp: 8 (over z, core).
Axes of the slice: x: 2, y: 2, z: 4, core: 2. Of those that a mesh axis runs over, the one named last changes fastest.
Arguments:
- layer_input: bfloat16 [8, 1024, 2048], P('fsdp', 'seq'), may hold values from -6 to 6
- mixer_gain: bfloat16 [2048], P('fsdp'), may hold values from 0.099609375 to 1.8984375
- query_weight: bfloat16 [2048, 2048], P('fsdp'), may hold values from -0.125 to 0.125
- key_weight: bfloat16 [2048, 2048], P('fsdp'), may hold values from -0.125 to 0.125
- value_weight: bfloat16 [2048, 3456], P('fsdp'), may hold values from -0.125 to 0.125
- swish_weight: bfloat16 [2048, 3456], P('fsdp'), may hold values from -0.125 to 0.125
- output_weight: bfloat16 [3456, 2048], P('fsdp'), may hold values from -0.21875 to 0.21875
- channel_gain: bfloat16 [2048], P('fsdp'), may hold values from 0.099609375 to 1.8984375
- gelu_weight: bfloat16 [2048, 3456], P('fsdp'), may hold values from -0.125 to 0.125
- linear_weight: bfloat16 [2048, 3456], P('fsdp'), may hold values from -0.125 to 0.125
- down_weight: bfloat16 [3456, 2048], P('fsdp'), may hold values from -0.21875 to 0.21875
- output_cotangent: bfloat16 [8, 1024, 2048], P('fsdp', 'seq'), may hold values from -6 to 6
Outputs:
- layer_output: bfloat16 [8, 1024, 2048], P('fsdp', 'seq')
- input_gradient: bfloat16 [8, 1024, 2048], P('fsdp', 'seq')
- mixer_gradient: float32 [2048], P('fsdp')
- query_gradient: float32 [2048, 2048], P('fsdp')
- key_gradient: float32 [2048, 2048], P('fsdp')
- value_gradient: float32 [2048, 3456], P('fsdp')
- swish_gradient: float32 [2048, 3456], P('fsdp')
- output_gradient: float32 [3456, 2048], P('fsdp')
- channel_gradient: float32 [2048], P('fsdp')
- gelu_gradient: float32 [2048, 3456], P('fsdp')
- linear_gradient: float32 [2048, 3456], P('fsdp')
- down_gradient: float32 [3456, 2048], P('fsdp')
All inputs are finite; a program needn't handle non-finite values.
Results may differ from a plain program's by a relative error of at most 0.024.
Values may be sent and summed in bfloat16 or wider, within the bound.
A program may use at most 576 MiB of HBM per device.

v0:
```python
import math

import jax
import jax.numpy as jnp
from jax import lax
from jax.sharding import PartitionSpec as P

HEADS = 8
KEY_HEAD = 256
VAL_HEAD = 432


EPSILON = 1e-05


def product(left, right):
    return jnp.dot(left, right, preferred_element_type=jnp.float32)


def times_transposed(left, right):
    return lax.dot_general(
        left, right, (((1,), (1,)), ((), ())), preferred_element_type=jnp.float32
    )


def transposed_times(left, right):
    return lax.dot_general(
        left, right, (((0,), (0,)), ((), ())), preferred_element_type=jnp.float32
    )


def normalize(values, gain):
    centered = values - jnp.mean(values, axis=-1, keepdims=True)
    spread = lax.rsqrt(jnp.mean(centered * centered, axis=-1, keepdims=True) + EPSILON)
    return centered * spread * gain


def group_norm(values):
    shaped = values.reshape(values.shape[0], HEADS, VAL_HEAD)
    centered = shaped - jnp.mean(shaped, axis=-1, keepdims=True)
    spread = lax.rsqrt(jnp.maximum(jnp.mean(centered * centered, axis=-1, keepdims=True), 1.0))
    return (centered * spread).reshape(values.shape)


def swish_mix(swish_value, retained_value):
    return jax.nn.silu(swish_value) * group_norm(retained_value)


def gelu_mix(gate_value, up_value):
    return jax.nn.gelu(gate_value, approximate=False) * up_value


def rotation_tables(positions, half_width):
    rates = jnp.exp(
        -math.log(10000.0) * jnp.arange(half_width, dtype=jnp.float32) / (half_width - 1)
    )
    turned = positions.astype(jnp.float32)[:, None] * rates[None, :]
    return (jnp.cos(turned), jnp.sin(turned))


def rotate(values, cosine_table, sine_table, heads_count):
    shaped = values.reshape(values.shape[0], heads_count, -1)
    half_width = shaped.shape[-1] // 2
    first_half = shaped[..., :half_width]
    second_half = shaped[..., half_width:]
    cosine_part = cosine_table[:, None, :]
    sine_part = sine_table[:, None, :]
    turned = jnp.concatenate(
        [
            first_half * cosine_part - second_half * sine_part,
            second_half * cosine_part + first_half * sine_part,
        ],
        axis=-1,
    )
    return turned.reshape(values.shape)


def decay_mask(head_ids, length):
    rates = jnp.log1p(-jnp.exp2(-5.0 - head_ids.astype(jnp.float32)))
    row_gaps = (
        jnp.arange(length, dtype=jnp.int32)[:, None] - jnp.arange(length, dtype=jnp.int32)[None, :]
    )
    gaps = jnp.maximum(row_gaps, 0).astype(jnp.float32)
    return jnp.where(row_gaps[None] >= 0, jnp.exp(gaps[None] * rates[:, None, None]), 0.0)


def split_heads(values, per_device, head_width):
    return values.reshape(values.shape[0], values.shape[1], per_device, head_width)


def on_device(
    layer_input,
    mixer_gain,
    query_weight,
    key_weight,
    value_weight,
    swish_weight,
    output_weight,
    channel_gain,
    gelu_weight,
    linear_weight,
    down_weight,
    output_cotangent,
):
    groups, local_length, width = layer_input.shape
    seq_count = lax.axis_size("seq")
    per_device = HEADS // seq_count
    rows_count = groups * local_length
    full_length = local_length * seq_count
    key_scale = KEY_HEAD ** (-0.5)
    full_query, full_key, full_value, full_swish, full_output, full_mixer = (
        lax.all_gather(query_weight, "fsdp", axis=0, tiled=True),
        lax.all_gather(key_weight, "fsdp", axis=0, tiled=True),
        lax.all_gather(value_weight, "fsdp", axis=0, tiled=True),
        lax.all_gather(swish_weight, "fsdp", axis=0, tiled=True),
        lax.all_gather(output_weight, "fsdp", axis=0, tiled=True),
        lax.all_gather(mixer_gain, "fsdp", axis=0, tiled=True),
    )
    mixer_scale = full_mixer.astype(jnp.float32)
    inputs = layer_input.reshape(rows_count, width).astype(jnp.float32)
    positions = jnp.tile(
        lax.axis_index("seq") * local_length + jnp.arange(local_length, dtype=jnp.int32), groups
    )
    cosine_table, sine_table = rotation_tables(positions, KEY_HEAD // 2)
    mixed_low = normalize(inputs, mixer_scale).astype(jnp.bfloat16)
    query_pre = product(mixed_low, full_query)
    key_pre = product(mixed_low, full_key)
    value_low = product(mixed_low, full_value).astype(jnp.bfloat16)
    swish_pre = product(mixed_low, full_swish)
    query_low = rotate(query_pre, cosine_table, sine_table, HEADS).astype(jnp.bfloat16)
    key_low = (rotate(key_pre, cosine_table, sine_table, HEADS) * key_scale).astype(jnp.bfloat16)
    query_heads, key_heads, value_heads = (
        lax.all_to_all(
            query_low.reshape(groups, local_length, -1),
            "seq",
            split_axis=2,
            concat_axis=1,
            tiled=True,
        ),
        lax.all_to_all(
            key_low.reshape(groups, local_length, -1),
            "seq",
            split_axis=2,
            concat_axis=1,
            tiled=True,
        ),
        lax.all_to_all(
            value_low.reshape(groups, local_length, -1),
            "seq",
            split_axis=2,
            concat_axis=1,
            tiled=True,
        ),
    )
    query_split = split_heads(query_heads, per_device, KEY_HEAD)
    key_split = split_heads(key_heads, per_device, KEY_HEAD)
    value_split = split_heads(value_heads, per_device, VAL_HEAD)
    head_ids = lax.axis_index("seq") * per_device + jnp.arange(per_device, dtype=jnp.int32)
    masks = decay_mask(head_ids, full_length)
    scores = jnp.einsum(
        "glhd,gmhd->ghlm", query_split, key_split, preferred_element_type=jnp.float32
    )
    weights_low = (scores * masks[None]).astype(jnp.bfloat16)
    retained_heads = jnp.einsum(
        "ghlm,gmhe->glhe", weights_low, value_split, preferred_element_type=jnp.float32
    )
    retained_send = retained_heads.reshape(groups, full_length, per_device * VAL_HEAD).astype(
        jnp.bfloat16
    )
    restored = lax.all_to_all(retained_send, "seq", split_axis=1, concat_axis=2, tiled=True)
    retained = restored.reshape(rows_count, -1).astype(jnp.float32)
    gated_low = swish_mix(swish_pre, retained).astype(jnp.bfloat16)
    middle = inputs + product(gated_low, full_output)
    full_gelu, full_linear, full_down, full_channel = (
        lax.all_gather(gelu_weight, "fsdp", axis=0, tiled=True),
        lax.all_gather(linear_weight, "fsdp", axis=0, tiled=True),
        lax.all_gather(down_weight, "fsdp", axis=0, tiled=True),
        lax.all_gather(channel_gain, "fsdp", axis=0, tiled=True),
    )
    channel_scale = full_channel.astype(jnp.float32)
    channel_low = normalize(middle, channel_scale).astype(jnp.bfloat16)
    gate_pre = product(channel_low, full_gelu)
    up_pre = product(channel_low, full_linear)
    hidden_low = gelu_mix(gate_pre, up_pre).astype(jnp.bfloat16)
    result = middle + product(hidden_low, full_down)
    layer_output = result.astype(jnp.bfloat16).reshape(groups, local_length, width)
    again_gelu, again_linear, again_down, again_channel = (
        lax.all_gather(gelu_weight, "fsdp", axis=0, tiled=True),
        lax.all_gather(linear_weight, "fsdp", axis=0, tiled=True),
        lax.all_gather(down_weight, "fsdp", axis=0, tiled=True),
        lax.all_gather(channel_gain, "fsdp", axis=0, tiled=True),
    )
    upstream = output_cotangent.reshape(rows_count, width)
    hidden_grad = times_transposed(upstream, again_down)
    _, gelu_back = jax.vjp(gelu_mix, gate_pre, up_pre)
    gate_grad, up_grad = gelu_back(hidden_grad)
    gate_low_grad = gate_grad.astype(jnp.bfloat16)
    up_low_grad = up_grad.astype(jnp.bfloat16)
    channel_grad = times_transposed(gate_low_grad, again_gelu) + times_transposed(
        up_low_grad, again_linear
    )
    _, channel_back = jax.vjp(normalize, middle, again_channel.astype(jnp.float32))
    middle_local, channel_term = channel_back(channel_grad)
    middle_grad = upstream.astype(jnp.float32) + middle_local
    down_term = transposed_times(hidden_low, upstream)
    gelu_term = transposed_times(channel_low, gate_low_grad)
    linear_term = transposed_times(channel_low, up_low_grad)
    gelu_share, linear_share, down_share, channel_share = (
        lax.psum_scatter(
            gelu_term.astype(jnp.bfloat16), "fsdp", scatter_dimension=0, tiled=True
        ).astype(jnp.float32),
        lax.psum_scatter(
            linear_term.astype(jnp.bfloat16), "fsdp", scatter_dimension=0, tiled=True
        ).astype(jnp.float32),
        lax.psum_scatter(
            down_term.astype(jnp.bfloat16), "fsdp", scatter_dimension=0, tiled=True
        ).astype(jnp.float32),
        lax.psum_scatter(
            channel_term.astype(jnp.bfloat16), "fsdp", scatter_dimension=0, tiled=True
        ).astype(jnp.float32),
    )
    again_query, again_key, again_value, again_swish, again_output, again_mixer = (
        lax.all_gather(query_weight, "fsdp", axis=0, tiled=True),
        lax.all_gather(key_weight, "fsdp", axis=0, tiled=True),
        lax.all_gather(value_weight, "fsdp", axis=0, tiled=True),
        lax.all_gather(swish_weight, "fsdp", axis=0, tiled=True),
        lax.all_gather(output_weight, "fsdp", axis=0, tiled=True),
        lax.all_gather(mixer_gain, "fsdp", axis=0, tiled=True),
    )
    branch_low_grad = middle_grad.astype(jnp.bfloat16)
    gated_grad = times_transposed(branch_low_grad, again_output)
    _, swish_back = jax.vjp(swish_mix, swish_pre, retained)
    swish_grad, retained_grad = swish_back(gated_grad)
    swish_low_grad = swish_grad.astype(jnp.bfloat16)
    retained_low_grad = retained_grad.astype(jnp.bfloat16).reshape(groups, local_length, -1)
    heads_grad = lax.all_to_all(retained_low_grad, "seq", split_axis=2, concat_axis=1, tiled=True)
    heads_split = split_heads(heads_grad, per_device, VAL_HEAD)
    scores_again = jnp.einsum(
        "glhd,gmhd->ghlm", query_split, key_split, preferred_element_type=jnp.float32
    )
    weights_again = (scores_again * masks[None]).astype(jnp.bfloat16)
    weights_grad = jnp.einsum(
        "glhe,gmhe->ghlm", heads_split, value_split, preferred_element_type=jnp.float32
    )
    value_heads_grad = jnp.einsum(
        "ghlm,glhe->gmhe", weights_again, heads_split, preferred_element_type=jnp.float32
    )
    score_low = (weights_grad * masks[None]).astype(jnp.bfloat16)
    query_heads_grad = jnp.einsum(
        "ghlm,gmhd->glhd", score_low, key_split, preferred_element_type=jnp.float32
    )
    key_heads_grad = jnp.einsum(
        "ghlm,glhd->gmhd", score_low, query_split, preferred_element_type=jnp.float32
    )
    back_query, back_key, back_value = (
        lax.all_to_all(
            query_heads_grad.reshape(groups, full_length, -1).astype(jnp.bfloat16),
            "seq",
            split_axis=1,
            concat_axis=2,
            tiled=True,
        ),
        lax.all_to_all(
            key_heads_grad.reshape(groups, full_length, -1).astype(jnp.bfloat16),
            "seq",
            split_axis=1,
            concat_axis=2,
            tiled=True,
        ),
        lax.all_to_all(
            value_heads_grad.reshape(groups, full_length, -1).astype(jnp.bfloat16),
            "seq",
            split_axis=1,
            concat_axis=2,
            tiled=True,
        ),
    )

    def rotate_local(values):
        return rotate(values, cosine_table, sine_table, HEADS)

    _, rotate_back = jax.vjp(rotate_local, query_pre)
    query_pre_grad = rotate_back(back_query.reshape(rows_count, -1).astype(jnp.float32))[0].astype(
        jnp.bfloat16
    )
    key_pre_grad = (
        rotate_back(back_key.reshape(rows_count, -1).astype(jnp.float32))[0] * key_scale
    ).astype(jnp.bfloat16)
    value_low_grad = back_value.reshape(rows_count, -1)
    mixed_grad = (
        times_transposed(query_pre_grad, again_query)
        + times_transposed(key_pre_grad, again_key)
        + times_transposed(value_low_grad, again_value)
        + times_transposed(swish_low_grad, again_swish)
    )
    _, mixer_back = jax.vjp(normalize, inputs, again_mixer.astype(jnp.float32))
    input_local, mixer_term = mixer_back(mixed_grad)
    input_gradient = (
        (middle_grad + input_local).astype(jnp.bfloat16).reshape(groups, local_length, width)
    )
    output_term = transposed_times(gated_low, branch_low_grad)
    query_term = transposed_times(mixed_low, query_pre_grad)
    key_term = transposed_times(mixed_low, key_pre_grad)
    value_term = transposed_times(mixed_low, value_low_grad)
    swish_term = transposed_times(mixed_low, swish_low_grad)
    query_share, key_share, value_share, swish_share, output_share, mixer_share = (
        lax.psum_scatter(
            query_term.astype(jnp.bfloat16), "fsdp", scatter_dimension=0, tiled=True
        ).astype(jnp.float32),
        lax.psum_scatter(
            key_term.astype(jnp.bfloat16), "fsdp", scatter_dimension=0, tiled=True
        ).astype(jnp.float32),
        lax.psum_scatter(
            value_term.astype(jnp.bfloat16), "fsdp", scatter_dimension=0, tiled=True
        ).astype(jnp.float32),
        lax.psum_scatter(
            swish_term.astype(jnp.bfloat16), "fsdp", scatter_dimension=0, tiled=True
        ).astype(jnp.float32),
        lax.psum_scatter(
            output_term.astype(jnp.bfloat16), "fsdp", scatter_dimension=0, tiled=True
        ).astype(jnp.float32),
        lax.psum_scatter(
            mixer_term.astype(jnp.bfloat16), "fsdp", scatter_dimension=0, tiled=True
        ).astype(jnp.float32),
    )
    summed = (
        lax.psum(mixer_share.astype(jnp.bfloat16), "seq").astype(jnp.float32),
        lax.psum(query_share.astype(jnp.bfloat16), "seq").astype(jnp.float32),
        lax.psum(key_share.astype(jnp.bfloat16), "seq").astype(jnp.float32),
        lax.psum(value_share.astype(jnp.bfloat16), "seq").astype(jnp.float32),
        lax.psum(swish_share.astype(jnp.bfloat16), "seq").astype(jnp.float32),
        lax.psum(output_share.astype(jnp.bfloat16), "seq").astype(jnp.float32),
        lax.psum(channel_share.astype(jnp.bfloat16), "seq").astype(jnp.float32),
        lax.psum(gelu_share.astype(jnp.bfloat16), "seq").astype(jnp.float32),
        lax.psum(linear_share.astype(jnp.bfloat16), "seq").astype(jnp.float32),
        lax.psum(down_share.astype(jnp.bfloat16), "seq").astype(jnp.float32),
    )
    return (
        layer_output,
        input_gradient,
        summed[0],
        summed[1],
        summed[2],
        summed[3],
        summed[4],
        summed[5],
        summed[6],
        summed[7],
        summed[8],
        summed[9],
    )


def solution(mesh):
    placed = (
        P("fsdp", "seq", None),
        P("fsdp"),
        P("fsdp", None),
        P("fsdp", None),
        P("fsdp", None),
        P("fsdp", None),
        P("fsdp", None),
        P("fsdp"),
        P("fsdp", None),
        P("fsdp", None),
        P("fsdp", None),
        P("fsdp", "seq", None),
    )
    return jax.shard_map(
        on_device,
        mesh=mesh,
        in_specs=placed,
        out_specs=(
            P("fsdp", "seq", None),
            P("fsdp", "seq", None),
            P("fsdp"),
            P("fsdp", None),
            P("fsdp", None),
            P("fsdp", None),
            P("fsdp", None),
            P("fsdp", None),
            P("fsdp"),
            P("fsdp", None),
            P("fsdp", None),
            P("fsdp", None),
        ),
        check_vma=False,
    )
```

profile of v0, /device:TPU:0, one launch (start us, length us, event | category | flops | bytes accessed | tf_op | source)
XLA Modules:
  0.0 2499.7 jit_solution(13115277579326325125)
XLA Ops:
  12.7 13.5 all-gather
  27.5 66.9 %all-gather.17.cloned.1.call-done = bf16[2048,2048]{1,0:T(8,128)(2,1)} async-done(((bf16[256,2048]{1,0:T(8,128)(2,1)}), bf16[2048,2048]{1,0:T(8,128)(2,1)}) %all-gather.17.cloned.1.call-update) | async-done | bytes 8388624 | tf_op jit(solution)/shard_map/all_gather | solution.py:113
  94.4 12.4 copy.87
  106.8 69.8 %all-gather.15.cloned.1.call-done = bf16[2048,2048]{1,0:T(8,128)(2,1)} async-done(((bf16[256,2048]{1,0:T(8,128)(2,1)}), bf16[2048,2048]{1,0:T(8,128)(2,1)}) %all-gather.15.cloned.1.call-update) | async-done | bytes 8388624 | tf_op jit(solution)/shard_map/all_gather | solution.py:112
  176.6 12.5 copy.84
  189.1 6.0 fusion.39
  199.4 11.7 copy.126
  211.7 11.6 reduce.3
  231.3 11.7 copy.127
  243.1 11.6 reduce.2
  262.4 44.1 %all-gather.13.cloned.1.call-done = bf16[2048,3456]{1,0:T(8,128)(2,1)} async-done(((bf16[256,3456]{1,0:T(8,128)(2,1)}), bf16[2048,3456]{1,0:T(8,128)(2,1)}) %all-gather.13.cloned.1.call-update) | async-done | bytes 14155792 | tf_op jit(solution)/shard_map/all_gather | solution.py:114
  306.5 10.3 fusion
  316.8 9.0 copy.82
  325.8 19.7 reduce.1
  366.6 6.2 multiply_convert_fusion.1
  387.2 6.7 copy.92
  393.9 11.7 reduce.4
  413.6 8.9 all-gather.1
  423.0 11.7 all-to-all-done.3
  467.4 17.6 multiply_convert_fusion.4
  485.0 80.3 %all-gather.19.cloned.1.call-done = bf16[3456,2048]{1,0:T(8,128)(2,1)} async-done(((bf16[432,2048]{1,0:T(8,128)(2,1)}), bf16[3456,2048]{1,0:T(8,128)(2,1)}) %all-gather.19.cloned.1.call-update) | async-done | bytes 14155792 | tf_op jit(solution)/shard_map/all_gather | solution.py:116
  565.3 9.8 fusion.61
  578.3 116.4 %all-gather.21.cloned.1.call-done = bf16[2048,3456]{1,0:T(8,128)(2,1)} async-done(((bf16[256,3456]{1,0:T(8,128)(2,1)}), bf16[2048,3456]{1,0:T(8,128)(2,1)}) %all-gather.21.cloned.1.call-update) | async-done | bytes 14155792 | tf_op jit(solution)/shard_map/all_gather | solution.py:175
  694.7 11.3 fusion.62
  706.0 118.2 %all-gather.25.cloned.1.call-done = bf16[3456,2048]{1,0:T(8,128)(2,1)} async-done(((bf16[432,2048]{1,0:T(8,128)(2,1)}), bf16[3456,2048]{1,0:T(8,128)(2,1)}) %all-gather.25.cloned.1.call-update) | async-done | bytes 14155792 | tf_op jit(solution)/shard_map/all_gather | solution.py:177
  824.2 17.7 multiply_convert_fusion.2
  841.9 111.8 %all-gather.23.cloned.1.call-done = bf16[2048,3456]{1,0:T(8,128)(2,1)} async-done(((bf16[256,3456]{1,0:T(8,128)(2,1)}), bf16[2048,3456]{1,0:T(8,128)(2,1)}) %all-gather.23.cloned.1.call-update) | async-done | bytes 14155792 | tf_op jit(solution)/shard_map/all_gather | solution.py:176
  953.7 14.4 add_convert_fusion
  968.2 9.5 fusion.63
  977.8 12.8 multiply_reduce_fusion.2
  996.1 14.7 fusion.8
  1030.9 7.1 fusion.33
  1037.9 8.9 copy.102
  1046.8 19.7 reduce.5
  1069.0 26.0 %all_to_all.102 = bf16[4,2,110592]{2,1,0:T(2,128)(2,1)} all-to-all(bf16[4,2,110592]{2,1,0:T(2,128)(2,1)S(1)} %reshape.560), channel_id=1, replica_groups=mesh['seq'=4,'fsdp'=8] {'seq'}, dimensions={0} | all-to-all | bytes 3538944 | tf_op jit(solution)/shard_map/all_to_all | solution.py:236
  1101.3 6.4 multiply_convert_fusion
  1114.8 7.0 reduce.7
  1136.7 8.0 reduce.6
  1156.3 9.1 all-to-all-done.6
  1180.7 6.0 convolution_convert_fusion.7
  1187.9 8.6 convolution_convert_fusion.3
  1197.7 9.1 convolution_convert_fusion.2
  1206.9 8.8 convolution_convert_fusion.1
  1217.2 7.5 convolution_convert_fusion.4
  1226.0 8.7 convolution_convert_fusion
  1241.6 9.9 copy.112
  1251.5 11.7 reduce.8
  1267.0 25.1 %all_to_all.103 = bf16[4,2,110592]{2,1,0:T(2,128)(2,1)S(1)} all-to-all(bf16[4,2,110592]{2,1,0:T(2,128)(2,1)} %reshape.566), channel_id=1, replica_groups=mesh['seq'=4,'fsdp'=8] {'seq'}, dimensions={0} | all-to-all | bytes 3538944 | tf_op jit(solution)/shard_map/all_to_all | solution.py:270
  1301.3 9.1 convolution_convert_fusion.5
  1310.7 47.1 %reduce-scatter.9.cloned.1.call-done = bf16[256,2048]{1,0:T(8,128)(2,1)} async-done(((bf16[2048,2048]{1,0:T(8,128)(2,1)}), bf16[256,2048]{1,0:T(8,128)(2,1)}) %reduce-scatter.9.cloned.1.call-update) | async-done | bytes 1048592 | tf_op jit(solution)/shard_map/reduce_scatter | solution.py:307
  1357.8 144.8 %reduce-scatter.17.cloned.1.call-done = bf16[432,2048]{1,0:T(8,128)(2,1)} async-done(((bf16[3456,2048]{1,0:T(8,128)(2,1)}), bf16[432,2048]{1,0:T(8,128)(2,1)}) %reduce-scatter.17.cloned.1.call-update) | async-done | bytes 1769488 | tf_op jit(solution)/shard_map/reduce_scatter | solution.py:319
  1502.6 144.6 %reduce-scatter.19.cloned.1.call-done = bf16[256,3456]{1,0:T(8,128)(2,1)} async-done(((bf16[2048,3456]{1,0:T(8,128)(2,1)}), bf16[256,3456]{1,0:T(8,128)(2,1)}) %reduce-scatter.19.cloned.1.call-update) | async-done | bytes 1769488 | tf_op jit(solution)/shard_map/reduce_scatter | solution.py:209
  1647.2 144.7 %reduce-scatter.21.cloned.1.call-done = bf16[256,3456]{1,0:T(8,128)(2,1)} async-done(((bf16[2048,3456]{1,0:T(8,128)(2,1)}), bf16[256,3456]{1,0:T(8,128)(2,1)}) %reduce-scatter.21.cloned.1.call-update) | async-done | bytes 1769488 | tf_op jit(solution)/shard_map/reduce_scatter | solution.py:212
  1791.9 144.6 %reduce-scatter.15.cloned.1.call-done = bf16[256,3456]{1,0:T(8,128)(2,1)} async-done(((bf16[2048,3456]{1,0:T(8,128)(2,1)}), bf16[256,3456]{1,0:T(8,128)(2,1)}) %reduce-scatter.15.cloned.1.call-update) | async-done | bytes 1769488 | tf_op jit(solution)/shard_map/reduce_scatter | solution.py:316
  1936.5 144.6 %reduce-scatter.23.cloned.1.call-done = bf16[432,2048]{1,0:T(8,128)(2,1)} async-done(((bf16[3456,2048]{1,0:T(8,128)(2,1)}), bf16[432,2048]{1,0:T(8,128)(2,1)}) %reduce-scatter.23.cloned.1.call-update) | async-done | bytes 1769488 | tf_op jit(solution)/shard_map/reduce_scatter | solution.py:215
  2081.1 144.6 %reduce-scatter.13.cloned.1.call-done = bf16[256,3456]{1,0:T(8,128)(2,1)} async-done(((bf16[2048,3456]{1,0:T(8,128)(2,1)}), bf16[256,3456]{1,0:T(8,128)(2,1)}) %reduce-scatter.13.cloned.1.call-update) | async-done | bytes 1769488 | tf_op jit(solution)/shard_map/reduce_scatter | solution.py:313
  2227.6 10.6 fusion.22
  2238.2 6.0 fusion.64
  2244.2 7.7 convolution_add_fusion.4
  2251.9 10.2 convolution_add_fusion.1
  2262.2 10.1 fusion.28
  2274.6 14.1 all-reduce.6
  2288.8 10.6 all-reduce.7
  2304.4 170.9 %all-reduce.11.cloned.1.call-done = (bf16[256,2048]{1,0:T(8,128)(2,1)}, bf16[256,2048]{1,0:T(8,128)(2,1)}, bf16[256,3456]{1,0:T(8,128)(2,1)}, bf16[256,3456]{1,0...) async-done(((bf16[256,2048]{1,0:T(8,128)(2,1)}, bf16[256,2048]{1,0:T(8,128)(2,1)}, ...) | async-done | bytes 12714000 | tf_op jit(solution)/shard_map/psum | solution.py:328
  (297 shorter events, 240.9 us)
Async XLA Ops:
  7.2 87.2 %all-gather.17.cloned.1.call-start = ((), (), s32[]{:S(2)}) async-start(), calls=%async_computation.19 | async-start | bytes 9437184 | tf_op jit(solution)/shard_map/all_gather | solution.py:113
  7.9 168.7 %all-gather.15.cloned.1.call-start = ((), (), s32[]{:S(2)}) async-start(), calls=%async_computation.18 | async-start | bytes 9437184 | tf_op jit(solution)/shard_map/all_gather | solution.py:112
  8.7 297.8 %all-gather.13.cloned.1.call-start = ((), (), s32[]{:S(2)}) async-start(), calls=%async_computation.17 | async-start | bytes 15925248 | tf_op jit(solution)/shard_map/all_gather | solution.py:114
  9.4 458.0 %all-gather.11.cloned.1.call-start = ((), (), s32[]{:S(2)}) async-start(), calls=%async_computation.16 | async-start | bytes 15925248 | tf_op jit(solution)/shard_map/all_gather | solution.py:115
  10.0 2.7 copy-start.65
  10.0 16.3 copy-start
  10.0 555.3 %all-gather.19.cloned.1.call-start = ((), (), s32[]{:S(2)}) async-start(), calls=%async_computation.20 | async-start | bytes 15925248 | tf_op jit(solution)/shard_map/all_gather | solution.py:116
  10.6 684.1 %all-gather.21.cloned.1.call-start = ((), (), s32[]{:S(2)}) async-start(), calls=%async_computation.21 | async-start | bytes 15925248 | tf_op jit(solution)/shard_map/all_gather | solution.py:175
  11.2 813.1 %all-gather.25.cloned.1.call-start = ((), (), s32[]{:S(2)}) async-start(), calls=%async_computation.23 | async-start | bytes 15925248 | tf_op jit(solution)/shard_map/all_gather | solution.py:177
  11.9 941.8 %all-gather.23.cloned.1.call-start = ((), (), s32[]{:S(2)}) async-start(), calls=%async_computation.22 | async-start | bytes 15925248 | tf_op jit(solution)/shard_map/all_gather | solution.py:176
  26.5 280.0 %copy-start.42 = (f32[256]{0:T(256)}, f32[256]{0:T(256)S(1)}, u32[]{:S(2)}) copy-start(f32[256]{0:T(256)S(1)} %broadcast_multiply_fusion.2) | copy-start | bytes 3076
  26.9 79.9 %copy-start.60 = (f32[256]{0:T(256)}, f32[256]{0:T(256)S(1)}, u32[]{:S(2)}) copy-start(f32[256]{0:T(256)S(1)} %fusion.27) | copy-start | bytes 3076
  27.0 279.5 %copy-start.44 = (f32[256]{0:T(256)}, f32[256]{0:T(256)S(1)}, u32[]{:S(2)}) copy-start(f32[256]{0:T(256)S(1)} %fusion.47) | copy-start | bytes 3076
  27.5 170.1 %copy-start.32 = (f32[256,128]{0,1:T(8,128)}, f32[256,128]{0,1:T(8,128)S(1)}, u32[]{:S(2)}) copy-start(f32[256,128]{0,1:T(8,128)S(1)} %get-tuple-element.51) | copy-start | bytes 393220
  27.5 170.1 %copy-start.34 = (f32[256,128]{0,1:T(8,128)}, f32[256,128]{0,1:T(8,128)S(1)}, u32[]{:S(2)}) copy-start(f32[256,128]{0,1:T(8,128)S(1)} %get-tuple-element.52) | copy-start | bytes 393220
  189.1 6.0 copy-start.11
  223.2 8.0 copy-start.19
  223.2 8.0 copy-start.20
  226.8 31.3 %all-to-all-start.2 = ((bf16[4,2,65536]{2,1,0:T(2,128)(2,1)}), bf16[4,2,65536]{2,1,0:T(2,128)(2,1)}, u32[]{:S(2)}, u32[]{:S(2)}) async-start(bf16[4,2,65536]{2,1,0:T(2,128)(2,1)} %reshape.556), calls=%async_computation.2 | async-start | bytes 2097152 | tf_op jit(solution)/shard_map/all_to_all | solution.py:140
  258.1 91.3 %all-to-all-start.1 = ((bf16[4,2,65536]{2,1,0:T(2,128)(2,1)}), bf16[4,2,65536]{2,1,0:T(2,128)(2,1)}, u32[]{:S(2)}, u32[]{:S(2)}) async-start(bf16[4,2,65536]{2,1,0:T(2,128)(2,1)} %reshape.554), calls=%async_computation.1 | async-start | bytes 2097152 | tf_op jit(solution)/shard_map/all_to_all | solution.py:133
  349.4 26.8 %all-to-all-start = ((bf16[4,2,110592]{2,1,0:T(2,128)(2,1)}), bf16[4,2,110592]{2,1,0:T(2,128)(2,1)}, u32[]{:S(2)}, u32[]{:S(2)}) async-start(bf16[4,2,110592]{2,1,0:T(2,128)(2,1)} %reshape.552), calls=%async_computation | async-start | bytes 3538944 | tf_op jit(solution)/shard_map/all_to_all | solution.py:147
  354.0 12.5 copy-start.68
  354.4 12.2 copy-start.40
  366.6 6.2 copy-start.38
  382.3 4.9 copy-start.26
  405.7 7.9 copy-start.66
  409.9 24.8 all-to-all-start.3
  449.4 2.7 copy-start.52
  565.3 11.7 copy-start.50
  968.2 9.5 copy-start.23
  968.2 9.5 copy-start.51
  968.2 9.5 copy-start.55
  968.2 9.6 copy-start.63
  977.7 12.8 copy-start.57
  990.5 4.3 copy-start.9
  1016.0 3.1 copy-start.2
  1016.0 3.1 copy-start.49
  1020.1 3.0 copy-start.47
  1025.2 5.7 copy-start.7
  1101.2 6.4 copy-start.24
  1101.2 6.4 copy-start.41
  1121.9 5.7 copy-start.39
  1123.9 24.5 all-to-all-start.5
  1148.4 17.1 all-to-all-start.6
  1152.7 158.0 %reduce-scatter.11.cloned.1.call-start = ((), (), s32[]{:S(2)}) async-start(), calls=%async_computation.25 | async-start | bytes 9437184 | tf_op jit(solution)/shard_map/reduce_scatter | solution.py:310
  1173.7 6.9 copy-start.17
  1180.6 177.2 %reduce-scatter.9.cloned.1.call-start = ((), (), s32[]{:S(2)}) async-start(), calls=%async_computation.24 | async-start | bytes 9437184 | tf_op jit(solution)/shard_map/reduce_scatter | solution.py:307
  1186.7 315.9 %reduce-scatter.17.cloned.1.call-start = ((), (), s32[]{:S(2)}) async-start(), calls=%async_computation.28 | async-start | bytes 15925248 | tf_op jit(solution)/shard_map/reduce_scatter | solution.py:319
  1196.5 450.7 %reduce-scatter.19.cloned.1.call-start = ((), (), s32[]{:S(2)}) async-start(), calls=%async_computation.29 | async-start | bytes 15925248 | tf_op jit(solution)/shard_map/reduce_scatter | solution.py:209
  1206.9 585.1 %reduce-scatter.21.cloned.1.call-start = ((), (), s32[]{:S(2)}) async-start(), calls=%async_computation.30 | async-start | bytes 15925248 | tf_op jit(solution)/shard_map/reduce_scatter | solution.py:212
  1215.7 720.8 %reduce-scatter.15.cloned.1.call-start = ((), (), s32[]{:S(2)}) async-start(), calls=%async_computation.27 | async-start | bytes 15925248 | tf_op jit(solution)/shard_map/reduce_scatter | solution.py:316
  1224.8 856.4 %reduce-scatter.23.cloned.1.call-start = ((), (), s32[]{:S(2)}) async-start(), calls=%async_computation.31 | async-start | bytes 15925248 | tf_op jit(solution)/shard_map/reduce_scatter | solution.py:215
  1234.7 991.0 %reduce-scatter.13.cloned.1.call-start = ((), (), s32[]{:S(2)}) async-start(), calls=%async_computation.26 | async-start | bytes 15925248 | tf_op jit(solution)/shard_map/reduce_scatter | solution.py:313
  1310.4 1165.0 %all-reduce.11.cloned.1.call-start = ((), (), s32[]{:S(2)}) async-start(), calls=%async_computation.32 | async-start | bytes 25427968 | tf_op jit(solution)/shard_map/psum | solution.py:328
  2227.6 10.6 copy-start.18
  2238.2 6.0 copy-start.16
  2244.2 7.8 copy-start.13
  2251.9 10.2 copy-start.22
  2262.1 10.2 copy-start.61
  2262.1 12.4 copy-start.64
  2262.2 38.5 %copy-start.59 = (f32[256]{0:T(256)S(1)}, f32[256]{0:T(256)}, u32[]{:S(2)}) copy-start(f32[256]{0:T(256)} %copy-done.58) | copy-start | bytes 3076
  2272.3 28.3 %copy-start.6 = (f32[256,2048]{1,0:T(8,128)S(1)}, f32[256,2048]{1,0:T(8,128)}, u32[]{:S(2)}) copy-start(f32[256,2048]{1,0:T(8,128)} %copy-done.5) | copy-start | bytes 6291460
  2475.4 3.6 copy-start.31
  2487.6 3.8 copy-start.36
  (30 other events, 48.1 us)
Sparse Core Ops, SparseCore 0:
  9.6 84.7 all-gather.16
  96.0 80.5 all-gather.14
  178.3 128.1 all-gather.12
  308.0 127.8 all-gather.10
  437.4 127.8 all-gather.18
  566.8 127.8 all-gather.20
  696.3 127.8 all-gather.24
  825.9 127.8 all-gather.22
  1180.7 86.9 reduce-scatter.10
  1269.8 87.9 reduce-scatter.8
  1360.1 142.4 reduce-scatter.16
  1504.7 142.4 reduce-scatter.18
  1649.5 142.4 reduce-scatter.20
  1794.1 142.4 reduce-scatter.14
  1938.7 142.4 reduce-scatter.22
  2083.3 142.4 reduce-scatter.12
  2230.2 245.1 all-reduce.10
where the time goes:
time: 2510 us; the launch traced here: 2500 us
  waiting for transfers between devices  1720 us (69%)
  matrix products  265 us (11%)
  local copies, waits for them, and re-layouts  219 us (9%)
  other arithmetic  153 us (6%)
  blocking collectives  98.2 us (4%)
  starting transfers between devices  25.8 us (1%)
    psum x1, waiting for transfers between devices, on_device(): lax.psum(query_share.astype(jnp.bfloat16), 'seq').astype(jnp.float32)  171 us
    reduce_scatter x1, waiting for transfers between devices, on_device(): lax.psum_scatter(output_term.astype(jnp.bfloat16), 'fsdp', scatter_dimens...  145 us
    reduce_scatter x1, waiting for transfers between devices, on_device(): lax.psum_scatter(linear_term.astype(jnp.bfloat16), 'fsdp', scatter_dimens...  145 us
    reduce_scatter x1, waiting for transfers between devices, on_device(): lax.psum_scatter(gelu_term.astype(jnp.bfloat16), 'fsdp', scatter_dimensio...  145 us
    reduce_scatter x1, waiting for transfers between devices, on_device(): lax.psum_scatter(swish_term.astype(jnp.bfloat16), 'fsdp', scatter_dimensi...  145 us
    reduce_scatter x1, waiting for transfers between devices, on_device(): lax.psum_scatter(value_term.astype(jnp.bfloat16), 'fsdp', scatter_dimensi...  145 us
    reduce_scatter x1, waiting for transfers between devices, on_device(): lax.psum_scatter(down_term.astype(jnp.bfloat16), 'fsdp', scatter_dimensio...  145 us
    all_gather x1, waiting for transfers between devices, on_device(): lax.all_gather(down_weight, 'fsdp', axis=0, tiled=True)  118 us
  transfers between devices with their start and end apart: 23, of which 18 were waited for; matrix products, arithmetic and copies ran while one was open for 18% of the time, Pallas kernels for 0%

commit v1 on v0

v1 whole, which is shorter than its diff:
```python
import functools
import math

import jax
import jax.numpy as jnp
from jax import lax
from jax.experimental import pallas as pl
from jax.experimental.pallas import tpu as pltpu
from jax.sharding import PartitionSpec as P

HEADS = 8
KEY_HEAD = 256
VAL_HEAD = 432
EPSILON = 1e-05
MESH = pl.DeviceIdType.MESH
BF = jnp.bfloat16
F32 = jnp.float32


def product(left, right):
    return jnp.dot(left, right, preferred_element_type=F32)


def times_transposed(left, right):
    return lax.dot_general(left, right, (((1,), (1,)), ((), ())), preferred_element_type=F32)


def transposed_times(left, right):
    return lax.dot_general(left, right, (((0,), (0,)), ((), ())), preferred_element_type=F32)


def normalize(values, gain):
    centered = values - jnp.mean(values, axis=-1, keepdims=True)
    spread = lax.rsqrt(jnp.mean(centered * centered, axis=-1, keepdims=True) + EPSILON)
    return centered * spread * gain


def group_norm_head(values):
    centered = values - jnp.mean(values, axis=-1, keepdims=True)
    return centered * lax.rsqrt(
        jnp.maximum(jnp.mean(centered * centered, axis=-1, keepdims=True), 1.0)
    )


def swish_mix(swish_value, retained_value):
    parts = [
        group_norm_head(retained_value[:, at : at + VAL_HEAD])
        for at in range(0, retained_value.shape[1], VAL_HEAD)
    ]
    return jax.nn.silu(swish_value) * jnp.concatenate(parts, axis=-1)


def gelu_mix(gate_value, up_value):
    return jax.nn.gelu(gate_value, approximate=False) * up_value


def rotation_tables(length, half_width):
    rates = jnp.exp(-math.log(10000.0) * jnp.arange(half_width, dtype=F32) / (half_width - 1))
    turned = jnp.arange(length, dtype=F32)[:, None] * rates[None, :]
    return (jnp.cos(turned), jnp.sin(turned))


def rotate(values, cosine, sine, back=False):
    half = KEY_HEAD // 2
    pieces = []
    for at in range(0, values.shape[1], KEY_HEAD):
        first = values[:, at : at + half]
        second = values[:, at + half : at + KEY_HEAD]
        if back:
            pieces += [first * cosine + second * sine, second * cosine - first * sine]
        else:
            pieces += [first * cosine - second * sine, second * cosine + first * sine]
    return jnp.concatenate(pieces, axis=-1)


def decay_mask(head_ids, length):
    rates = jnp.log1p(-jnp.exp2(-5.0 - head_ids.astype(F32)))
    row_gaps = (
        jnp.arange(length, dtype=jnp.int32)[:, None] - jnp.arange(length, dtype=jnp.int32)[None, :]
    )
    gaps = jnp.maximum(row_gaps, 0).astype(F32)
    return jnp.where(row_gaps[None] >= 0, jnp.exp(gaps[None] * rates[:, None, None]), 0.0)


def greet(peers):
    barrier = pltpu.get_barrier_semaphore()
    for peer in peers:
        pl.semaphore_signal(barrier, inc=1, device_id={"seq": peer}, device_id_type=MESH)
    pl.semaphore_wait(barrier, len(peers))


def remote(source, target, sends, recvs, k, to):
    return pltpu.make_async_remote_copy(
        src_ref=source,
        dst_ref=target,
        send_sem=sends.at[k],
        recv_sem=recvs.at[k],
        device_id={"seq": to},
        device_id_type=MESH,
    )


def gather_square_kernel(x_ref, o_ref, sends, recvs, local):
    me = lax.axis_index("seq")
    across, along = me ^ 1, me ^ 2
    half = x_ref.shape[0] // 2
    greet((across, along))
    own = pltpu.make_async_copy(x_ref, o_ref.at[me], local)
    own.start()

    def part(ref, i):
        return ref.at[pl.ds(i * half, half)]

    first = (
        remote(part(x_ref, 0), part(o_ref.at[me], 0), sends, recvs, 0, across),
        remote(part(x_ref, 1), part(o_ref.at[me], 1), sends, recvs, 1, along),
        remote(part(x_ref, 1), part(o_ref.at[me], 1), sends, recvs, 2, across),
        remote(part(x_ref, 0), part(o_ref.at[me], 0), sends, recvs, 3, along),
    )
    for copy in first:
        copy.start()
    first[0].wait_recv()
    on_along = remote(part(o_ref.at[across], 0), part(o_ref.at[across], 0), sends, recvs, 4, along)
    on_along.start()
    first[1].wait_recv()
    on_across = remote(part(o_ref.at[along], 1), part(o_ref.at[along], 1), sends, recvs, 5, across)
    on_across.start()
    first[2].wait_recv()
    first[3].wait_recv()
    on_along.wait_recv()
    on_across.wait_recv()
    for copy in first + (on_along, on_across):
        copy.wait_send()
    own.wait()


def gather_kernel(count, x_ref, o_ref, sends, recvs, local):
    me = lax.axis_index("seq")
    peers = [lax.rem(me + step, count) for step in range(1, count)]
    greet(peers)
    own = pltpu.make_async_copy(x_ref, o_ref.at[me], local)
    own.start()
    copies = [remote(x_ref, o_ref.at[me], sends, recvs, k, to) for k, to in enumerate(peers)]
    for copy in copies:
        copy.start()
    for copy in copies:
        copy.wait()
    own.wait()


def gather_seq(values, call):
    count = lax.axis_size("seq")
    square = count == 4 and values.shape[0] % 32 == 0
    body = gather_square_kernel if square else functools.partial(gather_kernel, count)
    copies = 6 if square else count - 1
    return pl.pallas_call(
        body,
        out_shape=jax.ShapeDtypeStruct((count,) + values.shape, values.dtype),
        in_specs=[pl.BlockSpec(memory_space=pl.ANY)],
        out_specs=pl.BlockSpec(memory_space=pl.ANY),
        scratch_shapes=[
            pltpu.SemaphoreType.DMA((copies,)),
            pltpu.SemaphoreType.DMA((copies,)),
            pltpu.SemaphoreType.DMA,
        ],
        compiler_params=pltpu.CompilerParams(collective_id=call, has_side_effects=True),
        name=f"gather_seq_{call}",
    )(values)


def exchange_kernel(count, x_ref, o_ref, sends, recvs, local):
    me = lax.axis_index("seq")
    peers = [lax.rem(me + step, count) for step in range(1, count)]
    greet(peers)
    own = pltpu.make_async_copy(x_ref.at[me], o_ref.at[me], local)
    own.start()
    copies = [remote(x_ref.at[to], o_ref.at[me], sends, recvs, k, to) for k, to in enumerate(peers)]
    for copy in copies:
        copy.start()
    for copy in copies:
        copy.wait()
    own.wait()


def exchange_seq(values, call):
    count = lax.axis_size("seq")
    return pl.pallas_call(
        functools.partial(exchange_kernel, count),
        out_shape=jax.ShapeDtypeStruct(values.shape, values.dtype),
        in_specs=[pl.BlockSpec(memory_space=pl.ANY)],
        out_specs=pl.BlockSpec(memory_space=pl.ANY),
        scratch_shapes=[
            pltpu.SemaphoreType.DMA((count - 1,)),
            pltpu.SemaphoreType.DMA((count - 1,)),
            pltpu.SemaphoreType.DMA,
        ],
        compiler_params=pltpu.CompilerParams(collective_id=call, has_side_effects=True),
        name=f"exchange_seq_{call}",
    )(values)


def scatter_square_kernel(p_ref, o_ref, inbox_x, inbox_y, via_x, via_y, out_x, out_y, sends, recvs):
    me = lax.axis_index("seq")
    across, along, corner = me ^ 1, me ^ 2, me ^ 3
    half = p_ref.shape[1] // 2
    low, high = pl.ds(0, half), pl.ds(half, half)
    greet((across, along))
    first = (
        remote(p_ref.at[corner, low], via_x, sends, recvs, 0, across),
        remote(p_ref.at[corner, high], via_y, sends, recvs, 1, along),
        remote(p_ref.at[across, low], inbox_x.at[low], sends, recvs, 2, across),
        remote(p_ref.at[along, high], inbox_y.at[high], sends, recvs, 3, along),
    )
    for copy in first:
        copy.start()
    first[0].wait_recv()
    out_y[...] = (p_ref[along, :half].astype(F32) + via_x[...].astype(F32)).astype(BF)
    to_along = remote(out_y, inbox_y.at[low], sends, recvs, 4, along)
    to_along.start()
    first[1].wait_recv()
    out_x[...] = (p_ref[across, half:].astype(F32) + via_y[...].astype(F32)).astype(BF)
    to_across = remote(out_x, inbox_x.at[high], sends, recvs, 5, across)
    to_across.start()
    first[2].wait_recv()
    first[3].wait_recv()
    to_along.wait_recv()
    to_across.wait_recv()
    o_ref[...] = (
        p_ref[me].astype(F32) + inbox_x[...].astype(F32) + inbox_y[...].astype(F32)
    )
    for copy in first + (to_along, to_across):
        copy.wait_send()


def scatter_kernel(count, p_ref, o_ref, inbox, sends, recvs):
    me = lax.axis_index("seq")
    peers = [lax.rem(me + step, count) for step in range(1, count)]
    greet(peers)
    copies = [remote(p_ref.at[to], inbox.at[k], sends, recvs, k, to) for k, to in enumerate(peers)]
    for copy in copies:
        copy.start()
    total = p_ref[me].astype(F32)
    for k, copy in enumerate(copies):
        copy.wait_recv()
        total = total + inbox[k].astype(F32)
    o_ref[...] = total
    for copy in copies:
        copy.wait_send()


def scatter_seq(parts, call):
    count = lax.axis_size("seq")
    rows, width = parts.shape[0] // count, parts.shape[1]
    parts = parts.reshape(count, rows, width)
    if count == 4 and rows % 32 == 0:
        body = scatter_square_kernel
        scratch = [pltpu.VMEM((rows, width), BF)] * 2 + [pltpu.VMEM((rows // 2, width), BF)] * 4
        copies = 6
    else:
        body = functools.partial(scatter_kernel, count)
        scratch = [pltpu.VMEM((count - 1, rows, width), BF)]
        copies = count - 1
    return pl.pallas_call(
        body,
        out_shape=jax.ShapeDtypeStruct((rows, width), F32),
        in_specs=[pl.BlockSpec(memory_space=pltpu.VMEM)],
        out_specs=pl.BlockSpec(memory_space=pltpu.VMEM),
        scratch_shapes=scratch
        + [pltpu.SemaphoreType.DMA((copies,)), pltpu.SemaphoreType.DMA((copies,))],
        compiler_params=pltpu.CompilerParams(
            collective_id=call, has_side_effects=True, vmem_limit_bytes=32 * 1024 * 1024
        ),
        name=f"scatter_seq_{call}",
    )(parts)


class Cut:
    def __init__(self, rows, count):
        self.rows, self.count = rows, count
        self.width = -(-rows // (count * 16)) * 16

    def start(self, piece):
        if isinstance(piece, int):
            return min(piece * self.width, self.rows - self.width)
        return jnp.minimum(piece * self.width, self.rows - self.width)

    def skip(self, piece):
        if isinstance(piece, int):
            return min(piece * self.width - self.start(piece), self.width)
        return jnp.minimum(piece * self.width - self.start(piece), self.width)

    def assemble(self, pieces, axis):
        kept = []
        for k, piece in enumerate(pieces):
            if self.skip(k) < self.width:
                kept.append(lax.slice_in_dim(piece, self.skip(k), self.width, axis=axis))
        return jnp.concatenate(kept, axis=axis)


def columns_of(weight, index, width, padded):
    piece = lax.dynamic_slice_in_dim(weight, index * width, width, axis=1)
    return jnp.pad(piece, ((0, 0), (0, padded - width)))


def on_device(
    layer_input,
    mixer_gain,
    query_weight,
    key_weight,
    value_weight,
    swish_weight,
    output_weight,
    channel_gain,
    gelu_weight,
    linear_weight,
    down_weight,
    output_cotangent,
):
    groups, local_length, width = layer_input.shape
    seq_count = lax.axis_size("seq")
    shards = lax.axis_size("fsdp")
    me = lax.axis_index("seq")
    per_device = HEADS // seq_count
    rows_count = groups * local_length
    length = local_length * seq_count
    key_scale = KEY_HEAD ** (-0.5)
    qk = query_weight.shape[1] // seq_count
    vd = value_weight.shape[1] // seq_count
    vd_pad = -(-vd // 128) * 128
    hidden_units = gelu_weight.shape[1]
    own_rows = down_weight.shape[0]
    cut = Cut(own_rows, seq_count)
    ff = shards * cut.width

    def gather_rows(values):
        return lax.all_gather(values, "fsdp", axis=0, tiled=True)

    def scatter_rows(values):
        return lax.psum_scatter(values.astype(BF), "fsdp", scatter_dimension=0, tiled=True)

    attention_piece = jnp.concatenate(
        [
            columns_of(query_weight, me, qk, qk),
            columns_of(key_weight, me, qk, qk),
            columns_of(value_weight, me, vd, vd_pad),
            columns_of(swish_weight, me, vd, vd_pad),
        ],
        axis=1,
    )
    attention_weight = gather_rows(attention_piece)
    output_piece = lax.dynamic_slice_in_dim(output_weight, cut.start(me), cut.width, axis=0)
    output_pieces = gather_rows(output_piece)
    column = lax.broadcasted_iota(jnp.int32, (hidden_units, ff), 0)
    slot = lax.broadcasted_iota(jnp.int32, (hidden_units, ff), 1)
    chosen = (slot // cut.width) * own_rows + cut.start(me) + slot % cut.width
    selector = (column == chosen).astype(BF)
    gate_piece = product(gelu_weight, selector).astype(BF)
    up_piece = product(linear_weight, selector).astype(BF)
    feed_weight = gather_rows(jnp.concatenate([gate_piece, up_piece], axis=1))
    gate_full, up_full = feed_weight[:, :ff], feed_weight[:, ff:]
    down_piece = lax.dynamic_slice_in_dim(down_weight, cut.start(me), cut.width, axis=0)
    kept_rows = lax.broadcasted_iota(jnp.int32, down_piece.shape, 0) >= cut.skip(me)
    down_full = gather_rows(jnp.where(kept_rows, down_piece, jnp.zeros_like(down_piece)))
    gains = lax.all_gather(jnp.stack([mixer_gain, channel_gain]), "fsdp", axis=1, tiled=True)
    mixer_scale, channel_scale = gains[0].astype(F32), gains[1].astype(F32)

    local_input = layer_input.reshape(rows_count, width)
    upstream = output_cotangent.reshape(rows_count, width)

    def whole(values, call):
        gathered = gather_seq(values, call)
        return gathered.reshape(length * groups, width)

    input_full = whole(local_input, 0)
    upstream_full = whole(upstream, 1)
    inputs = local_input.astype(F32)

    mixed_low = normalize(input_full.astype(F32), mixer_scale).astype(BF)
    projected = product(mixed_low, attention_weight)
    cosine, sine = rotation_tables(length, KEY_HEAD // 2)
    query_low = rotate(projected[:, :qk], cosine, sine).astype(BF)
    key_low = (rotate(projected[:, qk : 2 * qk], cosine, sine) * key_scale).astype(BF)
    value_low = projected[:, 2 * qk : 2 * qk + vd].astype(BF)
    swish_pre = projected[:, 2 * qk + vd_pad : 2 * qk + vd_pad + vd]
    head_ids = me * per_device + jnp.arange(per_device, dtype=jnp.int32)
    masks = decay_mask(head_ids, length)
    weights_low, retained_parts = [], []

    def key_of(values, head):
        return values[:, head * KEY_HEAD : (head + 1) * KEY_HEAD]

    def value_of(values, head):
        return values[:, head * VAL_HEAD : (head + 1) * VAL_HEAD]

    for head in range(per_device):
        scores = times_transposed(key_of(query_low, head), key_of(key_low, head))
        weights_low.append((scores * masks[head]).astype(BF))
        retained_parts.append(product(weights_low[head], value_of(value_low, head)).astype(BF))
    retained = jnp.concatenate(retained_parts, axis=1).astype(F32)
    gated_low = swish_mix(swish_pre, retained).astype(BF)

    blocks = shards // seq_count
    swapped = exchange_seq(output_pieces.reshape(seq_count, blocks, cut.width, width), 2)
    output_full = jnp.concatenate(
        [
            cut.assemble([swapped[piece, block] for piece in range(seq_count)], 0)
            for block in range(blocks)
        ],
        axis=0,
    )
    middle = inputs + scatter_seq(product(gated_low, output_full).astype(BF), 3)

    channel_low = normalize(middle, channel_scale).astype(BF)
    channel_full = whole(channel_low, 4)
    gate_pre = product(channel_full, gate_full)
    up_pre = product(channel_full, up_full)
    hidden_low = gelu_mix(gate_pre, up_pre).astype(BF)
    result = middle + scatter_seq(product(hidden_low, down_full).astype(BF), 5)
    layer_output = result.astype(BF).reshape(groups, local_length, width)

    hidden_grad = times_transposed(upstream_full, down_full)
    _, gelu_back = jax.vjp(gelu_mix, gate_pre, up_pre)
    gate_grad, up_grad = gelu_back(hidden_grad)
    gate_low_grad, up_low_grad = gate_grad.astype(BF), up_grad.astype(BF)
    channel_part = times_transposed(gate_low_grad, gate_full) + times_transposed(
        up_low_grad, up_full
    )
    channel_grad = scatter_seq(channel_part.astype(BF), 6)
    _, channel_back = jax.vjp(normalize, middle, channel_scale)
    middle_local, channel_term = channel_back(channel_grad)
    middle_grad = upstream.astype(F32) + middle_local
    down_share = scatter_rows(transposed_times(hidden_low, upstream_full))
    feed_share = scatter_rows(
        jnp.concatenate(
            [
                transposed_times(channel_full, gate_low_grad).astype(BF),
                transposed_times(channel_full, up_low_grad).astype(BF),
            ],
            axis=1,
        )
    )

    branch_full = whole(middle_grad.astype(BF), 7)
    gated_grad = times_transposed(branch_full, output_full)
    output_term = transposed_times(gated_low, branch_full).astype(BF)
    output_term = output_term.reshape(blocks, own_rows, width)
    output_send = jnp.stack(
        [
            lax.slice_in_dim(output_term, cut.start(k), cut.start(k) + cut.width, axis=1)
            for k in range(seq_count)
        ]
    )
    output_swapped = exchange_seq(output_send, 8)
    output_share = scatter_rows(output_swapped.reshape(shards * cut.width, width))
    _, swish_back = jax.vjp(swish_mix, swish_pre, retained)
    swish_grad, retained_grad = swish_back(gated_grad)
    swish_low_grad = swish_grad.astype(BF)
    retained_low_grad = retained_grad.astype(BF)
    query_parts, key_parts, value_parts = [], [], []
    for head in range(per_device):
        head_grad = value_of(retained_low_grad, head)
        weights_grad = times_transposed(head_grad, value_of(value_low, head))
        value_parts.append(transposed_times(weights_low[head], head_grad).astype(BF))
        score_low = (weights_grad * masks[head]).astype(BF)
        query_parts.append(product(score_low, key_of(key_low, head)).astype(BF))
        key_parts.append(transposed_times(score_low, key_of(query_low, head)).astype(BF))
    query_grad = jnp.concatenate(query_parts, axis=1).astype(F32)
    key_grad = jnp.concatenate(key_parts, axis=1).astype(F32)
    query_pre_grad = rotate(query_grad, cosine, sine, back=True).astype(BF)
    key_pre_grad = (rotate(key_grad, cosine, sine, back=True) * key_scale).astype(BF)
    gap = jnp.zeros((length, vd_pad - vd), BF)
    projected_grad = jnp.concatenate(
        [query_pre_grad, key_pre_grad] + value_parts + [gap, swish_low_grad, gap], axis=1
    )
    attention_share = scatter_rows(transposed_times(mixed_low, projected_grad))
    mixed_grad = scatter_seq(times_transposed(projected_grad, attention_weight).astype(BF), 9)
    _, mixer_back = jax.vjp(normalize, inputs, mixer_scale)
    input_local, mixer_term = mixer_back(mixed_grad)
    input_gradient = (middle_grad + input_local).astype(BF)
    input_gradient = input_gradient.reshape(groups, local_length, width)

    down_all = gather_seq(down_share, 10)
    feed_all = gather_seq(feed_share, 11)
    output_all = gather_seq(output_share, 12)
    attention_all = gather_seq(attention_share, 13)
    down_gradient = cut.assemble([down_all[k] for k in range(seq_count)], 0).astype(F32)
    output_gradient = cut.assemble([output_all[k] for k in range(seq_count)], 0).astype(F32)

    def hidden_order(at):
        pieces = [feed_all[k][:, at : at + ff] for k in range(seq_count)]
        return jnp.concatenate(
            [
                cut.assemble(
                    [piece[:, f * cut.width : (f + 1) * cut.width] for piece in pieces], 1
                )
                for f in range(shards)
            ],
            axis=1,
        ).astype(F32)

    def attention_order(at, wide):
        pieces = [attention_all[k][:, at : at + wide] for k in range(seq_count)]
        return jnp.concatenate(pieces, axis=1).astype(F32)

    gain_terms = lax.psum(jnp.stack([mixer_term, channel_term]), ("seq", "fsdp"))
    own_gain = width // shards
    gain_own = lax.dynamic_slice_in_dim(
        gain_terms, lax.axis_index("fsdp") * own_gain, own_gain, axis=1
    )
    return (
        layer_output,
        input_gradient,
        gain_own[0],
        attention_order(0, qk),
        attention_order(qk, qk),
        attention_order(2 * qk, vd),
        attention_order(2 * qk + vd_pad, vd),
        output_gradient,
        gain_own[1],
        hidden_order(0),
        hidden_order(ff),
        down_gradient,
    )


def solution(mesh):
    tokens, rows, vector = P("fsdp", "seq", None), P("fsdp", None), P("fsdp")
    return jax.shard_map(
        on_device,
        mesh=mesh,
        in_specs=(
            tokens, vector, rows, rows, rows, rows, rows, vector, rows, rows, rows, tokens,
        ),
        out_specs=(
            tokens, tokens, vector, rows, rows, rows, rows, rows, vector, rows, rows, rows,
        ),
        check_vma=False,
    )
```

time: 2510 us -> 919 us (0.37)
  waiting for transfers between devices: 1720 us -> 0.18 us
  Pallas kernels: 0 us -> 492 us
  local copies, waits for them, and re-layouts: 219 us -> 83.8 us
  matrix products: 265 us -> 181 us
  other arithmetic: 153 us -> 83.9 us
  blocking collectives: 98.2 us -> 53.5 us
    reduce_scatter x8 -> x4, waiting for transfers between devices: 915 us -> 0.03 us  [scatter_rows(): lax.psum_scatter(values.astype(BF), 'fsdp', scatter_dimension=0, tiled=True)]
    all_gather x8 -> x4, waiting for transfers between devices: 608 us -> 0.03 us  [gather_rows(): return lax.all_gather(values, 'fsdp', axis=0, tiled=True)]
    pallas_call x0 -> x14, Pallas kernels: none -> 492 us  [the longest x8 270 us: gather_seq(): pl.pallas_call(body, out_shape=jax.ShapeDtypeStruct((count,) + values.sha...]
    psum x1 -> x0, waiting for transfers between devices: 171 us -> none  [on_device(): lax.psum(query_share.astype(jnp.bfloat16), 'seq').astype(jnp.float32)]
    unnamed x8 -> x11, other arithmetic: 101 us -> 15.8 us
    convert_element_type x10 -> x0, local copies, waits for them, and re-layouts: 60.1 us -> none  [the longest x1 11.7 us: on_device(): (rotate(key_pre, cosine_table, sine_table, HEADS) * key_scale).astype(jnp...]
    all_to_all x2 -> x0, blocking collectives: 51.1 us -> none  [the longest x1 26 us: on_device(): lax.all_to_all(retained_low_grad, 'seq', split_axis=2, concat_axis=1, til...]
    dot_general x14 -> x11, matrix products: 112 us -> 65 us  [product(): return jnp.dot(left, right, preferred_element_type=F32)]
  transfers between devices with their start and end apart: 23 -> 8, of which waited for: 18 -> 0; matrix products, arithmetic and copies ran while one was open for 18% -> 30% of each run, Pallas kernels for 0% -> 49%
where the time goes in v1:
time: 919 us; the launch traced here: 912 us
  Pallas kernels  492 us (54%)
  matrix products  181 us (20%)
  other arithmetic  83.9 us (9%)
  local copies, waits for them, and re-layouts  83.8 us (9%)
  blocking collectives  53.5 us (6%)
  between operations  15.9 us (2%)
    pallas_call x8, Pallas kernels, gather_seq(): pl.pallas_call(body, out_shape=jax.ShapeDtypeStruct((count,) + values.sha...  270 us
    pallas_call x4, Pallas kernels, scatter_seq(): pl.pallas_call(body, out_shape=jax.ShapeDtypeStruct((rows, width), F32),...  142 us
    pallas_call x2, Pallas kernels, exchange_seq(): pl.pallas_call(functools.partial(exchange_kernel, count), out_shape=jax.S...  79.4 us
    dot_general x9, matrix products, times_transposed(): lax.dot_general(left, right, (((1,), (1,)), ((), ())), preferred_element_...  68.3 us
    dot_general x11, matrix products, product(): return jnp.dot(left, right, preferred_element_type=F32)  65 us
    dot_general x9, matrix products, transposed_times(): lax.dot_general(left, right, (((0,), (0,)), ((), ())), preferred_element_...  48 us
    unnamed x189, local copies, waits for them, and re-layouts  41.2 us
    psum x1, blocking collectives, on_device(): lax.psum(jnp.stack([mixer_term, channel_term]), ('seq', 'fsdp'))  39.8 us
  transfers between devices with their start and end apart: 8, of which 0 were waited for; matrix products, arithmetic and copies ran while one was open for 30% of the time, Pallas kernels for 49%

profile of v1, /device:TPU:0, one launch (start us, length us, event | category | flops | bytes accessed | tf_op | source)
XLA Modules:
  0.0 911.6 jit_solution(14316018111292856033)
XLA Ops:
  21.4 2.6 maximum_convert_fusion
  24.0 13.6 %all_gather.15 = bf16[2,2048]{1,0:T(2,128)(2,1)S(1)} all-gather(bf16[2,256]{1,0:T(2,128)(2,1)S(1)} %pad_maximum_fusion.11), channel_id=1, replica_groups=mesh['seq'=4,'fsdp'=8] {'fsdp'}, dimensions={1}, use_global_device_ids=true | all-gather | bytes 9216 | tf_op jit(solution)/shard_map/all_gather | solution.py:364
  37.7 38.0 %gather_seq_0.1 = bf16[4,256,2048]{2,1,0:T(8,128)(2,1)} custom-call(bf16[256,2048]{1,0:T(8,128)(2,1)} %bitcast.172), custom_call_target="tpu_custom_call" | custom-call | tf_op jit(solution)/shard_map/gather_seq_0/pallas_call | solution.py:156
  75.8 3.0 convert_reduce_fusion
  80.4 36.3 %gather_seq_1.1 = bf16[4,256,2048]{2,1,0:T(8,128)(2,1)} custom-call(bf16[256,2048]{1,0:T(8,128)(2,1)} %bitcast.174), custom_call_target="tpu_custom_call" | custom-call | tf_op jit(solution)/shard_map/gather_seq_1/pallas_call | solution.py:156
  116.8 4.8 fusion.3
  121.5 4.1 exponential_select_fusion
  125.6 40.9 %exchange_seq_2.1 = bf16[4,2,112,2048]{3,2,1,0:T(8,128)(2,1)} custom-call(bf16[4,2,112,2048]{3,2,1,0:T(8,128)(2,1)} %bitcast.184), custom_call_target="tpu_custom_call" | custom-call | tf_op jit(solution)/shard_map/exchange_seq_2/pallas_call | solution.py:187
  181.1 18.3 %fusion.117 = (bf16[1024,2816]{1,0:T(8,128)(2,1)}, f32[1024,2816]{1,0:T(8,128)S(1)}) fusion(bf16[1024,2048]{1,0:T(8,128)(2,1)} %fusion.3, bf16[2048,2816]{1,0:T(8,128)(2,1)} %all-gather.5.cloned.1.call-done), kind=kOutput, calls=%fused_computation.279 | convolution fusion | flops 11814043648 | bytes 33030144 | tf_op jit(solution)/shard_map/dot_general | solution.py:21
  199.3 4.2 copy-done.18
  204.8 2.0 copy.54
  206.8 2.0 copy.59
  212.5 4.3 subtract_convert_fusion.3
  217.1 3.8 multiply_convert_fusion.2
  221.0 2.1 multiply_convert_fusion.3
  223.1 3.7 convolution_convert_fusion.10
  226.8 4.1 slice.737
  230.9 3.9 copy.52
  234.9 4.3 convolution_convert_fusion.11
  246.1 7.0 convolution_convert_fusion.3
  253.1 36.7 %scatter_seq_3.1 = f32[256,2048]{1,0:T(8,128)S(1)} custom-call(bf16[4,256,2048]{2,1,0:T(8,128)(2,1)S(1)} %bitcast.167), custom_call_target="tpu_custom_call" | custom-call | tf_op jit(solution)/shard_map/scatter_seq_3/pallas_call | solution.py:263
  292.5 35.8 %gather_seq_4.1 = bf16[4,256,2048]{2,1,0:T(8,128)(2,1)} custom-call(bf16[256,2048]{1,0:T(8,128)(2,1)} %multiply_convert_fusion.6.x_ref), custom_call_target="tpu_custom_call" | custom-call | tf_op jit(solution)/shard_map/gather_seq_4/pallas_call | solution.py:156
  328.4 9.6 %fusion.25 = f32[1024,896]{1,0:T(8,128)} fusion(bf16[1024,2048]{1,0:T(8,128)(2,1)} %bitcast.177, bf16[2048,1792]{0,1:T(8,128)(2,1)} %all-gather.9.cloned.1.call-done), kind=kOutput, calls=%fused_computation.68 | convolution fusion | flops 3758096384 | bytes 11534336 | tf_op jit(solution)/shard_map/dot_general | solution.py:21
  338.0 17.9 %fusion.10 = (bf16[1024,896]{1,0:T(8,128)(2,1)}, f32[1024,896]{1,0:T(8,128)}, f32[896,1024]{0,1:T(8,128)}) fusion(f32[1024,896]{1,0:T(8,128)} %fusion.25, bf16[896,2048]{1,0:T(8,128)(2,1)} %all-gather.11.cloned.1.call-done, bf16[1024,2048]{1,0:T(8,128)(2,1)} %bitcast.175), kind=kOutput, calls=%fused_computation.34 | convolution fusion | flops 3818651648 | bytes 20709376 | tf_op jit(solution)/shard_map/dot_general | solution.py:25
  355.9 9.7 %add_convert_fusion.1 = (bf16[1024,896]{1,0:T(8,128)(2,1)}, bf16[1024,896]{1,0:T(8,128)(2,1)S(1)}) fusion(f32[1024,896]{1,0:T(8,128)} %get-tuple-element.27, f32[896,1024]{0,1:T(8,128)} %get-tuple-element.172, f32[1024,896]{1,0:T(8,128)} %fusion.25, bf16[1024,2048]{1,0:T(8,128)(2,1)S(1)} %bitcast.179, bf16[2048,1792]{0,1:T(8,128)(2,1)S(1)} %copy-done.71), kind=kOutput, calls=%fused_computation.35 | convolution fusion | flops 3774611456 | bytes 22544384 | tf_op jit(solution)/shard_map/dot_general | solution.py:21
  366.9 5.5 convolution_convert_fusion.4
  372.6 7.1 convolution_convert_fusion.2
  379.8 35.0 %scatter_seq_5.1 = f32[256,2048]{1,0:T(8,128)S(1)} custom-call(bf16[4,256,2048]{2,1,0:T(8,128)(2,1)S(1)} %bitcast.164), custom_call_target="tpu_custom_call" | custom-call | tf_op jit(solution)/shard_map/scatter_seq_5/pallas_call | solution.py:263
  414.8 6.7 fusion.23
  421.5 6.4 add_convert_fusion
  427.9 34.2 %scatter_seq_6.1 = f32[256,2048]{1,0:T(8,128)S(1)} custom-call(bf16[4,256,2048]{2,1,0:T(8,128)(2,1)S(1)} %bitcast.165), custom_call_target="tpu_custom_call" | custom-call | tf_op jit(solution)/shard_map/scatter_seq_6/pallas_call | solution.py:263
  467.0 34.7 %gather_seq_7.1 = bf16[4,256,2048]{2,1,0:T(8,128)(2,1)} custom-call(bf16[256,2048]{1,0:T(8,128)(2,1)} %fusion.45.x_ref), custom_call_target="tpu_custom_call" | custom-call | tf_op jit(solution)/shard_map/gather_seq_7/pallas_call | solution.py:156
  501.7 6.2 convolution_convert_fusion.7
  508.4 2.1 pad_maximum_fusion.1.x_ref
  510.4 38.5 %exchange_seq_8.1 = bf16[4,2,112,2048]{3,2,1,0:T(8,128)(2,1)} custom-call(bf16[4,2,112,2048]{3,2,1,0:T(8,128)(2,1)} %pad_maximum_fusion.1.x_ref), custom_call_target="tpu_custom_call" | custom-call | tf_op jit(solution)/shard_map/exchange_seq_8/pallas_call | solution.py:187
  549.0 7.5 convolution_convert_fusion.6
  556.6 6.0 convolution_convert_fusion.5
  562.6 5.5 pad_maximum_fusion
  568.6 8.8 fusion.71
  583.1 2.7 multiply_convert_fusion.1
  586.5 3.0 multiply_convert_fusion
  592.4 3.1 fusion.78
  595.5 2.9 fusion.79
  598.4 2.9 fusion.80
  601.4 2.9 fusion.81
  604.3 2.4 multiply_add_fusion.1
  613.1 2.6 fusion.40
  616.3 17.2 %convolution_convert_fusion = bf16[2048,2816]{1,0:T(8,128)(2,1)} fusion(bf16[1024,2048]{1,0:T(8,128)(2,1)S(1)} %copy-done.24, bf16[1024,2816]{0,1:T(8,128)(2,1)} %constant_dynamic-update-slice_fusion), kind=kOutput, calls=%fused_computation.2 | convolution fusion | flops 11816927232 | bytes 21495808 | tf_op jit(solution)/shard_map/dot_general | solution.py:29
  633.5 17.0 %convolution_convert_fusion.1 = bf16[1024,2048]{1,0:T(8,128)(2,1)S(1)} fusion(bf16[1024,2816]{0,1:T(8,128)(2,1)} %constant_dynamic-update-slice_fusion, bf16[2048,2816]{1,0:T(8,128)(2,1)} %all-gather.5.cloned.1.call-done), kind=kOutput, calls=%fused_computation.27 | convolution fusion | flops 11813257216 | bytes 21495808 | tf_op jit(solution)/shard_map/dot_general | solution.py:25
  650.6 36.6 %scatter_seq_9.1 = f32[256,2048]{1,0:T(8,128)S(1)} custom-call(bf16[4,256,2048]{2,1,0:T(8,128)(2,1)S(1)} %bitcast.166), custom_call_target="tpu_custom_call" | custom-call | tf_op jit(solution)/shard_map/scatter_seq_9/pallas_call | solution.py:263
  688.9 39.8 %psum.7 = f32[2,2048]{1,0:T(2,128)S(1)} all-reduce(f32[2,2048]{1,0:T(2,128)S(1)} %pad_maximum_fusion.10), channel_id=1, replica_groups=mesh['seq'=4,'fsdp'=8] {'seq','fsdp'}, use_global_device_ids=true, to_apply=%region_20.21 | all-reduce | flops 4096 | bytes 32768 | tf_op jit(solution)/shard_map/psum | solution.py:505
  729.3 3.8 fusion.61
  733.1 23.5 %gather_seq_10.1 = bf16[4,112,2048]{2,1,0:T(8,128)(2,1)} custom-call(bf16[112,2048]{1,0:T(8,128)(2,1)} %reduce-scatter.11.cloned.1.call-done.x_ref), custom_call_target="tpu_custom_call" | custom-call | tf_op jit(solution)/shard_map/gather_seq_10/pallas_call | solution.py:156
  756.7 22.7 %gather_seq_12.1 = bf16[4,112,2048]{2,1,0:T(8,128)(2,1)} custom-call(bf16[112,2048]{1,0:T(8,128)(2,1)} %reduce-scatter.7.cloned.1.call-done.x_ref), custom_call_target="tpu_custom_call" | custom-call | tf_op jit(solution)/shard_map/gather_seq_12/pallas_call | solution.py:156
  780.6 2.2 maximum_convert_fusion.3
  783.0 2.2 maximum_convert_fusion.2
  785.2 31.7 %gather_seq_11.1 = bf16[4,256,1792]{2,1,0:T(8,128)(2,1)} custom-call(bf16[256,1792]{1,0:T(8,128)(2,1)} %reduce-scatter.9.cloned.1.call-done.x_ref), custom_call_target="tpu_custom_call" | custom-call | tf_op jit(solution)/shard_map/gather_seq_11/pallas_call | solution.py:156
  816.9 2.2 slice_bitcast_fusion.10
  823.7 3.1 concatenate.87
  828.9 2.8 concatenate.88
  833.7 47.6 %gather_seq_13.1 = bf16[4,256,2816]{2,1,0:T(8,128)(2,1)} custom-call(bf16[256,2816]{1,0:T(8,128)(2,1)} %reduce-scatter.5.cloned.1.call-done.x_ref), custom_call_target="tpu_custom_call" | custom-call | tf_op jit(solution)/shard_map/gather_seq_13/pallas_call | solution.py:156
  881.4 3.0 slice_bitcast_fusion.5
  891.3 2.8 concatenate.83
  896.1 3.1 concatenate.84
  (305 shorter events, 94.8 us)
Async XLA Ops:
  7.2 118.4 %all-gather.7.cloned.1.call-start = ((), (), s32[]{:S(2)}) async-start(), calls=%async_computation.5 | async-start | bytes 4128768 | tf_op jit(solution)/shard_map/all_gather | solution.py:336
  9.6 171.5 %all-gather.5.cloned.1.call-start = ((), (), s32[]{:S(2)}) async-start(), calls=%async_computation.4 | async-start | bytes 12976128 | tf_op jit(solution)/shard_map/all_gather | solution.py:336
  9.6 4.4 copy-start.72
  13.9 314.5 %all-gather.9.cloned.1.call-start = ((), (), s32[]{:S(2)}) async-start(), calls=%async_computation.6 | async-start | bytes 8257536 | tf_op jit(solution)/shard_map/all_gather | solution.py:336
  18.8 5.1 copy-start.74
  18.8 5.2 copy-start.75
  18.8 319.2 %all-gather.11.cloned.1.call-start = ((), (), s32[]{:S(2)}) async-start(), calls=%async_computation.7 | async-start | bytes 4128768 | tf_op jit(solution)/shard_map/all_gather | solution.py:336
  20.9 712.1 %reduce-scatter.11.cloned.1.call-start = ((), (), s32[]{:S(2)}) async-start(), calls=%async_computation.11 | async-start | bytes 4128768 | tf_op jit(solution)/shard_map/reduce_scatter | solution.py:339
  21.0 191.4 %copy-start.66 = (f32[128]{0:T(128)}, f32[128]{0:T(128)S(1)}, u32[]{:S(2)}) copy-start(f32[128]{0:T(128)S(1)} %multiply_exponential_fusion) | copy-start | bytes 1540
  37.7 79.1 %copy-start.52 = (f32[1,2048]{1,0:T(1,128)}, f32[1,2048]{1,0:T(1,128)S(1)}, u32[]{:S(2)}) copy-start(f32[1,2048]{1,0:T(1,128)S(1)} %get-tuple-element.159) | copy-start | bytes 24580
  75.7 3.5 copy-start.4
  116.8 4.8 copy-start.10
  199.3 4.2 copy-start.18
  209.8 2.6 copy-start.28
  212.5 8.5 slice-start
  216.8 4.1 copy-start.40
  216.8 4.1 copy-start.42
  216.8 4.2 copy-start.44
  216.8 4.2 copy-start.46
  216.8 4.2 slice-start.1
  217.1 3.9 copy-start.19
  220.9 2.2 copy-start.25
  234.9 7.1 copy-start.5
  234.9 4.3 copy-start.48
  253.0 36.7 %copy-start.7 = (bf16[1,256,2048]{2,1,0:T(8,128)(2,1)S(1)}, bf16[1,256,2048]{2,1,0:T(8,128)(2,1)}, u32[]{:S(2)}) copy-start(bf16[1,256,2048]{2,1,0:T(8,128)(2,1)} %param.12) | copy-start | bytes 3145732
  338.0 17.9 %copy-start.22 = (bf16[4,256,2048]{2,1,0:T(8,128)(2,1)S(1)}, bf16[4,256,2048]{2,1,0:T(8,128)(2,1)}, u32[]{:S(2)}) copy-start(bf16[4,256,2048]{2,1,0:T(8,128)(2,1)} %gather_seq_4.1) | copy-start | bytes 12582916
  338.0 17.9 %copy-start.71 = (bf16[2048,1792]{0,1:T(8,128)(2,1)S(1)}, bf16[2048,1792]{0,1:T(8,128)(2,1)}, u32[]{:S(2)}) copy-start(bf16[2048,1792]{0,1:T(8,128)(2,1)} %all-gather.9.cloned.1.call-done) | copy-start | bytes 22020100
  355.9 11.0 %copy-start.21 = (bf16[4,256,2048]{2,1,0:T(8,128)(2,1)S(1)}, bf16[4,256,2048]{2,1,0:T(8,128)(2,1)}, u32[]{:S(2)}) copy-start(bf16[4,256,2048]{2,1,0:T(8,128)(2,1)} %gather_seq_1.1) | copy-start | bytes 12582916
  372.4 384.2 %reduce-scatter.7.cloned.1.call-start = ((), (), s32[]{:S(2)}) async-start(), calls=%async_computation.9 | async-start | bytes 4128768 | tf_op jit(solution)/shard_map/reduce_scatter | solution.py:339
  379.7 35.0 %copy-start.77 = (bf16[1024,896]{1,0:T(8,128)(2,1)S(1)}, bf16[1024,896]{1,0:T(8,128)(2,1)}, u32[]{:S(2)}) copy-start(bf16[1024,896]{1,0:T(8,128)(2,1)} %get-tuple-element.38) | copy-start | bytes 5505028
  379.7 41.7 %slice-start.4 = ((s8[7340032]{0:T(1024)(128)(4,1)}), s8[4194304]{0:T(1024)(128)(4,1)S(1)}, s32[]{:S(2)}) async-start(s8[7340032]{0:T(1024)(128)(4,1)} %bitcast.198), calls=%async_computation.16 | async-start | bytes 8388608
  414.7 6.7 slice-start.5
  462.7 3.0 copy-start.15
  467.0 34.7 %copy-start.31 = (bf16[1024,864]{0,1:T(8,128)(2,1)S(1)}, bf16[1024,864]{0,1:T(8,128)(2,1)}, u32[]{:S(2)}) copy-start(bf16[1024,864]{0,1:T(8,128)(2,1)} %copy-done.30) | copy-start | bytes 5308420
  549.0 236.2 %reduce-scatter.9.cloned.1.call-start = ((), (), s32[]{:S(2)}) async-start(), calls=%async_computation.10 | async-start | bytes 8257536 | tf_op jit(solution)/shard_map/reduce_scatter | solution.py:339
  549.0 7.5 copy-start.23
  549.0 7.5 copy-start.78
  568.2 9.3 %copy-start.3 = (f32[1024,864]{0,1:T(8,128)S(1)}, f32[1024,864]{0,1:T(8,128)}, u32[]{:S(2)}) copy-start(f32[1024,864]{0,1:T(8,128)} %copy-done.2) | copy-start | bytes 10616836
  568.2 9.3 %copy-start.57 = (f32[1024]{0:T(1024)S(1)}, f32[1024]{0:T(1024)}, u32[]{:S(2)}) copy-start(f32[1024]{0:T(1024)} %copy-done.56) | copy-start | bytes 12292
  568.2 265.6 %reduce-scatter.5.cloned.1.call-start = ((), (), s32[]{:S(2)}) async-start(), calls=%async_computation.8 | async-start | bytes 12976128 | tf_op jit(solution)/shard_map/reduce_scatter | solution.py:339
  579.5 2.2 slice-start.2
  579.5 3.5 slice-start.3
  583.1 2.7 copy-start.20
  604.3 3.7 copy-start.27
  608.0 4.7 copy-start.14
  610.1 2.7 copy-start.6
  610.1 3.0 copy-start.12
  613.1 3.2 copy-start.24
  650.6 36.6 %copy-start.70 = (f32[256]{0:T(256)S(1)}, f32[256]{0:T(256)}, u32[]{:S(2)}) copy-start(f32[256]{0:T(256)} %get-tuple-element.91) | copy-start | bytes 3076
  650.6 36.6 %copy-start.8 = (bf16[1,256,2048]{2,1,0:T(8,128)(2,1)S(1)}, bf16[1,256,2048]{2,1,0:T(8,128)(2,1)}, u32[]{:S(2)}) copy-start(bf16[1,256,2048]{2,1,0:T(8,128)(2,1)} %param.12) | copy-start | bytes 3145732
  650.6 36.6 %copy-start.53 = (f32[1,2048]{1,0:T(1,128)S(1)}, f32[1,2048]{1,0:T(1,128)}, u32[]{:S(2)}) copy-start(f32[1,2048]{1,0:T(1,128)} %copy-done.52) | copy-start | bytes 24580
  687.2 42.1 %copy-start.69 = (f32[256]{0:T(256)S(1)}, f32[256]{0:T(256)}, u32[]{:S(2)}) copy-start(f32[256]{0:T(256)} %copy-done.68) | copy-start | bytes 3076
  756.6 23.8 %copy-start.17 = (bf16[4,112,2048]{2,1,0:T(8,128)(2,1)S(1)}, bf16[4,112,2048]{2,1,0:T(8,128)(2,1)}, u32[]{:S(2)}) copy-start(bf16[4,112,2048]{2,1,0:T(8,128)(2,1)} %gather_seq_10.1) | copy-start | bytes 5505028
  780.4 2.4 copy-start.16
  826.9 2.1 copy-start.49
  899.2 2.1 copy-start.34
  899.2 2.1 copy-start.36
  899.2 2.1 copy-start.37
  899.2 2.1 copy-start.39
  899.3 3.7 copy-start.32
  899.3 3.7 copy-start.33
  899.3 3.7 copy-start.35
  899.3 3.6 copy-start.38
  899.3 5.2 copy-start.1
  (29 other events, 38.5 us)
Sparse Core Ops, SparseCore 0:
  10.2 45.5 all-gather.6
  58.0 106.9 all-gather.4
  167.2 72.1 all-gather.8
  241.4 40.7 all-gather.10
  372.5 42.5 reduce-scatter.10
  549.1 43.4 reduce-scatter.6
  594.9 78.0 reduce-scatter.8
  675.3 118.7 reduce-scatter.4

commit v2 on v1

--- a/solution.py
+++ b/solution.py
@@ -35,51 +35,249 @@
     return centered * spread * gain
 
 
-def group_norm_head(values):
-    centered = values - jnp.mean(values, axis=-1, keepdims=True)
-    return centered * lax.rsqrt(
-        jnp.maximum(jnp.mean(centered * centered, axis=-1, keepdims=True), 1.0)
-    )
-
-
-def swish_mix(swish_value, retained_value):
-    parts = [
-        group_norm_head(retained_value[:, at : at + VAL_HEAD])
-        for at in range(0, retained_value.shape[1], VAL_HEAD)
-    ]
-    return jax.nn.silu(swish_value) * jnp.concatenate(parts, axis=-1)
-
-
-def gelu_mix(gate_value, up_value):
-    return jax.nn.gelu(gate_value, approximate=False) * up_value
-
-
 def rotation_tables(length, half_width):
     rates = jnp.exp(-math.log(10000.0) * jnp.arange(half_width, dtype=F32) / (half_width - 1))
     turned = jnp.arange(length, dtype=F32)[:, None] * rates[None, :]
     return (jnp.cos(turned), jnp.sin(turned))
 
 
-def rotate(values, cosine, sine, back=False):
+def pad_lanes(pieces, width):
+    have = sum(piece.shape[1] for piece in pieces)
+    if have < width:
+        pieces = pieces + [jnp.zeros((pieces[0].shape[0], width - have), pieces[0].dtype)]
+    return jnp.concatenate(pieces, axis=1) if len(pieces) > 1 else pieces[0]
+
+
+def rotate_pair(values, cosine, sine, back=False):
     half = KEY_HEAD // 2
-    pieces = []
-    for at in range(0, values.shape[1], KEY_HEAD):
-        first = values[:, at : at + half]
-        second = values[:, at + half : at + KEY_HEAD]
-        if back:
-            pieces += [first * cosine + second * sine, second * cosine - first * sine]
-        else:
-            pieces += [first * cosine - second * sine, second * cosine + first * sine]
-    return jnp.concatenate(pieces, axis=-1)
-
-
-def decay_mask(head_ids, length):
-    rates = jnp.log1p(-jnp.exp2(-5.0 - head_ids.astype(F32)))
-    row_gaps = (
-        jnp.arange(length, dtype=jnp.int32)[:, None] - jnp.arange(length, dtype=jnp.int32)[None, :]
-    )
-    gaps = jnp.maximum(row_gaps, 0).astype(F32)
-    return jnp.where(row_gaps[None] >= 0, jnp.exp(gaps[None] * rates[:, None, None]), 0.0)
+    first, second = values[:, :half], values[:, half:]
+    if back:
+        return jnp.concatenate([first * cosine + second * sine, second * cosine - first * sine], 1)
+    return jnp.concatenate([first * cosine - second * sine, second * cosine + first * sine], 1)
+
+
+BLOCK = 256
+
+
+def head_rate(head):
+    ids = jnp.full((1, 1), head, jnp.int32).astype(F32)
+    return jnp.log1p(-jnp.exp2(-5.0 - ids))
+
+
+def decay_tile(rate):
+    gap = lax.broadcasted_iota(jnp.int32, (BLOCK, BLOCK), 0) - lax.broadcasted_iota(
+        jnp.int32, (BLOCK, BLOCK), 1
+    )
+    full = jnp.exp(gap.astype(F32) * rate)
+    return full, jnp.where(gap >= 0, full, 0.0)
+
+
+def norm_parts(values):
+    centered = values - jnp.mean(values, axis=-1, keepdims=True)
+    variance = jnp.mean(centered * centered, axis=-1, keepdims=True)
+    factor = lax.rsqrt(jnp.maximum(variance, 1.0))
+    return centered * factor, factor, variance > 1.0
+
+
+def rows_of(block):
+    return pl.ds(pl.multiple_of(block * BLOCK, BLOCK), BLOCK)
+
+
+def retention_kernel(
+    heads, offsets, x_ref, gain_ref, w_ref, cos_ref, sin_ref,
+    mixed_ref, q_ref, k_ref, v_ref, swish_ref, retained_ref, gated_ref,
+):
+    first_head = lax.axis_index("seq") * heads
+    at_key, at_value, at_swish = offsets
+    value_width = heads * VAL_HEAD
+    blocks = x_ref.shape[0] // BLOCK
+    rates = [head_rate(first_head + h) for h in range(heads)]
+
+    @pl.loop(0, blocks)
+    def _(i):
+        rows = rows_of(i)
+        x = x_ref[rows, :].astype(F32)
+        mixed = normalize(x, gain_ref[...]).astype(BF)
+        mixed_ref[rows, :] = mixed
+        cosine, sine = cos_ref[rows, :], sin_ref[rows, :]
+        query = product(mixed, w_ref[:, :at_key])
+        for h in range(heads):
+            lanes = slice(h * KEY_HEAD, (h + 1) * KEY_HEAD)
+            q_ref[rows, lanes] = rotate_pair(query[:, lanes], cosine, sine).astype(BF)
+        key = product(mixed, w_ref[:, at_key:at_value])
+        for h in range(heads):
+            lanes = slice(h * KEY_HEAD, (h + 1) * KEY_HEAD)
+            turned = rotate_pair(key[:, lanes], cosine, sine) * (KEY_HEAD**-0.5)
+            k_ref[rows, lanes] = turned.astype(BF)
+        value = product(mixed, w_ref[:, at_value:at_swish])
+        for h in range(heads):
+            v_ref[h, rows, :] = value[:, h * VAL_HEAD : (h + 1) * VAL_HEAD].astype(BF)
+        swish = product(mixed, w_ref[:, at_swish:])[:, :value_width]
+        swish_ref[rows, :] = swish
+
+        gated = []
+        for h in range(heads):
+            lanes = slice(h * KEY_HEAD, (h + 1) * KEY_HEAD)
+            full, lower = decay_tile(rates[h])
+            q = q_ref[rows, lanes]
+            scores = times_transposed(q, k_ref[rows, lanes])
+            total = product((scores * lower).astype(BF), v_ref[h, rows, :])
+
+            def earlier(j, total):
+                there = rows_of(j)
+                scores = times_transposed(q, k_ref[there, lanes])
+                far = jnp.exp(rates[h] * ((i - j) * BLOCK).astype(F32))
+                return total + product((scores * (full * far)).astype(BF), v_ref[h, there, :])
+
+            total = lax.fori_loop(0, i, earlier, total)
+            retained = total.astype(BF)
+            retained_ref[h, rows, :] = retained
+            unit, _, _ = norm_parts(retained.astype(F32))
+            s = swish[:, h * VAL_HEAD : (h + 1) * VAL_HEAD]
+            gated.append((s * jax.nn.sigmoid(s) * unit).astype(BF))
+        gated_ref[rows, :] = jnp.concatenate(gated, axis=1) if heads > 1 else gated[0]
+
+
+def vmem_call(body, out_shapes, scratch, limit, cost, name):
+    return pl.pallas_call(
+        body,
+        out_shape=out_shapes,
+        scratch_shapes=scratch,
+        compiler_params=pltpu.CompilerParams(vmem_limit_bytes=limit * 1024 * 1024),
+        cost_estimate=pl.CostEstimate(flops=cost, bytes_accessed=0, transcendentals=0),
+        name=name,
+    )
+
+
+def retention_forward(x, gain, weight, cosine, sine, heads, offsets):
+    length, width = x.shape
+    qk, vd = heads * KEY_HEAD, heads * VAL_HEAD
+    return vmem_call(
+        functools.partial(retention_kernel, heads, offsets),
+        (
+            jax.ShapeDtypeStruct((length, width), BF),
+            jax.ShapeDtypeStruct((length, qk), BF),
+            jax.ShapeDtypeStruct((length, qk), BF),
+            jax.ShapeDtypeStruct((heads, length, VAL_HEAD), BF),
+            jax.ShapeDtypeStruct((length, vd), F32),
+            jax.ShapeDtypeStruct((heads, length, VAL_HEAD), BF),
+            jax.ShapeDtypeStruct((length, vd), BF),
+        ),
+        [],
+        56,
+        30_000_000_000,
+        "retention",
+    )(x, gain, weight, cosine, sine)
+
+
+def gate_back_kernel(heads, branch_ref, w_ref, swish_ref, retained_ref, dswish_ref, dret_ref):
+    blocks = branch_ref.shape[0] // BLOCK
+
+    @pl.loop(0, blocks)
+    def _(i):
+        rows = rows_of(i)
+        gated_grad = times_transposed(branch_ref[rows, :], w_ref[...])
+        swish_parts = []
+        for h in range(heads):
+            lanes = slice(h * VAL_HEAD, (h + 1) * VAL_HEAD)
+            grad, s = gated_grad[:, lanes], swish_ref[rows, lanes]
+            gate = jax.nn.sigmoid(s)
+            unit, factor, above = norm_parts(retained_ref[h, rows, :].astype(F32))
+            swish_parts.append((grad * unit * (gate * (1.0 + s * (1.0 - gate)))).astype(BF))
+            g = grad * (s * gate)
+            along = jnp.where(above, jnp.mean(g * unit, axis=-1, keepdims=True), 0.0)
+            back = factor * (g - jnp.mean(g, axis=-1, keepdims=True) - unit * along)
+            dret_ref[h, rows, :] = back.astype(BF)
+        dswish_ref[rows, :] = pad_lanes(swish_parts, dswish_ref.shape[1])
+
+
+def gate_backward(branch, weight, swish, retained, heads, padded):
+    length = branch.shape[0]
+    return vmem_call(
+        functools.partial(gate_back_kernel, heads),
+        (
+            jax.ShapeDtypeStruct((length, padded), BF),
+            jax.ShapeDtypeStruct((heads, length, VAL_HEAD), BF),
+        ),
+        [],
+        48,
+        12_000_000_000,
+        "gate_back",
+    )(branch, weight, swish, retained)
+
+
+def retention_back_kernel(
+    heads, q_ref, k_ref, v_ref, dret_ref, cos_ref, sin_ref, dqk_ref, dv_ref, dq_sum, dv_sum
+):
+    first_head = lax.axis_index("seq") * heads
+    blocks = q_ref.shape[0] // BLOCK
+    qk = heads * KEY_HEAD
+    dq_sum[...] = jnp.zeros_like(dq_sum)
+    for h in range(heads):
+        rate = head_rate(first_head + h)
+        lanes = slice(h * KEY_HEAD, (h + 1) * KEY_HEAD)
+
+        @pl.loop(0, blocks)
+        def _(j):
+            there = rows_of(j)
+            full, lower = decay_tile(rate)
+            key, value = k_ref[there, lanes], v_ref[h, there, :]
+
+            def step(i, decay, sums):
+                rows = rows_of(i)
+                query, grad = q_ref[rows, lanes], dret_ref[h, rows, :]
+                weights = (times_transposed(query, key) * decay).astype(BF)
+                score = (times_transposed(grad, value) * decay).astype(BF)
+                dq_sum[rows, lanes] += product(score, key)
+                return (
+                    sums[0] + transposed_times(score, query),
+                    sums[1] + transposed_times(weights, grad),
+                )
+
+            sums = (jnp.zeros((BLOCK, KEY_HEAD), F32), jnp.zeros((BLOCK, VAL_HEAD), F32))
+            sums = step(j, lower, sums)
+
+            def later(i, sums):
+                return step(i, full * jnp.exp(rate * ((i - j) * BLOCK).astype(F32)), sums)
+
+            dk, dv = lax.fori_loop(j + 1, blocks, later, sums)
+            dk = rotate_pair(
+                dk.astype(BF).astype(F32), cos_ref[there, :], sin_ref[there, :], back=True
+            )
+            dqk_ref[there, qk + h * KEY_HEAD : qk + (h + 1) * KEY_HEAD] = (
+                dk * (KEY_HEAD**-0.5)
+            ).astype(BF)
+            dv_sum[h, there, :] = dv.astype(BF)
+
+    @pl.loop(0, blocks)
+    def _(i):
+        rows = rows_of(i)
+        cosine, sine = cos_ref[rows, :], sin_ref[rows, :]
+        for h in range(heads):
+            lanes = slice(h * KEY_HEAD, (h + 1) * KEY_HEAD)
+            dq = dq_sum[rows, lanes].astype(BF).astype(F32)
+            dqk_ref[rows, lanes] = rotate_pair(dq, cosine, sine, back=True).astype(BF)
+        dv_ref[rows, :] = pad_lanes([dv_sum[h, rows, :] for h in range(heads)], dv_ref.shape[1])
+
+
+def retention_backward(q, k, v, dret, cosine, sine, heads, padded):
+    length = q.shape[0]
+    qk = heads * KEY_HEAD
+    return vmem_call(
+        functools.partial(retention_back_kernel, heads),
+        (
+            jax.ShapeDtypeStruct((length, 2 * qk), BF),
+            jax.ShapeDtypeStruct((length, padded), BF),
+        ),
+        [pltpu.VMEM((length, qk), F32), pltpu.VMEM((heads, length, VAL_HEAD), BF)],
+        48,
+        12_000_000_000,
+        "retention_back",
+    )(q, k, v, dret, cosine, sine)
+
+
+def transfer_cost(elements):
+    return pl.CostEstimate(flops=0, bytes_accessed=elements * 240, transcendentals=0)
 
 
 def greet(peers):
@@ -164,6 +362,7 @@
             pltpu.SemaphoreType.DMA,
         ],
         compiler_params=pltpu.CompilerParams(collective_id=call, has_side_effects=True),
+        cost_estimate=transfer_cost(values.size),
         name=f"gather_seq_{call}",
     )(values)
 
@@ -195,6 +394,7 @@
             pltpu.SemaphoreType.DMA,
         ],
         compiler_params=pltpu.CompilerParams(collective_id=call, has_side_effects=True),
+        cost_estimate=transfer_cost(values.size),
         name=f"exchange_seq_{call}",
     )(values)
 
@@ -270,8 +470,552 @@
         compiler_params=pltpu.CompilerParams(
             collective_id=call, has_side_effects=True, vmem_limit_bytes=32 * 1024 * 1024
         ),
+        cost_estimate=transfer_cost(rows * width),
         name=f"scatter_seq_{call}",
     )(parts)
+
+
+def feed_forward_kernel(ff, x_ref, w_ref, gate_ref, up_ref, hidden_ref):
+    both = product(x_ref[...], w_ref[...])
+    gate, up = both[:, :ff], both[:, ff:]
+    gate_ref[...] = gate
+    up_ref[...] = up
+    hidden_ref[...] = (gate * (0.5 + 0.5 * lax.erf(gate * math.sqrt(0.5))) * up).astype(BF)
+
+
+def feed_back_kernel(
+    ff, c_ref, gate_ref, up_ref, hidden_ref, w_ref, down_ref, both_ref, part_ref, out_ref
+):
+    gate, up = gate_ref[...], up_ref[...]
+    out_ref[...] = product(hidden_ref[...], down_ref[...]).astype(BF)
+    hidden_grad = times_transposed(c_ref[...], down_ref[...])
+    bell = 0.5 + 0.5 * lax.erf(gate * math.sqrt(0.5))
+    slope = bell + gate * (math.sqrt(0.5 / math.pi) * jnp.exp(-0.5 * gate * gate))
+    both = jnp.concatenate([hidden_grad * up * slope, hidden_grad * (gate * bell)], axis=1)
+    both = both.astype(BF)
+    both_ref[...] = both
+    part_ref[...] = times_transposed(both, w_ref[...]).astype(BF)
+
+
+def by_rows(block, width):
+    return pl.BlockSpec((block, width), lambda i: (i, 0))
+
+
+def kept(shape):
+    return pl.BlockSpec(shape, lambda i: (0, 0), pipeline_mode=pl.Buffered(1))
+
+
+FEED_BLOCK = 256
+
+
+def feed_forward(x, weight):
+    length, width = x.shape
+    ff = weight.shape[1] // 2
+    return pl.pallas_call(
+        functools.partial(feed_forward_kernel, ff),
+        grid=(length // FEED_BLOCK,),
+        in_specs=[by_rows(FEED_BLOCK, width), kept(weight.shape)],
+        out_specs=[by_rows(FEED_BLOCK, ff)] * 3,
+        out_shape=(
+            jax.ShapeDtypeStruct((length, ff), F32),
+            jax.ShapeDtypeStruct((length, ff), F32),
+            jax.ShapeDtypeStruct((length, ff), BF),
+        ),
+        compiler_params=pltpu.CompilerParams(vmem_limit_bytes=48 * 1024 * 1024),
+        cost_estimate=pl.CostEstimate(
+            flops=4 * length * width * ff, bytes_accessed=weight.size * 4, transcendentals=0
+        ),
+        name="feed_forward",
+    )(x, weight)
+
+
+def feed_backward(cotangent, gate, up, hidden, weight, down):
+    length, width = cotangent.shape
+    ff = weight.shape[1] // 2
+    return pl.pallas_call(
+        functools.partial(feed_back_kernel, ff),
+        grid=(length // FEED_BLOCK,),
+        in_specs=[by_rows(FEED_BLOCK, width)]
+        + [by_rows(FEED_BLOCK, ff)] * 3
+        + [kept(weight.shape), kept(down.shape)],
+        out_specs=[
+            by_rows(FEED_BLOCK, 2 * ff),
+            by_rows(FEED_BLOCK, width),
+            by_rows(FEED_BLOCK, width),
+        ],
+        out_shape=(
+            jax.ShapeDtypeStruct((length, 2 * ff), BF),
+            jax.ShapeDtypeStruct((length, width), BF),
+            jax.ShapeDtypeStruct((length, width), BF),
+        ),
+        compiler_params=pltpu.CompilerParams(vmem_limit_bytes=56 * 1024 * 1024),
+        cost_estimate=pl.CostEstimate(
+            flops=8 * length * width * ff, bytes_accessed=weight.size * 4, transcendentals=0
+        ),
+        name="feed_back",
+    )(cotangent, gate, up, hidden, weight, down)
+
+
+def square_parts(parts, boxes, sends, recvs, first):
+    me = lax.axis_index("seq")
+    across, along = me ^ 1, me ^ 2
+    inbox_x, inbox_y, via_x, via_y, out_x, out_y = boxes
+    half = via_x.shape[0]
+    low, high = pl.ds(0, half), pl.ds(half, half)
+    copies = [
+        remote(parts.at[3, low], via_x, sends, recvs, first, across),
+        remote(parts.at[3, high], via_y, sends, recvs, first + 1, along),
+        remote(parts.at[1, low], inbox_x.at[low], sends, recvs, first + 2, across),
+        remote(parts.at[2, high], inbox_y.at[high], sends, recvs, first + 3, along),
+        remote(out_y, inbox_y.at[low], sends, recvs, first + 4, along),
+        remote(out_x, inbox_x.at[high], sends, recvs, first + 5, across),
+    ]
+
+    def finish():
+        copies[0].wait_recv()
+        out_y[...] = (parts[2, :half].astype(F32) + via_x[...].astype(F32)).astype(BF)
+        copies[4].start()
+        copies[1].wait_recv()
+        out_x[...] = (parts[1, half:].astype(F32) + via_y[...].astype(F32)).astype(BF)
+        copies[5].start()
+        for copy in copies[2:]:
+            copy.wait_recv()
+
+    def total(rows):
+        return (
+            parts[0, rows].astype(F32)
+            + inbox_x[rows, :].astype(F32)
+            + inbox_y[rows, :].astype(F32)
+        )
+
+    return copies, finish, total
+
+
+def square_gather(own, out_ref, sends, recvs, first):
+    me = lax.axis_index("seq")
+    across, along = me ^ 1, me ^ 2
+    half = own.shape[0] // 2
+
+    def part(ref, i):
+        return ref.at[pl.ds(i * half, half)]
+
+    copies = [
+        remote(part(own, 0), part(out_ref.at[me], 0), sends, recvs, first, across),
+        remote(part(own, 1), part(out_ref.at[me], 1), sends, recvs, first + 1, along),
+        remote(part(own, 1), part(out_ref.at[me], 1), sends, recvs, first + 2, across),
+        remote(part(own, 0), part(out_ref.at[me], 0), sends, recvs, first + 3, along),
+        remote(
+            part(out_ref.at[across], 0), part(out_ref.at[across], 0), sends, recvs, first + 4, along
+        ),
+        remote(
+            part(out_ref.at[along], 1), part(out_ref.at[along], 1), sends, recvs, first + 5, across
+        ),
+    ]
+
+    def finish():
+        copies[0].wait_recv()
+        copies[4].start()
+        copies[1].wait_recv()
+        copies[5].start()
+        for copy in copies[2:]:
+            copy.wait_recv()
+
+    return copies, finish
+
+
+def block_rows(k, rows):
+    return pl.ds(pl.multiple_of((lax.axis_index("seq") ^ k) * rows, rows), rows)
+
+
+def project_kernel(
+    g_ref, w_ref, x_ref, gain_ref, middle_ref, full_ref,
+    parts, inbox_x, inbox_y, via_x, via_y, out_x, out_y, own, sends, recvs, local,
+):
+    me = lax.axis_index("seq")
+    rows = x_ref.shape[0]
+    half = rows // 2
+    greet((me ^ 1, me ^ 2))
+    boxes = (inbox_x, inbox_y, via_x, via_y, out_x, out_y)
+    copies, finish, total = square_parts(parts, boxes, sends, recvs, 0)
+
+    def part(k):
+        parts[k] = product(g_ref[block_rows(k, rows), :], w_ref[...]).astype(BF)
+
+    part(3)
+    copies[0].start()
+    copies[1].start()
+    part(1)
+    copies[2].start()
+    part(2)
+    copies[3].start()
+    part(0)
+    finish()
+    spread, finish_gather = square_gather(own, full_ref, sends, recvs, 6)
+    for i in range(2):
+        here = slice(i * half, (i + 1) * half)
+        middle = x_ref[here, :].astype(F32) + total(here)
+        middle_ref[here, :] = middle
+        own[here, :] = normalize(middle, gain_ref[...]).astype(BF)
+        spread[i].start()
+    spread[2].start()
+    spread[3].start()
+    keep = pltpu.make_async_copy(own, full_ref.at[me], local)
+    keep.start()
+    finish_gather()
+    for copy in copies + spread:
+        copy.wait_send()
+    keep.wait()
+
+
+def square_scratch(rows, width):
+    return [
+        pltpu.VMEM((4, rows, width), BF),
+        pltpu.VMEM((rows, width), BF),
+        pltpu.VMEM((rows, width), BF),
+        pltpu.VMEM((rows // 2, width), BF),
+        pltpu.VMEM((rows // 2, width), BF),
+        pltpu.VMEM((rows // 2, width), BF),
+        pltpu.VMEM((rows // 2, width), BF),
+    ]
+
+
+IN_VMEM = pl.BlockSpec(memory_space=pltpu.VMEM)
+ANYWHERE = pl.BlockSpec(memory_space=pl.ANY)
+
+
+def square_call(body, out_shape, out_specs, scratch, inputs, call, cost, name):
+    return pl.pallas_call(
+        body,
+        out_shape=out_shape,
+        in_specs=[IN_VMEM] * len(inputs),
+        out_specs=out_specs,
+        scratch_shapes=scratch,
+        compiler_params=pltpu.CompilerParams(
+            collective_id=call, has_side_effects=True, vmem_limit_bytes=56 * 1024 * 1024
+        ),
+        cost_estimate=transfer_cost(cost),
+        name=name,
+    )(*inputs)
+
+
+def project_and_norm(gated, weight, x, gain, call):
+    rows, width = x.shape
+    middle, full = square_call(
+        project_kernel,
+        (
+            jax.ShapeDtypeStruct((rows, width), F32),
+            jax.ShapeDtypeStruct((4, rows, width), BF),
+        ),
+        (IN_VMEM, ANYWHERE),
+        square_scratch(rows, width)
+        + [
+            pltpu.VMEM((rows, width), BF),
+            pltpu.SemaphoreType.DMA((12,)),
+            pltpu.SemaphoreType.DMA((12,)),
+            pltpu.SemaphoreType.DMA,
+        ],
+        (gated, weight, x, gain[None, :]),
+        call,
+        2 * x.size,
+        "project_and_norm",
+    )
+    return middle, full.reshape(4 * rows, width)
+
+
+def norm_back(values, grad, gain):
+    centered = values - jnp.mean(values, axis=-1, keepdims=True)
+    spread = lax.rsqrt(jnp.mean(centered * centered, axis=-1, keepdims=True) + EPSILON)
+    unit = centered * spread
+    g = grad * gain
+    back = g - jnp.mean(g, axis=-1, keepdims=True)
+    back = spread * (back - unit * jnp.mean(g * unit, axis=-1, keepdims=True))
+    return back, grad * unit
+
+
+def middle_back_kernel(
+    p_ref, m_ref, c_ref, gain_ref, grad_ref, term_ref, full_ref,
+    parts, inbox_x, inbox_y, via_x, via_y, out_x, out_y, own, sends, recvs, local,
+):
+    me = lax.axis_index("seq")
+    rows = c_ref.shape[0]
+    half = rows // 2
+    greet((me ^ 1, me ^ 2))
+    boxes = (inbox_x, inbox_y, via_x, via_y, out_x, out_y)
+    copies, finish, total = square_parts(parts, boxes, sends, recvs, 0)
+    for k in (3, 1, 2, 0):
+        parts[k] = p_ref[block_rows(k, rows), :]
+        if k == 3:
+            copies[0].start()
+            copies[1].start()
+        if k == 1:
+            copies[2].start()
+        if k == 2:
+            copies[3].start()
+    finish()
+    spread, finish_gather = square_gather(own, full_ref, sends, recvs, 6)
+    term = jnp.zeros((1, p_ref.shape[1]), F32)
+    for i in range(2):
+        here = slice(i * half, (i + 1) * half)
+        back, terms = norm_back(m_ref[here, :], total(here), gain_ref[...])
+        grad = c_ref[here, :].astype(F32) + back
+        grad_ref[here, :] = grad
+        own[here, :] = grad.astype(BF)
+        spread[i].start()
+        term = term + jnp.sum(terms, axis=0, keepdims=True)
+    spread[2].start()
+    spread[3].start()
+    keep = pltpu.make_async_copy(own, full_ref.at[me], local)
+    keep.start()
+    term_ref[...] = term
+    finish_gather()
+    for copy in copies + spread:
+        copy.wait_send()
+    keep.wait()
+
+
+def middle_backward(part, middle, cotangent, gain, call):
+    rows, width = cotangent.shape
+    grad, term, full = square_call(
+        middle_back_kernel,
+        (
+            jax.ShapeDtypeStruct((rows, width), F32),
+            jax.ShapeDtypeStruct((1, width), F32),
+            jax.ShapeDtypeStruct((4, rows, width), BF),
+        ),
+        (IN_VMEM, IN_VMEM, ANYWHERE),
+        square_scratch(rows, width)
+        + [
+            pltpu.VMEM((rows, width), BF),
+            pltpu.SemaphoreType.DMA((12,)),
+            pltpu.SemaphoreType.DMA((12,)),
+            pltpu.SemaphoreType.DMA,
+        ],
+        (part, middle, cotangent, gain[None, :]),
+        call,
+        2 * cotangent.size,
+        "middle_backward",
+    )
+    return grad, term[0], full.reshape(4 * rows, width)
+
+
+def input_back_kernel(
+    at_value, at_swish, dqk_ref, dv_ref, ds_ref, w_ref, x_ref, grad_ref, gain_ref, dx_ref, term_ref,
+    parts, inbox_x, inbox_y, via_x, via_y, out_x, out_y, sends, recvs,
+):
+    me = lax.axis_index("seq")
+    rows = x_ref.shape[0]
+    half = rows // 2
+    greet((me ^ 1, me ^ 2))
+    boxes = (inbox_x, inbox_y, via_x, via_y, out_x, out_y)
+    copies, finish, total = square_parts(parts, boxes, sends, recvs, 0)
+
+    def part(k):
+        here = block_rows(k, rows)
+        parts[k] = (
+            times_transposed(dqk_ref[here, :], w_ref[:, :at_value])
+            + times_transposed(dv_ref[here, :], w_ref[:, at_value:at_swish])
+            + times_transposed(ds_ref[here, :], w_ref[:, at_swish:])
+        ).astype(BF)
+
+    part(3)
+    copies[0].start()
+    copies[1].start()
+    part(1)
+    copies[2].start()
+    part(2)
+    copies[3].start()
+    part(0)
+    finish()
+    term = jnp.zeros((1, x_ref.shape[1]), F32)
+    for i in range(2):
+        here = slice(i * half, (i + 1) * half)
+        back, terms = norm_back(x_ref[here, :].astype(F32), total(here), gain_ref[...])
+        dx_ref[here, :] = (grad_ref[here, :] + back).astype(BF)
+        term = term + jnp.sum(terms, axis=0, keepdims=True)
+    term_ref[...] = term
+    for copy in copies:
+        copy.wait_send()
+
+
+def input_backward(dqk, dv, ds, weight, x, grad, gain, at_value, at_swish, call):
+    rows, width = x.shape
+    dx, term = square_call(
+        functools.partial(input_back_kernel, at_value, at_swish),
+        (
+            jax.ShapeDtypeStruct((rows, width), BF),
+            jax.ShapeDtypeStruct((1, width), F32),
+        ),
+        (IN_VMEM, IN_VMEM),
+        square_scratch(rows, width)
+        + [pltpu.SemaphoreType.DMA((6,)), pltpu.SemaphoreType.DMA((6,))],
+        (dqk, dv, ds, weight, x, grad, gain[None, :]),
+        call,
+        x.size,
+        "input_backward",
+    )
+    return dx, term[0]
+
+
+def weight_rows(left_ref, right, out_ref):
+    @pl.loop(0, out_ref.shape[0] // BLOCK)
+    def _(b):
+        lanes = rows_of(b)
+        out_ref[lanes, :] = transposed_times(left_ref[:, lanes], right).astype(BF)
+
+
+def gate_back_gather_kernel(
+    heads, starts, branch_ref, w_ref, swish_ref, retained_ref, mixed_ref, gated_ref, column_ref,
+    share_ref, dswish_ref, dret_ref, dws_ref, dwo_ref, full_ref, wide, sends, recvs, local,
+):
+    me = lax.axis_index("seq")
+    greet((me ^ 1, me ^ 2))
+    keep = pltpu.make_async_copy(share_ref, full_ref.at[me], local)
+    keep.start()
+    copies, finish = square_gather_whole(share_ref, full_ref, sends, recvs, 0)
+    for copy in copies[:4]:
+        copy.start()
+    gate_back_kernel(heads, branch_ref, w_ref, swish_ref, retained_ref, dswish_ref, dret_ref)
+    padded = dswish_ref.shape[1]
+    spare = lax.broadcasted_iota(jnp.int32, (BLOCK, padded), 1) == heads * VAL_HEAD
+
+    @pl.loop(0, dws_ref.shape[0] // BLOCK)
+    def _(b):
+        lanes = rows_of(b)
+        term = transposed_times(mixed_ref[:, lanes], dswish_ref[...])
+        dws_ref[lanes, :] = jnp.where(spare, column_ref[lanes, :], term).astype(BF)
+
+    finish()
+    for h in range(heads):
+        value_lanes = slice(h * VAL_HEAD, (h + 1) * VAL_HEAD)
+
+        @pl.loop(0, branch_ref.shape[1] // (2 * BLOCK))
+        def _(b):
+            lanes = pl.ds(pl.multiple_of(b * 2 * BLOCK, 2 * BLOCK), 2 * BLOCK)
+            wide[...] = transposed_times(gated_ref[:, value_lanes], branch_ref[:, lanes]).astype(BF)
+            for k, start in enumerate(starts):
+                dwo_ref[k, h, :, lanes] = wide[start : start + dwo_ref.shape[2], :]
+
+    for copy in copies:
+        copy.wait_send()
+    keep.wait()
+
+
+def square_gather_whole(own, out_ref, sends, recvs, first):
+    rows = own.shape[0]
+    half = -(-rows // 32) * 16
+    me = lax.axis_index("seq")
+    across, along = me ^ 1, me ^ 2
+    spans = (pl.ds(0, half), pl.ds(half, rows - half))
+
+    def part(ref, i):
+        return ref.at[spans[i]]
+
+    copies = [
+        remote(part(own, 0), part(out_ref.at[me], 0), sends, recvs, first, across),
+        remote(part(own, 1), part(out_ref.at[me], 1), sends, recvs, first + 1, along),
+        remote(part(own, 1), part(out_ref.at[me], 1), sends, recvs, first + 2, across),
+        remote(part(own, 0), part(out_ref.at[me], 0), sends, recvs, first + 3, along),
+        remote(
+            part(out_ref.at[across], 0), part(out_ref.at[across], 0), sends, recvs, first + 4, along
+        ),
+        remote(
+            part(out_ref.at[along], 1), part(out_ref.at[along], 1), sends, recvs, first + 5, across
+        ),
+    ]
+
+    def finish():
+        copies[0].wait_recv()
+        copies[4].start()
+        copies[1].wait_recv()
+        copies[5].start()
+        for copy in copies[2:]:
+            copy.wait_recv()
+
+    return copies, finish
+
+
+def gate_backward_gather(
+    branch, weight, swish, retained, mixed, gated, column, share, heads, padded, cut, call
+):
+    length, width = branch.shape
+    starts = [cut.start(k) for k in range(4)]
+    return pl.pallas_call(
+        functools.partial(gate_back_gather_kernel, heads, starts),
+        out_shape=(
+            jax.ShapeDtypeStruct((length, padded), BF),
+            jax.ShapeDtypeStruct((heads, length, VAL_HEAD), BF),
+            jax.ShapeDtypeStruct((width, padded), BF),
+            jax.ShapeDtypeStruct((4, heads, cut.width, width), BF),
+            jax.ShapeDtypeStruct((4,) + share.shape, BF),
+        ),
+        in_specs=[IN_VMEM] * 7 + [ANYWHERE],
+        out_specs=(IN_VMEM,) * 4 + (ANYWHERE,),
+        scratch_shapes=[
+            pltpu.VMEM((VAL_HEAD, 2 * BLOCK), BF),
+            pltpu.SemaphoreType.DMA((6,)),
+            pltpu.SemaphoreType.DMA((6,)),
+            pltpu.SemaphoreType.DMA,
+        ],
+        compiler_params=pltpu.CompilerParams(
+            collective_id=call, has_side_effects=True, vmem_limit_bytes=56 * 1024 * 1024
+        ),
+        cost_estimate=transfer_cost(share.size),
+        name="gate_back_gather",
+    )(branch, weight, swish, retained, mixed, gated, column, share)
+
+
+def retention_back_exchange_kernel(
+    heads, q_ref, k_ref, v_ref, dret_ref, cos_ref, sin_ref, mixed_ref, send_ref,
+    dqk_ref, dv_ref, dwqk_ref, came_ref, dq_sum, dv_sum, sends, recvs, local,
+):
+    me = lax.axis_index("seq")
+    greet((me ^ 1, me ^ 2, me ^ 3))
+    keep = pltpu.make_async_copy(send_ref.at[me], came_ref.at[me], local)
+    keep.start()
+    copies = [
+        remote(send_ref.at[me ^ k], came_ref.at[me], sends, recvs, k - 1, me ^ k) for k in (3, 1, 2)
+    ]
+    for copy in copies:
+        copy.start()
+    retention_back_kernel(
+        heads, q_ref, k_ref, v_ref, dret_ref, cos_ref, sin_ref, dqk_ref, dv_ref, dq_sum, dv_sum
+    )
+    weight_rows(mixed_ref, dqk_ref[...], dwqk_ref)
+    for copy in copies:
+        copy.wait()
+    keep.wait()
+
+
+def retention_backward_exchange(q, k, v, dret, cosine, sine, mixed, send, heads, padded, call):
+    length, width = mixed.shape
+    qk = heads * KEY_HEAD
+    return pl.pallas_call(
+        functools.partial(retention_back_exchange_kernel, heads),
+        out_shape=(
+            jax.ShapeDtypeStruct((length, 2 * qk), BF),
+            jax.ShapeDtypeStruct((length, padded), BF),
+            jax.ShapeDtypeStruct((width, 2 * qk), BF),
+            jax.ShapeDtypeStruct(send.shape, BF),
+        ),
+        in_specs=[IN_VMEM] * 7 + [ANYWHERE],
+        out_specs=(IN_VMEM,) * 3 + (ANYWHERE,),
+        scratch_shapes=[
+            pltpu.VMEM((length, qk), F32),
+            pltpu.VMEM((heads, length, VAL_HEAD), BF),
+            pltpu.SemaphoreType.DMA((3,)),
+            pltpu.SemaphoreType.DMA((3,)),
+            pltpu.SemaphoreType.DMA,
+        ],
+        compiler_params=pltpu.CompilerParams(
+            collective_id=call, has_side_effects=True, vmem_limit_bytes=56 * 1024 * 1024
+        ),
+        cost_estimate=transfer_cost(send.size // 4 * 3 // 2),
+        name="retention_back_exchange",
+    )(q, k, v, dret, cosine, sine, mixed, send)
+
+
+def after(values, *others):
+    return lax.optimization_barrier((values,) + others)[0]
 
 
 class Cut:
@@ -322,6 +1066,7 @@
     me = lax.axis_index("seq")
     per_device = HEADS // seq_count
     rows_count = groups * local_length
+    square = seq_count == 4 and rows_count % 32 == 0
     length = local_length * seq_count
     key_scale = KEY_HEAD ** (-0.5)
     qk = query_weight.shape[1] // seq_count
@@ -356,11 +1101,8 @@
     selector = (column == chosen).astype(BF)
     gate_piece = product(gelu_weight, selector).astype(BF)
     up_piece = product(linear_weight, selector).astype(BF)
-    feed_weight = gather_rows(jnp.concatenate([gate_piece, up_piece], axis=1))
-    gate_full, up_full = feed_weight[:, :ff], feed_weight[:, ff:]
+    feed_piece = jnp.concatenate([gate_piece, up_piece], axis=1)
     down_piece = lax.dynamic_slice_in_dim(down_weight, cut.start(me), cut.width, axis=0)
-    kept_rows = lax.broadcasted_iota(jnp.int32, down_piece.shape, 0) >= cut.skip(me)
-    down_full = gather_rows(jnp.where(kept_rows, down_piece, jnp.zeros_like(down_piece)))
     gains = lax.all_gather(jnp.stack([mixer_gain, channel_gain]), "fsdp", axis=1, tiled=True)
     mixer_scale, channel_scale = gains[0].astype(F32), gains[1].astype(F32)
 
@@ -372,34 +1114,11 @@
         return gathered.reshape(length * groups, width)
 
     input_full = whole(local_input, 0)
-    upstream_full = whole(upstream, 1)
+    upstream_full = whole(after(upstream, input_full), 1)
     inputs = local_input.astype(F32)
 
-    mixed_low = normalize(input_full.astype(F32), mixer_scale).astype(BF)
-    projected = product(mixed_low, attention_weight)
-    cosine, sine = rotation_tables(length, KEY_HEAD // 2)
-    query_low = rotate(projected[:, :qk], cosine, sine).astype(BF)
-    key_low = (rotate(projected[:, qk : 2 * qk], cosine, sine) * key_scale).astype(BF)
-    value_low = projected[:, 2 * qk : 2 * qk + vd].astype(BF)
-    swish_pre = projected[:, 2 * qk + vd_pad : 2 * qk + vd_pad + vd]
-    head_ids = me * per_device + jnp.arange(per_device, dtype=jnp.int32)
-    masks = decay_mask(head_ids, length)
-    weights_low, retained_parts = [], []
-
-    def key_of(values, head):
-        return values[:, head * KEY_HEAD : (head + 1) * KEY_HEAD]
-
-    def value_of(values, head):
-        return values[:, head * VAL_HEAD : (head + 1) * VAL_HEAD]
-
-    for head in range(per_device):
-        scores = times_transposed(key_of(query_low, head), key_of(key_low, head))
-        weights_low.append((scores * masks[head]).astype(BF))
-        retained_parts.append(product(weights_low[head], value_of(value_low, head)).astype(BF))
-    retained = jnp.concatenate(retained_parts, axis=1).astype(F32)
-    gated_low = swish_mix(swish_pre, retained).astype(BF)
-
     blocks = shards // seq_count
+    output_pieces = after(output_pieces, upstream_full)
     swapped = exchange_seq(output_pieces.reshape(seq_count, blocks, cut.width, width), 2)
     output_full = jnp.concatenate(
         [
@@ -408,81 +1127,109 @@
         ],
         axis=0,
     )
-    middle = inputs + scatter_seq(product(gated_low, output_full).astype(BF), 3)
-
-    channel_low = normalize(middle, channel_scale).astype(BF)
-    channel_full = whole(channel_low, 4)
-    gate_pre = product(channel_full, gate_full)
-    up_pre = product(channel_full, up_full)
-    hidden_low = gelu_mix(gate_pre, up_pre).astype(BF)
-    result = middle + scatter_seq(product(hidden_low, down_full).astype(BF), 5)
+    feed_weight = gather_rows(after(feed_piece, swapped))
+
+    cosine, sine = rotation_tables(length, KEY_HEAD // 2)
+    mixed_low, query_low, key_low, value_low, swish_pre, retained, gated_low = retention_forward(
+        input_full, mixer_scale[None, :], attention_weight, cosine, sine, per_device,
+        (qk, 2 * qk, 2 * qk + vd_pad),
+    )
+
+    kept_rows = lax.broadcasted_iota(jnp.int32, down_piece.shape, 0) >= cut.skip(me)
+    down_full = gather_rows(after(jnp.where(kept_rows, down_piece, jnp.zeros_like(down_piece)), gated_low))
+    if square:
+        middle, channel_full = project_and_norm(
+            gated_low, output_full, local_input, channel_scale, 3
+        )
+    else:
+        middle = inputs + scatter_seq(product(gated_low, output_full).astype(BF), 3)
+        channel_full = whole(normalize(middle, channel_scale).astype(BF), 4)
+
+    gate_pre, up_pre, hidden_low = feed_forward(channel_full, feed_weight)
+    down_term = transposed_times(hidden_low, upstream_full).astype(BF)
+    down_share = scatter_rows(down_term)
+
+    feed_low_grad, channel_part, hidden_part = feed_backward(
+        after(upstream_full, down_term), gate_pre, up_pre, hidden_low, feed_weight, down_full
+    )
+    feed_term = transposed_times(channel_full, feed_low_grad).astype(BF)
+    feed_share = scatter_rows(feed_term)
+    channel_part = after(channel_part, feed_term)
+    if square:
+        middle_grad, channel_term, branch_full = middle_backward(
+            channel_part, middle, upstream, channel_scale, 6
+        )
+    else:
+        middle_local, channel_terms = norm_back(
+            middle, scatter_seq(channel_part, 6), channel_scale
+        )
+        channel_term = jnp.sum(channel_terms, axis=0)
+        middle_grad = upstream.astype(F32) + middle_local
+        branch_full = whole(middle_grad.astype(BF), 7)
+
+    at_value, at_swish = 2 * qk, 2 * qk + vd_pad
+    spare = lax.broadcasted_iota(jnp.int32, (width, vd_pad), 1) == vd
+    if square:
+        swish_grad, retained_grad, swish_term, output_send, down_all = gate_backward_gather(
+            branch_full, output_full, swish_pre, retained, mixed_low, gated_low,
+            channel_term[:, None], down_share, per_device, vd_pad, cut, 10,
+        )
+        swish_share = scatter_rows(swish_term)
+        key_grad, value_grad, key_term, output_swapped = retention_backward_exchange(
+            query_low, key_low, value_low, retained_grad, cosine, sine, mixed_low,
+            after(output_send, feed_share), per_device, vd_pad, 8,
+        )
+        output_share = scatter_rows(output_swapped.reshape(shards * cut.width, width))
+        key_share = scatter_rows(key_term)
+        input_gradient, mixer_term = input_backward(
+            key_grad, value_grad, swish_grad, attention_weight, local_input, middle_grad,
+            mixer_scale, at_value, at_swish, 9,
+        )
+    else:
+        swish_grad, retained_grad = gate_backward(
+            branch_full, output_full, swish_pre, retained, per_device, vd_pad
+        )
+        swish_term = transposed_times(mixed_low, swish_grad)
+        swish_term = jnp.where(spare, channel_term[:, None], swish_term).astype(BF)
+        swish_share = scatter_rows(swish_term)
+        down_all = gather_seq(down_share, 10)
+        key_grad, value_grad = retention_backward(
+            query_low, key_low, value_low, retained_grad, cosine, sine, per_device, vd_pad
+        )
+        key_term = transposed_times(mixed_low, key_grad).astype(BF)
+        key_share = scatter_rows(key_term)
+        mixed_part = (
+            times_transposed(key_grad, attention_weight[:, :at_value])
+            + times_transposed(value_grad, attention_weight[:, at_value:at_swish])
+            + times_transposed(swish_grad, attention_weight[:, at_swish:])
+        )
+        input_local, mixer_terms = norm_back(
+            inputs, scatter_seq(mixed_part.astype(BF), 9), mixer_scale
+        )
+        mixer_term = jnp.sum(mixer_terms, axis=0)
+        input_gradient = (middle_grad + input_local).astype(BF)
+        output_term = transposed_times(gated_low, branch_full).astype(BF)
+        output_term = output_term.reshape(blocks, own_rows, width)
+        output_send = jnp.stack(
+            [
+                lax.slice_in_dim(output_term, cut.start(k), cut.start(k) + cut.width, axis=1)
+                for k in range(seq_count)
+            ]
+        )
+        output_swapped = exchange_seq(output_send, 8)
+        output_share = scatter_rows(output_swapped.reshape(shards * cut.width, width))
+    input_gradient = input_gradient.reshape(groups, local_length, width)
+    value_term = transposed_times(mixed_low, value_grad)
+    value_term = jnp.where(spare, mixer_term[:, None], value_term).astype(BF)
+    value_share = scatter_rows(value_term)
+
+    result = middle + scatter_seq(after(hidden_part, value_term), 5)
     layer_output = result.astype(BF).reshape(groups, local_length, width)
-
-    hidden_grad = times_transposed(upstream_full, down_full)
-    _, gelu_back = jax.vjp(gelu_mix, gate_pre, up_pre)
-    gate_grad, up_grad = gelu_back(hidden_grad)
-    gate_low_grad, up_low_grad = gate_grad.astype(BF), up_grad.astype(BF)
-    channel_part = times_transposed(gate_low_grad, gate_full) + times_transposed(
-        up_low_grad, up_full
-    )
-    channel_grad = scatter_seq(channel_part.astype(BF), 6)
-    _, channel_back = jax.vjp(normalize, middle, channel_scale)
-    middle_local, channel_term = channel_back(channel_grad)
-    middle_grad = upstream.astype(F32) + middle_local
-    down_share = scatter_rows(transposed_times(hidden_low, upstream_full))
-    feed_share = scatter_rows(
-        jnp.concatenate(
-            [
-                transposed_times(channel_full, gate_low_grad).astype(BF),
-                transposed_times(channel_full, up_low_grad).astype(BF),
-            ],
-            axis=1,
-        )
-    )
-
-    branch_full = whole(middle_grad.astype(BF), 7)
-    gated_grad = times_transposed(branch_full, output_full)
-    output_term = transposed_times(gated_low, branch_full).astype(BF)
-    output_term = output_term.reshape(blocks, own_rows, width)
-    output_send = jnp.stack(
-        [
-            lax.slice_in_dim(output_term, cut.start(k), cut.start(k) + cut.width, axis=1)
-            for k in range(seq_count)
-        ]
-    )
-    output_swapped = exchange_seq(output_send, 8)
-    output_share = scatter_rows(output_swapped.reshape(shards * cut.width, width))
-    _, swish_back = jax.vjp(swish_mix, swish_pre, retained)
-    swish_grad, retained_grad = swish_back(gated_grad)
-    swish_low_grad = swish_grad.astype(BF)
-    retained_low_grad = retained_grad.astype(BF)
-    query_parts, key_parts, value_parts = [], [], []
-    for head in range(per_device):
-        head_grad = value_of(retained_low_grad, head)
-        weights_grad = times_transposed(head_grad, value_of(value_low, head))
-        value_parts.append(transposed_times(weights_low[head], head_grad).astype(BF))
-        score_low = (weights_grad * masks[head]).astype(BF)
-        query_parts.append(product(score_low, key_of(key_low, head)).astype(BF))
-        key_parts.append(transposed_times(score_low, key_of(query_low, head)).astype(BF))
-    query_grad = jnp.concatenate(query_parts, axis=1).astype(F32)
-    key_grad = jnp.concatenate(key_parts, axis=1).astype(F32)
-    query_pre_grad = rotate(query_grad, cosine, sine, back=True).astype(BF)
-    key_pre_grad = (rotate(key_grad, cosine, sine, back=True) * key_scale).astype(BF)
-    gap = jnp.zeros((length, vd_pad - vd), BF)
-    projected_grad = jnp.concatenate(
-        [query_pre_grad, key_pre_grad] + value_parts + [gap, swish_low_grad, gap], axis=1
-    )
-    attention_share = scatter_rows(transposed_times(mixed_low, projected_grad))
-    mixed_grad = scatter_seq(times_transposed(projected_grad, attention_weight).astype(BF), 9)
-    _, mixer_back = jax.vjp(normalize, inputs, mixer_scale)
-    input_local, mixer_term = mixer_back(mixed_grad)
-    input_gradient = (middle_grad + input_local).astype(BF)
-    input_gradient = input_gradient.reshape(groups, local_length, width)
-
-    down_all = gather_seq(down_share, 10)
-    feed_all = gather_seq(feed_share, 11)
-    output_all = gather_seq(output_share, 12)
-    attention_all = gather_seq(attention_share, 13)
+    feed_all = gather_seq(after(feed_share, layer_output), 11)
+    swish_all = gather_seq(after(swish_share, feed_all), 13)
+    output_all = gather_seq(after(output_share, swish_all), 12)
+    key_all = gather_seq(after(key_share, output_all), 15)
+    value_all = gather_seq(after(value_share, key_all), 14)
     down_gradient = cut.assemble([down_all[k] for k in range(seq_count)], 0).astype(F32)
     output_gradient = cut.assemble([output_all[k] for k in range(seq_count)], 0).astype(F32)
 
@@ -498,25 +1245,23 @@
             axis=1,
         ).astype(F32)
 
-    def attention_order(at, wide):
-        pieces = [attention_all[k][:, at : at + wide] for k in range(seq_count)]
+    def attention_order(gathered, at, wide):
+        pieces = [gathered[k][:, at : at + wide] for k in range(seq_count)]
         return jnp.concatenate(pieces, axis=1).astype(F32)
 
-    gain_terms = lax.psum(jnp.stack([mixer_term, channel_term]), ("seq", "fsdp"))
-    own_gain = width // shards
-    gain_own = lax.dynamic_slice_in_dim(
-        gain_terms, lax.axis_index("fsdp") * own_gain, own_gain, axis=1
-    )
+    def gain_order(gathered):
+        return sum(gathered[k][:, vd].astype(F32) for k in range(seq_count))
+
     return (
         layer_output,
         input_gradient,
-        gain_own[0],
-        attention_order(0, qk),
-        attention_order(qk, qk),
-        attention_order(2 * qk, vd),
-        attention_order(2 * qk + vd_pad, vd),
+        gain_order(value_all),
+        attention_order(key_all, 0, qk),
+        attention_order(key_all, qk, qk),
+        attention_order(value_all, 0, vd),
+        attention_order(swish_all, 0, vd),
         output_gradient,
-        gain_own[1],
+        gain_order(swish_all),
         hidden_order(0),
         hidden_order(ff),
         down_gradient,

time: 919 us -> 781 us (0.85)
  matrix products: 181 us -> 29.3 us
  Pallas kernels: 492 us -> 622 us
  other arithmetic: 83.9 us -> 27 us
  blocking collectives: 53.5 us -> 12.4 us
  local copies, waits for them, and re-layouts: 83.8 us -> 53.9 us
  waiting for transfers between devices: 0.18 us -> 12.9 us
    pallas_call x0 -> x8, Pallas kernels: none -> 367 us  [the longest x3 205 us: square_call(): pl.pallas_call(body, out_shape=out_shape, in_specs=[IN_VMEM] * len(inputs...]
    pallas_call x4 -> x1, Pallas kernels: 142 us -> 35.9 us  [scatter_seq(): pl.pallas_call(body, out_shape=jax.ShapeDtypeStruct((rows, width), F32),...]
    pallas_call x8 -> x7, Pallas kernels: 270 us -> 178 us  [gather_seq(): pl.pallas_call(body, out_shape=jax.ShapeDtypeStruct((count,) + values.sha...]
    dot_general x9 -> x0, matrix products: 68.3 us -> none  [times_transposed(): lax.dot_general(left, right, (((1,), (1,)), ((), ())), preferred_element_...]
    dot_general x11 -> x2, matrix products: 65 us -> 4.79 us  [product(): return jnp.dot(left, right, preferred_element_type=F32)]
    psum x1 -> x0, blocking collectives: 39.8 us -> none  [on_device(): lax.psum(jnp.stack([mixer_term, channel_term]), ('seq', 'fsdp'))]
    pallas_call x2 -> x1, Pallas kernels: 79.4 us -> 40.4 us  [exchange_seq(): pl.pallas_call(functools.partial(exchange_kernel, count), out_shape=jax.S...]
    unnamed x189 -> x62, local copies, waits for them, and re-layouts: 41.2 us -> 17.3 us
  transfers between devices with their start and end apart: 8 -> 10, of which waited for: 0 -> 1; matrix products, arithmetic and copies ran while one was open for 30% -> 11% of each run, Pallas kernels for 49% -> 78%
where the time goes in v2:
time: 781 us; the launch traced here: 774 us
  Pallas kernels  622 us (80%)
  local copies, waits for them, and re-layouts  53.9 us (7%)
  matrix products  29.3 us (4%)
  other arithmetic  27 us (3%)
  between operations  15.2 us (2%)
  waiting for transfers between devices  12.9 us (2%)
  blocking collectives  12.4 us (2%)
    pallas_call x3, Pallas kernels, square_call(): pl.pallas_call(body, out_shape=out_shape, in_specs=[IN_VMEM] * len(inputs...  205 us
    pallas_call x7, Pallas kernels, gather_seq(): pl.pallas_call(body, out_shape=jax.ShapeDtypeStruct((count,) + values.sha...  178 us
    pallas_call x1, Pallas kernels, retention_backward_exchange(): pl.pallas_call(functools.partial(retention_back_exchange_kernel, heads),...  46.2 us
    pallas_call x1, Pallas kernels, gate_backward_gather(): pl.pallas_call(functools.partial(gate_back_gather_kernel, heads, starts),...  40.4 us
    pallas_call x1, Pallas kernels, exchange_seq(): pl.pallas_call(functools.partial(exchange_kernel, count), out_shape=jax.S...  40.4 us
    pallas_call x1, Pallas kernels, retention_forward(): vmem_call(functools.partial(retention_kernel, heads, offsets), (jax.Shape...  37.6 us
    pallas_call x1, Pallas kernels, scatter_seq(): pl.pallas_call(body, out_shape=jax.ShapeDtypeStruct((rows, width), F32),...  35.9 us
    pallas_call x1, Pallas kernels, feed_backward(): pl.pallas_call(functools.partial(feed_back_kernel, ff), grid=(length // F...  25.3 us
  transfers between devices with their start and end apart: 10, of which 1 were waited for; matrix products, arithmetic and copies ran while one was open for 11% of the time, Pallas kernels for 78%

profile of v2, /device:TPU:0, one launch (start us, length us, event | category | flops | bytes accessed | tf_op | source)
XLA Modules:
  0.0 774.1 jit_solution(861735737344319035)
XLA Ops:
  7.2 1.4 copy-done
  9.6 1.1 constant_dynamic-slice_fusion.3
  10.7 1.8 constant_dynamic-slice_fusion.1
  12.5 1.2 fusion.4
  13.8 39.0 %gather_seq_0.1 = bf16[4,256,2048]{2,1,0:T(8,128)(2,1)} custom-call(bf16[256,2048]{1,0:T(8,128)(2,1)} %bitcast.99), custom_call_target="tpu_custom_call" | custom-call | bytes 125829120 | tf_op jit(solution)/shard_map/gather_seq_0/pallas_call | solution.py:354
  52.8 35.7 %gather_seq_1.1 = bf16[4,256,2048]{2,1,0:T(8,128)(2,1)} custom-call(bf16[256,2048]{1,0:T(8,128)(2,1)} %bitcast.106), custom_call_target="tpu_custom_call" | custom-call | bytes 125829120 | tf_op jit(solution)/shard_map/gather_seq_1/pallas_call | solution.py:354
  88.6 2.4 fusion.6
  91.1 2.4 fusion.5
  94.5 40.4 %exchange_seq_2.1 = bf16[4,2,112,2048]{3,2,1,0:T(8,128)(2,1)} custom-call(bf16[4,2,112,2048]{3,2,1,0:T(8,128)(2,1)} %bitcast.109), custom_call_target="tpu_custom_call" | custom-call | bytes 440401920 | tf_op jit(solution)/shard_map/exchange_seq_2/pallas_call | solution.py:386
  135.0 12.4 %all_gather.15 = bf16[2,2048]{1,0:T(2,128)(2,1)S(1)} all-gather(bf16[2,256]{1,0:T(2,128)(2,1)S(1)} %pad_maximum_fusion.1), channel_id=1, replica_groups=mesh['seq'=4,'fsdp'=8] {'fsdp'}, dimensions={1}, use_global_device_ids=true | all-gather | bytes 9216 | tf_op jit(solution)/shard_map/all_gather | solution.py:1106
  147.4 2.8 fusion.8
  150.8 2.0 dynamic-slice_select_fusion
  152.8 12.0 %all-gather.5.cloned.1.call-done.w_ref = bf16[2048,2816]{1,0:T(8,128)(2,1)} async-done(((bf16[256,2816]{1,0:T(8,128)(2,1)}), bf16[2048,2816]{1,0:T(8,128)(2,1)}) %all-gather.5.cloned.1.call-update) | async-done | bytes 11534352 | tf_op jit(solution)/shard_map/all_gather | solution.py:1081
  164.8 37.6 %retention.1 = (bf16[1024,2048]{1,0:T(8,128)(2,1)}, bf16[1024,512]{1,0:T(8,128)(2,1)}, bf16[1024,512]{1,0:T(8,128)(2,1)}, bf16[2,1024,432]{2,1,0:T(8,128)(2,1)},...) custom-call(bf16[1024,2048]{1,0:T(8,128)(2,1)} %bitcast.105, ...), custom_call_target="tpu_custom_call" | custom-call | flops 30000001024 | tf_op jit(solution)/shard_map/retention/pallas_call | solution.py:155
  202.7 1.0 bitcast_dynamic-update-slice_fusion.5
  203.8 1.1 bitcast_dynamic-update-slice_fusion.4
  204.8 1.1 bitcast_dynamic-update-slice_fusion.3
  206.9 1.1 bitcast_dynamic-update-slice_fusion.2
  208.0 1.1 bitcast_dynamic-update-slice_fusion.1
  209.0 1.1 bitcast_dynamic-update-slice_fusion
  211.1 1.8 copy-done.6
  212.9 79.1 %project_and_norm.1 = (f32[256,2048]{1,0:T(8,128)}, bf16[4,256,2048]{2,1,0:T(8,128)(2,1)}) custom-call(bf16[1024,864]{1,0:T(8,128)(2,1)} %get-tuple-element.54.g_ref.gated_ref, bf16[864,2048]{1,0:T(8,128)(2,1)} %copy-done.6, bf16[256,2048]{1,0:T(8,128)(2,1)} %bitcast.100, f32[1,2048]{1,0:T(1,128)} %get-tuple-element.190.gain_ref), custom_call_target="tpu_custom_call" | custom-call | bytes 251658240 | tf_op jit(solution)/shard_map/project_and_norm/pallas_call | solution.py:687
  292.0 12.8 %feed_forward.1 = (f32[1024,896]{1,0:T(8,128)S(1)}, f32[1024,896]{1,0:T(8,128)}, bf16[1024,896]{1,0:T(8,128)(2,1)S(1)}) custom-call(bf16[1024,2048]{1,0:T(8,128)(2,1)} %bitcast.120, bf16[2048,1792]{1,0:T(8,128)(2,1)} %all-gather.9.cloned.1.call-done.w_ref), custom_call_target="tpu_custom_call" | custom-call | flops 7516192768 | bytes 14680064 | tf_op jit(solution)/shard_map/feed_forward/pallas_call | solution.py:514
  304.9 1.8 copy-done.4
  306.7 5.5 convolution_convert_fusion.1
  312.8 25.3 %feed_back.1 = (bf16[1024,1792]{1,0:T(8,128)(2,1)}, bf16[1024,2048]{1,0:T(8,128)(2,1)}, bf16[1024,2048]{1,0:T(8,128)(2,1)}) custom-call(bf16[1024,2048]{1,0:T(8,128)(2,1)} %bitcast.103, f32[1024,896]{1,0:T(8,128)} %copy-done.4, f32[1024,896]{1,0:T(8,128)} %get-tuple-element.63.up_ref, bf16[1024,896]{1,0:T(8,128)(2,1)} %copy-done.3, ...), custom_call_target="tpu_custom_call" | custom-call | flops 15032385536 | bytes 14680064 | tf_op jit(solution)/shard_map/feed_back/pallas_call | solution.py:535
  338.2 12.0 %convolution_convert_fusion = bf16[2048,1792]{1,0:T(8,128)(2,1)} fusion(bf16[1024,2048]{1,0:T(8,128)(2,1)S(1)} %bitcast.121, bf16[1024,1792]{1,0:T(8,128)(2,1)} %get-tuple-element.70), kind=kOutput, calls=%fused_computation.1 | convolution fusion | flops 7519862784 | bytes 15204352 | tf_op jit(solution)/shard_map/dot_general | solution.py:29
  350.4 76.1 %middle_backward.1 = (f32[256,2048]{1,0:T(8,128)}, f32[1,2048]{1,0:T(1,128)}, bf16[4,256,2048]{2,1,0:T(8,128)(2,1)}) custom-call(bf16[1024,2048]{1,0:T(8,128)(2,1)} %get-tuple-element.71.p_ref, f32[256,2048]{1,0:T(8,128)} %get-tuple-element.57.m_ref, bf16[256,2048]{1,0:T(8,128)(2,1)} %bitcast.107, f32[1,2048]{1,0:T(1,128)} %get-tuple-element.190.gain_ref), custom_call_target="tpu_custom_call" | custom-call | bytes 251658240 | tf_op jit(solution)/shard_map/middle_backward/pallas_call | solution.py:687
  426.5 2.0 copy.31.column_ref
  428.6 40.4 %gate_back_gather.1 = (bf16[1024,896]{1,0:T(8,128)(2,1)}, bf16[2,1024,432]{2,1,0:T(8,128)(2,1)}, bf16[2048,896]{1,0:T(8,128)(2,1)}, bf16[4,2,112,2048]{3,2,1,0:T(8,128)(2,1)}, bf16[4,112,2048]{2,1,0:T(8,128)(2,1)}) custom-call(bf16[1024,2048]{1,0:T(8,128)(2,1)} %bitcast.102, bf16[864,2048]{1,0:T(8,128)(2,1)} %copy-done.6, ...), custom_call_target="tpu_custom_call" | custom-call | bytes 55050240 | tf_op jit(solution)/shard_map/gate_back_gather/pallas_call | solution.py:942
  469.1 46.2 %retention_back_exchange.1 = (bf16[1024,1024]{1,0:T(8,128)(2,1)}, bf16[1024,896]{1,0:T(8,128)(2,1)}, bf16[2048,1024]{1,0:T(8,128)(2,1)}, bf16[4,2,112,2048]{3,2,1,0:T(8,128)(2,1)}) custom-call(bf16[1024,512]{1,0:T(8,128)(2,1)} %get-tuple-element.66.q_ref, bf16[1024,512]{1,0:T(8,128)(2,1)} %get-tuple-element.67.k_ref, ...), custom_call_target="tpu_custom_call" | custom-call | bytes 165150720 | tf_op jit(solution)/shard_map/retention_back_exchange/pallas_call | solution.py:992
  516.4 49.8 %input_backward.1 = (bf16[256,2048]{1,0:T(8,128)(2,1)}, f32[1,2048]{1,0:T(1,128)}) custom-call(bf16[1024,1024]{1,0:T(8,128)(2,1)} %get-tuple-element.80.dqk_ref, bf16[1024,896]{1,0:T(8,128)(2,1)} %get-tuple-element.81.dv_ref, bf16[1024,896]{1,0:T(8,128)(2,1)} %get-tuple-element.82.ds_ref, bf16[2048,2816]{1,0:T(8,128)(2,1)} %all-gather.5.cloned.1.call-done.w_ref, ...), custom_call_target="tpu_custom_call" | custom-call | bytes 125829120 | tf_op jit(solution)/shard_map/input_backward/pallas_call | solution.py:687
  566.2 7.0 select_convert_fusion
  573.2 1.5 copy-done.13
  574.9 2.2 maximum_convert_fusion.1
  577.1 1.1 copy-done.2
  578.2 35.9 %scatter_seq_5.1 = f32[256,2048]{1,0:T(8,128)S(1)} custom-call(bf16[4,256,2048]{2,1,0:T(8,128)(2,1)S(1)} %bitcast.98), custom_call_target="tpu_custom_call" | custom-call | bytes 125829120 | tf_op jit(solution)/shard_map/scatter_seq_5/pallas_call | solution.py:463
  614.2 1.2 fusion.7
  615.4 30.8 %gather_seq_11.1 = bf16[4,256,1792]{2,1,0:T(8,128)(2,1)} custom-call(bf16[256,1792]{1,0:T(8,128)(2,1)} %reduce-scatter.9.cloned.1.call-done.x_ref), custom_call_target="tpu_custom_call" | custom-call | bytes 110100480 | tf_op jit(solution)/shard_map/gather_seq_11/pallas_call | solution.py:354
  646.2 16.9 %gather_seq_13.1 = bf16[4,256,896]{2,1,0:T(8,128)(2,1)} custom-call(bf16[256,896]{1,0:T(8,128)(2,1)} %reduce-scatter.17.cloned.1.call-done.x_ref), custom_call_target="tpu_custom_call" | custom-call | bytes 55050240 | tf_op jit(solution)/shard_map/gather_seq_13/pallas_call | solution.py:354
  663.1 2.4 slice_bitcast_fusion.14
  665.5 2.8 concatenate.39
  668.3 2.0 convert_element_type.109
  670.3 1.3 copy-done.7
  671.8 1.1 fusion.19
  672.9 1.3 fusion.18
  674.2 1.4 fusion.17
  675.6 1.3 fusion.16
  676.9 3.2 concatenate.41
  680.1 2.0 convert_element_type.115
  682.1 3.1 concatenate.42
  685.2 2.0 convert_element_type.116
  687.3 1.6 add_reduce_fusion
  688.9 20.1 %gather_seq_12.1 = bf16[4,112,2048]{2,1,0:T(8,128)(2,1)} custom-call(bf16[112,2048]{1,0:T(8,128)(2,1)} %reduce-scatter.15.cloned.1.call-done.x_ref), custom_call_target="tpu_custom_call" | custom-call | bytes 55050240 | tf_op jit(solution)/shard_map/gather_seq_12/pallas_call | solution.py:354
  710.0 1.4 slice_bitcast_fusion.13
  711.4 2.2 maximum_convert_fusion
  713.6 19.3 %gather_seq_15.1 = bf16[4,256,1024]{2,1,0:T(8,128)(2,1)} custom-call(bf16[256,1024]{1,0:T(8,128)(2,1)} %reduce-scatter.13.cloned.1.call-done.x_ref), custom_call_target="tpu_custom_call" | custom-call | bytes 62914560 | tf_op jit(solution)/shard_map/gather_seq_15/pallas_call | solution.py:354
  732.9 2.6 slice_bitcast_fusion.7
  735.5 16.5 %gather_seq_14.1 = bf16[4,256,896]{2,1,0:T(8,128)(2,1)} custom-call(bf16[256,896]{1,0:T(8,128)(2,1)} %reduce-scatter.11.cloned.1.call-done.x_ref), custom_call_target="tpu_custom_call" | custom-call | bytes 55050240 | tf_op jit(solution)/shard_map/gather_seq_14/pallas_call | solution.py:354
  752.0 1.6 slice_bitcast_fusion.21
  757.8 2.8 concatenate.38
  760.7 2.0 convert_element_type.108
  762.7 1.6 maximum_convert_fusion.2
  764.3 1.6 maximum_convert_fusion.3
  (101 shorter events, 13.7 us)
Async XLA Ops:
  7.2 1.5 copy-start
  7.2 87.3 %all-gather.7.cloned.1.call-start = ((), (), s32[]{:S(2)}) async-start(), calls=%async_computation.7 | async-start | bytes 4128768 | tf_op jit(solution)/shard_map/all_gather | solution.py:1081
  9.6 155.2 %all-gather.5.cloned.1.call-start = ((), (), s32[]{:S(2)}) async-start(), calls=%async_computation.6 | async-start | bytes 12976128 | tf_op jit(solution)/shard_map/all_gather | solution.py:1081
  13.7 278.3 %all-gather.9.cloned.1.call-start = ((), (), s32[]{:S(2)}) async-start(), calls=%async_computation.8 | async-start | bytes 8257536 | tf_op jit(solution)/shard_map/all_gather | solution.py:1081
  52.8 35.8 %copy-start.23 = (bf16[256,3456]{1,0:T(8,128)(2,1)S(1)}, bf16[256,3456]{1,0:T(8,128)(2,1)}, u32[]{:S(2)}) copy-start(bf16[256,3456]{1,0:T(8,128)(2,1)} %param.21) | copy-start | bytes 5308420
  88.6 2.4 copy-start.24
  94.5 40.5 %copy-start.25 = (bf16[256]{0:T(256)(128)(2,1)S(1)}, bf16[256]{0:T(256)(128)(2,1)}, u32[]{:S(2)}) copy-start(bf16[256]{0:T(256)(128)(2,1)} %param.19) | copy-start | bytes 1540
  94.5 40.5 %copy-start.26 = (bf16[256]{0:T(256)(128)(2,1)S(1)}, bf16[256]{0:T(256)(128)(2,1)}, u32[]{:S(2)}) copy-start(bf16[256]{0:T(256)(128)(2,1)} %param.13) | copy-start | bytes 1540
  134.9 177.9 %all-gather.11.cloned.1.call-start = ((), (), s32[]{:S(2)}) async-start(), calls=%async_computation.9 | async-start | bytes 4128768 | tf_op jit(solution)/shard_map/all_gather | solution.py:1081
  202.4 226.2 %reduce-scatter.7.cloned.1.call-start = ((), (), s32[]{:S(2)}) async-start(), calls=%async_computation.10 | async-start | bytes 4128768 | tf_op jit(solution)/shard_map/reduce_scatter | solution.py:1084
  211.1 1.8 copy-start.6
  292.0 14.7 %copy-start.9 = (bf16[4,256,2048]{2,1,0:T(8,128)(2,1)S(1)}, bf16[4,256,2048]{2,1,0:T(8,128)(2,1)}, u32[]{:S(2)}) copy-start(bf16[4,256,2048]{2,1,0:T(8,128)(2,1)} %gather_seq_1.1) | copy-start | bytes 12582916
  304.9 1.8 copy-start.4
  306.7 5.5 copy-start.3
  312.3 156.8 %reduce-scatter.9.cloned.1.call-start = ((), (), s32[]{:S(2)}) async-start(), calls=%async_computation.11 | async-start | bytes 8257536 | tf_op jit(solution)/shard_map/reduce_scatter | solution.py:1084
  312.8 25.3 %copy-start.22 = (bf16[4,256,2048]{2,1,0:T(8,128)(2,1)S(1)}, bf16[4,256,2048]{2,1,0:T(8,128)(2,1)}, u32[]{:S(2)}) copy-start(bf16[4,256,2048]{2,1,0:T(8,128)(2,1)} %get-tuple-element.58) | copy-start | bytes 12582916
  350.2 296.0 %reduce-scatter.17.cloned.1.call-start = ((), (), s32[]{:S(2)}) async-start(), calls=%async_computation.15 | async-start | bytes 4128768 | tf_op jit(solution)/shard_map/reduce_scatter | solution.py:1084
  469.1 219.8 %reduce-scatter.15.cloned.1.call-start = ((), (), s32[]{:S(2)}) async-start(), calls=%async_computation.14 | async-start | bytes 4128768 | tf_op jit(solution)/shard_map/reduce_scatter | solution.py:1084
  515.4 198.2 %reduce-scatter.13.cloned.1.call-start = ((), (), s32[]{:S(2)}) async-start(), calls=%async_computation.13 | async-start | bytes 4718592 | tf_op jit(solution)/shard_map/reduce_scatter | solution.py:1084
  516.1 219.3 %reduce-scatter.11.cloned.1.call-start = ((), (), s32[]{:S(2)}) async-start(), calls=%async_computation.12 | async-start | bytes 4128768 | tf_op jit(solution)/shard_map/reduce_scatter | solution.py:1084
  516.4 49.8 %copy-start.5 = (bf16[1024,2048]{1,0:T(8,128)(2,1)S(1)}, bf16[1024,2048]{1,0:T(8,128)(2,1)}, u32[]{:S(2)}) copy-start(bf16[1024,2048]{1,0:T(8,128)(2,1)} %get-tuple-element.75.mixed_ref) | copy-start | bytes 12582916
  516.4 49.8 %copy-start.12 = (bf16[1024,896]{1,0:T(8,128)(2,1)S(1)}, bf16[1024,896]{1,0:T(8,128)(2,1)}, u32[]{:S(2)}) copy-start(bf16[1024,896]{1,0:T(8,128)(2,1)} %get-tuple-element.81.dv_ref) | copy-start | bytes 5505028
  573.2 1.5 copy-start.13
  574.7 3.5 copy-start.2
  577.1 37.0 %copy-start.8 = (f32[256,2048]{1,0:T(8,128)S(1)}, f32[256,2048]{1,0:T(8,128)}, u32[]{:S(2)}) copy-start(f32[256,2048]{1,0:T(8,128)} %get-tuple-element.57.m_ref) | copy-start | bytes 6291460
  668.2 3.3 copy-start.7
  752.0 1.7 copy-start.11
  753.6 4.2 copy-start.10
  760.6 2.1 copy-start.17
  760.6 2.1 copy-start.18
  760.6 2.1 copy-start.20
  760.6 2.1 copy-start.21
  760.6 3.7 copy-start.15
  760.6 3.6 copy-start.16
  760.7 3.6 copy-start.19
  762.7 3.2 copy-start.14
  762.7 4.1 copy-start.1
Sparse Core Ops, SparseCore 0:
  10.2 45.2 all-gather.6
  57.8 106.9 all-gather.4
  167.0 71.7 all-gather.8
  240.8 41.1 all-gather.10
  312.4 42.5 reduce-scatter.6
  357.1 78.0 reduce-scatter.8
  469.2 42.2 reduce-scatter.16
  515.5 42.2 reduce-scatter.14
  560.1 48.3 reduce-scatter.12
  610.7 43.1 reduce-scatter.10

commit v3 on v2

--- a/solution.py
+++ b/solution.py
@@ -627,13 +627,34 @@
     return pl.ds(pl.multiple_of((lax.axis_index("seq") ^ k) * rows, rows), rows)
 
 
+class Moves:
+    def __init__(self, sems):
+        self.sems, self.used, self.open = sems, 0, []
+
+    def start(self, source, target):
+        copy = pltpu.make_async_copy(source, target, self.sems.at[self.used])
+        self.used += 1
+        copy.start()
+        return copy
+
+    def store(self, source, target):
+        self.open.append(self.start(source, target))
+
+    def close(self):
+        for copy in self.open:
+            copy.wait()
+
+
 def project_kernel(
-    g_ref, w_ref, x_ref, gain_ref, middle_ref, full_ref,
-    parts, inbox_x, inbox_y, via_x, via_y, out_x, out_y, own, sends, recvs, local,
+    g_any, w_any, x_ref, gain_ref, middle_ref, own_ref,
+    g_ref, w_ref, parts, inbox_x, inbox_y, via_x, via_y, out_x, out_y, sends, recvs, locals_,
 ):
     me = lax.axis_index("seq")
     rows = x_ref.shape[0]
     half = rows // 2
+    moves = Moves(locals_)
+    load_w = moves.start(w_any, w_ref)
+    load_g = moves.start(g_any, g_ref)
     greet((me ^ 1, me ^ 2))
     boxes = (inbox_x, inbox_y, via_x, via_y, out_x, out_y)
     copies, finish, total = square_parts(parts, boxes, sends, recvs, 0)
@@ -641,6 +662,8 @@
     def part(k):
         parts[k] = product(g_ref[block_rows(k, rows), :], w_ref[...]).astype(BF)
 
+    load_w.wait()
+    load_g.wait()
     part(3)
     copies[0].start()
     copies[1].start()
@@ -650,21 +673,13 @@
     copies[3].start()
     part(0)
     finish()
-    spread, finish_gather = square_gather(own, full_ref, sends, recvs, 6)
     for i in range(2):
         here = slice(i * half, (i + 1) * half)
         middle = x_ref[here, :].astype(F32) + total(here)
         middle_ref[here, :] = middle
-        own[here, :] = normalize(middle, gain_ref[...]).astype(BF)
-        spread[i].start()
-    spread[2].start()
-    spread[3].start()
-    keep = pltpu.make_async_copy(own, full_ref.at[me], local)
-    keep.start()
-    finish_gather()
-    for copy in copies + spread:
+        own_ref[here, :] = normalize(middle, gain_ref[...]).astype(BF)
+    for copy in copies:
         copy.wait_send()
-    keep.wait()
 
 
 def square_scratch(rows, width):
@@ -698,28 +713,238 @@
     )(*inputs)
 
 
+def comm_call(body, inputs, outputs, scratch, remotes, moves, call, cost, name):
+    return pl.pallas_call(
+        body,
+        out_shape=tuple(jax.ShapeDtypeStruct(shape, kind) for shape, kind, _ in outputs),
+        in_specs=[IN_VMEM if whole else ANYWHERE for _, whole in inputs],
+        out_specs=tuple(IN_VMEM if whole else ANYWHERE for _, _, whole in outputs),
+        scratch_shapes=scratch
+        + [
+            pltpu.SemaphoreType.DMA((remotes,)),
+            pltpu.SemaphoreType.DMA((remotes,)),
+            pltpu.SemaphoreType.DMA((moves,)),
+        ],
+        compiler_params=pltpu.CompilerParams(
+            collective_id=call, has_side_effects=True, vmem_limit_bytes=60 * 1024 * 1024
+        ),
+        cost_estimate=transfer_cost(cost),
+        name=name,
+    )(*[value for value, _ in inputs])
+
+
 def project_and_norm(gated, weight, x, gain, call):
     rows, width = x.shape
-    middle, full = square_call(
+    return comm_call(
         project_kernel,
-        (
-            jax.ShapeDtypeStruct((rows, width), F32),
-            jax.ShapeDtypeStruct((4, rows, width), BF),
-        ),
-        (IN_VMEM, ANYWHERE),
-        square_scratch(rows, width)
-        + [
-            pltpu.VMEM((rows, width), BF),
-            pltpu.SemaphoreType.DMA((12,)),
-            pltpu.SemaphoreType.DMA((12,)),
-            pltpu.SemaphoreType.DMA,
+        [(gated, False), (weight, False), (x, True), (gain[None, :], True)],
+        [((rows, width), F32, True), ((rows, width), BF, True)],
+        [pltpu.VMEM(gated.shape, BF), pltpu.VMEM(weight.shape, BF)] + square_scratch(rows, width),
+        6,
+        2,
+        call,
+        x.size,
+        "project_and_norm",
+    )
+
+
+def feed_forward_gather_kernel(
+    ff, x_any, w_any, c_any, both_any, hidden_any, down_any, full_any,
+    full, w_ref, c_ref, both_ref, hidden_ref, total, down_ref, sends, recvs, locals_,
+):
+    me = lax.axis_index("seq")
+    rows = x_any.shape[0]
+    moves = Moves(locals_)
+    load_x = moves.start(x_any, full.at[me])
+    load_w = moves.start(w_any, w_ref)
+    load_c = moves.start(c_any, c_ref)
+    greet((me ^ 1, me ^ 2))
+    load_x.wait()
+    copies, _ = square_gather(full.at[me], full, sends, recvs, 0)
+    for copy in copies[:4]:
+        copy.start()
+
+    def block(k):
+        here = block_rows(k, rows)
+        x = full[me ^ k]
+        moves.store(full.at[me ^ k], full_any.at[me ^ k])
+        both = product(x, w_ref[...])
+        gate, up = both[:, :ff], both[:, ff:]
+        both_ref[here, :] = both
+        moves.store(both_ref.at[here], both_any.at[here])
+        hidden = (gate * (0.5 + 0.5 * lax.erf(gate * math.sqrt(0.5))) * up).astype(BF)
+        hidden_ref[here, :] = hidden
+        moves.store(hidden_ref.at[here], hidden_any.at[here])
+        term = transposed_times(hidden, c_ref[here, :])
+        if k == 0:
+            total[...] = term
+        elif k < 3:
+            total[...] += term
+        else:
+            down_ref[...] = (total[...] + term).astype(BF)
+
+    load_w.wait()
+    load_c.wait()
+    block(0)
+    copies[0].wait_recv()
+    copies[4].start()
+    copies[1].wait_recv()
+    copies[5].start()
+    copies[2].wait_recv()
+    block(1)
+    copies[3].wait_recv()
+    block(2)
+    copies[4].wait_recv()
+    copies[5].wait_recv()
+    block(3)
+    moves.store(down_ref, down_any)
+    moves.close()
+    for copy in copies:
+        copy.wait_send()
+
+
+def feed_forward_gather(own, weight, cotangent, call):
+    rows, width = own.shape
+    length, ff = 4 * rows, weight.shape[1] // 2
+    both, hidden, down, full = comm_call(
+        functools.partial(feed_forward_gather_kernel, ff),
+        [(own, False), (weight, False), (cotangent, False)],
+        [
+            ((length, 2 * ff), F32, False),
+            ((length, ff), BF, False),
+            ((ff, width), BF, False),
+            ((4, rows, width), BF, False),
         ],
-        (gated, weight, x, gain[None, :]),
+        [
+            pltpu.VMEM((4, rows, width), BF),
+            pltpu.VMEM(weight.shape, BF),
+            pltpu.VMEM(cotangent.shape, BF),
+            pltpu.VMEM((length, 2 * ff), F32),
+            pltpu.VMEM((length, ff), BF),
+            pltpu.VMEM((ff, width), F32),
+            pltpu.VMEM((ff, width), BF),
+        ],
+        6,
+        16,
         call,
-        2 * x.size,
-        "project_and_norm",
-    )
-    return middle, full.reshape(4 * rows, width)
+        own.size,
+        "feed_forward_gather",
+    )
+    return both, hidden, down, full.reshape(length, width)
+
+
+def feed_back_scatter_kernel(
+    ff, c_any, both_any, w_any, down_any, x_any, m_ref, own_c_ref, gain_ref,
+    grad_ref, term_ref, branch_ref, dw_any,
+    c_ref, both_ref, w_ref, down_ref, x_ref, low, dw_ref,
+    parts, inbox_x, inbox_y, via_x, via_y, out_x, out_y, sends, recvs, locals_,
+):
+    me = lax.axis_index("seq")
+    rows = own_c_ref.shape[0]
+    half = rows // 2
+    moves = Moves(locals_)
+    load_down = moves.start(down_any, down_ref)
+    load_w = moves.start(w_any, w_ref)
+    order = (3, 1, 2, 0)
+    loads = []
+    for k in order:
+        here = block_rows(k, rows)
+        loads.append(moves.start(c_any.at[here], c_ref.at[here]))
+        loads.append(moves.start(both_any.at[here], both_ref.at[here]))
+    load_x = moves.start(x_any, x_ref)
+    greet((me ^ 1, me ^ 2))
+    boxes = (inbox_x, inbox_y, via_x, via_y, out_x, out_y)
+    copies, _, total = square_parts(parts, boxes, sends, recvs, 0)
+
+    def part(k):
+        here = block_rows(k, rows)
+        at = order.index(k)
+        loads[2 * at].wait()
+        loads[2 * at + 1].wait()
+        gate, up = both_ref[here, :ff], both_ref[here, ff:]
+        hidden_grad = times_transposed(c_ref[here, :], down_ref[...])
+        bell = 0.5 + 0.5 * lax.erf(gate * math.sqrt(0.5))
+        slope = bell + gate * (math.sqrt(0.5 / math.pi) * jnp.exp(-0.5 * gate * gate))
+        grads = jnp.concatenate([hidden_grad * up * slope, hidden_grad * (gate * bell)], axis=1)
+        grads = grads.astype(BF)
+        low[here, :] = grads
+        parts[k] = times_transposed(grads, w_ref[...]).astype(BF)
+
+    load_down.wait()
+    load_w.wait()
+    part(3)
+    copies[0].start()
+    copies[1].start()
+    part(1)
+    copies[2].start()
+    part(2)
+    copies[3].start()
+    copies[0].wait_recv()
+    out_y[...] = (parts[2, :half].astype(F32) + via_x[...].astype(F32)).astype(BF)
+    copies[4].start()
+    copies[1].wait_recv()
+    out_x[...] = (parts[1, half:].astype(F32) + via_y[...].astype(F32)).astype(BF)
+    copies[5].start()
+    part(0)
+    load_x.wait()
+    for b in range(x_ref.shape[1] // BLOCK):
+        lanes = slice(b * BLOCK, (b + 1) * BLOCK)
+        dw_ref[lanes, :] = transposed_times(x_ref[:, lanes], low[...]).astype(BF)
+        moves.store(dw_ref.at[lanes], dw_any.at[lanes])
+    for copy in copies[2:]:
+        copy.wait_recv()
+    term = jnp.zeros((1, gain_ref.shape[1]), F32)
+    for i in range(2):
+        here = slice(i * half, (i + 1) * half)
+        back, terms = norm_back(m_ref[here, :], total(here), gain_ref[...])
+        grad = own_c_ref[here, :].astype(F32) + back
+        grad_ref[here, :] = grad
+        branch_ref[here, :] = grad.astype(BF)
+        term = term + jnp.sum(terms, axis=0, keepdims=True)
+    term_ref[...] = term
+    moves.close()
+    for copy in copies:
+        copy.wait_send()
+
+
+def feed_back_scatter(cotangent, both, weight, down, x, middle, own_cotangent, gain, call):
+    rows, width = own_cotangent.shape
+    length, ff = cotangent.shape[0], weight.shape[1] // 2
+    grad, term, branch, dw = comm_call(
+        functools.partial(feed_back_scatter_kernel, ff),
+        [
+            (cotangent, False),
+            (both, False),
+            (weight, False),
+            (down, False),
+            (x, False),
+            (middle, True),
+            (own_cotangent, True),
+            (gain[None, :], True),
+        ],
+        [
+            ((rows, width), F32, True),
+            ((1, width), F32, True),
+            ((rows, width), BF, True),
+            ((width, 2 * ff), BF, False),
+        ],
+        [
+            pltpu.VMEM(cotangent.shape, BF),
+            pltpu.VMEM(both.shape, F32),
+            pltpu.VMEM(weight.shape, BF),
+            pltpu.VMEM(down.shape, BF),
+            pltpu.VMEM(x.shape, BF),
+            pltpu.VMEM((length, 2 * ff), BF),
+            pltpu.VMEM((width, 2 * ff), BF),
+        ]
+        + square_scratch(rows, width),
+        6,
+        11 + width // BLOCK,
+        call,
+        own_cotangent.size,
+        "feed_back_scatter",
+    )
+    return grad, term[0], branch, dw
 
 
 def norm_back(values, grad, gain):
@@ -730,72 +955,6 @@
     back = g - jnp.mean(g, axis=-1, keepdims=True)
     back = spread * (back - unit * jnp.mean(g * unit, axis=-1, keepdims=True))
     return back, grad * unit
-
-
-def middle_back_kernel(
-    p_ref, m_ref, c_ref, gain_ref, grad_ref, term_ref, full_ref,
-    parts, inbox_x, inbox_y, via_x, via_y, out_x, out_y, own, sends, recvs, local,
-):
-    me = lax.axis_index("seq")
-    rows = c_ref.shape[0]
-    half = rows // 2
-    greet((me ^ 1, me ^ 2))
-    boxes = (inbox_x, inbox_y, via_x, via_y, out_x, out_y)
-    copies, finish, total = square_parts(parts, boxes, sends, recvs, 0)
-    for k in (3, 1, 2, 0):
-        parts[k] = p_ref[block_rows(k, rows), :]
-        if k == 3:
-            copies[0].start()
-            copies[1].start()
-        if k == 1:
-            copies[2].start()
-        if k == 2:
-            copies[3].start()
-    finish()
-    spread, finish_gather = square_gather(own, full_ref, sends, recvs, 6)
-    term = jnp.zeros((1, p_ref.shape[1]), F32)
-    for i in range(2):
-        here = slice(i * half, (i + 1) * half)
-        back, terms = norm_back(m_ref[here, :], total(here), gain_ref[...])
-        grad = c_ref[here, :].astype(F32) + back
-        grad_ref[here, :] = grad
-        own[here, :] = grad.astype(BF)
-        spread[i].start()
-        term = term + jnp.sum(terms, axis=0, keepdims=True)
-    spread[2].start()
-    spread[3].start()
-    keep = pltpu.make_async_copy(own, full_ref.at[me], local)
-    keep.start()
-    term_ref[...] = term
-    finish_gather()
-    for copy in copies + spread:
-        copy.wait_send()
-    keep.wait()
-
-
-def middle_backward(part, middle, cotangent, gain, call):
-    rows, width = cotangent.shape
-    grad, term, full = square_call(
-        middle_back_kernel,
-        (
-            jax.ShapeDtypeStruct((rows, width), F32),
-            jax.ShapeDtypeStruct((1, width), F32),
-            jax.ShapeDtypeStruct((4, rows, width), BF),
-        ),
-        (IN_VMEM, IN_VMEM, ANYWHERE),
-        square_scratch(rows, width)
-        + [
-            pltpu.VMEM((rows, width), BF),
-            pltpu.SemaphoreType.DMA((12,)),
-            pltpu.SemaphoreType.DMA((12,)),
-            pltpu.SemaphoreType.DMA,
-        ],
-        (part, middle, cotangent, gain[None, :]),
-        call,
-        2 * cotangent.size,
-        "middle_backward",
-    )
-    return grad, term[0], full.reshape(4 * rows, width)
 
 
 def input_back_kernel(
@@ -863,105 +1022,119 @@
         out_ref[lanes, :] = transposed_times(left_ref[:, lanes], right).astype(BF)
 
 
-def gate_back_gather_kernel(
-    heads, starts, branch_ref, w_ref, swish_ref, retained_ref, mixed_ref, gated_ref, column_ref,
-    share_ref, dswish_ref, dret_ref, dws_ref, dwo_ref, full_ref, wide, sends, recvs, local,
+def gate_back_scatter_kernel(
+    heads, starts, branch_ref, w_ref, swish_ref, retained_ref, column_ref, hidden_any, down_any,
+    mixed_any, gated_any, m_any, dswish_ref, dret_ref, dws_any, dwo_any, out_ref,
+    hidden_ref, down_ref, mixed_ref, gated_ref, m_ref, dws_ref, dwo_ref, wide,
+    parts, inbox_x, inbox_y, via_x, via_y, out_x, out_y, sends, recvs, locals_,
 ):
     me = lax.axis_index("seq")
+    rows = out_ref.shape[0]
+    moves = Moves(locals_)
+    load_hidden = moves.start(hidden_any, hidden_ref)
+    load_down = moves.start(down_any, down_ref)
+    load_mixed = moves.start(mixed_any, mixed_ref)
+    load_gated = moves.start(gated_any, gated_ref)
+    load_m = moves.start(m_any, m_ref)
     greet((me ^ 1, me ^ 2))
-    keep = pltpu.make_async_copy(share_ref, full_ref.at[me], local)
-    keep.start()
-    copies, finish = square_gather_whole(share_ref, full_ref, sends, recvs, 0)
-    for copy in copies[:4]:
-        copy.start()
+    boxes = (inbox_x, inbox_y, via_x, via_y, out_x, out_y)
+    copies, finish, total = square_parts(parts, boxes, sends, recvs, 0)
+
+    def part(k):
+        here = block_rows(k, rows)
+        parts[k] = product(hidden_ref[here, :], down_ref[...]).astype(BF)
+
+    load_hidden.wait()
+    load_down.wait()
+    part(3)
+    copies[0].start()
+    copies[1].start()
+    part(1)
+    copies[2].start()
+    part(2)
+    copies[3].start()
+    part(0)
     gate_back_kernel(heads, branch_ref, w_ref, swish_ref, retained_ref, dswish_ref, dret_ref)
+    half = rows // 2
+    copies[0].wait_recv()
+    out_y[...] = (parts[2, :half].astype(F32) + via_x[...].astype(F32)).astype(BF)
+    copies[4].start()
+    copies[1].wait_recv()
+    out_x[...] = (parts[1, half:].astype(F32) + via_y[...].astype(F32)).astype(BF)
+    copies[5].start()
     padded = dswish_ref.shape[1]
     spare = lax.broadcasted_iota(jnp.int32, (BLOCK, padded), 1) == heads * VAL_HEAD
-
-    @pl.loop(0, dws_ref.shape[0] // BLOCK)
-    def _(b):
-        lanes = rows_of(b)
+    load_mixed.wait()
+    for b in range(dws_ref.shape[0] // BLOCK):
+        lanes = slice(b * BLOCK, (b + 1) * BLOCK)
         term = transposed_times(mixed_ref[:, lanes], dswish_ref[...])
         dws_ref[lanes, :] = jnp.where(spare, column_ref[lanes, :], term).astype(BF)
-
-    finish()
+        moves.store(dws_ref.at[lanes], dws_any.at[lanes])
+    load_gated.wait()
+    step = 2 * BLOCK
     for h in range(heads):
         value_lanes = slice(h * VAL_HEAD, (h + 1) * VAL_HEAD)
-
-        @pl.loop(0, branch_ref.shape[1] // (2 * BLOCK))
-        def _(b):
-            lanes = pl.ds(pl.multiple_of(b * 2 * BLOCK, 2 * BLOCK), 2 * BLOCK)
+        for b in range(branch_ref.shape[1] // step):
+            lanes = slice(b * step, (b + 1) * step)
             wide[...] = transposed_times(gated_ref[:, value_lanes], branch_ref[:, lanes]).astype(BF)
             for k, start in enumerate(starts):
                 dwo_ref[k, h, :, lanes] = wide[start : start + dwo_ref.shape[2], :]
-
+    moves.store(dwo_ref, dwo_any)
+    load_m.wait()
+    for copy in copies[2:]:
+        copy.wait_recv()
+    out_ref[...] = (m_ref[...] + total(slice(0, rows))).astype(BF)
+    moves.close()
     for copy in copies:
         copy.wait_send()
-    keep.wait()
-
-
-def square_gather_whole(own, out_ref, sends, recvs, first):
-    rows = own.shape[0]
-    half = -(-rows // 32) * 16
-    me = lax.axis_index("seq")
-    across, along = me ^ 1, me ^ 2
-    spans = (pl.ds(0, half), pl.ds(half, rows - half))
-
-    def part(ref, i):
-        return ref.at[spans[i]]
-
-    copies = [
-        remote(part(own, 0), part(out_ref.at[me], 0), sends, recvs, first, across),
-        remote(part(own, 1), part(out_ref.at[me], 1), sends, recvs, first + 1, along),
-        remote(part(own, 1), part(out_ref.at[me], 1), sends, recvs, first + 2, across),
-        remote(part(own, 0), part(out_ref.at[me], 0), sends, recvs, first + 3, along),
-        remote(
-            part(out_ref.at[across], 0), part(out_ref.at[across], 0), sends, recvs, first + 4, along
-        ),
-        remote(
-            part(out_ref.at[along], 1), part(out_ref.at[along], 1), sends, recvs, first + 5, across
-        ),
-    ]
-
-    def finish():
-        copies[0].wait_recv()
-        copies[4].start()
-        copies[1].wait_recv()
-        copies[5].start()
-        for copy in copies[2:]:
-            copy.wait_recv()
-
-    return copies, finish
-
-
-def gate_backward_gather(
-    branch, weight, swish, retained, mixed, gated, column, share, heads, padded, cut, call
+
+
+def gate_backward_scatter(
+    branch, weight, swish, retained, column, hidden, down, mixed, gated, middle, heads, padded, cut,
+    call,
 ):
     length, width = branch.shape
+    rows = middle.shape[0]
     starts = [cut.start(k) for k in range(4)]
-    return pl.pallas_call(
-        functools.partial(gate_back_gather_kernel, heads, starts),
-        out_shape=(
-            jax.ShapeDtypeStruct((length, padded), BF),
-            jax.ShapeDtypeStruct((heads, length, VAL_HEAD), BF),
-            jax.ShapeDtypeStruct((width, padded), BF),
-            jax.ShapeDtypeStruct((4, heads, cut.width, width), BF),
-            jax.ShapeDtypeStruct((4,) + share.shape, BF),
-        ),
-        in_specs=[IN_VMEM] * 7 + [ANYWHERE],
-        out_specs=(IN_VMEM,) * 4 + (ANYWHERE,),
-        scratch_shapes=[
+    dwo = (4, heads, cut.width, width)
+    return comm_call(
+        functools.partial(gate_back_scatter_kernel, heads, starts),
+        [
+            (branch, True),
+            (weight, True),
+            (swish, True),
+            (retained, True),
+            (column, True),
+            (hidden, False),
+            (down, False),
+            (mixed, False),
+            (gated, False),
+            (middle, False),
+        ],
+        [
+            ((length, padded), BF, True),
+            ((heads, length, VAL_HEAD), BF, True),
+            ((width, padded), BF, False),
+            (dwo, BF, False),
+            ((rows, width), BF, True),
+        ],
+        [
+            pltpu.VMEM(hidden.shape, BF),
+            pltpu.VMEM(down.shape, BF),
+            pltpu.VMEM(mixed.shape, BF),
+            pltpu.VMEM(gated.shape, BF),
+            pltpu.VMEM(middle.shape, F32),
+            pltpu.VMEM((width, padded), BF),
+            pltpu.VMEM(dwo, BF),
             pltpu.VMEM((VAL_HEAD, 2 * BLOCK), BF),
-            pltpu.SemaphoreType.DMA((6,)),
-            pltpu.SemaphoreType.DMA((6,)),
-            pltpu.SemaphoreType.DMA,
-        ],
-        compiler_params=pltpu.CompilerParams(
-            collective_id=call, has_side_effects=True, vmem_limit_bytes=56 * 1024 * 1024
-        ),
-        cost_estimate=transfer_cost(share.size),
-        name="gate_back_gather",
-    )(branch, weight, swish, retained, mixed, gated, column, share)
+        ]
+        + square_scratch(rows, width),
+        6,
+        6 + width // BLOCK,
+        call,
+        middle.size,
+        "gate_back_scatter",
+    )
 
 
 def retention_back_exchange_kernel(
@@ -1138,28 +1311,28 @@
     kept_rows = lax.broadcasted_iota(jnp.int32, down_piece.shape, 0) >= cut.skip(me)
     down_full = gather_rows(after(jnp.where(kept_rows, down_piece, jnp.zeros_like(down_piece)), gated_low))
     if square:
-        middle, channel_full = project_and_norm(
+        middle, channel_own = project_and_norm(
             gated_low, output_full, local_input, channel_scale, 3
         )
+        both_pre, hidden_low, down_term, channel_full = feed_forward_gather(
+            channel_own, feed_weight, upstream_full, 4
+        )
+        down_share = scatter_rows(down_term)
+        middle_grad, channel_term, branch_own, feed_term = feed_back_scatter(
+            after(upstream_full, down_term), both_pre, feed_weight, down_full, channel_full,
+            middle, upstream, channel_scale, 6,
+        )
+        feed_share = scatter_rows(feed_term)
+        branch_full = whole(branch_own, 7)
     else:
         middle = inputs + scatter_seq(product(gated_low, output_full).astype(BF), 3)
         channel_full = whole(normalize(middle, channel_scale).astype(BF), 4)
-
-    gate_pre, up_pre, hidden_low = feed_forward(channel_full, feed_weight)
-    down_term = transposed_times(hidden_low, upstream_full).astype(BF)
-    down_share = scatter_rows(down_term)
-
-    feed_low_grad, channel_part, hidden_part = feed_backward(
-        after(upstream_full, down_term), gate_pre, up_pre, hidden_low, feed_weight, down_full
-    )
-    feed_term = transposed_times(channel_full, feed_low_grad).astype(BF)
-    feed_share = scatter_rows(feed_term)
-    channel_part = after(channel_part, feed_term)
-    if square:
-        middle_grad, channel_term, branch_full = middle_backward(
-            channel_part, middle, upstream, channel_scale, 6
+        gate_pre, up_pre, hidden_low = feed_forward(channel_full, feed_weight)
+        down_share = scatter_rows(transposed_times(hidden_low, upstream_full).astype(BF))
+        feed_low_grad, channel_part, hidden_part = feed_backward(
+            upstream_full, gate_pre, up_pre, hidden_low, feed_weight, down_full
         )
-    else:
+        feed_share = scatter_rows(transposed_times(channel_full, feed_low_grad).astype(BF))
         middle_local, channel_terms = norm_back(
             middle, scatter_seq(channel_part, 6), channel_scale
         )
@@ -1170,9 +1343,10 @@
     at_value, at_swish = 2 * qk, 2 * qk + vd_pad
     spare = lax.broadcasted_iota(jnp.int32, (width, vd_pad), 1) == vd
     if square:
-        swish_grad, retained_grad, swish_term, output_send, down_all = gate_backward_gather(
-            branch_full, output_full, swish_pre, retained, mixed_low, gated_low,
-            channel_term[:, None], down_share, per_device, vd_pad, cut, 10,
+        swish_grad, retained_grad, swish_term, output_send, layer_output = gate_backward_scatter(
+            after(branch_full, down_share), output_full, swish_pre, retained,
+            channel_term[:, None], hidden_low, down_full, mixed_low, gated_low, middle,
+            per_device, vd_pad, cut, 5,
         )
         swish_share = scatter_rows(swish_term)
         key_grad, value_grad, key_term, output_swapped = retention_backward_exchange(
@@ -1192,7 +1366,8 @@
         swish_term = transposed_times(mixed_low, swish_grad)
         swish_term = jnp.where(spare, channel_term[:, None], swish_term).astype(BF)
         swish_share = scatter_rows(swish_term)
-        down_all = gather_seq(down_share, 10)
+        result = middle + scatter_seq(hidden_part, 5)
+        layer_output = result.astype(BF)
         key_grad, value_grad = retention_backward(
             query_low, key_low, value_low, retained_grad, cosine, sine, per_device, vd_pad
         )
@@ -1223,9 +1398,9 @@
     value_term = jnp.where(spare, mixer_term[:, None], value_term).astype(BF)
     value_share = scatter_rows(value_term)
 
-    result = middle + scatter_seq(after(hidden_part, value_term), 5)
-    layer_output = result.astype(BF).reshape(groups, local_length, width)
-    feed_all = gather_seq(after(feed_share, layer_output), 11)
+    layer_output = layer_output.reshape(groups, local_length, width)
+    down_all = gather_seq(after(down_share, value_term), 10)
+    feed_all = gather_seq(after(feed_share, down_all), 11)
     swish_all = gather_seq(after(swish_share, feed_all), 13)
     output_all = gather_seq(after(output_share, swish_all), 12)
     key_all = gather_seq(after(key_share, output_all), 15)

time: 781 us -> 734 us (0.940)
  Pallas kernels: 622 us -> 602 us
  matrix products: 29.3 us -> 11.9 us
    pallas_call x3 -> x1, Pallas kernels: 205 us -> 50 us  [square_call(): pl.pallas_call(body, out_shape=out_shape, in_specs=[IN_VMEM] * len(inputs...]
    pallas_call x4, Pallas kernels: 114 us -> 188 us  [comm_call(): pl.pallas_call(body, out_shape=tuple((jax.ShapeDtypeStruct(shape, kind) f...]
    pallas_call x7 -> x9, Pallas kernels: 178 us -> 239 us  [gather_seq(): pl.pallas_call(body, out_shape=jax.ShapeDtypeStruct((count,) + values.sha...]
    dot_general x3 -> x1, matrix products: 24.5 us -> 7.1 us  [transposed_times(): lax.dot_general(left, right, (((0,), (0,)), ((), ())), preferred_element_...]
    unnamed x62 -> x51, local copies, waits for them, and re-layouts: 17.3 us -> 12.7 us
  transfers between devices with their start and end apart: 10 -> 10, of which waited for: 1 -> 1; matrix products, arithmetic and copies ran while one was open for 11% -> 9% of each run, Pallas kernels for 78% -> 81%
where the time goes in v3:
time: 734 us; the launch traced here: 727 us
  Pallas kernels  602 us (82%)
  local copies, waits for them, and re-layouts  46.6 us (6%)
  other arithmetic  25.7 us (4%)
  between operations  14.9 us (2%)
  waiting for transfers between devices  12.9 us (2%)
  blocking collectives  12.4 us (2%)
  matrix products  11.9 us (2%)
    pallas_call x9, Pallas kernels, gather_seq(): pl.pallas_call(body, out_shape=jax.ShapeDtypeStruct((count,) + values.sha...  239 us
    pallas_call x4, Pallas kernels, comm_call(): pl.pallas_call(body, out_shape=tuple((jax.ShapeDtypeStruct(shape, kind) f...  188 us
    pallas_call x1, Pallas kernels, square_call(): pl.pallas_call(body, out_shape=out_shape, in_specs=[IN_VMEM] * len(inputs...  50 us
    pallas_call x1, Pallas kernels, retention_backward_exchange(): pl.pallas_call(functools.partial(retention_back_exchange_kernel, heads),...  47.5 us
    pallas_call x1, Pallas kernels, exchange_seq(): pl.pallas_call(functools.partial(exchange_kernel, count), out_shape=jax.S...  40.4 us
    pallas_call x1, Pallas kernels, retention_forward(): vmem_call(functools.partial(retention_kernel, heads, offsets), (jax.Shape...  37.4 us
  transfers between devices with their start and end apart: 10, of which 1 were waited for; matrix products, arithmetic and copies ran while one was open for 9% of the time, Pallas kernels for 81%

profile of v3, /device:TPU:0, one launch (start us, length us, event | category | flops | bytes accessed | tf_op | source)
XLA Modules:
  0.0 727.3 jit_solution(6412191983460126523)
XLA Ops:
  7.2 1.4 copy-done
  9.6 1.1 constant_dynamic-slice_fusion.3
  10.7 1.8 constant_dynamic-slice_fusion.1
  12.5 1.2 fusion.4
  13.8 39.0 %gather_seq_0.1 = bf16[4,256,2048]{2,1,0:T(8,128)(2,1)} custom-call(bf16[256,2048]{1,0:T(8,128)(2,1)} %bitcast.95), custom_call_target="tpu_custom_call" | custom-call | bytes 125829120 | tf_op jit(solution)/shard_map/gather_seq_0/pallas_call | solution.py:354
  52.8 35.7 %gather_seq_1.1 = bf16[4,256,2048]{2,1,0:T(8,128)(2,1)} custom-call(bf16[256,2048]{1,0:T(8,128)(2,1)} %bitcast.98), custom_call_target="tpu_custom_call" | custom-call | bytes 125829120 | tf_op jit(solution)/shard_map/gather_seq_1/pallas_call | solution.py:354
  88.6 2.4 fusion.5
  91.1 2.4 fusion.6
  93.5 1.0 pad_maximum_fusion
  94.5 40.4 %exchange_seq_2.1 = bf16[4,2,112,2048]{3,2,1,0:T(8,128)(2,1)} custom-call(bf16[4,2,112,2048]{3,2,1,0:T(8,128)(2,1)} %bitcast.103), custom_call_target="tpu_custom_call" | custom-call | bytes 440401920 | tf_op jit(solution)/shard_map/exchange_seq_2/pallas_call | solution.py:386
  135.0 12.4 %all_gather.15 = bf16[2,2048]{1,0:T(2,128)(2,1)S(1)} all-gather(bf16[2,256]{1,0:T(2,128)(2,1)S(1)} %pad_maximum_fusion.1), channel_id=1, replica_groups=mesh['seq'=4,'fsdp'=8] {'fsdp'}, dimensions={1}, use_global_device_ids=true | all-gather | bytes 9216 | tf_op jit(solution)/shard_map/all_gather | solution.py:1279
  147.4 2.8 fusion.7
  150.8 2.0 dynamic-slice_select_fusion
  152.8 12.0 %all-gather.5.cloned.1.call-done.w_ref = bf16[2048,2816]{1,0:T(8,128)(2,1)} async-done(((bf16[256,2816]{1,0:T(8,128)(2,1)}), bf16[2048,2816]{1,0:T(8,128)(2,1)}) %all-gather.5.cloned.1.call-update) | async-done | bytes 11534352 | tf_op jit(solution)/shard_map/all_gather | solution.py:1254
  164.8 37.4 %retention.1 = (bf16[1024,2048]{1,0:T(8,128)(2,1)}, bf16[1024,512]{1,0:T(8,128)(2,1)}, bf16[1024,512]{1,0:T(8,128)(2,1)}, bf16[2,1024,432]{2,1,0:T(8,128)(2,1)},...) custom-call(bf16[1024,2048]{1,0:T(8,128)(2,1)} %bitcast.100, ...), custom_call_target="tpu_custom_call" | custom-call | flops 30000001024 | tf_op jit(solution)/shard_map/retention/pallas_call | solution.py:155
  202.7 1.0 bitcast_dynamic-update-slice_fusion.5
  203.7 1.1 bitcast_dynamic-update-slice_fusion.4
  204.8 1.1 bitcast_dynamic-update-slice_fusion.3
  205.8 1.0 bitcast_dynamic-update-slice_fusion.7
  206.9 1.1 bitcast_dynamic-update-slice_fusion.2
  207.9 1.1 bitcast_dynamic-update-slice_fusion.1
  209.0 1.1 bitcast_dynamic-update-slice_fusion
  210.0 1.0 bitcast_dynamic-update-slice_fusion.6.w_any.w_ref
  211.1 1.8 copy-done.3
  212.9 44.4 %project_and_norm.1 = (f32[256,2048]{1,0:T(8,128)}, bf16[256,2048]{1,0:T(8,128)(2,1)}) custom-call(bf16[1024,864]{1,0:T(8,128)(2,1)} %get-tuple-element.54.g_any.gated_any, bf16[864,2048]{1,0:T(8,128)(2,1)} %copy-done.3, bf16[256,2048]{1,0:T(8,128)(2,1)} %bitcast.96, f32[1,2048]{1,0:T(1,128)} %get-tuple-element.188.gain_ref), custom_call_target="tpu_custom_call" | custom-call | bytes 125829120 | tf_op jit(solution)/shard_map/project_and_norm/pallas_call | solution.py:717
  257.3 51.2 %feed_forward_gather.1 = (f32[1024,1792]{1,0:T(8,128)}, bf16[1024,896]{1,0:T(8,128)(2,1)}, bf16[896,2048]{1,0:T(8,128)(2,1)}, bf16[4,256,2048]{2,1,0:T(8,128)(2,1)}) custom-call(bf16[256,2048]{1,0:T(8,128)(2,1)} %get-tuple-element.56.x_any, bf16[2048,1792]{1,0:T(8,128)(2,1)} %all-gather.9.cloned.1.call-done.w_any, bf16[1024,2048]{1,0:T(8,128)(2,1)} %bitcast.92), custom_call_target="tpu_custom_call" | custom-call | bytes 125829120 | tf_op jit(solution)/shard_map/feed_forward_gather/pallas_call | solution.py:717
  308.6 47.5 %feed_back_scatter.1 = (f32[256,2048]{1,0:T(8,128)}, f32[1,2048]{1,0:T(1,128)}, bf16[256,2048]{1,0:T(8,128)(2,1)}, bf16[2048,1792]{1,0:T(8,128)(2,1)}) custom-call(bf16[1024,2048]{1,0:T(8,128)(2,1)} %bitcast.93, f32[1024,1792]{1,0:T(8,128)} %get-tuple-element.60.both_any, bf16[2048,1792]{1,0:T(8,128)(2,1)} %all-gather.9.cloned.1.call-done.w_any, ...), custom_call_target="tpu_custom_call" | custom-call | bytes 125829120 | tf_op jit(solution)/shard_map/feed_back_scatter/pallas_call | solution.py:717
  356.2 34.9 %gather_seq_7.1 = bf16[4,256,2048]{2,1,0:T(8,128)(2,1)} custom-call(bf16[256,2048]{1,0:T(8,128)(2,1)} %get-tuple-element.64.x_ref), custom_call_target="tpu_custom_call" | custom-call | bytes 125829120 | tf_op jit(solution)/shard_map/gather_seq_7/pallas_call | solution.py:354
  391.1 1.3 copy.31.column_ref
  392.4 44.9 %gate_back_scatter.1 = (bf16[1024,896]{1,0:T(8,128)(2,1)}, bf16[2,1024,432]{2,1,0:T(8,128)(2,1)}, bf16[2048,896]{1,0:T(8,128)(2,1)}, bf16[4,2,112,2048]{3,2,1,0:T(8,128)(2,1)}, bf16[256,2048]{1,0:T(8,128)(2,1)}) custom-call(bf16[1024,2048]{1,0:T(8,128)(2,1)} %bitcast.94, bf16[864,2048]{1,0:T(8,128)(2,1)} %copy-done.3, ...), custom_call_target="tpu_custom_call" | custom-call | bytes 125829120 | tf_op jit(solution)/shard_map/gate_back_scatter/pallas_call | solution.py:717
  437.4 47.5 %retention_back_exchange.1 = (bf16[1024,1024]{1,0:T(8,128)(2,1)}, bf16[1024,896]{1,0:T(8,128)(2,1)}, bf16[2048,1024]{1,0:T(8,128)(2,1)}, bf16[4,2,112,2048]{3,2,1,0:T(8,128)(2,1)}) custom-call(bf16[1024,512]{1,0:T(8,128)(2,1)} %get-tuple-element.72.q_ref, bf16[1024,512]{1,0:T(8,128)(2,1)} %get-tuple-element.73.k_ref, ...), custom_call_target="tpu_custom_call" | custom-call | bytes 165150720 | tf_op jit(solution)/shard_map/retention_back_exchange/pallas_call | solution.py:1165
  486.0 50.0 %input_backward.1 = (bf16[256,2048]{1,0:T(8,128)(2,1)}, f32[1,2048]{1,0:T(1,128)}) custom-call(bf16[1024,1024]{1,0:T(8,128)(2,1)} %get-tuple-element.79.dqk_ref, bf16[1024,896]{1,0:T(8,128)(2,1)} %get-tuple-element.80.dv_ref, bf16[1024,896]{1,0:T(8,128)(2,1)} %get-tuple-element.81.ds_ref, bf16[2048,2816]{1,0:T(8,128)(2,1)} %all-gather.5.cloned.1.call-done.w_ref, ...), custom_call_target="tpu_custom_call" | custom-call | bytes 125829120 | tf_op jit(solution)/shard_map/input_backward/pallas_call | solution.py:702
  536.1 7.1 select_convert_fusion
  543.2 21.9 %gather_seq_10.1 = bf16[4,112,2048]{2,1,0:T(8,128)(2,1)} custom-call(bf16[112,2048]{1,0:T(8,128)(2,1)} %reduce-scatter.7.cloned.1.call-done.x_ref), custom_call_target="tpu_custom_call" | custom-call | bytes 55050240 | tf_op jit(solution)/shard_map/gather_seq_10/pallas_call | solution.py:354
  565.0 32.3 %gather_seq_11.1 = bf16[4,256,1792]{2,1,0:T(8,128)(2,1)} custom-call(bf16[256,1792]{1,0:T(8,128)(2,1)} %reduce-scatter.9.cloned.1.call-done.x_ref), custom_call_target="tpu_custom_call" | custom-call | bytes 110100480 | tf_op jit(solution)/shard_map/gather_seq_11/pallas_call | solution.py:354
  597.3 2.3 slice_bitcast_fusion
  599.6 1.1 fusion.15
  600.7 1.1 fusion.16
  601.8 1.1 fusion.17
  602.9 1.2 fusion.18
  604.2 3.2 concatenate.42
  607.4 2.0 convert_element_type.104
  609.4 2.8 concatenate.41
  612.2 2.0 convert_element_type.103
  614.2 16.9 %gather_seq_13.1 = bf16[4,256,896]{2,1,0:T(8,128)(2,1)} custom-call(bf16[256,896]{1,0:T(8,128)(2,1)} %reduce-scatter.17.cloned.1.call-done.x_ref), custom_call_target="tpu_custom_call" | custom-call | bytes 55050240 | tf_op jit(solution)/shard_map/gather_seq_13/pallas_call | solution.py:354
  631.1 2.4 slice_bitcast_fusion.14
  633.4 2.8 concatenate.39
  636.2 2.0 convert_element_type.97
  638.2 1.6 add_reduce_fusion
  640.0 2.2 maximum_convert_fusion.1
  642.2 22.0 %gather_seq_12.1 = bf16[4,112,2048]{2,1,0:T(8,128)(2,1)} custom-call(bf16[112,2048]{1,0:T(8,128)(2,1)} %reduce-scatter.15.cloned.1.call-done.x_ref), custom_call_target="tpu_custom_call" | custom-call | bytes 55050240 | tf_op jit(solution)/shard_map/gather_seq_12/pallas_call | solution.py:354
  664.3 1.0 slice_bitcast_fusion.23
  665.3 1.4 slice_bitcast_fusion.13
  666.7 2.2 maximum_convert_fusion
  668.9 19.5 %gather_seq_15.1 = bf16[4,256,1024]{2,1,0:T(8,128)(2,1)} custom-call(bf16[256,1024]{1,0:T(8,128)(2,1)} %reduce-scatter.13.cloned.1.call-done.x_ref), custom_call_target="tpu_custom_call" | custom-call | bytes 62914560 | tf_op jit(solution)/shard_map/gather_seq_15/pallas_call | solution.py:354
  688.5 2.9 slice_bitcast_fusion.7
  691.3 16.2 %gather_seq_14.1 = bf16[4,256,896]{2,1,0:T(8,128)(2,1)} custom-call(bf16[256,896]{1,0:T(8,128)(2,1)} %reduce-scatter.11.cloned.1.call-done.x_ref), custom_call_target="tpu_custom_call" | custom-call | bytes 55050240 | tf_op jit(solution)/shard_map/gather_seq_14/pallas_call | solution.py:354
  707.6 1.6 slice_bitcast_fusion.21
  710.0 2.8 concatenate.38
  712.8 2.0 convert_element_type.96
  715.2 1.6 maximum_convert_fusion.3
  716.8 1.6 maximum_convert_fusion.2
  718.3 1.0 copy.43
  719.3 1.0 copy.44
  (87 shorter events, 4.8 us)
Async XLA Ops:
  7.2 1.5 copy-start
  7.2 87.3 %all-gather.7.cloned.1.call-start = ((), (), s32[]{:S(2)}) async-start(), calls=%async_computation.7 | async-start | bytes 4128768 | tf_op jit(solution)/shard_map/all_gather | solution.py:1254
  9.6 155.2 %all-gather.5.cloned.1.call-start = ((), (), s32[]{:S(2)}) async-start(), calls=%async_computation.6 | async-start | bytes 12976128 | tf_op jit(solution)/shard_map/all_gather | solution.py:1254
  13.7 243.6 %all-gather.9.cloned.1.call-start = ((), (), s32[]{:S(2)}) async-start(), calls=%async_computation.8 | async-start | bytes 8257536 | tf_op jit(solution)/shard_map/all_gather | solution.py:1254
  52.8 35.8 %copy-start.17 = (bf16[256,3456]{1,0:T(8,128)(2,1)S(1)}, bf16[256,3456]{1,0:T(8,128)(2,1)}, u32[]{:S(2)}) copy-start(bf16[256,3456]{1,0:T(8,128)(2,1)} %param.20) | copy-start | bytes 5308420
  88.6 2.4 copy-start.18
  94.5 40.5 %copy-start.19 = (bf16[256]{0:T(256)(128)(2,1)S(1)}, bf16[256]{0:T(256)(128)(2,1)}, u32[]{:S(2)}) copy-start(bf16[256]{0:T(256)(128)(2,1)} %param.19) | copy-start | bytes 1540
  94.5 40.5 %copy-start.20 = (bf16[256]{0:T(256)(128)(2,1)S(1)}, bf16[256]{0:T(256)(128)(2,1)}, u32[]{:S(2)}) copy-start(bf16[256]{0:T(256)(128)(2,1)} %param.13) | copy-start | bytes 1540
  134.9 173.7 %all-gather.11.cloned.1.call-start = ((), (), s32[]{:S(2)}) async-start(), calls=%async_computation.9 | async-start | bytes 4128768 | tf_op jit(solution)/shard_map/all_gather | solution.py:1254
  202.2 190.2 %reduce-scatter.7.cloned.1.call-start = ((), (), s32[]{:S(2)}) async-start(), calls=%async_computation.10 | async-start | bytes 4128768 | tf_op jit(solution)/shard_map/reduce_scatter | solution.py:1257
  211.1 1.8 copy-start.3
  308.5 128.9 %reduce-scatter.9.cloned.1.call-start = ((), (), s32[]{:S(2)}) async-start(), calls=%async_computation.11 | async-start | bytes 8257536 | tf_op jit(solution)/shard_map/reduce_scatter | solution.py:1257
  356.1 35.0 %copy-start.16 = (f32[1,2048]{1,0:T(1,128)S(1)}, f32[1,2048]{1,0:T(1,128)}, u32[]{:S(2)}) copy-start(f32[1,2048]{1,0:T(1,128)} %get-tuple-element.68) | copy-start | bytes 24580
  356.1 258.1 %reduce-scatter.17.cloned.1.call-start = ((), (), s32[]{:S(2)}) async-start(), calls=%async_computation.15 | async-start | bytes 4128768 | tf_op jit(solution)/shard_map/reduce_scatter | solution.py:1257
  437.3 204.9 %reduce-scatter.15.cloned.1.call-start = ((), (), s32[]{:S(2)}) async-start(), calls=%async_computation.14 | async-start | bytes 4128768 | tf_op jit(solution)/shard_map/reduce_scatter | solution.py:1257
  485.0 183.9 %reduce-scatter.13.cloned.1.call-start = ((), (), s32[]{:S(2)}) async-start(), calls=%async_computation.13 | async-start | bytes 4718592 | tf_op jit(solution)/shard_map/reduce_scatter | solution.py:1257
  485.7 205.6 %reduce-scatter.11.cloned.1.call-start = ((), (), s32[]{:S(2)}) async-start(), calls=%async_computation.12 | async-start | bytes 4128768 | tf_op jit(solution)/shard_map/reduce_scatter | solution.py:1257
  486.0 50.0 %copy-start.2 = (bf16[1024,2048]{1,0:T(8,128)(2,1)S(1)}, bf16[1024,2048]{1,0:T(8,128)(2,1)}, u32[]{:S(2)}) copy-start(bf16[1024,2048]{1,0:T(8,128)(2,1)} %get-tuple-element.70.mixed_any.mixed_ref) | copy-start | bytes 12582916
  486.0 50.0 %copy-start.10 = (bf16[1024,896]{1,0:T(8,128)(2,1)S(1)}, bf16[1024,896]{1,0:T(8,128)(2,1)}, u32[]{:S(2)}) copy-start(bf16[1024,896]{1,0:T(8,128)(2,1)} %get-tuple-element.80.dv_ref) | copy-start | bytes 5505028
  607.3 2.1 copy-start.13
  607.3 2.0 copy-start.14
  607.3 2.0 copy-start.15
  636.2 3.7 copy-start.4
  709.2 0.8 copy-start.5
  712.8 2.1 copy-start.9
  712.8 2.1 copy-start.8
  712.8 2.1 copy-start.7
  712.8 2.3 copy-start.6
  715.1 3.2 copy-start.11
  715.2 4.1 copy-start.12
  716.8 3.5 copy-start.1
Sparse Core Ops, SparseCore 0:
  10.2 45.2 all-gather.6
  57.8 106.9 all-gather.4
  167.0 71.7 all-gather.8
  240.8 41.1 all-gather.10
  308.6 42.4 reduce-scatter.6
  356.2 77.5 reduce-scatter.8
  437.5 42.8 reduce-scatter.16
  485.1 42.8 reduce-scatter.14
  530.3 48.3 reduce-scatter.12
  580.9 43.1 reduce-scatter.10

commit v4 on v3

--- a/solution.py
+++ b/solution.py
@@ -15,6 +15,8 @@
 MESH = pl.DeviceIdType.MESH
 BF = jnp.bfloat16
 F32 = jnp.float32
+IN_VMEM = pl.BlockSpec(memory_space=pltpu.VMEM)
+ANYWHERE = pl.BlockSpec(memory_space=pl.ANY)
 
 
 def product(left, right):
@@ -59,17 +61,14 @@
 BLOCK = 256
 
 
-def head_rate(head):
-    ids = jnp.full((1, 1), head, jnp.int32).astype(F32)
-    return jnp.log1p(-jnp.exp2(-5.0 - ids))
-
-
-def decay_tile(rate):
-    gap = lax.broadcasted_iota(jnp.int32, (BLOCK, BLOCK), 0) - lax.broadcasted_iota(
-        jnp.int32, (BLOCK, BLOCK), 1
-    )
-    full = jnp.exp(gap.astype(F32) * rate)
-    return full, jnp.where(gap >= 0, full, 0.0)
+def decay_table(head_ids, length):
+    rates = jnp.log1p(-jnp.exp2(-5.0 - head_ids.astype(F32)))
+    gap = (
+        jnp.arange(length - BLOCK, length, dtype=jnp.int32)[:, None]
+        - jnp.arange(length, dtype=jnp.int32)[None, :]
+    )
+    decay = jnp.exp(jnp.maximum(gap, 0).astype(F32)[None] * rates[:, None, None])
+    return jnp.where(gap[None] >= 0, decay, 0.0)
 
 
 def norm_parts(values):
@@ -83,197 +82,215 @@
     return pl.ds(pl.multiple_of(block * BLOCK, BLOCK), BLOCK)
 
 
+def head_lanes(head, width):
+    return slice(head * width, (head + 1) * width)
+
+
+class Moves:
+    def __init__(self, sems):
+        self.sems, self.used, self.open = sems, 0, []
+
+    def start(self, source, target):
+        copy = pltpu.make_async_copy(source, target, self.sems.at[self.used])
+        self.used += 1
+        copy.start()
+        return copy
+
+    def store(self, source, target):
+        self.open.append(self.start(source, target))
+
+    def close(self):
+        for copy in self.open:
+            copy.wait()
+
+
 def retention_kernel(
-    heads, offsets, x_ref, gain_ref, w_ref, cos_ref, sin_ref,
-    mixed_ref, q_ref, k_ref, v_ref, swish_ref, retained_ref, gated_ref,
+    heads, offsets, mixed_any, w_any, cos_ref, sin_ref, table_ref,
+    q_any, k_any, v_any, swish_any, retained_any, gated_any,
+    mixed_ref, w_ref, q_ref, k_ref, v_ref, swish_ref, retained_ref, gated_ref, sems,
 ):
-    first_head = lax.axis_index("seq") * heads
     at_key, at_value, at_swish = offsets
-    value_width = heads * VAL_HEAD
-    blocks = x_ref.shape[0] // BLOCK
-    rates = [head_rate(first_head + h) for h in range(heads)]
-
-    @pl.loop(0, blocks)
-    def _(i):
-        rows = rows_of(i)
-        x = x_ref[rows, :].astype(F32)
-        mixed = normalize(x, gain_ref[...]).astype(BF)
-        mixed_ref[rows, :] = mixed
+    blocks = mixed_ref.shape[0] // BLOCK
+    moves = Moves(sems)
+    spans = (
+        slice(0, at_key), slice(at_key, at_value), slice(at_value, at_swish),
+        slice(at_swish, w_ref.shape[1]),
+    )
+    loads = []
+    for i in range(blocks):
+        rows = slice(i * BLOCK, (i + 1) * BLOCK)
+        loads.append(moves.start(mixed_any.at[rows], mixed_ref.at[rows]))
+        if i == 0:
+            weights = [moves.start(w_any.at[:, span], w_ref.at[:, span]) for span in spans]
+    for i in range(blocks):
+        rows = slice(i * BLOCK, (i + 1) * BLOCK)
+        seen = slice(0, (i + 1) * BLOCK)
+        loads[i].wait()
+        mixed = mixed_ref[rows, :]
         cosine, sine = cos_ref[rows, :], sin_ref[rows, :]
-        query = product(mixed, w_ref[:, :at_key])
+        for n, (target, scale) in enumerate(((q_ref, 1.0), (k_ref, KEY_HEAD**-0.5))):
+            if i == 0:
+                weights[n].wait()
+            pre = product(mixed, w_ref[:, spans[n]])
+            for h in range(heads):
+                lanes = head_lanes(h, KEY_HEAD)
+                turned = rotate_pair(pre[:, lanes], cosine, sine)
+                target[rows, lanes] = (turned * scale if n else turned).astype(BF)
+        if i == 0:
+            weights[2].wait()
+        value = product(mixed, w_ref[:, spans[2]])
         for h in range(heads):
-            lanes = slice(h * KEY_HEAD, (h + 1) * KEY_HEAD)
-            q_ref[rows, lanes] = rotate_pair(query[:, lanes], cosine, sine).astype(BF)
-        key = product(mixed, w_ref[:, at_key:at_value])
-        for h in range(heads):
-            lanes = slice(h * KEY_HEAD, (h + 1) * KEY_HEAD)
-            turned = rotate_pair(key[:, lanes], cosine, sine) * (KEY_HEAD**-0.5)
-            k_ref[rows, lanes] = turned.astype(BF)
-        value = product(mixed, w_ref[:, at_value:at_swish])
-        for h in range(heads):
-            v_ref[h, rows, :] = value[:, h * VAL_HEAD : (h + 1) * VAL_HEAD].astype(BF)
-        swish = product(mixed, w_ref[:, at_swish:])[:, :value_width]
+            v_ref[h, rows, :] = value[:, head_lanes(h, VAL_HEAD)].astype(BF)
+        if i == 0:
+            weights[3].wait()
+        swish = product(mixed, w_ref[:, spans[3]])[:, : heads * VAL_HEAD]
         swish_ref[rows, :] = swish
-
         gated = []
         for h in range(heads):
-            lanes = slice(h * KEY_HEAD, (h + 1) * KEY_HEAD)
-            full, lower = decay_tile(rates[h])
-            q = q_ref[rows, lanes]
-            scores = times_transposed(q, k_ref[rows, lanes])
-            total = product((scores * lower).astype(BF), v_ref[h, rows, :])
-
-            def earlier(j, total):
-                there = rows_of(j)
-                scores = times_transposed(q, k_ref[there, lanes])
-                far = jnp.exp(rates[h] * ((i - j) * BLOCK).astype(F32))
-                return total + product((scores * (full * far)).astype(BF), v_ref[h, there, :])
-
-            total = lax.fori_loop(0, i, earlier, total)
-            retained = total.astype(BF)
+            lanes = head_lanes(h, KEY_HEAD)
+            scores = times_transposed(q_ref[rows, lanes], k_ref[seen, lanes])
+            decay = table_ref[h, :, (blocks - 1 - i) * BLOCK :]
+            retained = product((scores * decay).astype(BF), v_ref[h, seen, :]).astype(BF)
             retained_ref[h, rows, :] = retained
             unit, _, _ = norm_parts(retained.astype(F32))
-            s = swish[:, h * VAL_HEAD : (h + 1) * VAL_HEAD]
+            s = swish[:, head_lanes(h, VAL_HEAD)]
             gated.append((s * jax.nn.sigmoid(s) * unit).astype(BF))
         gated_ref[rows, :] = jnp.concatenate(gated, axis=1) if heads > 1 else gated[0]
-
-
-def vmem_call(body, out_shapes, scratch, limit, cost, name):
+        for ref, out in (
+            (q_ref, q_any), (k_ref, k_any), (swish_ref, swish_any), (gated_ref, gated_any)
+        ):
+            moves.store(ref.at[rows], out.at[rows])
+        moves.store(v_ref.at[:, rows], v_any.at[:, rows])
+        moves.store(retained_ref.at[:, rows], retained_any.at[:, rows])
+    moves.close()
+
+
+def retention_forward(mixed, weight, cosine, sine, table, heads, offsets):
+    length, width = mixed.shape
+    qk, vd = heads * KEY_HEAD, heads * VAL_HEAD
+    outputs = (
+        ((length, qk), BF),
+        ((length, qk), BF),
+        ((heads, length, VAL_HEAD), BF),
+        ((length, vd), F32),
+        ((heads, length, VAL_HEAD), BF),
+        ((length, vd), BF),
+    )
+    blocks = length // BLOCK
     return pl.pallas_call(
-        body,
-        out_shape=out_shapes,
-        scratch_shapes=scratch,
-        compiler_params=pltpu.CompilerParams(vmem_limit_bytes=limit * 1024 * 1024),
-        cost_estimate=pl.CostEstimate(flops=cost, bytes_accessed=0, transcendentals=0),
-        name=name,
-    )
-
-
-def retention_forward(x, gain, weight, cosine, sine, heads, offsets):
-    length, width = x.shape
-    qk, vd = heads * KEY_HEAD, heads * VAL_HEAD
-    return vmem_call(
         functools.partial(retention_kernel, heads, offsets),
-        (
-            jax.ShapeDtypeStruct((length, width), BF),
-            jax.ShapeDtypeStruct((length, qk), BF),
-            jax.ShapeDtypeStruct((length, qk), BF),
-            jax.ShapeDtypeStruct((heads, length, VAL_HEAD), BF),
-            jax.ShapeDtypeStruct((length, vd), F32),
-            jax.ShapeDtypeStruct((heads, length, VAL_HEAD), BF),
-            jax.ShapeDtypeStruct((length, vd), BF),
+        out_shape=tuple(jax.ShapeDtypeStruct(*out) for out in outputs),
+        in_specs=[ANYWHERE, ANYWHERE, IN_VMEM, IN_VMEM, IN_VMEM],
+        out_specs=(ANYWHERE,) * 6,
+        scratch_shapes=[pltpu.VMEM(mixed.shape, BF), pltpu.VMEM(weight.shape, BF)]
+        + [pltpu.VMEM(*out) for out in outputs]
+        + [pltpu.SemaphoreType.DMA((4 + 7 * blocks,))],
+        compiler_params=pltpu.CompilerParams(vmem_limit_bytes=60 * 1024 * 1024),
+        cost_estimate=pl.CostEstimate(
+            flops=30_000_000_000, bytes_accessed=0, transcendentals=0
         ),
-        [],
-        56,
-        30_000_000_000,
-        "retention",
-    )(x, gain, weight, cosine, sine)
+        name="retention",
+    )(mixed, weight, cosine, sine, table)
+
+
+def gate_back_rows(heads, rows, branch, w_ref, swish_ref, retained_ref, dswish_ref, dret_ref):
+    gated_grad = times_transposed(branch, w_ref[...])
+    swish_parts = []
+    for h in range(heads):
+        lanes = head_lanes(h, VAL_HEAD)
+        grad, s = gated_grad[:, lanes], swish_ref[rows, lanes]
+        gate = jax.nn.sigmoid(s)
+        unit, factor, above = norm_parts(retained_ref[h, rows, :].astype(F32))
+        swish_parts.append((grad * unit * (gate * (1.0 + s * (1.0 - gate)))).astype(BF))
+        g = grad * (s * gate)
+        along = jnp.where(above, jnp.mean(g * unit, axis=-1, keepdims=True), 0.0)
+        back = factor * (g - jnp.mean(g, axis=-1, keepdims=True) - unit * along)
+        dret_ref[h, rows, :] = back.astype(BF)
+    dswish_ref[rows, :] = pad_lanes(swish_parts, dswish_ref.shape[1])
 
 
 def gate_back_kernel(heads, branch_ref, w_ref, swish_ref, retained_ref, dswish_ref, dret_ref):
-    blocks = branch_ref.shape[0] // BLOCK
-
-    @pl.loop(0, blocks)
-    def _(i):
-        rows = rows_of(i)
-        gated_grad = times_transposed(branch_ref[rows, :], w_ref[...])
-        swish_parts = []
-        for h in range(heads):
-            lanes = slice(h * VAL_HEAD, (h + 1) * VAL_HEAD)
-            grad, s = gated_grad[:, lanes], swish_ref[rows, lanes]
-            gate = jax.nn.sigmoid(s)
-            unit, factor, above = norm_parts(retained_ref[h, rows, :].astype(F32))
-            swish_parts.append((grad * unit * (gate * (1.0 + s * (1.0 - gate)))).astype(BF))
-            g = grad * (s * gate)
-            along = jnp.where(above, jnp.mean(g * unit, axis=-1, keepdims=True), 0.0)
-            back = factor * (g - jnp.mean(g, axis=-1, keepdims=True) - unit * along)
-            dret_ref[h, rows, :] = back.astype(BF)
-        dswish_ref[rows, :] = pad_lanes(swish_parts, dswish_ref.shape[1])
+    for i in range(branch_ref.shape[0] // BLOCK):
+        rows = slice(i * BLOCK, (i + 1) * BLOCK)
+        gate_back_rows(
+            heads, rows, branch_ref[rows, :], w_ref, swish_ref, retained_ref, dswish_ref, dret_ref
+        )
 
 
 def gate_backward(branch, weight, swish, retained, heads, padded):
     length = branch.shape[0]
-    return vmem_call(
+    return pl.pallas_call(
         functools.partial(gate_back_kernel, heads),
-        (
+        out_shape=(
             jax.ShapeDtypeStruct((length, padded), BF),
             jax.ShapeDtypeStruct((heads, length, VAL_HEAD), BF),
         ),
-        [],
-        48,
-        12_000_000_000,
-        "gate_back",
+        compiler_params=pltpu.CompilerParams(vmem_limit_bytes=48 * 1024 * 1024),
+        name="gate_back",
     )(branch, weight, swish, retained)
 
 
+def retention_back_head(
+    h, heads, q_ref, k_ref, v_ref, dret_ref, table_ref, cos_ref, sin_ref, dqk_ref, dv_ref,
+    dk_sum, dv_sum,
+):
+    blocks = q_ref.shape[0] // BLOCK
+    lanes = head_lanes(h, KEY_HEAD)
+    for i in reversed(range(blocks)):
+        rows = slice(i * BLOCK, (i + 1) * BLOCK)
+        seen = slice(0, (i + 1) * BLOCK)
+        query, grad = q_ref[rows, lanes], dret_ref[h, rows, :]
+        key, value = k_ref[seen, lanes], v_ref[h, seen, :]
+        decay = table_ref[h, :, (blocks - 1 - i) * BLOCK :]
+        weights = (times_transposed(query, key) * decay).astype(BF)
+        score = (times_transposed(grad, value) * decay).astype(BF)
+        dq = product(score, key).astype(BF).astype(F32)
+        dqk_ref[rows, lanes] = rotate_pair(
+            dq, cos_ref[rows, :], sin_ref[rows, :], back=True
+        ).astype(BF)
+        if i == blocks - 1:
+            dk_sum[...] = transposed_times(score, query)
+            dv_sum[...] = transposed_times(weights, grad)
+        else:
+            dk_sum[seen, :] += transposed_times(score, query)
+            dv_sum[seen, :] += transposed_times(weights, grad)
+    dk = rotate_pair(
+        dk_sum[...].astype(BF).astype(F32), cos_ref[...], sin_ref[...], back=True
+    ) * (KEY_HEAD**-0.5)
+    dqk_ref[:, head_lanes(heads + h, KEY_HEAD)] = dk.astype(BF)
+    return dv_sum[...].astype(BF)
+
+
 def retention_back_kernel(
-    heads, q_ref, k_ref, v_ref, dret_ref, cos_ref, sin_ref, dqk_ref, dv_ref, dq_sum, dv_sum
+    heads, q_ref, k_ref, v_ref, dret_ref, table_ref, cos_ref, sin_ref, dqk_ref, dv_ref,
+    dk_sum, dv_sum,
 ):
-    first_head = lax.axis_index("seq") * heads
-    blocks = q_ref.shape[0] // BLOCK
-    qk = heads * KEY_HEAD
-    dq_sum[...] = jnp.zeros_like(dq_sum)
-    for h in range(heads):
-        rate = head_rate(first_head + h)
-        lanes = slice(h * KEY_HEAD, (h + 1) * KEY_HEAD)
-
-        @pl.loop(0, blocks)
-        def _(j):
-            there = rows_of(j)
-            full, lower = decay_tile(rate)
-            key, value = k_ref[there, lanes], v_ref[h, there, :]
-
-            def step(i, decay, sums):
-                rows = rows_of(i)
-                query, grad = q_ref[rows, lanes], dret_ref[h, rows, :]
-                weights = (times_transposed(query, key) * decay).astype(BF)
-                score = (times_transposed(grad, value) * decay).astype(BF)
-                dq_sum[rows, lanes] += product(score, key)
-                return (
-                    sums[0] + transposed_times(score, query),
-                    sums[1] + transposed_times(weights, grad),
-                )
-
-            sums = (jnp.zeros((BLOCK, KEY_HEAD), F32), jnp.zeros((BLOCK, VAL_HEAD), F32))
-            sums = step(j, lower, sums)
-
-            def later(i, sums):
-                return step(i, full * jnp.exp(rate * ((i - j) * BLOCK).astype(F32)), sums)
-
-            dk, dv = lax.fori_loop(j + 1, blocks, later, sums)
-            dk = rotate_pair(
-                dk.astype(BF).astype(F32), cos_ref[there, :], sin_ref[there, :], back=True
-            )
-            dqk_ref[there, qk + h * KEY_HEAD : qk + (h + 1) * KEY_HEAD] = (
-                dk * (KEY_HEAD**-0.5)
-            ).astype(BF)
-            dv_sum[h, there, :] = dv.astype(BF)
-
-    @pl.loop(0, blocks)
-    def _(i):
-        rows = rows_of(i)
-        cosine, sine = cos_ref[rows, :], sin_ref[rows, :]
-        for h in range(heads):
-            lanes = slice(h * KEY_HEAD, (h + 1) * KEY_HEAD)
-            dq = dq_sum[rows, lanes].astype(BF).astype(F32)
-            dqk_ref[rows, lanes] = rotate_pair(dq, cosine, sine, back=True).astype(BF)
-        dv_ref[rows, :] = pad_lanes([dv_sum[h, rows, :] for h in range(heads)], dv_ref.shape[1])
-
-
-def retention_backward(q, k, v, dret, cosine, sine, heads, padded):
+    parts = [
+        retention_back_head(
+            h, heads, q_ref, k_ref, v_ref, dret_ref, table_ref, cos_ref, sin_ref, dqk_ref, dv_ref,
+            dk_sum, dv_sum,
+        )
+        for h in range(heads)
+    ]
+    dv_ref[...] = pad_lanes(parts, dv_ref.shape[1])
+
+
+def retention_backward(q, k, v, dret, table, cosine, sine, heads, padded):
     length = q.shape[0]
     qk = heads * KEY_HEAD
-    return vmem_call(
+    return pl.pallas_call(
         functools.partial(retention_back_kernel, heads),
-        (
+        out_shape=(
             jax.ShapeDtypeStruct((length, 2 * qk), BF),
             jax.ShapeDtypeStruct((length, padded), BF),
         ),
-        [pltpu.VMEM((length, qk), F32), pltpu.VMEM((heads, length, VAL_HEAD), BF)],
-        48,
-        12_000_000_000,
-        "retention_back",
-    )(q, k, v, dret, cosine, sine)
+        scratch_shapes=[
+            pltpu.VMEM((length, KEY_HEAD), F32),
+            pltpu.VMEM((length, VAL_HEAD), F32),
+        ],
+        compiler_params=pltpu.CompilerParams(vmem_limit_bytes=48 * 1024 * 1024),
+        name="retention_back",
+    )(q, k, v, dret, table, cosine, sine)
 
 
 def transfer_cost(elements):
@@ -627,34 +644,30 @@
     return pl.ds(pl.multiple_of((lax.axis_index("seq") ^ k) * rows, rows), rows)
 
 
-class Moves:
-    def __init__(self, sems):
-        self.sems, self.used, self.open = sems, 0, []
-
-    def start(self, source, target):
-        copy = pltpu.make_async_copy(source, target, self.sems.at[self.used])
-        self.used += 1
-        copy.start()
-        return copy
-
-    def store(self, source, target):
-        self.open.append(self.start(source, target))
-
-    def close(self):
-        for copy in self.open:
-            copy.wait()
+def load_output(moves, cut, swapped_any, w_ref):
+    loads = []
+    for block in range(swapped_any.shape[1]):
+        for k in range(swapped_any.shape[0]):
+            skip, at = cut.skip(k), block * cut.rows + cut.start(k)
+            loads.append(
+                moves.start(
+                    swapped_any.at[k, block, slice(skip, cut.width)],
+                    w_ref.at[slice(at + skip, at + cut.width)],
+                )
+            )
+    return loads
 
 
 def project_kernel(
-    g_any, w_any, x_ref, gain_ref, middle_ref, own_ref,
+    cut, g_any, w_any, x_ref, gain_ref, middle_ref, own_ref,
     g_ref, w_ref, parts, inbox_x, inbox_y, via_x, via_y, out_x, out_y, sends, recvs, locals_,
 ):
     me = lax.axis_index("seq")
     rows = x_ref.shape[0]
     half = rows // 2
     moves = Moves(locals_)
-    load_w = moves.start(w_any, w_ref)
-    load_g = moves.start(g_any, g_ref)
+    loads = load_output(moves, cut, w_any, w_ref)
+    loads.append(moves.start(g_any, g_ref))
     greet((me ^ 1, me ^ 2))
     boxes = (inbox_x, inbox_y, via_x, via_y, out_x, out_y)
     copies, finish, total = square_parts(parts, boxes, sends, recvs, 0)
@@ -662,8 +675,8 @@
     def part(k):
         parts[k] = product(g_ref[block_rows(k, rows), :], w_ref[...]).astype(BF)
 
-    load_w.wait()
-    load_g.wait()
+    for load in loads:
+        load.wait()
     part(3)
     copies[0].start()
     copies[1].start()
@@ -692,10 +705,6 @@
         pltpu.VMEM((rows // 2, width), BF),
         pltpu.VMEM((rows // 2, width), BF),
     ]
-
-
-IN_VMEM = pl.BlockSpec(memory_space=pltpu.VMEM)
-ANYWHERE = pl.BlockSpec(memory_space=pl.ANY)
 
 
 def square_call(body, out_shape, out_specs, scratch, inputs, call, cost, name):
@@ -733,15 +742,16 @@
     )(*[value for value, _ in inputs])
 
 
-def project_and_norm(gated, weight, x, gain, call):
+def project_and_norm(gated, swapped, x, gain, cut, call):
     rows, width = x.shape
     return comm_call(
-        project_kernel,
-        [(gated, False), (weight, False), (x, True), (gain[None, :], True)],
+        functools.partial(project_kernel, cut),
+        [(gated, False), (swapped, False), (x, True), (gain[None, :], True)],
         [((rows, width), F32, True), ((rows, width), BF, True)],
-        [pltpu.VMEM(gated.shape, BF), pltpu.VMEM(weight.shape, BF)] + square_scratch(rows, width),
+        [pltpu.VMEM(gated.shape, BF), pltpu.VMEM((gated.shape[1], width), BF)]
+        + square_scratch(rows, width),
         6,
-        2,
+        9,
         call,
         x.size,
         "project_and_norm",
@@ -957,88 +967,71 @@
     return back, grad * unit
 
 
-def input_back_kernel(
-    at_value, at_swish, dqk_ref, dv_ref, ds_ref, w_ref, x_ref, grad_ref, gain_ref, dx_ref, term_ref,
-    parts, inbox_x, inbox_y, via_x, via_y, out_x, out_y, sends, recvs,
-):
+def square_pass(own, out_ref, sends, recvs, first, half):
     me = lax.axis_index("seq")
-    rows = x_ref.shape[0]
-    half = rows // 2
-    greet((me ^ 1, me ^ 2))
-    boxes = (inbox_x, inbox_y, via_x, via_y, out_x, out_y)
-    copies, finish, total = square_parts(parts, boxes, sends, recvs, 0)
-
-    def part(k):
-        here = block_rows(k, rows)
-        parts[k] = (
-            times_transposed(dqk_ref[here, :], w_ref[:, :at_value])
-            + times_transposed(dv_ref[here, :], w_ref[:, at_value:at_swish])
-            + times_transposed(ds_ref[here, :], w_ref[:, at_swish:])
-        ).astype(BF)
-
-    part(3)
-    copies[0].start()
-    copies[1].start()
-    part(1)
-    copies[2].start()
-    part(2)
-    copies[3].start()
-    part(0)
-    finish()
-    term = jnp.zeros((1, x_ref.shape[1]), F32)
-    for i in range(2):
-        here = slice(i * half, (i + 1) * half)
-        back, terms = norm_back(x_ref[here, :].astype(F32), total(here), gain_ref[...])
-        dx_ref[here, :] = (grad_ref[here, :] + back).astype(BF)
-        term = term + jnp.sum(terms, axis=0, keepdims=True)
-    term_ref[...] = term
-    for copy in copies:
-        copy.wait_send()
-
-
-def input_backward(dqk, dv, ds, weight, x, grad, gain, at_value, at_swish, call):
-    rows, width = x.shape
-    dx, term = square_call(
-        functools.partial(input_back_kernel, at_value, at_swish),
-        (
-            jax.ShapeDtypeStruct((rows, width), BF),
-            jax.ShapeDtypeStruct((1, width), F32),
+    across, along = me ^ 1, me ^ 2
+    spans = (slice(0, half), slice(half, own.shape[0]))
+
+    def part(ref, i):
+        return ref.at[spans[i]]
+
+    return [
+        remote(part(own, 0), part(out_ref.at[me], 0), sends, recvs, first, across),
+        remote(part(own, 1), part(out_ref.at[me], 1), sends, recvs, first + 1, along),
+        remote(part(own, 1), part(out_ref.at[me], 1), sends, recvs, first + 2, across),
+        remote(part(own, 0), part(out_ref.at[me], 0), sends, recvs, first + 3, along),
+        remote(
+            part(out_ref.at[across], 0), part(out_ref.at[across], 0), sends, recvs, first + 4, along
         ),
-        (IN_VMEM, IN_VMEM),
-        square_scratch(rows, width)
-        + [pltpu.SemaphoreType.DMA((6,)), pltpu.SemaphoreType.DMA((6,))],
-        (dqk, dv, ds, weight, x, grad, gain[None, :]),
-        call,
-        x.size,
-        "input_backward",
-    )
-    return dx, term[0]
-
-
-def weight_rows(left_ref, right, out_ref):
-    @pl.loop(0, out_ref.shape[0] // BLOCK)
-    def _(b):
-        lanes = rows_of(b)
-        out_ref[lanes, :] = transposed_times(left_ref[:, lanes], right).astype(BF)
+        remote(
+            part(out_ref.at[along], 1), part(out_ref.at[along], 1), sends, recvs, first + 5, across
+        ),
+    ]
+
+
+def pass_on(copies):
+    copies[0].wait_recv()
+    copies[4].start()
+    copies[1].wait_recv()
+    copies[5].start()
+
+
+def half_rows(rows):
+    return -(-rows // 32) * 16
 
 
 def gate_back_scatter_kernel(
-    heads, starts, branch_ref, w_ref, swish_ref, retained_ref, column_ref, hidden_any, down_any,
-    mixed_any, gated_any, m_any, dswish_ref, dret_ref, dws_any, dwo_any, out_ref,
-    hidden_ref, down_ref, mixed_ref, gated_ref, m_ref, dws_ref, dwo_ref, wide,
+    heads, cut, branch_any, w_any, swish_any, retained_any, column_any, hidden_any, down_any,
+    mixed_any, gated_any, m_any, dswish_any, dret_any, dws_any, dwo_any, out_ref,
+    branch_ref, w_ref, swish_ref, retained_ref, column_ref, hidden_ref, down_ref, mixed_ref,
+    gated_ref, m_ref, dswish_ref, dret_ref, dws_ref, dwo_ref,
     parts, inbox_x, inbox_y, via_x, via_y, out_x, out_y, sends, recvs, locals_,
 ):
     me = lax.axis_index("seq")
     rows = out_ref.shape[0]
+    half = rows // 2
     moves = Moves(locals_)
+    load_down = moves.start(down_any, down_ref)
     load_hidden = moves.start(hidden_any, hidden_ref)
-    load_down = moves.start(down_any, down_ref)
+    load_gate = load_output(moves, cut, w_any, w_ref)
+    blocks = branch_ref.shape[0] // BLOCK
+    load_rows = []
+    for i in range(blocks):
+        here = slice(i * BLOCK, (i + 1) * BLOCK)
+        load_rows.append(
+            [
+                moves.start(branch_any.at[here], branch_ref.at[here]),
+                moves.start(swish_any.at[here], swish_ref.at[here]),
+                moves.start(retained_any.at[:, here], retained_ref.at[:, here]),
+            ]
+        )
     load_mixed = moves.start(mixed_any, mixed_ref)
+    load_column = moves.start(column_any, column_ref)
     load_gated = moves.start(gated_any, gated_ref)
     load_m = moves.start(m_any, m_ref)
     greet((me ^ 1, me ^ 2))
     boxes = (inbox_x, inbox_y, via_x, via_y, out_x, out_y)
-    copies, finish, total = square_parts(parts, boxes, sends, recvs, 0)
+    copies, _, total = square_parts(parts, boxes, sends, recvs, 0)
 
     def part(k):
         here = block_rows(k, rows)
@@ -1053,9 +1046,17 @@
     copies[2].start()
     part(2)
     copies[3].start()
-    part(0)
-    gate_back_kernel(heads, branch_ref, w_ref, swish_ref, retained_ref, dswish_ref, dret_ref)
-    half = rows // 2
+    for load in load_gate:
+        load.wait()
+    for i in range(blocks):
+        here = slice(i * BLOCK, (i + 1) * BLOCK)
+        for load in load_rows[i]:
+            load.wait()
+        gate_back_rows(
+            heads, here, branch_ref[here, :], w_ref, swish_ref, retained_ref, dswish_ref, dret_ref
+        )
+    moves.store(dswish_ref, dswish_any)
+    moves.store(dret_ref, dret_any)
     copies[0].wait_recv()
     out_y[...] = (parts[2, :half].astype(F32) + via_x[...].astype(F32)).astype(BF)
     copies[4].start()
@@ -1065,21 +1066,30 @@
     padded = dswish_ref.shape[1]
     spare = lax.broadcasted_iota(jnp.int32, (BLOCK, padded), 1) == heads * VAL_HEAD
     load_mixed.wait()
+    load_column.wait()
     for b in range(dws_ref.shape[0] // BLOCK):
-        lanes = slice(b * BLOCK, (b + 1) * BLOCK)
-        term = transposed_times(mixed_ref[:, lanes], dswish_ref[...])
-        dws_ref[lanes, :] = jnp.where(spare, column_ref[lanes, :], term).astype(BF)
-        moves.store(dws_ref.at[lanes], dws_any.at[lanes])
+        here = slice(b * BLOCK, (b + 1) * BLOCK)
+        term = product(mixed_ref[here, :], dswish_ref[...])
+        dws_ref[here, :] = jnp.where(spare, column_ref[here, :], term).astype(BF)
+        moves.store(dws_ref.at[here], dws_any.at[here])
     load_gated.wait()
-    step = 2 * BLOCK
+    step, tile, lane = 2 * BLOCK, 16, 128
     for h in range(heads):
-        value_lanes = slice(h * VAL_HEAD, (h + 1) * VAL_HEAD)
+        value_lanes = head_lanes(h, VAL_HEAD)
         for b in range(branch_ref.shape[1] // step):
             lanes = slice(b * step, (b + 1) * step)
-            wide[...] = transposed_times(gated_ref[:, value_lanes], branch_ref[:, lanes]).astype(BF)
-            for k, start in enumerate(starts):
-                dwo_ref[k, h, :, lanes] = wide[start : start + dwo_ref.shape[2], :]
-    moves.store(dwo_ref, dwo_any)
+            wide = transposed_times(gated_ref[:, value_lanes], branch_ref[:, lanes]).astype(BF)
+            for k in range(4):
+                for r in range(cut.width // tile):
+                    at = cut.start(k) + r * tile
+                    for c in range(step // lane):
+                        dwo_ref[
+                            h, k,
+                            (b * step // lane + c) * tile : (b * step // lane + c + 1) * tile,
+                            r * lane : (r + 1) * lane,
+                        ] = wide[at : at + tile, c * lane : (c + 1) * lane]
+        moves.store(dwo_ref.at[h], dwo_any.at[h])
+    part(0)
     load_m.wait()
     for copy in copies[2:]:
         copy.wait_recv()
@@ -1090,47 +1100,30 @@
 
 
 def gate_backward_scatter(
-    branch, weight, swish, retained, column, hidden, down, mixed, gated, middle, heads, padded, cut,
-    call,
+    branch, swapped, swish, retained, column, hidden, down, mixed_t, gated, middle, heads, padded,
+    cut, call,
 ):
     length, width = branch.shape
     rows = middle.shape[0]
-    starts = [cut.start(k) for k in range(4)]
-    dwo = (4, heads, cut.width, width)
+    dwo = (heads, 4, width // 8, cut.width * 8)
+    inputs = (branch, swapped, swish, retained, column, hidden, down, mixed_t, gated, middle)
+    weight = jax.ShapeDtypeStruct((heads * VAL_HEAD, width), BF)
+    outputs = [
+        ((length, padded), BF, False),
+        ((heads, length, VAL_HEAD), BF, False),
+        ((width, padded), BF, False),
+        (dwo, BF, False),
+        ((rows, width), BF, True),
+    ]
     return comm_call(
-        functools.partial(gate_back_scatter_kernel, heads, starts),
-        [
-            (branch, True),
-            (weight, True),
-            (swish, True),
-            (retained, True),
-            (column, True),
-            (hidden, False),
-            (down, False),
-            (mixed, False),
-            (gated, False),
-            (middle, False),
-        ],
-        [
-            ((length, padded), BF, True),
-            ((heads, length, VAL_HEAD), BF, True),
-            ((width, padded), BF, False),
-            (dwo, BF, False),
-            ((rows, width), BF, True),
-        ],
-        [
-            pltpu.VMEM(hidden.shape, BF),
-            pltpu.VMEM(down.shape, BF),
-            pltpu.VMEM(mixed.shape, BF),
-            pltpu.VMEM(gated.shape, BF),
-            pltpu.VMEM(middle.shape, F32),
-            pltpu.VMEM((width, padded), BF),
-            pltpu.VMEM(dwo, BF),
-            pltpu.VMEM((VAL_HEAD, 2 * BLOCK), BF),
-        ]
+        functools.partial(gate_back_scatter_kernel, heads, cut),
+        [(value, False) for value in inputs],
+        outputs,
+        [pltpu.VMEM(v.shape, v.dtype) for v in (branch, weight) + inputs[2:]]
+        + [pltpu.VMEM(shape, kind) for shape, kind, _ in outputs[:4]]
         + square_scratch(rows, width),
         6,
-        6 + width // BLOCK,
+        20 + 3 * length // BLOCK + width // BLOCK,
         call,
         middle.size,
         "gate_back_scatter",
@@ -1138,57 +1131,294 @@
 
 
 def retention_back_exchange_kernel(
-    heads, q_ref, k_ref, v_ref, dret_ref, cos_ref, sin_ref, mixed_ref, send_ref,
-    dqk_ref, dv_ref, dwqk_ref, came_ref, dq_sum, dv_sum, sends, recvs, local,
+    heads, q_any, k_any, v_any, dret_any, table_ref, cos_ref, sin_ref, mixed_any, send_any, share_any,
+    dqk_any, dv_any, merged_any, full_any,
+    q_ref, k_ref, v_ref, dret_ref, mixed_ref, send_ref, dqk_ref, dv_ref, dwqk_ref, twin_ref, sum_ref,
+    zero_ref, dk_sum, dv_sum, sends, recvs, locals_,
 ):
     me = lax.axis_index("seq")
-    greet((me ^ 1, me ^ 2, me ^ 3))
-    keep = pltpu.make_async_copy(send_ref.at[me], came_ref.at[me], local)
-    keep.start()
-    copies = [
-        remote(send_ref.at[me ^ k], came_ref.at[me], sends, recvs, k - 1, me ^ k) for k in (3, 1, 2)
+    shard = lax.axis_index("fsdp")
+    core = lax.rem(shard, 2)
+    moves = Moves(locals_)
+    load_send = moves.start(send_any, send_ref)
+    loads = [
+        moves.start(source, target)
+        for source, target in (
+            (q_any, q_ref), (k_any, k_ref), (v_any, v_ref), (dret_any, dret_ref)
+        )
     ]
-    for copy in copies:
+    load_mixed = moves.start(mixed_any, mixed_ref)
+    barrier = pltpu.get_barrier_semaphore()
+    for k in (1, 2, 3):
+        pl.semaphore_signal(barrier, inc=1, device_id={"seq": me ^ k}, device_id_type=MESH)
+    pl.semaphore_signal(barrier, inc=1, device_id={"fsdp": shard ^ 1}, device_id_type=MESH)
+    pl.semaphore_wait(barrier, 4)
+    load_send.wait()
+    twin = pltpu.make_async_remote_copy(
+        src_ref=send_ref.at[1 - core],
+        dst_ref=twin_ref,
+        send_sem=sends.at[9],
+        recv_sem=recvs.at[9],
+        device_id={"fsdp": shard ^ 1},
+        device_id_type=MESH,
+    )
+    twin.start()
+    passed = square_pass(share_any, full_any, sends, recvs, 0, half_rows(share_any.shape[0]))
+    for copy in passed[:4]:
         copy.start()
-    retention_back_kernel(
-        heads, q_ref, k_ref, v_ref, dret_ref, cos_ref, sin_ref, dqk_ref, dv_ref, dq_sum, dv_sum
-    )
-    weight_rows(mixed_ref, dqk_ref[...], dwqk_ref)
-    for copy in copies:
-        copy.wait()
-    keep.wait()
-
-
-def retention_backward_exchange(q, k, v, dret, cosine, sine, mixed, send, heads, padded, call):
-    length, width = mixed.shape
+    moves.store(share_any, full_any.at[me])
+    step, wide = sum_ref.shape[1:]
+    at = dqk_ref.shape[1]
+
+    def place(column, parity):
+        return merged_any.at[
+            pl.ds(pl.multiple_of((2 * column + parity) * step, step), step), pl.ds(at, wide)
+        ]
+
+    zero_ref[...] = jnp.zeros_like(zero_ref)
+    for column in range(4):
+        moves.store(zero_ref, place(column, 1 - core))
+    for load in loads:
+        load.wait()
+    parts = []
+    swaps = [
+        remote(sum_ref.at[me ^ k], place(me, core), sends, recvs, 5 + k, me ^ k) for k in (3, 1, 2)
+    ]
+    for h in range(heads):
+        parts.append(
+            retention_back_head(
+                h, heads, q_ref, k_ref, v_ref, dret_ref, table_ref, cos_ref, sin_ref, dqk_ref,
+                dv_ref, dk_sum, dv_sum,
+            )
+        )
+        if h == 0:
+            twin.wait_recv()
+            for k in range(4):
+                sum_ref[k] = (send_ref[core, k].astype(F32) + twin_ref[k].astype(F32)).astype(BF)
+            for copy in swaps:
+                copy.start()
+            moves.store(sum_ref.at[me], place(me, core))
+            pass_on(passed)
+    dv_ref[...] = pad_lanes(parts, dv_ref.shape[1])
+    moves.store(dv_ref, dv_any)
+    moves.store(dqk_ref, dqk_any)
+    load_mixed.wait()
+    for b in range(mixed_ref.shape[0] // BLOCK):
+        here = slice(b * BLOCK, (b + 1) * BLOCK)
+        dwqk_ref[here, :] = product(mixed_ref[here, :], dqk_ref[...]).astype(BF)
+        moves.store(dwqk_ref.at[here], merged_any.at[here, slice(0, at)])
+    for copy in passed[2:] + swaps:
+        copy.wait_recv()
+    moves.close()
+    for copy in passed + swaps + [twin]:
+        copy.wait_send()
+
+
+def retention_backward_exchange(
+    q, k, v, dret, table, cosine, sine, mixed_t, send, share, heads, padded, call
+):
+    width, length = mixed_t.shape
     qk = heads * KEY_HEAD
+    inputs = (
+        (q, False), (k, False), (v, False), (dret, False), (table, True), (cosine, True),
+        (sine, True), (mixed_t, False), (send, False), (share, False),
+    )
+    staged = (q, k, v, dret, mixed_t, send)
+    block = send.shape[1:]
+    return comm_call(
+        functools.partial(retention_back_exchange_kernel, heads),
+        inputs,
+        [
+            ((length, 2 * qk), BF, False),
+            ((length, padded), BF, False),
+            ((width, 2 * qk + block[2]), BF, False),
+            ((4,) + share.shape, BF, False),
+        ],
+        [pltpu.VMEM(value.shape, BF) for value in staged]
+        + [
+            pltpu.VMEM((length, 2 * qk), BF),
+            pltpu.VMEM((length, padded), BF),
+            pltpu.VMEM((width, 2 * qk), BF),
+            pltpu.VMEM(block, BF),
+            pltpu.VMEM(block, BF),
+            pltpu.VMEM(block[1:], BF),
+            pltpu.VMEM((length, KEY_HEAD), F32),
+            pltpu.VMEM((length, VAL_HEAD), F32),
+        ],
+        10,
+        16 + width // BLOCK,
+        call,
+        send.size // 4,
+        "retention_back_exchange",
+    )
+
+
+def input_back_kernel(
+    offsets, dqk_any, dv_any, ds_any, w_any, x_any, grad_any, gain_ref, share_any,
+    dx_ref, term_ref, full_any, dqk_ref, dv_ref, ds_ref, w_ref, x_ref, grad_ref,
+    parts, inbox_x, inbox_y, via_x, via_y, out_x, out_y, sends, recvs, locals_,
+):
+    at_value, at_swish = offsets
+    me = lax.axis_index("seq")
+    rows = x_ref.shape[0]
+    half = rows // 2
+    moves = Moves(locals_)
+    spans = (slice(0, at_value), slice(at_value, at_swish), slice(at_swish, w_ref.shape[1]))
+    grads = ((dqk_any, dqk_ref), (dv_any, dv_ref), (ds_any, ds_ref))
+    loads = []
+    for span, (source, target) in zip(spans, grads, strict=True):
+        loads.append(moves.start(source, target))
+        loads.append(moves.start(w_any.at[:, span], w_ref.at[:, span]))
+    load_x = moves.start(x_any, x_ref)
+    load_grad = moves.start(grad_any, grad_ref)
+    greet((me ^ 1, me ^ 2))
+    boxes = (inbox_x, inbox_y, via_x, via_y, out_x, out_y)
+    copies, _, total = square_parts(parts, boxes, sends, recvs, 0)
+    passed = square_pass(share_any, full_any, sends, recvs, 6, half_rows(share_any.shape[0]))
+    passed[0].start()
+    passed[1].start()
+    moves.store(share_any, full_any.at[me])
+
+    def part(k):
+        here = block_rows(k, rows)
+        whole = 0.0
+        for n, (_, ref) in enumerate(grads):
+            if k == 3:
+                loads[2 * n].wait()
+                loads[2 * n + 1].wait()
+            whole = whole + times_transposed(ref[here, :], w_ref[:, spans[n]])
+        parts[k] = whole.astype(BF)
+
+    part(3)
+    copies[0].start()
+    copies[1].start()
+    part(1)
+    copies[2].start()
+    part(2)
+    copies[3].start()
+    pass_on(passed)
+    copies[0].wait_recv()
+    out_y[...] = (parts[2, :half].astype(F32) + via_x[...].astype(F32)).astype(BF)
+    copies[4].start()
+    copies[1].wait_recv()
+    out_x[...] = (parts[1, half:].astype(F32) + via_y[...].astype(F32)).astype(BF)
+    copies[5].start()
+    passed[2].start()
+    passed[3].start()
+    part(0)
+    for copy in copies[2:]:
+        copy.wait_recv()
+    load_x.wait()
+    load_grad.wait()
+    term = jnp.zeros((1, x_ref.shape[1]), F32)
+    for i in range(2):
+        here = slice(i * half, (i + 1) * half)
+        back, terms = norm_back(x_ref[here, :].astype(F32), total(here), gain_ref[...])
+        dx_ref[here, :] = (grad_ref[here, :] + back).astype(BF)
+        term = term + jnp.sum(terms, axis=0, keepdims=True)
+    term_ref[...] = term
+    for copy in passed[2:]:
+        copy.wait_recv()
+    moves.close()
+    for copy in copies + passed:
+        copy.wait_send()
+
+
+def input_backward(dqk, dv, ds, weight, x, grad, gain, share, offsets, call):
+    rows, width = x.shape
+    staged = (dqk, dv, ds, weight, x, grad)
+    dx, term, full = comm_call(
+        functools.partial(input_back_kernel, offsets),
+        [(value, False) for value in staged] + [(gain[None, :], True), (share, False)],
+        [
+            ((rows, width), BF, True),
+            ((1, width), F32, True),
+            ((4,) + share.shape, BF, False),
+        ],
+        [pltpu.VMEM(value.shape, value.dtype) for value in staged] + square_scratch(rows, width),
+        12,
+        9,
+        call,
+        x.size + share.size,
+        "input_backward",
+    )
+    return dx, term[0], full
+
+
+def join(pieces):
+    return jnp.concatenate(pieces, axis=1) if len(pieces) > 1 else pieces[0]
+
+
+def unpack_columns_kernel(width, in_ref, out_ref):
+    out_ref[...] = join([in_ref[k][:, :width].astype(F32) for k in range(in_ref.shape[0])])
+
+
+def unpack_columns(gathered, at, width):
+    count, rows, whole = gathered.shape
+    block = rows // 4 if rows % 64 == 0 else rows
+    padded = -(-width // 128) * 128
     return pl.pallas_call(
-        functools.partial(retention_back_exchange_kernel, heads),
-        out_shape=(
-            jax.ShapeDtypeStruct((length, 2 * qk), BF),
-            jax.ShapeDtypeStruct((length, padded), BF),
-            jax.ShapeDtypeStruct((width, 2 * qk), BF),
-            jax.ShapeDtypeStruct(send.shape, BF),
-        ),
-        in_specs=[IN_VMEM] * 7 + [ANYWHERE],
-        out_specs=(IN_VMEM,) * 3 + (ANYWHERE,),
-        scratch_shapes=[
-            pltpu.VMEM((length, qk), F32),
-            pltpu.VMEM((heads, length, VAL_HEAD), BF),
-            pltpu.SemaphoreType.DMA((3,)),
-            pltpu.SemaphoreType.DMA((3,)),
-            pltpu.SemaphoreType.DMA,
-        ],
-        compiler_params=pltpu.CompilerParams(
-            collective_id=call, has_side_effects=True, vmem_limit_bytes=56 * 1024 * 1024
-        ),
-        cost_estimate=transfer_cost(send.size // 4 * 3 // 2),
-        name="retention_back_exchange",
-    )(q, k, v, dret, cosine, sine, mixed, send)
-
-
-def after(values, *others):
-    return lax.optimization_barrier((values,) + others)[0]
+        functools.partial(unpack_columns_kernel, width),
+        grid=(rows // block,),
+        in_specs=[pl.BlockSpec((count, block, padded), lambda i: (0, i, at // padded))],
+        out_specs=pl.BlockSpec((block, count * width), lambda i: (i, 0)),
+        out_shape=jax.ShapeDtypeStruct((rows, count * width), F32),
+        name="unpack_columns",
+    )(gathered)
+
+
+def unpack_hidden_kernel(cut, shards, in_ref, gate_ref, up_ref):
+    count = in_ref.shape[0]
+    for n, out_ref in enumerate((gate_ref, up_ref)):
+        pieces = []
+        for f in range(shards):
+            for k in range(count):
+                at = (n * shards + f) * cut.width
+                if cut.skip(k) < cut.width:
+                    piece = in_ref[k][:, at + cut.skip(k) : at + cut.width]
+                    pieces.append(piece.astype(F32))
+        out_ref[...] = join(pieces)
+
+
+def unpack_hidden(gathered, cut, shards):
+    count, rows, whole = gathered.shape
+    block = rows // 4 if rows % 64 == 0 else rows
+    wide = shards * cut.rows
+    return pl.pallas_call(
+        functools.partial(unpack_hidden_kernel, cut, shards),
+        grid=(rows // block,),
+        in_specs=[pl.BlockSpec((count, block, whole), lambda i: (0, i, 0))],
+        out_specs=[pl.BlockSpec((block, wide), lambda i: (i, 0))] * 2,
+        out_shape=[jax.ShapeDtypeStruct((rows, wide), F32)] * 2,
+        name="unpack_hidden",
+    )(gathered)
+
+
+def unpack_output_kernel(cut, in_ref, out_ref):
+    tile, lane = 16, 128
+    for k in range(in_ref.shape[0]):
+        for r in range(cut.skip(k) // tile, cut.width // tile):
+            at = cut.start(k) + r * tile
+            for c in range(out_ref.shape[1] // lane):
+                out_ref[at : at + tile, c * lane : (c + 1) * lane] = in_ref[
+                    k, c * tile : (c + 1) * tile, r * lane : (r + 1) * lane
+                ].astype(F32)
+
+
+def unpack_output(gathered, at, cut, width):
+    count, rows, whole = gathered.shape
+    wide = whole - at
+    return pl.pallas_call(
+        functools.partial(unpack_output_kernel, cut),
+        out_shape=jax.ShapeDtypeStruct((cut.rows, width), F32),
+        compiler_params=pltpu.CompilerParams(vmem_limit_bytes=32 * 1024 * 1024),
+        name="unpack_output",
+    )(gathered[:, :, at:])
+
+
+def after(values, *others, all_of=False):
+    held = lax.optimization_barrier((values,) + others)
+    return held if all_of else held[0]
 
 
 class Cut:
@@ -1291,28 +1521,27 @@
     inputs = local_input.astype(F32)
 
     blocks = shards // seq_count
-    output_pieces = after(output_pieces, upstream_full)
+    mixed_low = normalize(input_full.astype(F32), mixer_scale).astype(BF)
+    mixed_turned = mixed_low.T
+    output_pieces = after(output_pieces, upstream_full, gains)
     swapped = exchange_seq(output_pieces.reshape(seq_count, blocks, cut.width, width), 2)
-    output_full = jnp.concatenate(
-        [
-            cut.assemble([swapped[piece, block] for piece in range(seq_count)], 0)
-            for block in range(blocks)
-        ],
-        axis=0,
-    )
     feed_weight = gather_rows(after(feed_piece, swapped))
 
     cosine, sine = rotation_tables(length, KEY_HEAD // 2)
-    mixed_low, query_low, key_low, value_low, swish_pre, retained, gated_low = retention_forward(
-        input_full, mixer_scale[None, :], attention_weight, cosine, sine, per_device,
-        (qk, 2 * qk, 2 * qk + vd_pad),
+    head_ids = me * per_device + jnp.arange(per_device, dtype=jnp.int32)
+    table = decay_table(head_ids, length)
+    attention_weight, mixed_low, mixed_turned, table = after(
+        attention_weight, mixed_low, mixed_turned, table, all_of=True
+    )
+    query_low, key_low, value_low, swish_pre, retained, gated_low = retention_forward(
+        mixed_low, attention_weight, cosine, sine, table, per_device, (qk, 2 * qk, 2 * qk + vd_pad)
     )
 
     kept_rows = lax.broadcasted_iota(jnp.int32, down_piece.shape, 0) >= cut.skip(me)
     down_full = gather_rows(after(jnp.where(kept_rows, down_piece, jnp.zeros_like(down_piece)), gated_low))
     if square:
         middle, channel_own = project_and_norm(
-            gated_low, output_full, local_input, channel_scale, 3
+            gated_low, swapped, local_input, channel_scale, cut, 3
         )
         both_pre, hidden_low, down_term, channel_full = feed_forward_gather(
             channel_own, feed_weight, upstream_full, 4
@@ -1325,6 +1554,13 @@
         feed_share = scatter_rows(feed_term)
         branch_full = whole(branch_own, 7)
     else:
+        output_full = jnp.concatenate(
+            [
+                cut.assemble([swapped[piece, block] for piece in range(seq_count)], 0)
+                for block in range(blocks)
+            ],
+            axis=0,
+        )
         middle = inputs + scatter_seq(product(gated_low, output_full).astype(BF), 3)
         channel_full = whole(normalize(middle, channel_scale).astype(BF), 4)
         gate_pre, up_pre, hidden_low = feed_forward(channel_full, feed_weight)
@@ -1344,20 +1580,19 @@
     spare = lax.broadcasted_iota(jnp.int32, (width, vd_pad), 1) == vd
     if square:
         swish_grad, retained_grad, swish_term, output_send, layer_output = gate_backward_scatter(
-            after(branch_full, down_share), output_full, swish_pre, retained,
-            channel_term[:, None], hidden_low, down_full, mixed_low, gated_low, middle,
+            after(branch_full, down_share), swapped, swish_pre, retained,
+            channel_term[:, None], hidden_low, down_full, mixed_turned, gated_low, middle,
             per_device, vd_pad, cut, 5,
         )
         swish_share = scatter_rows(swish_term)
-        key_grad, value_grad, key_term, output_swapped = retention_backward_exchange(
-            query_low, key_low, value_low, retained_grad, cosine, sine, mixed_low,
-            after(output_send, feed_share), per_device, vd_pad, 8,
-        )
-        output_share = scatter_rows(output_swapped.reshape(shards * cut.width, width))
-        key_share = scatter_rows(key_term)
-        input_gradient, mixer_term = input_backward(
+        key_grad, value_grad, merged_term, down_all = retention_backward_exchange(
+            query_low, key_low, value_low, after(retained_grad, feed_share), table, cosine, sine,
+            mixed_turned, output_send, down_share, per_device, vd_pad, 8,
+        )
+        merged_share = scatter_rows(merged_term)
+        input_gradient, mixer_term, feed_all = input_backward(
             key_grad, value_grad, swish_grad, attention_weight, local_input, middle_grad,
-            mixer_scale, at_value, at_swish, 9,
+            mixer_scale, feed_share, (at_value, at_swish), 9,
         )
     else:
         swish_grad, retained_grad = gate_backward(
@@ -1369,7 +1604,7 @@
         result = middle + scatter_seq(hidden_part, 5)
         layer_output = result.astype(BF)
         key_grad, value_grad = retention_backward(
-            query_low, key_low, value_low, retained_grad, cosine, sine, per_device, vd_pad
+            query_low, key_low, value_low, retained_grad, table, cosine, sine, per_device, vd_pad
         )
         key_term = transposed_times(mixed_low, key_grad).astype(BF)
         key_share = scatter_rows(key_term)
@@ -1399,46 +1634,44 @@
     value_share = scatter_rows(value_term)
 
     layer_output = layer_output.reshape(groups, local_length, width)
-    down_all = gather_seq(after(down_share, value_term), 10)
-    feed_all = gather_seq(after(feed_share, down_all), 11)
-    swish_all = gather_seq(after(swish_share, feed_all), 13)
-    output_all = gather_seq(after(output_share, swish_all), 12)
-    key_all = gather_seq(after(key_share, output_all), 15)
-    value_all = gather_seq(after(value_share, key_all), 14)
-    down_gradient = cut.assemble([down_all[k] for k in range(seq_count)], 0).astype(F32)
-    output_gradient = cut.assemble([output_all[k] for k in range(seq_count)], 0).astype(F32)
-
-    def hidden_order(at):
-        pieces = [feed_all[k][:, at : at + ff] for k in range(seq_count)]
-        return jnp.concatenate(
-            [
-                cut.assemble(
-                    [piece[:, f * cut.width : (f + 1) * cut.width] for piece in pieces], 1
-                )
-                for f in range(shards)
-            ],
-            axis=1,
-        ).astype(F32)
-
-    def attention_order(gathered, at, wide):
-        pieces = [gathered[k][:, at : at + wide] for k in range(seq_count)]
-        return jnp.concatenate(pieces, axis=1).astype(F32)
+    if square:
+        down_gradient = cut.assemble([down_all[k] for k in range(seq_count)], 0).astype(F32)
+        gelu_gradient, linear_gradient = unpack_hidden(after(feed_all, value_term), cut, shards)
+        swish_all = gather_seq(after(swish_share, gelu_gradient), 13)
+        merged_all = gather_seq(after(merged_share, swish_all), 15)
+        output_gradient = unpack_output(merged_all, at_value, cut, width)
+        query_gradient = unpack_columns(merged_all, 0, qk)
+        key_gradient = unpack_columns(merged_all, qk, qk)
+        value_share = after(value_share, merged_all)
+    else:
+        down_all = gather_seq(down_share, 10)
+        feed_all = gather_seq(after(feed_share, down_all), 11)
+        swish_all = gather_seq(after(swish_share, feed_all), 13)
+        output_all = gather_seq(after(output_share, swish_all), 12)
+        key_all = gather_seq(after(key_share, output_all), 15)
+        value_share = after(value_share, key_all)
+        down_gradient = cut.assemble([down_all[k] for k in range(seq_count)], 0).astype(F32)
+        output_gradient = cut.assemble([output_all[k] for k in range(seq_count)], 0).astype(F32)
+        gelu_gradient, linear_gradient = unpack_hidden(feed_all, cut, shards)
+        query_gradient = unpack_columns(key_all, 0, qk)
+        key_gradient = unpack_columns(key_all, qk, qk)
+    value_all = gather_seq(value_share, 14)
 
     def gain_order(gathered):
-        return sum(gathered[k][:, vd].astype(F32) for k in range(seq_count))
+        return jnp.sum(gathered[:, :, vd].astype(F32), axis=0)
 
     return (
         layer_output,
         input_gradient,
         gain_order(value_all),
-        attention_order(key_all, 0, qk),
-        attention_order(key_all, qk, qk),
-        attention_order(value_all, 0, vd),
-        attention_order(swish_all, 0, vd),
+        query_gradient,
+        key_gradient,
+        unpack_columns(value_all, 0, vd),
+        unpack_columns(swish_all, 0, vd),
         output_gradient,
         gain_order(swish_all),
-        hidden_order(0),
-        hidden_order(ff),
+        gelu_gradient,
+        linear_gradient,
         down_gradient,
     )
 

time: 734 us -> 660 us (0.90)
  Pallas kernels: 602 us -> 557 us
  local copies, waits for them, and re-layouts: 46.6 us -> 29.1 us
  waiting for transfers between devices: 12.9 us -> 2.5 us
    pallas_call x4 -> x6, Pallas kernels: 188 us -> 280 us  [comm_call(): pl.pallas_call(body, out_shape=tuple((jax.ShapeDtypeStruct(shape, kind) f...]
    pallas_call x3 -> x7, Pallas kernels: 135 us -> 59.1 us  [the longest x1 34.7 us: retention_forward(): pl.pallas_call(functools.partial(retention_kernel, heads, offsets), out_s...]
    pallas_call x9 -> x6, Pallas kernels: 239 us -> 175 us  [gather_seq(): pl.pallas_call(body, out_shape=jax.ShapeDtypeStruct((count,) + values.sha...]
    concatenate x5 -> x0, local copies, waits for them, and re-layouts: 12.5 us -> none  [the longest x2 5.93 us: hidden_order(): jnp.concatenate([cut.assemble([piece[:, f * cut.width:(f + 1) * cut.width...]
    all_gather x4, waiting for transfers between devices: 12 us -> 0.04 us  [gather_rows(): return lax.all_gather(values, 'fsdp', axis=0, tiled=True)]
    convert_element_type x7 -> x2, other arithmetic: 13.4 us -> 2.94 us  [the longest x1 2.74 us: on_device(): mixed_low = normalize(input_full.astype(F32), mixer_scale).astype(BF)]
    squeeze x5 -> x0, local copies, waits for them, and re-layouts: 10.5 us -> none  [the longest x2 5.21 us: attention_order(): pieces = [gathered[k][:, at:at + wide] for k in range(seq_count)]]
    reduce_sum x0 -> x4, other arithmetic: none -> 7.8 us  [the longest x2 3.6 us: gain_order(): return jnp.sum(gathered[:, :, vd].astype(F32), axis=0)]
  transfers between devices with their start and end apart: 10 -> 9, of which waited for: 1 -> 1; matrix products, arithmetic and copies ran while one was open for 9% -> 9% of each run, Pallas kernels for 81% -> 81%
where the time goes in v4:
time: 660 us; the launch traced here: 657 us
  Pallas kernels  557 us (84%)
  local copies, waits for them, and re-layouts  29.1 us (4%)
  other arithmetic  27.2 us (4%)
  between operations  14.5 us (2%)
  matrix products  12.9 us (2%)
  blocking collectives  12.1 us (2%)
    pallas_call x6, Pallas kernels, comm_call(): pl.pallas_call(body, out_shape=tuple((jax.ShapeDtypeStruct(shape, kind) f...  280 us
    pallas_call x6, Pallas kernels, gather_seq(): pl.pallas_call(body, out_shape=jax.ShapeDtypeStruct((count,) + values.sha...  175 us
    pallas_call x1, Pallas kernels, exchange_seq(): pl.pallas_call(functools.partial(exchange_kernel, count), out_shape=jax.S...  42.7 us
    pallas_call x1, Pallas kernels, retention_forward(): pl.pallas_call(functools.partial(retention_kernel, heads, offsets), out_s...  34.7 us
    pallas_call x4, Pallas kernels, unpack_columns(): pl.pallas_call(functools.partial(unpack_columns_kernel, width), grid=(row...  15.6 us
  transfers between devices with their start and end apart: 9, of which 1 were waited for; matrix products, arithmetic and copies ran while one was open for 9% of the time, Pallas kernels for 81%

profile of v4, /device:TPU:0, one launch (start us, length us, event | category | flops | bytes accessed | tf_op | source)
XLA Modules:
  0.0 656.7 jit_solution(2057967838423826135)
XLA Ops:
  7.2 0.0 all-gather.7.cloned.1.call-start
  7.2 1.4 copy-done
  8.7 0.9 constant_dynamic-slice_fusion
  9.6 0.0 all-gather.5.cloned.1.call-start
  9.6 1.1 constant_dynamic-slice_fusion.3
  10.7 1.8 constant_dynamic-slice_fusion.1
  12.5 1.2 fusion.6
  13.7 0.0 all-gather.9.cloned.1.call-start
  13.8 39.0 %gather_seq_0.1 = bf16[4,256,2048]{2,1,0:T(8,128)(2,1)} custom-call(bf16[256,2048]{1,0:T(8,128)(2,1)} %bitcast.40), custom_call_target="tpu_custom_call" | custom-call | bytes 125829120 | tf_op jit(solution)/shard_map/gather_seq_0/pallas_call | solution.py:371
  52.8 6.4 copy.35
  59.3 35.8 %gather_seq_1.1 = bf16[4,256,2048]{2,1,0:T(8,128)(2,1)} custom-call(bf16[256,2048]{1,0:T(8,128)(2,1)} %bitcast.43), custom_call_target="tpu_custom_call" | custom-call | bytes 125829120 | tf_op jit(solution)/shard_map/gather_seq_1/pallas_call | solution.py:371
  95.1 12.1 %all_gather.16 = bf16[2,2048]{1,0:T(2,128)(2,1)S(1)} all-gather(bf16[2,256]{1,0:T(2,128)(2,1)S(1)} %pad_maximum_fusion.1), channel_id=1, replica_groups=mesh['seq'=4,'fsdp'=8] {'fsdp'}, dimensions={1}, use_global_device_ids=true | all-gather | bytes 9216 | tf_op jit(solution)/shard_map/all_gather | solution.py:1509
  107.2 2.4 fusion.7
  109.6 2.4 fusion.8
  112.0 1.0 pad_maximum_fusion
  113.0 42.7 %exchange_seq_2.1.w_any = bf16[4,2,112,2048]{3,2,1,0:T(8,128)(2,1)} custom-call(bf16[4,2,112,2048]{3,2,1,0:T(8,128)(2,1)} %bitcast.46), custom_call_target="tpu_custom_call" | custom-call | bytes 440401920 | tf_op jit(solution)/shard_map/exchange_seq_2/pallas_call | solution.py:403
  155.8 0.3 all-gather.11.cloned.1.call-start
  156.1 3.0 convert_reduce_fusion
  159.0 0.6 copy-done.3
  159.6 1.2 fusion.1
  160.9 0.2 fusion.9
  161.2 2.8 fusion.10
  164.0 0.2 maximum_convert_fusion.1
  164.2 1.7 exponential_select_fusion.table_ref
  166.0 0.6 slice_convert_fusion
  166.6 2.0 dynamic-slice_select_fusion
  168.6 4.6 fusion.23.mixed_any
  173.1 2.7 multiply_convert_fusion
  175.8 6.7 %copy.29.mixed_any = bf16[1024,2048]{1,0:T(8,128)(2,1)} copy(bf16[1024,2048]{0,1:T(8,128)(2,1)} %multiply_convert_fusion) | data formatting | bytes 8388608 | tf_op jit(solution)/shard_map/optimization_barrier | solution.py:1420
  182.6 34.7 %retention.1 = (bf16[1024,512]{1,0:T(8,128)(2,1)}, bf16[1024,512]{1,0:T(8,128)(2,1)}, bf16[2,1024,432]{2,1,0:T(8,128)(2,1)}, f32[1024,864]{1,0:T(8,128)}, bf16[2...) custom-call(bf16[1024,2048]{1,0:T(8,128)(2,1)} %copy.29.mixed_any, ...), custom_call_target="tpu_custom_call" | custom-call | flops 30000001024 | tf_op jit(solution)/shard_map/retention/pallas_call | solution.py:180
  217.3 0.0 reduce-scatter.6.cloned.1.call-start
  217.4 44.1 %project_and_norm.1 = (f32[256,2048]{1,0:T(8,128)}, bf16[256,2048]{1,0:T(8,128)(2,1)}) custom-call(bf16[1024,864]{1,0:T(8,128)(2,1)} %get-tuple-element.61.g_any.gated_any, bf16[4,2,112,2048]{3,2,1,0:T(8,128)(2,1)} %exchange_seq_2.1.w_any, bf16[256,2048]{1,0:T(8,128)(2,1)} %bitcast.41, f32[1,2048]{1,0:T(1,128)} %get-tuple-element.105.gain_ref), custom_call_target="tpu_custom_call" | custom-call | bytes 125829120 | tf_op jit(solution)/shard_map/project_and_norm/pallas_call | solution.py:726
  261.5 0.0 all-gather.9.cloned.1.call-done.w_any
  261.5 41.8 %feed_forward_gather.1 = (f32[1024,1792]{1,0:T(8,128)}, bf16[1024,896]{1,0:T(8,128)(2,1)}, bf16[896,2048]{1,0:T(8,128)(2,1)}, bf16[4,256,2048]{2,1,0:T(8,128)(2,1)}) custom-call(bf16[256,2048]{1,0:T(8,128)(2,1)} %get-tuple-element.63.x_any, bf16[2048,1792]{1,0:T(8,128)(2,1)} %all-gather.9.cloned.1.call-done.w_any, bf16[1024,2048]{1,0:T(8,128)(2,1)} %bitcast.37), custom_call_target="tpu_custom_call" | custom-call | bytes 125829120 | tf_op jit(solution)/shard_map/feed_forward_gather/pallas_call | solution.py:726
  303.3 0.0 reduce-scatter.8.cloned.1.call-start
  303.4 49.4 %feed_back_scatter.1 = (f32[256,2048]{1,0:T(8,128)}, f32[1,2048]{1,0:T(1,128)}, bf16[256,2048]{1,0:T(8,128)(2,1)}, bf16[2048,1792]{1,0:T(8,128)(2,1)}) custom-call(bf16[1024,2048]{1,0:T(8,128)(2,1)} %bitcast.38, f32[1024,1792]{1,0:T(8,128)} %get-tuple-element.67.both_any, bf16[2048,1792]{1,0:T(8,128)(2,1)} %all-gather.9.cloned.1.call-done.w_any, ...), custom_call_target="tpu_custom_call" | custom-call | bytes 125829120 | tf_op jit(solution)/shard_map/feed_back_scatter/pallas_call | solution.py:726
  352.8 0.3 reduce-scatter.14.cloned.1.call-start
  353.1 35.1 %gather_seq_7.1 = bf16[4,256,2048]{2,1,0:T(8,128)(2,1)} custom-call(bf16[256,2048]{1,0:T(8,128)(2,1)} %get-tuple-element.71.x_ref), custom_call_target="tpu_custom_call" | custom-call | bytes 125829120 | tf_op jit(solution)/shard_map/gather_seq_7/pallas_call | solution.py:371
  388.2 1.3 copy.32.column_any
  389.6 38.4 %gate_back_scatter.1 = (bf16[1024,896]{1,0:T(8,128)(2,1)}, bf16[2,1024,432]{2,1,0:T(8,128)(2,1)}, bf16[2048,896]{1,0:T(8,128)(2,1)}, bf16[2,4,256,896]{3,2,1,0:T(8,128)(2,1)}, bf16[256,2048]{1,0:T(8,128)(2,1)}) custom-call(bf16[1024,2048]{1,0:T(8,128)(2,1)} %bitcast.39, bf16[4,2,112,2048]{3,2,1,0:T(8,128)(2,1)} %exchange_seq_2.1.w_any, ...), custom_call_target="tpu_custom_call" | custom-call | bytes 125829120 | tf_op jit(solution)/shard_map/gate_back_scatter/pallas_call | solution.py:726
  428.1 0.2 reduce-scatter.12.cloned.1.call-start
  428.3 2.3 reduce-scatter.8.cloned.1.call-done.share_any
  430.6 40.5 %retention_back_exchange.1 = (bf16[1024,1024]{1,0:T(8,128)(2,1)}, bf16[1024,896]{1,0:T(8,128)(2,1)}, bf16[2048,1920]{1,0:T(8,128)(2,1)}, bf16[4,112,2048]{2,1,0:T(8,128)(2,1)}) custom-call(bf16[1024,512]{1,0:T(8,128)(2,1)} %get-tuple-element.79.q_any, bf16[1024,512]{1,0:T(8,128)(2,1)} %get-tuple-element.80.k_any, ...), custom_call_target="tpu_custom_call" | custom-call | bytes 110100480 | tf_op jit(solution)/shard_map/retention_back_exchange/pallas_call | solution.py:726
  471.1 0.3 reduce-scatter.10.cloned.1.call-start
  471.4 66.1 %input_backward.1 = (bf16[256,2048]{1,0:T(8,128)(2,1)}, f32[1,2048]{1,0:T(1,128)}, bf16[4,256,1792]{2,1,0:T(8,128)(2,1)}) custom-call(bf16[1024,1024]{1,0:T(8,128)(2,1)} %get-tuple-element.86.dqk_any, bf16[1024,896]{1,0:T(8,128)(2,1)} %get-tuple-element.87.dv_any, bf16[1024,896]{1,0:T(8,128)(2,1)} %get-tuple-element.88.ds_any, ...), custom_call_target="tpu_custom_call" | custom-call | bytes 235929600 | tf_op jit(solution)/shard_map/input_backward/pallas_call | solution.py:726
  537.6 8.2 %select_convert_fusion = bf16[2048,896]{1,0:T(8,128)(2,1)} fusion(f32[2048]{0:T(1024)} %bitcast.56, pred[896]{0:T(1024)(128)(4,1)S(1)} %iota_compare_fusion.3, bf16[1024,2048]{0,1:T(8,128)(2,1)} %multiply_convert_fusion, bf16[1024,896]{1,0:T(8,128)(2,1)S(1)} %copy-done.5), kind=kOutput, calls=%fused_computation.6 | convolution fusion | flops 3759931392 | bytes 9708416 | tf_op jit(solution)/shard_map/dot_general | solution.py:31
  545.8 6.7 %unpack_hidden.1 = (f32[256,3456]{1,0:T(8,128)}, f32[256,3456]{1,0:T(8,128)}) custom-call(bf16[4,256,1792]{2,1,0:T(8,128)(2,1)} %get-tuple-element.95.in_ref), custom_call_target="tpu_custom_call" | custom-call | tf_op jit(solution)/shard_map/unpack_hidden/pallas_call | solution.py:1387
  552.5 16.6 %gather_seq_13.1.in_ref = bf16[4,256,896]{2,1,0:T(8,128)(2,1)} custom-call(bf16[256,896]{1,0:T(8,128)(2,1)} %reduce-scatter.14.cloned.1.call-done.x_ref), custom_call_target="tpu_custom_call" | custom-call | bytes 55050240 | tf_op jit(solution)/shard_map/gather_seq_13/pallas_call | solution.py:371
  569.1 4.2 unpack_columns.7
  573.3 1.7 convert_reduce_fusion.1
  575.0 1.0 slice_bitcast_fusion.3
  576.0 1.5 slice_bitcast_fusion.2
  577.5 2.2 maximum_convert_fusion
  579.7 32.6 %gather_seq_15.1.in_ref = bf16[4,256,1920]{2,1,0:T(8,128)(2,1)} custom-call(bf16[256,1920]{1,0:T(8,128)(2,1)} %reduce-scatter.12.cloned.1.call-done.x_ref), custom_call_target="tpu_custom_call" | custom-call | bytes 117964800 | tf_op jit(solution)/shard_map/gather_seq_15/pallas_call | solution.py:371
  612.3 2.9 slice.35.in_ref
  615.2 3.6 unpack_columns.4
  618.8 3.6 unpack_columns.5
  622.3 16.0 %gather_seq_14.1.in_ref = bf16[4,256,896]{2,1,0:T(8,128)(2,1)} custom-call(bf16[256,896]{1,0:T(8,128)(2,1)} %reduce-scatter.10.cloned.1.call-done.x_ref), custom_call_target="tpu_custom_call" | custom-call | bytes 55050240 | tf_op jit(solution)/shard_map/gather_seq_14/pallas_call | solution.py:371
  638.3 4.2 unpack_columns.6
  642.6 1.9 convert_reduce_fusion.2
  644.4 1.5 copy-done.2
  645.9 2.0 unpack_output.1
  647.9 1.0 copy.40
  648.9 1.0 copy.41
  (56 shorter events, 0.4 us)
Async XLA Ops:
  7.2 1.5 copy-start
  7.2 105.8 %all-gather.7.cloned.1.call-start = ((), (), s32[]{:S(2)}) async-start(), calls=%async_computation.6 | async-start | bytes 4128768 | tf_op jit(solution)/shard_map/all_gather | solution.py:1484
  9.6 166.3 %all-gather.5.cloned.1.call-start = ((), (), s32[]{:S(2)}) async-start(), calls=%async_computation.5 | async-start | bytes 12976128 | tf_op jit(solution)/shard_map/all_gather | solution.py:1484
  13.7 247.7 %all-gather.9.cloned.1.call-start = ((), (), s32[]{:S(2)}) async-start(), calls=%async_computation.7 | async-start | bytes 8257536 | tf_op jit(solution)/shard_map/all_gather | solution.py:1484
  52.8 6.4 copy-start.12
  52.8 6.4 copy-start.13
  59.2 48.0 %copy-start.10 = (bf16[256,3456]{1,0:T(8,128)(2,1)S(1)}, bf16[256,3456]{1,0:T(8,128)(2,1)}, u32[]{:S(2)}) copy-start(bf16[256,3456]{1,0:T(8,128)(2,1)} %param.20) | copy-start | bytes 5308420
  107.2 2.4 copy-start.11
  155.8 147.6 %all-gather.11.cloned.1.call-start = ((), (), s32[]{:S(2)}) async-start(), calls=%async_computation.8 | async-start | bytes 4128768 | tf_op jit(solution)/shard_map/all_gather | solution.py:1484
  156.0 3.6 copy-start.3
  166.6 6.5 copy-start.8
  168.5 4.6 copy-start.4
  217.3 172.3 %reduce-scatter.6.cloned.1.call-start = ((), (), s32[]{:S(2)}) async-start(), calls=%async_computation.9 | async-start | bytes 4128768 | tf_op jit(solution)/shard_map/reduce_scatter | solution.py:1487
  303.3 127.3 %reduce-scatter.8.cloned.1.call-start = ((), (), s32[]{:S(2)}) async-start(), calls=%async_computation.10 | async-start | bytes 8257536 | tf_op jit(solution)/shard_map/reduce_scatter | solution.py:1487
  352.8 35.4 %copy-start.9 = (f32[1,2048]{1,0:T(1,128)S(1)}, f32[1,2048]{1,0:T(1,128)}, u32[]{:S(2)}) copy-start(f32[1,2048]{1,0:T(1,128)} %get-tuple-element.75) | copy-start | bytes 24580
  352.8 199.6 %reduce-scatter.14.cloned.1.call-start = ((), (), s32[]{:S(2)}) async-start(), calls=%async_computation.13 | async-start | bytes 4128768 | tf_op jit(solution)/shard_map/reduce_scatter | solution.py:1487
  428.1 151.7 %reduce-scatter.12.cloned.1.call-start = ((), (), s32[]{:S(2)}) async-start(), calls=%async_computation.12 | async-start | bytes 8847360 | tf_op jit(solution)/shard_map/reduce_scatter | solution.py:1487
  471.1 151.2 %reduce-scatter.10.cloned.1.call-start = ((), (), s32[]{:S(2)}) async-start(), calls=%async_computation.11 | async-start | bytes 4128768 | tf_op jit(solution)/shard_map/reduce_scatter | solution.py:1487
  471.4 66.2 %copy-start.5 = (bf16[1024,896]{1,0:T(8,128)(2,1)S(1)}, bf16[1024,896]{1,0:T(8,128)(2,1)}, u32[]{:S(2)}) copy-start(bf16[1024,896]{1,0:T(8,128)(2,1)} %get-tuple-element.87.dv_any) | copy-start | bytes 5505028
  642.5 7.3 %copy-start.1 = (bf16[432,2048]{1,0:T(8,128)(2,1)S(1)}, bf16[432,2048]{1,0:T(8,128)(2,1)}, u32[]{:S(2)}) copy-start(bf16[432,2048]{1,0:T(8,128)(2,1)} %param.18) | copy-start | bytes 5308420
  644.4 1.5 copy-start.2
  645.9 2.0 copy-start.6
  645.9 3.0 copy-start.7
Sparse Core Ops, SparseCore 0:
  10.2 45.2 all-gather.6
  57.8 107.0 all-gather.4
  167.1 71.6 all-gather.8
  240.9 41.1 all-gather.10
  303.4 43.7 reduce-scatter.5
  352.9 77.5 reduce-scatter.7
  432.9 43.3 reduce-scatter.13
  478.6 83.1 reduce-scatter.11
  564.1 43.3 reduce-scatter.9

commit v5 on v4

--- a/solution.py
+++ b/solution.py
@@ -61,14 +61,18 @@
 BLOCK = 256
 
 
-def decay_table(head_ids, length):
-    rates = jnp.log1p(-jnp.exp2(-5.0 - head_ids.astype(F32)))
-    gap = (
-        jnp.arange(length - BLOCK, length, dtype=jnp.int32)[:, None]
-        - jnp.arange(length, dtype=jnp.int32)[None, :]
-    )
-    decay = jnp.exp(jnp.maximum(gap, 0).astype(F32)[None] * rates[:, None, None])
-    return jnp.where(gap[None] >= 0, decay, 0.0)
+def decay_tables(head_ids, length):
+    rates = jnp.log1p(-jnp.exp2(-5.0 - head_ids.astype(F32)))[:, None, None]
+    short = jnp.arange(BLOCK, dtype=jnp.int32)
+    long = jnp.arange(2 * length - BLOCK, dtype=jnp.int32)
+
+    def decay(gap):
+        far = jnp.exp(jnp.maximum(gap, 0).astype(F32)[None] * rates)
+        return jnp.where(gap[None] >= 0, far, 0.0)
+
+    by_row = decay(length - BLOCK + short[:, None] - long[None, :])
+    by_column = decay(long[:, None] - (length - BLOCK) - short[None, :])
+    return by_row, by_column
 
 
 def norm_parts(values):
@@ -104,71 +108,142 @@
             copy.wait()
 
 
+def norm_kernel(x_ref, gain_ref, out_ref, turned_ref):
+    normed = normalize(x_ref[...].astype(F32), gain_ref[...])
+    out_ref[...] = normed.astype(BF)
+    turned_ref[...] = normed.T.astype(BF)
+
+
+def norm_and_turn(x, gain):
+    length, width = x.shape
+    return pl.pallas_call(
+        norm_kernel,
+        grid=(length // BLOCK,),
+        in_specs=[
+            pl.BlockSpec((BLOCK, width), lambda i: (i, 0)),
+            pl.BlockSpec((1, width), lambda i: (0, 0)),
+        ],
+        out_specs=[
+            pl.BlockSpec((BLOCK, width), lambda i: (i, 0)),
+            pl.BlockSpec((width, BLOCK), lambda i: (0, i)),
+        ],
+        out_shape=[
+            jax.ShapeDtypeStruct((length, width), BF),
+            jax.ShapeDtypeStruct((width, length), BF),
+        ],
+        compiler_params=pltpu.CompilerParams(vmem_limit_bytes=32 * 1024 * 1024),
+        name="norm_and_turn",
+    )(x, gain[None, :])
+
+
+class Series:
+    def __init__(self, moves, count, ends):
+        self.sems, self.first, self.count, self.ends = moves.sems, moves.used, count, ends
+        moves.used += count
+
+    def copy(self, i):
+        return pltpu.make_async_copy(*self.ends(i), self.sems.at[self.first + i])
+
+    def start_all(self):
+        for i in range(self.count):
+            self.copy(i).start()
+        return self
+
+    def wait_all(self):
+        for i in range(self.count):
+            self.copy(i).wait()
+
+
+def by_block(moves, count, source, target, rows=BLOCK):
+    def ends(i):
+        here = pl.ds(i * rows if isinstance(i, int) else pl.multiple_of(i * rows, rows), rows)
+        if len(source.shape) == 3:
+            return source.at[:, here], target.at[:, here]
+        return source.at[here], target.at[here]
+
+    return Series(moves, count, ends)
+
+
 def retention_kernel(
     heads, offsets, mixed_any, w_any, cos_ref, sin_ref, table_ref,
     q_any, k_any, v_any, swish_any, retained_any, gated_any,
     mixed_ref, w_ref, q_ref, k_ref, v_ref, swish_ref, retained_ref, gated_ref, sems,
+    between=None,
 ):
     at_key, at_value, at_swish = offsets
-    blocks = mixed_ref.shape[0] // BLOCK
-    moves = Moves(sems)
+    length = mixed_ref.shape[0]
+    blocks = length // BLOCK
+    moves = sems if isinstance(sems, Moves) else Moves(sems)
     spans = (
         slice(0, at_key), slice(at_key, at_value), slice(at_value, at_swish),
         slice(at_swish, w_ref.shape[1]),
     )
-    loads = []
-    for i in range(blocks):
-        rows = slice(i * BLOCK, (i + 1) * BLOCK)
-        loads.append(moves.start(mixed_any.at[rows], mixed_ref.at[rows]))
-        if i == 0:
-            weights = [moves.start(w_any.at[:, span], w_ref.at[:, span]) for span in spans]
-    for i in range(blocks):
-        rows = slice(i * BLOCK, (i + 1) * BLOCK)
-        seen = slice(0, (i + 1) * BLOCK)
-        loads[i].wait()
+    loads = by_block(moves, blocks, mixed_any, mixed_ref)
+    loads.copy(0).start()
+    weights = [moves.start(w_any.at[:, span], w_ref.at[:, span]) for span in spans]
+    for i in range(1, blocks):
+        loads.copy(i).start()
+    stores = [
+        by_block(moves, blocks, source, target)
+        for source, target in (
+            (q_ref, q_any), (k_ref, k_any), (v_ref, v_any), (swish_ref, swish_any),
+            (retained_ref, retained_any), (gated_ref, gated_any),
+        )
+    ]
+    k_ref[...] = jnp.zeros_like(k_ref)
+    v_ref[...] = jnp.zeros_like(v_ref)
+    if between is not None:
+        between(-1)
+
+    @pl.loop(0, blocks)
+    def _(i):
+        rows = rows_of(i)
+        loads.copy(i).wait()
         mixed = mixed_ref[rows, :]
         cosine, sine = cos_ref[rows, :], sin_ref[rows, :]
+
+        def projected(n):
+            @pl.when(i == 0)
+            def _():
+                weights[n].wait()
+
+            return product(mixed, w_ref[:, spans[n]])
+
         for n, (target, scale) in enumerate(((q_ref, 1.0), (k_ref, KEY_HEAD**-0.5))):
-            if i == 0:
-                weights[n].wait()
-            pre = product(mixed, w_ref[:, spans[n]])
+            pre = projected(n)
             for h in range(heads):
                 lanes = head_lanes(h, KEY_HEAD)
                 turned = rotate_pair(pre[:, lanes], cosine, sine)
                 target[rows, lanes] = (turned * scale if n else turned).astype(BF)
-        if i == 0:
-            weights[2].wait()
-        value = product(mixed, w_ref[:, spans[2]])
+        value = projected(2)
         for h in range(heads):
             v_ref[h, rows, :] = value[:, head_lanes(h, VAL_HEAD)].astype(BF)
-        if i == 0:
-            weights[3].wait()
-        swish = product(mixed, w_ref[:, spans[3]])[:, : heads * VAL_HEAD]
-        swish_ref[rows, :] = swish
+        swish_ref[rows, :] = projected(3)[:, : heads * VAL_HEAD]
         gated = []
         for h in range(heads):
             lanes = head_lanes(h, KEY_HEAD)
-            scores = times_transposed(q_ref[rows, lanes], k_ref[seen, lanes])
-            decay = table_ref[h, :, (blocks - 1 - i) * BLOCK :]
-            retained = product((scores * decay).astype(BF), v_ref[h, seen, :]).astype(BF)
+            scores = times_transposed(q_ref[rows, lanes], k_ref[:, lanes])
+            decay = table_ref[
+                h, :, pl.ds(pl.multiple_of((blocks - 1 - i) * BLOCK, BLOCK), length)
+            ]
+            retained = product((scores * decay).astype(BF), v_ref[h]).astype(BF)
             retained_ref[h, rows, :] = retained
             unit, _, _ = norm_parts(retained.astype(F32))
-            s = swish[:, head_lanes(h, VAL_HEAD)]
+            s = swish_ref[rows, head_lanes(h, VAL_HEAD)]
             gated.append((s * jax.nn.sigmoid(s) * unit).astype(BF))
         gated_ref[rows, :] = jnp.concatenate(gated, axis=1) if heads > 1 else gated[0]
-        for ref, out in (
-            (q_ref, q_any), (k_ref, k_any), (swish_ref, swish_any), (gated_ref, gated_any)
-        ):
-            moves.store(ref.at[rows], out.at[rows])
-        moves.store(v_ref.at[:, rows], v_any.at[:, rows])
-        moves.store(retained_ref.at[:, rows], retained_any.at[:, rows])
-    moves.close()
-
-
-def retention_forward(mixed, weight, cosine, sine, table, heads, offsets):
-    length, width = mixed.shape
+        for store in stores:
+            store.copy(i).start()
+        if between is not None:
+            between(i)
+
+    for store in stores:
+        store.wait_all()
+
+
+def retention_outputs(length, heads):
     qk, vd = heads * KEY_HEAD, heads * VAL_HEAD
-    outputs = (
+    return (
         ((length, qk), BF),
         ((length, qk), BF),
         ((heads, length, VAL_HEAD), BF),
@@ -176,6 +251,11 @@
         ((heads, length, VAL_HEAD), BF),
         ((length, vd), BF),
     )
+
+
+def retention_forward(mixed, weight, cosine, sine, table, heads, offsets):
+    length, width = mixed.shape
+    outputs = retention_outputs(length, heads)
     blocks = length // BLOCK
     return pl.pallas_call(
         functools.partial(retention_kernel, heads, offsets),
@@ -210,8 +290,9 @@
 
 
 def gate_back_kernel(heads, branch_ref, w_ref, swish_ref, retained_ref, dswish_ref, dret_ref):
-    for i in range(branch_ref.shape[0] // BLOCK):
-        rows = slice(i * BLOCK, (i + 1) * BLOCK)
+    @pl.loop(0, branch_ref.shape[0] // BLOCK)
+    def _(i):
+        rows = rows_of(i)
         gate_back_rows(
             heads, rows, branch_ref[rows, :], w_ref, swish_ref, retained_ref, dswish_ref, dret_ref
         )
@@ -231,48 +312,47 @@
 
 
 def retention_back_head(
-    h, heads, q_ref, k_ref, v_ref, dret_ref, table_ref, cos_ref, sin_ref, dqk_ref, dv_ref,
-    dk_sum, dv_sum,
+    h, heads, q_ref, k_ref, v_ref, dret_ref, table_ref, cos_ref, sin_ref, dqk_ref, dv_head,
+    dq_sum,
 ):
-    blocks = q_ref.shape[0] // BLOCK
+    length = q_ref.shape[0]
+    blocks = length // BLOCK
     lanes = head_lanes(h, KEY_HEAD)
-    for i in reversed(range(blocks)):
-        rows = slice(i * BLOCK, (i + 1) * BLOCK)
-        seen = slice(0, (i + 1) * BLOCK)
-        query, grad = q_ref[rows, lanes], dret_ref[h, rows, :]
-        key, value = k_ref[seen, lanes], v_ref[h, seen, :]
-        decay = table_ref[h, :, (blocks - 1 - i) * BLOCK :]
+    dq_sum[...] = jnp.zeros_like(dq_sum)
+
+    @pl.loop(0, blocks)
+    def _(j):
+        there = rows_of(j)
+        query, grad = q_ref[:, lanes], dret_ref[h]
+        key, value = k_ref[there, lanes], v_ref[h, there, :]
+        decay = table_ref[h, pl.ds(pl.multiple_of((blocks - 1 - j) * BLOCK, BLOCK), length), :]
         weights = (times_transposed(query, key) * decay).astype(BF)
         score = (times_transposed(grad, value) * decay).astype(BF)
-        dq = product(score, key).astype(BF).astype(F32)
+        dq_sum[...] += product(score, key)
+        dk = transposed_times(score, query).astype(BF).astype(F32)
+        dk = rotate_pair(dk, cos_ref[there, :], sin_ref[there, :], back=True)
+        dqk_ref[there, head_lanes(heads + h, KEY_HEAD)] = (dk * (KEY_HEAD**-0.5)).astype(BF)
+        dv_head[there, :] = transposed_times(weights, grad).astype(BF)
+
+    @pl.loop(0, blocks)
+    def _(i):
+        rows = rows_of(i)
+        dq = dq_sum[rows, :].astype(BF).astype(F32)
         dqk_ref[rows, lanes] = rotate_pair(
             dq, cos_ref[rows, :], sin_ref[rows, :], back=True
         ).astype(BF)
-        if i == blocks - 1:
-            dk_sum[...] = transposed_times(score, query)
-            dv_sum[...] = transposed_times(weights, grad)
-        else:
-            dk_sum[seen, :] += transposed_times(score, query)
-            dv_sum[seen, :] += transposed_times(weights, grad)
-    dk = rotate_pair(
-        dk_sum[...].astype(BF).astype(F32), cos_ref[...], sin_ref[...], back=True
-    ) * (KEY_HEAD**-0.5)
-    dqk_ref[:, head_lanes(heads + h, KEY_HEAD)] = dk.astype(BF)
-    return dv_sum[...].astype(BF)
 
 
 def retention_back_kernel(
     heads, q_ref, k_ref, v_ref, dret_ref, table_ref, cos_ref, sin_ref, dqk_ref, dv_ref,
-    dk_sum, dv_sum,
+    dv_heads, dq_sum,
 ):
-    parts = [
+    for h in range(heads):
         retention_back_head(
-            h, heads, q_ref, k_ref, v_ref, dret_ref, table_ref, cos_ref, sin_ref, dqk_ref, dv_ref,
-            dk_sum, dv_sum,
-        )
-        for h in range(heads)
-    ]
-    dv_ref[...] = pad_lanes(parts, dv_ref.shape[1])
+            h, heads, q_ref, k_ref, v_ref, dret_ref, table_ref, cos_ref, sin_ref, dqk_ref,
+            dv_heads.at[h], dq_sum,
+        )
+    dv_ref[...] = pad_lanes([dv_heads[h] for h in range(heads)], dv_ref.shape[1])
 
 
 def retention_backward(q, k, v, dret, table, cosine, sine, heads, padded):
@@ -285,8 +365,8 @@
             jax.ShapeDtypeStruct((length, padded), BF),
         ),
         scratch_shapes=[
+            pltpu.VMEM((heads, length, VAL_HEAD), BF),
             pltpu.VMEM((length, KEY_HEAD), F32),
-            pltpu.VMEM((length, VAL_HEAD), F32),
         ],
         compiler_params=pltpu.CompilerParams(vmem_limit_bytes=48 * 1024 * 1024),
         name="retention_back",
@@ -589,12 +669,7 @@
     ]
 
     def finish():
-        copies[0].wait_recv()
-        out_y[...] = (parts[2, :half].astype(F32) + via_x[...].astype(F32)).astype(BF)
-        copies[4].start()
-        copies[1].wait_recv()
-        out_x[...] = (parts[1, half:].astype(F32) + via_y[...].astype(F32)).astype(BF)
-        copies[5].start()
+        forward_sums(copies, parts, boxes)
         for copy in copies[2:]:
             copy.wait_recv()
 
@@ -644,30 +719,47 @@
     return pl.ds(pl.multiple_of((lax.axis_index("seq") ^ k) * rows, rows), rows)
 
 
-def load_output(moves, cut, swapped_any, w_ref):
-    loads = []
-    for block in range(swapped_any.shape[1]):
-        for k in range(swapped_any.shape[0]):
-            skip, at = cut.skip(k), block * cut.rows + cut.start(k)
-            loads.append(
-                moves.start(
-                    swapped_any.at[k, block, slice(skip, cut.width)],
-                    w_ref.at[slice(at + skip, at + cut.width)],
-                )
-            )
-    return loads
+def forward_sums(copies, parts, boxes):
+    inbox_x, inbox_y, via_x, via_y, out_x, out_y = boxes
+    half = via_x.shape[0]
+    copies[0].wait_recv()
+    out_y[...] = (parts[2, :half].astype(F32) + via_x[...].astype(F32)).astype(BF)
+    copies[4].start()
+    copies[1].wait_recv()
+    out_x[...] = (parts[1, half:].astype(F32) + via_y[...].astype(F32)).astype(BF)
+    copies[5].start()
+
+
+def send_parts(part, copies, then=None):
+    @pl.loop(0, 4)
+    def _(i):
+        if then is not None:
+            pl.when(i == 3)(then)
+        part(jnp.where(i == 0, 3, jnp.where(i == 3, 0, i)))
+
+        @pl.when(i == 0)
+        def _():
+            copies[0].start()
+            copies[1].start()
+
+        @pl.when(i == 1)
+        def _():
+            copies[2].start()
+
+        @pl.when(i == 2)
+        def _():
+            copies[3].start()
 
 
 def project_kernel(
-    cut, g_any, w_any, x_ref, gain_ref, middle_ref, own_ref,
+    g_any, w_any, x_ref, gain_ref, middle_ref, own_ref,
     g_ref, w_ref, parts, inbox_x, inbox_y, via_x, via_y, out_x, out_y, sends, recvs, locals_,
 ):
     me = lax.axis_index("seq")
     rows = x_ref.shape[0]
     half = rows // 2
     moves = Moves(locals_)
-    loads = load_output(moves, cut, w_any, w_ref)
-    loads.append(moves.start(g_any, g_ref))
+    loads = [moves.start(w_any, w_ref), moves.start(g_any, g_ref)]
     greet((me ^ 1, me ^ 2))
     boxes = (inbox_x, inbox_y, via_x, via_y, out_x, out_y)
     copies, finish, total = square_parts(parts, boxes, sends, recvs, 0)
@@ -677,20 +769,16 @@
 
     for load in loads:
         load.wait()
-    part(3)
-    copies[0].start()
-    copies[1].start()
-    part(1)
-    copies[2].start()
-    part(2)
-    copies[3].start()
-    part(0)
+    send_parts(part, copies)
     finish()
-    for i in range(2):
-        here = slice(i * half, (i + 1) * half)
+
+    @pl.loop(0, 2)
+    def _(i):
+        here = pl.ds(pl.multiple_of(i * half, half), half)
         middle = x_ref[here, :].astype(F32) + total(here)
         middle_ref[here, :] = middle
         own_ref[here, :] = normalize(middle, gain_ref[...]).astype(BF)
+
     for copy in copies:
         copy.wait_send()
 
@@ -742,16 +830,136 @@
     )(*[value for value, _ in inputs])
 
 
-def project_and_norm(gated, swapped, x, gain, cut, call):
+def retention_exchange_kernel(
+    heads, offsets, cut, mixed_any, w_any, cos_ref, sin_ref, table_ref,
+    q_any, k_any, v_any, swish_any, retained_any, gated_any, wo_any,
+    mixed_ref, w_ref, q_ref, k_ref, v_ref, swish_ref, retained_ref, gated_ref, both_ref, wo_ref,
+    via_x, via_y, sends, recvs, locals_,
+):
+    me = lax.axis_index("seq")
+    shard = lax.axis_index("fsdp")
+    core = lax.rem(shard, 2)
+    step, wide = both_ref.shape[2:]
+    moves = Moves(locals_)
+
+    def piece(column):
+        rows = pl.ds(pl.multiple_of((2 * column + core) * step, step), step)
+        return w_any.at[rows, slice(w_ref.shape[1], w_ref.shape[1] + wide)]
+
+    across, along, corner = me ^ 1, me ^ 2, me ^ 3
+    half = step // 2
+    low, high = slice(0, half), slice(half, step)
+    swaps = [
+        remote(piece(corner).at[low], via_x, sends, recvs, 0, across),
+        remote(piece(corner).at[high], via_y, sends, recvs, 1, along),
+        remote(piece(across), both_ref.at[core, me], sends, recvs, 2, across),
+        remote(piece(along), both_ref.at[core, me], sends, recvs, 3, along),
+        remote(via_x, both_ref.at[core, across, low], sends, recvs, 4, along),
+        remote(via_y, both_ref.at[core, along, high], sends, recvs, 5, across),
+    ]
+    kept_here = []
+
+    def twin(k):
+        return pltpu.make_async_remote_copy(
+            src_ref=both_ref.at[core, me ^ k],
+            dst_ref=both_ref.at[core, me ^ k],
+            send_sem=sends.at[6 + k],
+            recv_sem=recvs.at[6 + k],
+            device_id={"fsdp": shard ^ 1},
+            device_id_type=MESH,
+        )
+
+    def between(i):
+        if isinstance(i, int):
+            greet_all(me, shard)
+            for copy in swaps[:4]:
+                copy.start()
+            kept_here.append(moves.start(piece(me), both_ref.at[core, me]))
+            return
+
+        @pl.when(i == 0)
+        def _():
+            swaps[0].wait_recv()
+            swaps[4].start()
+            swaps[1].wait_recv()
+            swaps[5].start()
+            kept_here[0].wait()
+            twin(0).start()
+
+        @pl.when(i == 2)
+        def _():
+            for k in (1, 2):
+                swaps[1 + k].wait_recv()
+                twin(k).start()
+
+        @pl.when(i == 3)
+        def _():
+            swaps[4].wait_recv()
+            swaps[5].wait_recv()
+            twin(3).start()
+
+    retention_kernel(
+        heads, offsets, mixed_any, w_any, cos_ref, sin_ref, table_ref,
+        q_any, k_any, v_any, swish_any, retained_any, gated_any,
+        mixed_ref, w_ref, q_ref, k_ref, v_ref, swish_ref, retained_ref, gated_ref, moves, between,
+    )
+    for k in range(4):
+        twin(k).wait_recv()
+    tile, lane = 16, 128
+
+    @pl.loop(0, heads * (wo_ref.shape[1] // lane))
+    def _(n):
+        h, c = n // (wo_ref.shape[1] // lane), lax.rem(n, wo_ref.shape[1] // lane)
+        lanes = pl.ds(pl.multiple_of(c * lane, lane), lane)
+        for k in range(4):
+            for r in range(cut.skip(k) // tile, cut.width // tile):
+                at = pl.multiple_of(h * cut.rows + (cut.start(k) + r * tile), tile)
+                wo_ref[pl.ds(at, tile), lanes] = both_ref[
+                    h, k, pl.ds(pl.multiple_of(c * tile, tile), tile), head_lanes(r, lane)
+                ]
+
+    moves.start(wo_ref, wo_any).wait()
+    for copy in swaps + [twin(k) for k in range(4)]:
+        copy.wait_send()
+
+
+def greet_all(me, shard):
+    barrier = pltpu.get_barrier_semaphore()
+    for k in (1, 2, 3):
+        pl.semaphore_signal(barrier, inc=1, device_id={"seq": me ^ k}, device_id_type=MESH)
+    pl.semaphore_signal(barrier, inc=1, device_id={"fsdp": shard ^ 1}, device_id_type=MESH)
+    pl.semaphore_wait(barrier, 4)
+
+
+def retention_exchange(mixed, weight, cosine, sine, table, heads, offsets, cut, call):
+    length, width = mixed.shape
+    wide = cut.width * width // 256
+    outputs = retention_outputs(length, heads) + (((heads * VAL_HEAD, width), BF),)
+    return comm_call(
+        functools.partial(retention_exchange_kernel, heads, offsets, cut),
+        [(mixed, False), (weight, False), (cosine, True), (sine, True), (table, True)],
+        [(shape, kind, False) for shape, kind in outputs],
+        [pltpu.VMEM(mixed.shape, BF), pltpu.VMEM((width, weight.shape[1] - wide), BF)]
+        + [pltpu.VMEM(*out) for out in outputs[:-1]]
+        + [pltpu.VMEM((heads, 4, 256, wide), BF), pltpu.VMEM(outputs[-1][0], BF)]
+        + [pltpu.VMEM((128, wide), BF)] * 2,
+        10,
+        6 + 7 * (length // BLOCK),
+        call,
+        mixed.size // 2,
+        "retention_exchange",
+    )
+
+
+def project_and_norm(gated, weight, x, gain, call):
     rows, width = x.shape
     return comm_call(
-        functools.partial(project_kernel, cut),
-        [(gated, False), (swapped, False), (x, True), (gain[None, :], True)],
+        project_kernel,
+        [(gated, False), (weight, False), (x, True), (gain[None, :], True)],
         [((rows, width), F32, True), ((rows, width), BF, True)],
-        [pltpu.VMEM(gated.shape, BF), pltpu.VMEM((gated.shape[1], width), BF)]
-        + square_scratch(rows, width),
+        [pltpu.VMEM(gated.shape, BF), pltpu.VMEM(weight.shape, BF)] + square_scratch(rows, width),
         6,
-        9,
+        2,
         call,
         x.size,
         "project_and_norm",
@@ -773,41 +981,48 @@
     copies, _ = square_gather(full.at[me], full, sends, recvs, 0)
     for copy in copies[:4]:
         copy.start()
-
-    def block(k):
+    stores = [
+        by_block(moves, 4, both_ref, both_any, rows),
+        by_block(moves, 4, hidden_ref, hidden_any, rows),
+        Series(moves, 4, lambda n: (full.at[n], full_any.at[n])),
+    ]
+    total[...] = jnp.zeros_like(total)
+    load_w.wait()
+    load_c.wait()
+
+    @pl.loop(0, 4)
+    def _(k):
+        @pl.when(k == 1)
+        def _():
+            copies[0].wait_recv()
+            copies[4].start()
+            copies[1].wait_recv()
+            copies[5].start()
+            copies[2].wait_recv()
+
+        @pl.when(k == 2)
+        def _():
+            copies[3].wait_recv()
+
+        @pl.when(k == 3)
+        def _():
+            copies[4].wait_recv()
+            copies[5].wait_recv()
+
         here = block_rows(k, rows)
-        x = full[me ^ k]
-        moves.store(full.at[me ^ k], full_any.at[me ^ k])
-        both = product(x, w_ref[...])
+        both = product(full[me ^ k], w_ref[...])
         gate, up = both[:, :ff], both[:, ff:]
         both_ref[here, :] = both
-        moves.store(both_ref.at[here], both_any.at[here])
         hidden = (gate * (0.5 + 0.5 * lax.erf(gate * math.sqrt(0.5))) * up).astype(BF)
         hidden_ref[here, :] = hidden
-        moves.store(hidden_ref.at[here], hidden_any.at[here])
-        term = transposed_times(hidden, c_ref[here, :])
-        if k == 0:
-            total[...] = term
-        elif k < 3:
-            total[...] += term
-        else:
-            down_ref[...] = (total[...] + term).astype(BF)
-
-    load_w.wait()
-    load_c.wait()
-    block(0)
-    copies[0].wait_recv()
-    copies[4].start()
-    copies[1].wait_recv()
-    copies[5].start()
-    copies[2].wait_recv()
-    block(1)
-    copies[3].wait_recv()
-    block(2)
-    copies[4].wait_recv()
-    copies[5].wait_recv()
-    block(3)
+        for store in stores:
+            store.copy(me ^ k).start()
+        total[...] += transposed_times(hidden, c_ref[here, :])
+
+    down_ref[...] = total[...].astype(BF)
     moves.store(down_ref, down_any)
+    for store in stores:
+        store.wait_all()
     moves.close()
     for copy in copies:
         copy.wait_send()
@@ -843,6 +1058,14 @@
     return both, hidden, down, full.reshape(length, width)
 
 
+def column_of(halves):
+    total = 0.0
+    for terms in halves:
+        ones = jnp.ones((terms.shape[0], 128), BF)
+        total = total + transposed_times(terms.astype(BF), ones)
+    return total
+
+
 def feed_back_scatter_kernel(
     ff, c_any, both_any, w_any, down_any, x_any, m_ref, own_c_ref, gain_ref,
     grad_ref, term_ref, branch_ref, dw_any,
@@ -853,14 +1076,15 @@
     rows = own_c_ref.shape[0]
     half = rows // 2
     moves = Moves(locals_)
+    load_c = by_block(moves, 4, c_any, c_ref, rows)
+    load_both = by_block(moves, 4, both_any, both_ref, rows)
+    load_c.copy(me ^ 3).start()
     load_down = moves.start(down_any, down_ref)
+    load_both.copy(me ^ 3).start()
     load_w = moves.start(w_any, w_ref)
-    order = (3, 1, 2, 0)
-    loads = []
-    for k in order:
-        here = block_rows(k, rows)
-        loads.append(moves.start(c_any.at[here], c_ref.at[here]))
-        loads.append(moves.start(both_any.at[here], both_ref.at[here]))
+    for k in (1, 2, 0):
+        load_c.copy(me ^ k).start()
+        load_both.copy(me ^ k).start()
     load_x = moves.start(x_any, x_ref)
     greet((me ^ 1, me ^ 2))
     boxes = (inbox_x, inbox_y, via_x, via_y, out_x, out_y)
@@ -868,51 +1092,41 @@
 
     def part(k):
         here = block_rows(k, rows)
-        at = order.index(k)
-        loads[2 * at].wait()
-        loads[2 * at + 1].wait()
+        load_c.copy(me ^ k).wait()
+        load_both.copy(me ^ k).wait()
         gate, up = both_ref[here, :ff], both_ref[here, ff:]
         hidden_grad = times_transposed(c_ref[here, :], down_ref[...])
         bell = 0.5 + 0.5 * lax.erf(gate * math.sqrt(0.5))
         slope = bell + gate * (math.sqrt(0.5 / math.pi) * jnp.exp(-0.5 * gate * gate))
-        grads = jnp.concatenate([hidden_grad * up * slope, hidden_grad * (gate * bell)], axis=1)
-        grads = grads.astype(BF)
-        low[here, :] = grads
-        parts[k] = times_transposed(grads, w_ref[...]).astype(BF)
+        low[here, :ff] = (hidden_grad * up * slope).astype(BF)
+        low[here, ff:] = (hidden_grad * (gate * bell)).astype(BF)
+        pl.when(k == 3)(load_w.wait)
+        parts[k] = times_transposed(low[here, :], w_ref[...]).astype(BF)
 
     load_down.wait()
-    load_w.wait()
-    part(3)
-    copies[0].start()
-    copies[1].start()
-    part(1)
-    copies[2].start()
-    part(2)
-    copies[3].start()
-    copies[0].wait_recv()
-    out_y[...] = (parts[2, :half].astype(F32) + via_x[...].astype(F32)).astype(BF)
-    copies[4].start()
-    copies[1].wait_recv()
-    out_x[...] = (parts[1, half:].astype(F32) + via_y[...].astype(F32)).astype(BF)
-    copies[5].start()
-    part(0)
+    send_parts(part, copies, lambda: forward_sums(copies, parts, boxes))
     load_x.wait()
-    for b in range(x_ref.shape[1] // BLOCK):
-        lanes = slice(b * BLOCK, (b + 1) * BLOCK)
+    stores = by_block(moves, x_ref.shape[1] // BLOCK, dw_ref, dw_any)
+
+    @pl.loop(0, stores.count)
+    def _(b):
+        lanes = rows_of(b)
         dw_ref[lanes, :] = transposed_times(x_ref[:, lanes], low[...]).astype(BF)
-        moves.store(dw_ref.at[lanes], dw_any.at[lanes])
+        stores.copy(b).start()
+
     for copy in copies[2:]:
         copy.wait_recv()
-    term = jnp.zeros((1, gain_ref.shape[1]), F32)
-    for i in range(2):
+
+    def back_half(i):
         here = slice(i * half, (i + 1) * half)
-        back, terms = norm_back(m_ref[here, :], total(here), gain_ref[...])
+        back, term = norm_back(m_ref[here, :], total(here), gain_ref[...])
         grad = own_c_ref[here, :].astype(F32) + back
         grad_ref[here, :] = grad
         branch_ref[here, :] = grad.astype(BF)
-        term = term + jnp.sum(terms, axis=0, keepdims=True)
-    term_ref[...] = term
-    moves.close()
+        return term
+
+    term_ref[...] = column_of([back_half(i) for i in range(2)])
+    stores.wait_all()
     for copy in copies:
         copy.wait_send()
 
@@ -934,7 +1148,7 @@
         ],
         [
             ((rows, width), F32, True),
-            ((1, width), F32, True),
+            ((width, 128), F32, True),
             ((rows, width), BF, True),
             ((width, 2 * ff), BF, False),
         ],
@@ -954,7 +1168,7 @@
         own_cotangent.size,
         "feed_back_scatter",
     )
-    return grad, term[0], branch, dw
+    return grad, term, branch, dw
 
 
 def norm_back(values, grad, gain):
@@ -1000,6 +1214,12 @@
     return -(-rows // 32) * 16
 
 
+def put_column(ref, rows, at, column):
+    first = ref.shape[1] - 128
+    spare = lax.broadcasted_iota(jnp.int32, column.shape, 1) == at - first
+    ref[rows, first:] = jnp.where(spare, column, ref[rows, first:].astype(F32)).astype(BF)
+
+
 def gate_back_scatter_kernel(
     heads, cut, branch_any, w_any, swish_any, retained_any, column_any, hidden_any, down_any,
     mixed_any, gated_any, m_any, dswish_any, dret_any, dws_any, dwo_any, out_ref,
@@ -1009,22 +1229,16 @@
 ):
     me = lax.axis_index("seq")
     rows = out_ref.shape[0]
-    half = rows // 2
     moves = Moves(locals_)
     load_down = moves.start(down_any, down_ref)
     load_hidden = moves.start(hidden_any, hidden_ref)
-    load_gate = load_output(moves, cut, w_any, w_ref)
+    load_gate = moves.start(w_any, w_ref)
     blocks = branch_ref.shape[0] // BLOCK
-    load_rows = []
-    for i in range(blocks):
-        here = slice(i * BLOCK, (i + 1) * BLOCK)
-        load_rows.append(
-            [
-                moves.start(branch_any.at[here], branch_ref.at[here]),
-                moves.start(swish_any.at[here], swish_ref.at[here]),
-                moves.start(retained_any.at[:, here], retained_ref.at[:, here]),
-            ]
-        )
+    load_rows = [
+        by_block(moves, blocks, branch_any, branch_ref).start_all(),
+        by_block(moves, blocks, swish_any, swish_ref).start_all(),
+        by_block(moves, blocks, retained_any, retained_ref).start_all(),
+    ]
     load_mixed = moves.start(mixed_any, mixed_ref)
     load_column = moves.start(column_any, column_ref)
     load_gated = moves.start(gated_any, gated_ref)
@@ -1039,87 +1253,81 @@
 
     load_hidden.wait()
     load_down.wait()
-    part(3)
-    copies[0].start()
-    copies[1].start()
-    part(1)
-    copies[2].start()
-    part(2)
-    copies[3].start()
-    for load in load_gate:
-        load.wait()
-    for i in range(blocks):
-        here = slice(i * BLOCK, (i + 1) * BLOCK)
-        for load in load_rows[i]:
-            load.wait()
+    send_parts(part, copies)
+    load_gate.wait()
+
+    @pl.loop(0, blocks)
+    def _(i):
+        here = rows_of(i)
+        for load in load_rows:
+            load.copy(i).wait()
         gate_back_rows(
             heads, here, branch_ref[here, :], w_ref, swish_ref, retained_ref, dswish_ref, dret_ref
         )
+
     moves.store(dswish_ref, dswish_any)
     moves.store(dret_ref, dret_any)
-    copies[0].wait_recv()
-    out_y[...] = (parts[2, :half].astype(F32) + via_x[...].astype(F32)).astype(BF)
-    copies[4].start()
-    copies[1].wait_recv()
-    out_x[...] = (parts[1, half:].astype(F32) + via_y[...].astype(F32)).astype(BF)
-    copies[5].start()
-    padded = dswish_ref.shape[1]
-    spare = lax.broadcasted_iota(jnp.int32, (BLOCK, padded), 1) == heads * VAL_HEAD
+    forward_sums(copies, parts, boxes)
     load_mixed.wait()
     load_column.wait()
-    for b in range(dws_ref.shape[0] // BLOCK):
-        here = slice(b * BLOCK, (b + 1) * BLOCK)
-        term = product(mixed_ref[here, :], dswish_ref[...])
-        dws_ref[here, :] = jnp.where(spare, column_ref[here, :], term).astype(BF)
-        moves.store(dws_ref.at[here], dws_any.at[here])
+    stores = by_block(moves, dws_ref.shape[0] // BLOCK, dws_ref, dws_any)
+
+    @pl.loop(0, stores.count)
+    def _(b):
+        here = rows_of(b)
+        dws_ref[here, :] = product(mixed_ref[here, :], dswish_ref[...]).astype(BF)
+        put_column(dws_ref, here, heads * VAL_HEAD, column_ref[here, :])
+        stores.copy(b).start()
+
     load_gated.wait()
     step, tile, lane = 2 * BLOCK, 16, 128
     for h in range(heads):
         value_lanes = head_lanes(h, VAL_HEAD)
-        for b in range(branch_ref.shape[1] // step):
-            lanes = slice(b * step, (b + 1) * step)
+
+        @pl.loop(0, branch_ref.shape[1] // step)
+        def _(b):
+            lanes = pl.ds(pl.multiple_of(b * step, step), step)
             wide = transposed_times(gated_ref[:, value_lanes], branch_ref[:, lanes]).astype(BF)
             for k in range(4):
                 for r in range(cut.width // tile):
                     at = cut.start(k) + r * tile
                     for c in range(step // lane):
-                        dwo_ref[
-                            h, k,
-                            (b * step // lane + c) * tile : (b * step // lane + c + 1) * tile,
-                            r * lane : (r + 1) * lane,
-                        ] = wide[at : at + tile, c * lane : (c + 1) * lane]
-        moves.store(dwo_ref.at[h], dwo_any.at[h])
-    part(0)
+                        to = pl.ds(pl.multiple_of((b * (step // lane) + c) * tile, tile), tile)
+                        dwo_ref[h, k, to, head_lanes(r, lane)] = wide[
+                            at : at + tile, head_lanes(c, lane)
+                        ]
+
+    moves.store(dwo_ref, dwo_any)
     load_m.wait()
     for copy in copies[2:]:
         copy.wait_recv()
-    out_ref[...] = (m_ref[...] + total(slice(0, rows))).astype(BF)
+    out_ref[...] = m_ref[...] + total(slice(0, rows))
+    stores.wait_all()
     moves.close()
     for copy in copies:
         copy.wait_send()
 
 
 def gate_backward_scatter(
-    branch, swapped, swish, retained, column, hidden, down, mixed_t, gated, middle, heads, padded,
+    branch, weight, swish, retained, column, hidden, down, mixed_t, gated, middle, heads, padded,
     cut, call,
 ):
     length, width = branch.shape
     rows = middle.shape[0]
     dwo = (heads, 4, width // 8, cut.width * 8)
-    inputs = (branch, swapped, swish, retained, column, hidden, down, mixed_t, gated, middle)
-    weight = jax.ShapeDtypeStruct((heads * VAL_HEAD, width), BF)
+    inputs = (branch, weight, swish, retained, column, hidden, down, mixed_t, gated, middle)
     outputs = [
         ((length, padded), BF, False),
         ((heads, length, VAL_HEAD), BF, False),
         ((width, padded), BF, False),
         (dwo, BF, False),
-        ((rows, width), BF, True),
+        ((rows, width), F32, True),
     ]
     return comm_call(
         functools.partial(gate_back_scatter_kernel, heads, cut),
         [(value, False) for value in inputs],
         outputs,
-        [pltpu.VMEM(v.shape, v.dtype) for v in (branch, weight) + inputs[2:]]
+        [pltpu.VMEM(v.shape, v.dtype) for v in inputs]
         + [pltpu.VMEM(shape, kind) for shape, kind, _ in outputs[:4]]
         + square_scratch(rows, width),
         6,
@@ -1134,7 +1342,7 @@
     heads, q_any, k_any, v_any, dret_any, table_ref, cos_ref, sin_ref, mixed_any, send_any, share_any,
     dqk_any, dv_any, merged_any, full_any,
     q_ref, k_ref, v_ref, dret_ref, mixed_ref, send_ref, dqk_ref, dv_ref, dwqk_ref, twin_ref, sum_ref,
-    zero_ref, dk_sum, dv_sum, sends, recvs, locals_,
+    zero_ref, dv_heads, dq_sum, sends, recvs, locals_,
 ):
     me = lax.axis_index("seq")
     shard = lax.axis_index("fsdp")
@@ -1148,11 +1356,7 @@
         )
     ]
     load_mixed = moves.start(mixed_any, mixed_ref)
-    barrier = pltpu.get_barrier_semaphore()
-    for k in (1, 2, 3):
-        pl.semaphore_signal(barrier, inc=1, device_id={"seq": me ^ k}, device_id_type=MESH)
-    pl.semaphore_signal(barrier, inc=1, device_id={"fsdp": shard ^ 1}, device_id_type=MESH)
-    pl.semaphore_wait(barrier, 4)
+    greet_all(me, shard)
     load_send.wait()
     twin = pltpu.make_async_remote_copy(
         src_ref=send_ref.at[1 - core],
@@ -1180,35 +1384,44 @@
         moves.store(zero_ref, place(column, 1 - core))
     for load in loads:
         load.wait()
-    parts = []
     swaps = [
         remote(sum_ref.at[me ^ k], place(me, core), sends, recvs, 5 + k, me ^ k) for k in (3, 1, 2)
     ]
     for h in range(heads):
-        parts.append(
-            retention_back_head(
-                h, heads, q_ref, k_ref, v_ref, dret_ref, table_ref, cos_ref, sin_ref, dqk_ref,
-                dv_ref, dk_sum, dv_sum,
-            )
+        retention_back_head(
+            h, heads, q_ref, k_ref, v_ref, dret_ref, table_ref, cos_ref, sin_ref, dqk_ref,
+            dv_heads.at[h], dq_sum,
         )
         if h == 0:
             twin.wait_recv()
-            for k in range(4):
+
+            @pl.loop(0, 4)
+            def _(k):
                 sum_ref[k] = (send_ref[core, k].astype(F32) + twin_ref[k].astype(F32)).astype(BF)
+
             for copy in swaps:
                 copy.start()
             moves.store(sum_ref.at[me], place(me, core))
             pass_on(passed)
-    dv_ref[...] = pad_lanes(parts, dv_ref.shape[1])
+    dv_ref[...] = pad_lanes([dv_heads[h] for h in range(heads)], dv_ref.shape[1])
     moves.store(dv_ref, dv_any)
     moves.store(dqk_ref, dqk_any)
     load_mixed.wait()
-    for b in range(mixed_ref.shape[0] // BLOCK):
-        here = slice(b * BLOCK, (b + 1) * BLOCK)
+    stores = Series(
+        moves,
+        mixed_ref.shape[0] // BLOCK,
+        lambda b: (dwqk_ref.at[rows_of(b)], merged_any.at[rows_of(b), slice(0, at)]),
+    )
+
+    @pl.loop(0, stores.count)
+    def _(b):
+        here = rows_of(b)
         dwqk_ref[here, :] = product(mixed_ref[here, :], dqk_ref[...]).astype(BF)
-        moves.store(dwqk_ref.at[here], merged_any.at[here, slice(0, at)])
+        stores.copy(b).start()
+
     for copy in passed[2:] + swaps:
         copy.wait_recv()
+    stores.wait_all()
     moves.close()
     for copy in passed + swaps + [twin]:
         copy.wait_send()
@@ -1242,8 +1455,8 @@
             pltpu.VMEM(block, BF),
             pltpu.VMEM(block, BF),
             pltpu.VMEM(block[1:], BF),
+            pltpu.VMEM((heads, length, VAL_HEAD), BF),
             pltpu.VMEM((length, KEY_HEAD), F32),
-            pltpu.VMEM((length, VAL_HEAD), F32),
         ],
         10,
         16 + width // BLOCK,
@@ -1254,8 +1467,8 @@
 
 
 def input_back_kernel(
-    offsets, dqk_any, dv_any, ds_any, w_any, x_any, grad_any, gain_ref, share_any,
-    dx_ref, term_ref, full_any, dqk_ref, dv_ref, ds_ref, w_ref, x_ref, grad_ref,
+    offsets, spare, dqk_any, dv_any, ds_any, w_any, x_any, grad_any, mixed_any, gain_ref, share_any,
+    dx_ref, dwv_any, full_any, dqk_ref, dv_ref, ds_ref, w_ref, x_ref, grad_ref, mixed_ref, dwv_ref,
     parts, inbox_x, inbox_y, via_x, via_y, out_x, out_y, sends, recvs, locals_,
 ):
     at_value, at_swish = offsets
@@ -1271,6 +1484,7 @@
         loads.append(moves.start(w_any.at[:, span], w_ref.at[:, span]))
     load_x = moves.start(x_any, x_ref)
     load_grad = moves.start(grad_any, grad_ref)
+    load_mixed = moves.start(mixed_any, mixed_ref)
     greet((me ^ 1, me ^ 2))
     boxes = (inbox_x, inbox_y, via_x, via_y, out_x, out_y)
     copies, _, total = square_parts(parts, boxes, sends, recvs, 0)
@@ -1283,40 +1497,41 @@
         here = block_rows(k, rows)
         whole = 0.0
         for n, (_, ref) in enumerate(grads):
-            if k == 3:
+
+            @pl.when(k == 3)
+            def _():
                 loads[2 * n].wait()
                 loads[2 * n + 1].wait()
+
             whole = whole + times_transposed(ref[here, :], w_ref[:, spans[n]])
         parts[k] = whole.astype(BF)
 
-    part(3)
-    copies[0].start()
-    copies[1].start()
-    part(1)
-    copies[2].start()
-    part(2)
-    copies[3].start()
-    pass_on(passed)
-    copies[0].wait_recv()
-    out_y[...] = (parts[2, :half].astype(F32) + via_x[...].astype(F32)).astype(BF)
-    copies[4].start()
-    copies[1].wait_recv()
-    out_x[...] = (parts[1, half:].astype(F32) + via_y[...].astype(F32)).astype(BF)
-    copies[5].start()
-    passed[2].start()
-    passed[3].start()
-    part(0)
+    def pass_all():
+        pass_on(passed)
+        forward_sums(copies, parts, boxes)
+        passed[2].start()
+        passed[3].start()
+
+    send_parts(part, copies, pass_all)
+    load_mixed.wait()
+
+    @pl.loop(0, dwv_ref.shape[0] // BLOCK)
+    def _(b):
+        here = rows_of(b)
+        dwv_ref[here, :] = product(mixed_ref[here, :], dv_ref[...]).astype(BF)
+
     for copy in copies[2:]:
         copy.wait_recv()
     load_x.wait()
     load_grad.wait()
-    term = jnp.zeros((1, x_ref.shape[1]), F32)
+    terms = []
     for i in range(2):
         here = slice(i * half, (i + 1) * half)
-        back, terms = norm_back(x_ref[here, :].astype(F32), total(here), gain_ref[...])
-        dx_ref[here, :] = (grad_ref[here, :] + back).astype(BF)
-        term = term + jnp.sum(terms, axis=0, keepdims=True)
-    term_ref[...] = term
+        back, term = norm_back(x_ref[here, :].astype(F32), total(here), gain_ref[...])
+        dx_ref[here, :] = grad_ref[here, :] + back
+        terms.append(term)
+    put_column(dwv_ref, slice(0, dwv_ref.shape[0]), spare, column_of(terms))
+    moves.store(dwv_ref, dwv_any)
     for copy in passed[2:]:
         copy.wait_recv()
     moves.close()
@@ -1324,52 +1539,75 @@
         copy.wait_send()
 
 
-def input_backward(dqk, dv, ds, weight, x, grad, gain, share, offsets, call):
+def input_backward(dqk, dv, ds, weight, x, grad, mixed_t, gain, share, offsets, spare, call):
     rows, width = x.shape
-    staged = (dqk, dv, ds, weight, x, grad)
-    dx, term, full = comm_call(
-        functools.partial(input_back_kernel, offsets),
+    staged = (dqk, dv, ds, weight, x, grad, mixed_t)
+    return comm_call(
+        functools.partial(input_back_kernel, offsets, spare),
         [(value, False) for value in staged] + [(gain[None, :], True), (share, False)],
         [
-            ((rows, width), BF, True),
-            ((1, width), F32, True),
+            ((rows, width), F32, True),
+            ((width, dv.shape[1]), BF, False),
             ((4,) + share.shape, BF, False),
         ],
-        [pltpu.VMEM(value.shape, value.dtype) for value in staged] + square_scratch(rows, width),
+        [pltpu.VMEM(value.shape, value.dtype) for value in staged[:3]]
+        + [pltpu.VMEM((width, dqk.shape[1] + dv.shape[1] + ds.shape[1]), BF)]
+        + [pltpu.VMEM(value.shape, value.dtype) for value in staged[4:]]
+        + [pltpu.VMEM((width, dv.shape[1]), BF)]
+        + square_scratch(rows, width),
         12,
-        9,
+        11,
         call,
         x.size + share.size,
         "input_backward",
     )
-    return dx, term[0], full
 
 
 def join(pieces):
     return jnp.concatenate(pieces, axis=1) if len(pieces) > 1 else pieces[0]
 
 
-def unpack_columns_kernel(width, in_ref, out_ref):
-    out_ref[...] = join([in_ref[k][:, :width].astype(F32) for k in range(in_ref.shape[0])])
-
-
-def unpack_columns(gathered, at, width):
+def unpack_columns_kernel(width, in_ref, out_ref, gain_ref):
+    count = in_ref.shape[0]
+    out_ref[...] = join([in_ref[k][:, :width].astype(F32) for k in range(count)])
+    last = in_ref.shape[2] - 128
+    tile = sum(in_ref[k][:, last:].astype(F32) for k in range(count))
+    gain_ref[...] = tile.T[width - last : width - last + 1, :]
+
+
+def unpack_columns(gathered, width):
     count, rows, whole = gathered.shape
-    block = rows // 4 if rows % 64 == 0 else rows
-    padded = -(-width // 128) * 128
-    return pl.pallas_call(
+    block = min(rows, 128)
+    out, gain = pl.pallas_call(
         functools.partial(unpack_columns_kernel, width),
         grid=(rows // block,),
-        in_specs=[pl.BlockSpec((count, block, padded), lambda i: (0, i, at // padded))],
-        out_specs=pl.BlockSpec((block, count * width), lambda i: (i, 0)),
-        out_shape=jax.ShapeDtypeStruct((rows, count * width), F32),
+        in_specs=[pl.BlockSpec((count, block, whole), lambda i: (0, i, 0))],
+        out_specs=[
+            pl.BlockSpec((block, count * width), lambda i: (i, 0)),
+            pl.BlockSpec((1, block), lambda i: (0, i)),
+        ],
+        out_shape=[
+            jax.ShapeDtypeStruct((rows, count * width), F32),
+            jax.ShapeDtypeStruct((1, rows), F32),
+        ],
         name="unpack_columns",
     )(gathered)
-
-
-def unpack_hidden_kernel(cut, shards, in_ref, gate_ref, up_ref):
+    return out, gain[0]
+
+
+def unpack_feed_kernel(cut, shards, in_ref, down_ref, gate_ref, up_ref, out_ref):
     count = in_ref.shape[0]
-    for n, out_ref in enumerate((gate_ref, up_ref)):
+
+    @pl.when(pl.program_id(0) == 0)
+    def _():
+        for k in range(count):
+            if cut.skip(k) < cut.width:
+                at = cut.start(k)
+                out_ref[at + cut.skip(k) : at + cut.width, :] = down_ref[
+                    k, cut.skip(k) : cut.width, :
+                ].astype(F32)
+
+    for n, target in enumerate((gate_ref, up_ref)):
         pieces = []
         for f in range(shards):
             for k in range(count):
@@ -1377,43 +1615,62 @@
                 if cut.skip(k) < cut.width:
                     piece = in_ref[k][:, at + cut.skip(k) : at + cut.width]
                     pieces.append(piece.astype(F32))
-        out_ref[...] = join(pieces)
-
-
-def unpack_hidden(gathered, cut, shards):
+        target[...] = join(pieces)
+
+
+def unpack_feed(gathered, down, cut, shards):
     count, rows, whole = gathered.shape
     block = rows // 4 if rows % 64 == 0 else rows
-    wide = shards * cut.rows
+    wide, width = shards * cut.rows, down.shape[2]
     return pl.pallas_call(
-        functools.partial(unpack_hidden_kernel, cut, shards),
+        functools.partial(unpack_feed_kernel, cut, shards),
         grid=(rows // block,),
-        in_specs=[pl.BlockSpec((count, block, whole), lambda i: (0, i, 0))],
-        out_specs=[pl.BlockSpec((block, wide), lambda i: (i, 0))] * 2,
-        out_shape=[jax.ShapeDtypeStruct((rows, wide), F32)] * 2,
-        name="unpack_hidden",
-    )(gathered)
-
-
-def unpack_output_kernel(cut, in_ref, out_ref):
-    tile, lane = 16, 128
-    for k in range(in_ref.shape[0]):
+        in_specs=[
+            pl.BlockSpec((count, block, whole), lambda i: (0, i, 0)),
+            pl.BlockSpec(down.shape, lambda i: (0, 0, 0)),
+        ],
+        out_specs=[
+            pl.BlockSpec((block, wide), lambda i: (i, 0)),
+            pl.BlockSpec((block, wide), lambda i: (i, 0)),
+            pl.BlockSpec((cut.rows, width), lambda i: (0, 0)),
+        ],
+        out_shape=[
+            jax.ShapeDtypeStruct((rows, wide), F32),
+            jax.ShapeDtypeStruct((rows, wide), F32),
+            jax.ShapeDtypeStruct((cut.rows, width), F32),
+        ],
+        compiler_params=pltpu.CompilerParams(vmem_limit_bytes=40 * 1024 * 1024),
+        name="unpack_feed",
+    )(gathered, down)
+
+
+def unpack_merged_kernel(cut, in_ref, query_ref, key_ref, out_ref):
+    tile, lane, count = 16, 128, in_ref.shape[0]
+    wide = query_ref.shape[1] // count
+    for k in range(count):
+        query_ref[:, head_lanes(k, wide)] = in_ref[k, :, :wide].astype(F32)
+        key_ref[:, head_lanes(k, wide)] = in_ref[k, :, wide : 2 * wide].astype(F32)
         for r in range(cut.skip(k) // tile, cut.width // tile):
             at = cut.start(k) + r * tile
+            lanes = slice(2 * wide + r * lane, 2 * wide + (r + 1) * lane)
             for c in range(out_ref.shape[1] // lane):
-                out_ref[at : at + tile, c * lane : (c + 1) * lane] = in_ref[
-                    k, c * tile : (c + 1) * tile, r * lane : (r + 1) * lane
+                out_ref[at : at + tile, head_lanes(c, lane)] = in_ref[
+                    k, c * tile : (c + 1) * tile, lanes
                 ].astype(F32)
 
 
-def unpack_output(gathered, at, cut, width):
-    count, rows, whole = gathered.shape
-    wide = whole - at
+def unpack_merged(gathered, wide, cut, width):
+    count, rows, _ = gathered.shape
     return pl.pallas_call(
-        functools.partial(unpack_output_kernel, cut),
-        out_shape=jax.ShapeDtypeStruct((cut.rows, width), F32),
-        compiler_params=pltpu.CompilerParams(vmem_limit_bytes=32 * 1024 * 1024),
-        name="unpack_output",
-    )(gathered[:, :, at:])
+        functools.partial(unpack_merged_kernel, cut),
+        out_shape=(
+            jax.ShapeDtypeStruct((rows, count * wide), F32),
+            jax.ShapeDtypeStruct((rows, count * wide), F32),
+            jax.ShapeDtypeStruct((cut.rows, width), F32),
+        ),
+        compiler_params=pltpu.CompilerParams(vmem_limit_bytes=40 * 1024 * 1024),
+        name="unpack_merged",
+    )(gathered)
 
 
 def after(values, *others, all_of=False):
@@ -1469,7 +1726,7 @@
     me = lax.axis_index("seq")
     per_device = HEADS // seq_count
     rows_count = groups * local_length
-    square = seq_count == 4 and rows_count % 32 == 0
+    square = seq_count == 4 and shards == 8 and rows_count % 32 == 0
     length = local_length * seq_count
     key_scale = KEY_HEAD ** (-0.5)
     qk = query_weight.shape[1] // seq_count
@@ -1486,18 +1743,19 @@
     def scatter_rows(values):
         return lax.psum_scatter(values.astype(BF), "fsdp", scatter_dimension=0, tiled=True)
 
-    attention_piece = jnp.concatenate(
-        [
-            columns_of(query_weight, me, qk, qk),
-            columns_of(key_weight, me, qk, qk),
-            columns_of(value_weight, me, vd, vd_pad),
-            columns_of(swish_weight, me, vd, vd_pad),
-        ],
-        axis=1,
-    )
-    attention_weight = gather_rows(attention_piece)
     output_piece = lax.dynamic_slice_in_dim(output_weight, cut.start(me), cut.width, axis=0)
-    output_pieces = gather_rows(output_piece)
+    attention_pieces = [
+        columns_of(query_weight, me, qk, qk),
+        columns_of(key_weight, me, qk, qk),
+        columns_of(value_weight, me, vd, vd_pad),
+        columns_of(swish_weight, me, vd, vd_pad),
+    ]
+    if square:
+        tiles = output_piece.reshape(cut.width // 16, 16, width // 128, 128)
+        attention_pieces.append(tiles.transpose(2, 1, 0, 3).reshape(width // 8, cut.width * 8))
+    else:
+        output_pieces = gather_rows(output_piece)
+    attention_weight = gather_rows(jnp.concatenate(attention_pieces, axis=1))
     column = lax.broadcasted_iota(jnp.int32, (hidden_units, ff), 0)
     slot = lax.broadcasted_iota(jnp.int32, (hidden_units, ff), 1)
     chosen = (slot // cut.width) * own_rows + cut.start(me) + slot % cut.width
@@ -1512,6 +1770,8 @@
     local_input = layer_input.reshape(rows_count, width)
     upstream = output_cotangent.reshape(rows_count, width)
 
+    upstream = after(upstream, gains)
+
     def whole(values, call):
         gathered = gather_seq(values, call)
         return gathered.reshape(length * groups, width)
@@ -1521,39 +1781,29 @@
     inputs = local_input.astype(F32)
 
     blocks = shards // seq_count
-    mixed_low = normalize(input_full.astype(F32), mixer_scale).astype(BF)
-    mixed_turned = mixed_low.T
-    output_pieces = after(output_pieces, upstream_full, gains)
-    swapped = exchange_seq(output_pieces.reshape(seq_count, blocks, cut.width, width), 2)
-    feed_weight = gather_rows(after(feed_piece, swapped))
-
+    mixed_low, mixed_turned = norm_and_turn(input_full, mixer_scale)
+    head_ids = me * per_device + jnp.arange(per_device, dtype=jnp.int32)
+    table, table_back = decay_tables(head_ids, length)
     cosine, sine = rotation_tables(length, KEY_HEAD // 2)
-    head_ids = me * per_device + jnp.arange(per_device, dtype=jnp.int32)
-    table = decay_table(head_ids, length)
-    attention_weight, mixed_low, mixed_turned, table = after(
-        attention_weight, mixed_low, mixed_turned, table, all_of=True
+    feed_weight = gather_rows(after(feed_piece, upstream_full))
+
+    offsets = (qk, 2 * qk, 2 * qk + vd_pad)
+    attention_weight = after(
+        attention_weight, mixed_low, mixed_turned, table, table_back, cosine, feed_piece
     )
-    query_low, key_low, value_low, swish_pre, retained, gated_low = retention_forward(
-        mixed_low, attention_weight, cosine, sine, table, per_device, (qk, 2 * qk, 2 * qk + vd_pad)
-    )
-
-    kept_rows = lax.broadcasted_iota(jnp.int32, down_piece.shape, 0) >= cut.skip(me)
-    down_full = gather_rows(after(jnp.where(kept_rows, down_piece, jnp.zeros_like(down_piece)), gated_low))
     if square:
-        middle, channel_own = project_and_norm(
-            gated_low, swapped, local_input, channel_scale, cut, 3
-        )
-        both_pre, hidden_low, down_term, channel_full = feed_forward_gather(
-            channel_own, feed_weight, upstream_full, 4
-        )
-        down_share = scatter_rows(down_term)
-        middle_grad, channel_term, branch_own, feed_term = feed_back_scatter(
-            after(upstream_full, down_term), both_pre, feed_weight, down_full, channel_full,
-            middle, upstream, channel_scale, 6,
-        )
-        feed_share = scatter_rows(feed_term)
-        branch_full = whole(branch_own, 7)
+        query_low, key_low, value_low, swish_pre, retained, gated_low, output_full = (
+            retention_exchange(
+                mixed_low, attention_weight, cosine, sine, table, per_device, offsets, cut, 2
+            )
+        )
     else:
+        query_low, key_low, value_low, swish_pre, retained, gated_low = retention_forward(
+            mixed_low, attention_weight, cosine, sine, table, per_device, offsets
+        )
+        swapped = exchange_seq(
+            output_pieces.reshape(seq_count, blocks, cut.width, width), 2
+        )
         output_full = jnp.concatenate(
             [
                 cut.assemble([swapped[piece, block] for piece in range(seq_count)], 0)
@@ -1561,6 +1811,24 @@
             ],
             axis=0,
         )
+
+    kept_rows = lax.broadcasted_iota(jnp.int32, down_piece.shape, 0) >= cut.skip(me)
+    down_full = gather_rows(after(jnp.where(kept_rows, down_piece, jnp.zeros_like(down_piece)), gated_low))
+    if square:
+        middle, channel_own = project_and_norm(
+            gated_low, output_full, local_input, channel_scale, 3
+        )
+        both_pre, hidden_low, down_term, channel_full = feed_forward_gather(
+            channel_own, feed_weight, upstream_full, 4
+        )
+        down_share = scatter_rows(down_term)
+        middle_grad, channel_term, branch_own, feed_term = feed_back_scatter(
+            after(upstream_full, down_term), both_pre, feed_weight, down_full, channel_full,
+            middle, upstream, channel_scale, 6,
+        )
+        feed_share = scatter_rows(feed_term)
+        branch_full = whole(branch_own, 7)
+    else:
         middle = inputs + scatter_seq(product(gated_low, output_full).astype(BF), 3)
         channel_full = whole(normalize(middle, channel_scale).astype(BF), 4)
         gate_pre, up_pre, hidden_low = feed_forward(channel_full, feed_weight)
@@ -1577,34 +1845,33 @@
         branch_full = whole(middle_grad.astype(BF), 7)
 
     at_value, at_swish = 2 * qk, 2 * qk + vd_pad
-    spare = lax.broadcasted_iota(jnp.int32, (width, vd_pad), 1) == vd
     if square:
         swish_grad, retained_grad, swish_term, output_send, layer_output = gate_backward_scatter(
-            after(branch_full, down_share), swapped, swish_pre, retained,
-            channel_term[:, None], hidden_low, down_full, mixed_turned, gated_low, middle,
+            after(branch_full, down_share), output_full, swish_pre, retained,
+            channel_term, hidden_low, down_full, mixed_turned, gated_low, middle,
             per_device, vd_pad, cut, 5,
         )
         swish_share = scatter_rows(swish_term)
         key_grad, value_grad, merged_term, down_all = retention_backward_exchange(
-            query_low, key_low, value_low, after(retained_grad, feed_share), table, cosine, sine,
+            query_low, key_low, value_low, after(retained_grad, feed_share), table_back, cosine, sine,
             mixed_turned, output_send, down_share, per_device, vd_pad, 8,
         )
         merged_share = scatter_rows(merged_term)
-        input_gradient, mixer_term, feed_all = input_backward(
+        input_gradient, value_term, feed_all = input_backward(
             key_grad, value_grad, swish_grad, attention_weight, local_input, middle_grad,
-            mixer_scale, feed_share, (at_value, at_swish), 9,
+            mixed_turned, mixer_scale, feed_share, (at_value, at_swish), vd, 9,
         )
     else:
         swish_grad, retained_grad = gate_backward(
             branch_full, output_full, swish_pre, retained, per_device, vd_pad
         )
+        spare = lax.broadcasted_iota(jnp.int32, (width, vd_pad), 1) == vd
         swish_term = transposed_times(mixed_low, swish_grad)
         swish_term = jnp.where(spare, channel_term[:, None], swish_term).astype(BF)
         swish_share = scatter_rows(swish_term)
-        result = middle + scatter_seq(hidden_part, 5)
-        layer_output = result.astype(BF)
+        layer_output = middle + scatter_seq(hidden_part, 5)
         key_grad, value_grad = retention_backward(
-            query_low, key_low, value_low, retained_grad, table, cosine, sine, per_device, vd_pad
+            query_low, key_low, value_low, retained_grad, table_back, cosine, sine, per_device, vd_pad
         )
         key_term = transposed_times(mixed_low, key_grad).astype(BF)
         key_share = scatter_rows(key_term)
@@ -1617,7 +1884,7 @@
             inputs, scatter_seq(mixed_part.astype(BF), 9), mixer_scale
         )
         mixer_term = jnp.sum(mixer_terms, axis=0)
-        input_gradient = (middle_grad + input_local).astype(BF)
+        input_gradient = middle_grad + input_local
         output_term = transposed_times(gated_low, branch_full).astype(BF)
         output_term = output_term.reshape(blocks, own_rows, width)
         output_send = jnp.stack(
@@ -1628,21 +1895,23 @@
         )
         output_swapped = exchange_seq(output_send, 8)
         output_share = scatter_rows(output_swapped.reshape(shards * cut.width, width))
-    input_gradient = input_gradient.reshape(groups, local_length, width)
-    value_term = transposed_times(mixed_low, value_grad)
-    value_term = jnp.where(spare, mixer_term[:, None], value_term).astype(BF)
+        value_term = transposed_times(mixed_low, value_grad)
+        value_term = jnp.where(spare, mixer_term[:, None], value_term).astype(BF)
+    input_gradient = input_gradient.astype(BF).reshape(groups, local_length, width)
     value_share = scatter_rows(value_term)
 
-    layer_output = layer_output.reshape(groups, local_length, width)
+    layer_output = layer_output.astype(BF).reshape(groups, local_length, width)
     if square:
-        down_gradient = cut.assemble([down_all[k] for k in range(seq_count)], 0).astype(F32)
-        gelu_gradient, linear_gradient = unpack_hidden(after(feed_all, value_term), cut, shards)
-        swish_all = gather_seq(after(swish_share, gelu_gradient), 13)
-        merged_all = gather_seq(after(merged_share, swish_all), 15)
-        output_gradient = unpack_output(merged_all, at_value, cut, width)
-        query_gradient = unpack_columns(merged_all, 0, qk)
-        key_gradient = unpack_columns(merged_all, qk, qk)
-        value_share = after(value_share, merged_all)
+        gelu_gradient, linear_gradient, down_gradient = unpack_feed(
+            after(feed_all, value_term), down_all, cut, shards
+        )
+        swish_all = gather_seq(
+            after(swish_share, gelu_gradient, layer_output, input_gradient), 13
+        )
+        swish_gradient, channel_own_gradient = unpack_columns(swish_all, vd)
+        merged_all = gather_seq(after(merged_share, swish_gradient), 15)
+        query_gradient, key_gradient, output_gradient = unpack_merged(merged_all, qk, cut, width)
+        value_share = after(value_share, query_gradient)
     else:
         down_all = gather_seq(down_share, 10)
         feed_all = gather_seq(after(feed_share, down_all), 11)
@@ -1650,26 +1919,29 @@
         output_all = gather_seq(after(output_share, swish_all), 12)
         key_all = gather_seq(after(key_share, output_all), 15)
         value_share = after(value_share, key_all)
-        down_gradient = cut.assemble([down_all[k] for k in range(seq_count)], 0).astype(F32)
+        swish_gradient, channel_own_gradient = unpack_columns(swish_all, vd)
         output_gradient = cut.assemble([output_all[k] for k in range(seq_count)], 0).astype(F32)
-        gelu_gradient, linear_gradient = unpack_hidden(feed_all, cut, shards)
-        query_gradient = unpack_columns(key_all, 0, qk)
-        key_gradient = unpack_columns(key_all, qk, qk)
+        gelu_gradient, linear_gradient, down_gradient = unpack_feed(
+            feed_all, down_all, cut, shards
+        )
+        query_gradient, key_gradient = (
+            jnp.concatenate(
+                [key_all[k][:, at : at + qk] for k in range(seq_count)], axis=1
+            ).astype(F32)
+            for at in (0, qk)
+        )
     value_all = gather_seq(value_share, 14)
-
-    def gain_order(gathered):
-        return jnp.sum(gathered[:, :, vd].astype(F32), axis=0)
-
+    value_gradient, mixer_own_gradient = unpack_columns(value_all, vd)
     return (
         layer_output,
         input_gradient,
-        gain_order(value_all),
+        mixer_own_gradient,
         query_gradient,
         key_gradient,
-        unpack_columns(value_all, 0, vd),
-        unpack_columns(swish_all, 0, vd),
+        value_gradient,
+        swish_gradient,
         output_gradient,
-        gain_order(swish_all),
+        channel_own_gradient,
         gelu_gradient,
         linear_gradient,
         down_gradient,

time: 660 us -> 616 us (0.933)
  Pallas kernels: 557 us -> 512 us
  waiting for transfers between devices: 2.5 us -> 27 us
  other arithmetic: 27.2 us -> 15 us
  local copies, waits for them, and re-layouts: 29.1 us -> 19.2 us
  matrix products: 12.9 us -> 4.79 us
    pallas_call x4 -> x3, Pallas kernels: 86.2 us -> 13.8 us  [the longest x1 6.17 us: unpack_feed(): pl.pallas_call(functools.partial(unpack_feed_kernel, cut, shards), grid=(...]
    pallas_call x6 -> x7, Pallas kernels: 280 us -> 317 us  [comm_call(): pl.pallas_call(body, out_shape=tuple((jax.ShapeDtypeStruct(shape, kind) f...]
    all_gather x4 -> x3, waiting for transfers between devices: 0.04 us -> 24.9 us  [gather_rows(): return lax.all_gather(values, 'fsdp', axis=0, tiled=True)]
    unnamed x32 -> x38, local copies, waits for them, and re-layouts: 5.49 us -> 16.9 us
    pallas_call x4 -> x2, Pallas kernels: 15.6 us -> 6.7 us  [unpack_columns(): pl.pallas_call(functools.partial(unpack_columns_kernel, width), grid=(row...]
    dot_general x1 -> x0, matrix products: 8.15 us -> none  [transposed_times(): lax.dot_general(left, right, (((0,), (0,)), ((), ())), preferred_element_...]
    reduce_sum x4 -> x0, other arithmetic: 7.8 us -> none  [the longest x2 3.6 us: gain_order(): return jnp.sum(gathered[:, :, vd].astype(F32), axis=0)]
    optimization_barrier x1 -> x0, local copies, waits for them, and re-layouts: 6.74 us -> none  [after(): held = lax.optimization_barrier((values,) + others)]
  transfers between devices with their start and end apart: 9 -> 8, of which waited for: 1 -> 2; matrix products, arithmetic and copies ran while one was open for 9% -> 3% of each run, Pallas kernels for 81% -> 81%
where the time goes in v5:
time: 616 us; the launch traced here: 608 us
  Pallas kernels  512 us (83%)
  waiting for transfers between devices  27 us (4%)
  local copies, waits for them, and re-layouts  19.2 us (3%)
  other arithmetic  15 us (2%)
  between operations  14.8 us (2%)
  blocking collectives  13.5 us (2%)
    pallas_call x7, Pallas kernels, comm_call(): pl.pallas_call(body, out_shape=tuple((jax.ShapeDtypeStruct(shape, kind) f...  317 us
    pallas_call x6, Pallas kernels, gather_seq(): pl.pallas_call(body, out_shape=jax.ShapeDtypeStruct((count,) + values.sha...  175 us
    all_gather x3, waiting for transfers between devices, gather_rows(): return lax.all_gather(values, 'fsdp', axis=0, tiled=True)  24.9 us
    unnamed x38, local copies, waits for them, and re-layouts  16.9 us
    all_gather x1, blocking collectives, on_device(): lax.all_gather(jnp.stack([mixer_gain, channel_gain]), 'fsdp', axis=1, til...  13.5 us
  transfers between devices with their start and end apart: 8, of which 2 were waited for; matrix products, arithmetic and copies ran while one was open for 3% of the time, Pallas kernels for 81%

profile of v5, /device:TPU:0, one launch (start us, length us, event | category | flops | bytes accessed | tf_op | source)
XLA Modules:
  0.0 607.6 jit_solution(17249298661937017697)
XLA Ops:
  7.2 0.0 all-gather.4.cloned.1.call-start
  7.2 1.4 copy-done
  8.7 0.1 dynamic-slice_bitcast_fusion
  8.8 0.1 copy.31
  8.9 0.3 copy.26
  9.3 1.0 dynamic-slice_dynamic-update-slice_fusion.1
  10.2 1.0 dynamic-slice_dynamic-update-slice_fusion
  11.2 1.8 constant_dynamic-slice_fusion
  13.0 0.1 pad_dynamic-update-slice_fusion.1
  13.1 0.1 pad_dynamic-update-slice_fusion
  13.2 0.1 bitcast_dynamic-update-slice_fusion
  13.3 1.2 copy-done.9
  14.6 0.0 all-gather.6.cloned.1.call-start
  14.7 13.5 %all_gather.12 = bf16[2,2048]{1,0:T(2,128)(2,1)S(1)} all-gather(bf16[2,256]{1,0:T(2,128)(2,1)S(1)} %pad_maximum_fusion.1), channel_id=1, replica_groups=mesh['seq'=4,'fsdp'=8] {'fsdp'}, dimensions={1}, use_global_device_ids=true | all-gather | bytes 9216 | tf_op jit(solution)/shard_map/all_gather | solution.py:1767
  28.1 38.0 %gather_seq_0.1 = bf16[4,256,2048]{2,1,0:T(8,128)(2,1)} custom-call(bf16[256,2048]{1,0:T(8,128)(2,1)} %bitcast.34), custom_call_target="tpu_custom_call" | custom-call | bytes 125829120 | tf_op jit(solution)/shard_map/gather_seq_0/pallas_call | solution.py:451
  66.1 36.3 %gather_seq_1.1 = bf16[4,256,2048]{2,1,0:T(8,128)(2,1)} custom-call(bf16[256,2048]{1,0:T(8,128)(2,1)} %bitcast.37), custom_call_target="tpu_custom_call" | custom-call | bytes 125829120 | tf_op jit(solution)/shard_map/gather_seq_1/pallas_call | solution.py:451
  102.5 2.4 fusion.3
  104.9 2.4 fusion.2
  107.3 1.0 pad_maximum_fusion
  108.3 0.3 all-gather.8.cloned.1.call-start
  108.6 0.6 slice_convert_fusion
  109.2 2.2 copy-done.3
  111.4 4.1 norm_and_turn.1
  115.6 1.9 copy-done.2
  117.5 2.0 copy-done.5
  119.6 2.8 fusion.4
  122.4 2.0 dynamic-slice_select_fusion
  124.4 0.4 fusion.1
  124.8 0.4 fusion
  125.2 0.3 maximum_convert_fusion.1
  125.5 0.3 maximum_convert_fusion
  125.8 2.5 exponential_select_fusion.table_ref
  128.3 2.4 exponential_select_fusion.1.table_ref
  130.7 24.9 %all-gather.4.cloned.1.call-done.w_any = bf16[2048,3712]{1,0:T(8,128)(2,1)} async-done(((bf16[256,3712]{1,0:T(8,128)(2,1)}), bf16[2048,3712]{1,0:T(8,128)(2,1)}) %all-gather.4.cloned.1.call-update) | async-done | bytes 15204368 | tf_op jit(solution)/shard_map/all_gather | solution.py:1741
  155.6 33.1 %retention_exchange.1 = (bf16[1024,512]{1,0:T(8,128)(2,1)}, bf16[1024,512]{1,0:T(8,128)(2,1)}, bf16[2,1024,432]{2,1,0:T(8,128)(2,1)}, f32[1024,864]{1,0:T(8,128)...) custom-call(bf16[1024,2048]{1,0:T(8,128)(2,1)} %copy-done.5, ...), custom_call_target="tpu_custom_call" | custom-call | bytes 251658240 | tf_op jit(solution)/shard_map/retention_exchange/pallas_call | solution.py:814
  188.7 0.0 all-gather.8.cloned.1.call-update
  188.7 0.4 reduce-scatter.6.cloned.1.call-start
  189.2 44.6 %project_and_norm.1 = (f32[256,2048]{1,0:T(8,128)}, bf16[256,2048]{1,0:T(8,128)(2,1)}) custom-call(bf16[1024,864]{1,0:T(8,128)(2,1)} %get-tuple-element.70.g_any.gated_any, bf16[864,2048]{1,0:T(8,128)(2,1)} %get-tuple-element.71.w_any, bf16[256,2048]{1,0:T(8,128)(2,1)} %bitcast.35, f32[1,2048]{1,0:T(1,128)} %get-tuple-element.118.gain_ref), custom_call_target="tpu_custom_call" | custom-call | bytes 125829120 | tf_op jit(solution)/shard_map/project_and_norm/pallas_call | solution.py:814
  233.8 0.0 all-gather.6.cloned.1.call-done.w_any
  233.8 42.6 %feed_forward_gather.1 = (f32[1024,1792]{1,0:T(8,128)}, bf16[1024,896]{1,0:T(8,128)(2,1)}, bf16[896,2048]{1,0:T(8,128)(2,1)}, bf16[4,256,2048]{2,1,0:T(8,128)(2,1)}) custom-call(bf16[256,2048]{1,0:T(8,128)(2,1)} %get-tuple-element.72.x_any, bf16[2048,1792]{1,0:T(8,128)(2,1)} %all-gather.6.cloned.1.call-done.w_any, bf16[1024,2048]{1,0:T(8,128)(2,1)} %bitcast.31), custom_call_target="tpu_custom_call" | custom-call | bytes 125829120 | tf_op jit(solution)/shard_map/feed_forward_gather/pallas_call | solution.py:814
  276.4 0.0 reduce-scatter.8.cloned.1.call-start
  276.5 0.0 all-gather.8.cloned.1.call-done.down_any
  276.5 49.5 %feed_back_scatter.1 = (f32[256,2048]{1,0:T(8,128)}, f32[2048,128]{1,0:T(8,128)}, bf16[256,2048]{1,0:T(8,128)(2,1)}, bf16[2048,1792]{1,0:T(8,128)(2,1)}) custom-call(bf16[1024,2048]{1,0:T(8,128)(2,1)} %bitcast.32, f32[1024,1792]{1,0:T(8,128)} %get-tuple-element.76.both_any, bf16[2048,1792]{1,0:T(8,128)(2,1)} %all-gather.6.cloned.1.call-done.w_any, ...), custom_call_target="tpu_custom_call" | custom-call | bytes 125829120 | tf_op jit(solution)/shard_map/feed_back_scatter/pallas_call | solution.py:814
  326.0 0.2 reduce-scatter.14.cloned.1.call-start
  326.3 35.9 %gather_seq_7.1 = bf16[4,256,2048]{2,1,0:T(8,128)(2,1)} custom-call(bf16[256,2048]{1,0:T(8,128)(2,1)} %get-tuple-element.80.x_ref), custom_call_target="tpu_custom_call" | custom-call | bytes 125829120 | tf_op jit(solution)/shard_map/gather_seq_7/pallas_call | solution.py:451
  362.2 0.0 reduce-scatter.6.cloned.1.call-done.share_any
  362.2 39.1 %gate_back_scatter.1 = (bf16[1024,896]{1,0:T(8,128)(2,1)}, bf16[2,1024,432]{2,1,0:T(8,128)(2,1)}, bf16[2048,896]{1,0:T(8,128)(2,1)}, bf16[2,4,256,896]{3,2,1,0:T(8,128)(2,1)}, f32[256,2048]{1,0:T(8,128)}) custom-call(bf16[1024,2048]{1,0:T(8,128)(2,1)} %bitcast.33, bf16[864,2048]{1,0:T(8,128)(2,1)} %get-tuple-element.71.w_any, ...), custom_call_target="tpu_custom_call" | custom-call | bytes 125829120 | tf_op jit(solution)/shard_map/gate_back_scatter/pallas_call | solution.py:814
  401.4 0.0 reduce-scatter.12.cloned.1.call-start
  401.4 1.9 reduce-scatter.8.cloned.1.call-done.share_any
  403.3 41.0 %retention_back_exchange.1 = (bf16[1024,1024]{1,0:T(8,128)(2,1)}, bf16[1024,896]{1,0:T(8,128)(2,1)}, bf16[2048,1920]{1,0:T(8,128)(2,1)}, bf16[4,112,2048]{2,1,0:T(8,128)(2,1)}) custom-call(bf16[1024,512]{1,0:T(8,128)(2,1)} %get-tuple-element.87.q_any, bf16[1024,512]{1,0:T(8,128)(2,1)} %get-tuple-element.88.k_any, ...), custom_call_target="tpu_custom_call" | custom-call | bytes 110100480 | tf_op jit(solution)/shard_map/retention_back_exchange/pallas_call | solution.py:814
  444.4 0.3 reduce-scatter.10.cloned.1.call-start
  444.6 66.8 %input_backward.1 = (f32[256,2048]{1,0:T(8,128)}, bf16[2048,896]{1,0:T(8,128)(2,1)}, bf16[4,256,1792]{2,1,0:T(8,128)(2,1)}) custom-call(bf16[1024,1024]{1,0:T(8,128)(2,1)} %get-tuple-element.94.dqk_any, bf16[1024,896]{1,0:T(8,128)(2,1)} %get-tuple-element.95.dv_any, bf16[1024,896]{1,0:T(8,128)(2,1)} %get-tuple-element.96.ds_any, ...), custom_call_target="tpu_custom_call" | custom-call | bytes 235929600 | tf_op jit(solution)/shard_map/input_backward/pallas_call | solution.py:814
  511.5 1.5 copy-done.10
  513.0 1.1 convert_bitcast_fusion.1
  514.1 2.1 copy-done.6
  516.2 6.2 %unpack_feed.1 = (f32[256,3456]{1,0:T(8,128)}, f32[256,3456]{1,0:T(8,128)}, f32[432,2048]{1,0:T(8,128)}) custom-call(bf16[4,256,1792]{2,1,0:T(8,128)(2,1)S(1)} %copy-done.6, bf16[4,112,2048]{2,1,0:T(8,128)(2,1)S(1)} %copy-done.7), custom_call_target="tpu_custom_call" | custom-call | tf_op jit(solution)/shard_map/unpack_feed/pallas_call | solution.py:1625
  522.4 1.1 convert_bitcast_fusion
  523.5 16.5 %gather_seq_13.1.in_ref = bf16[4,256,896]{2,1,0:T(8,128)(2,1)} custom-call(bf16[256,896]{1,0:T(8,128)(2,1)} %reduce-scatter.14.cloned.1.call-done.x_ref), custom_call_target="tpu_custom_call" | custom-call | bytes 55050240 | tf_op jit(solution)/shard_map/gather_seq_13/pallas_call | solution.py:451
  540.0 3.4 unpack_columns.2
  543.5 31.5 %gather_seq_15.1.in_ref = bf16[4,256,1920]{2,1,0:T(8,128)(2,1)} custom-call(bf16[256,1920]{1,0:T(8,128)(2,1)} %reduce-scatter.12.cloned.1.call-done.x_ref), custom_call_target="tpu_custom_call" | custom-call | bytes 117964800 | tf_op jit(solution)/shard_map/gather_seq_15/pallas_call | solution.py:451
  575.0 2.1 copy-done.4
  577.2 3.5 unpack_merged.1
  580.6 16.6 %gather_seq_14.1.in_ref = bf16[4,256,896]{2,1,0:T(8,128)(2,1)} custom-call(bf16[256,896]{1,0:T(8,128)(2,1)} %reduce-scatter.10.cloned.1.call-done.x_ref), custom_call_target="tpu_custom_call" | custom-call | bytes 55050240 | tf_op jit(solution)/shard_map/gather_seq_14/pallas_call | solution.py:451
  597.2 3.2 unpack_columns.3
  (46 shorter events, 0.3 us)
Async XLA Ops:
  7.2 1.5 copy-start
  7.2 148.4 %all-gather.4.cloned.1.call-start = ((), (), s32[]{:S(2)}) async-start(), calls=%async_computation.5 | async-start | bytes 17104896 | tf_op jit(solution)/shard_map/all_gather | solution.py:1741
  13.1 1.5 copy-start.14
  13.1 1.5 copy-start.15
  13.3 1.3 copy-start.9
  14.6 219.2 %all-gather.6.cloned.1.call-start = ((), (), s32[]{:S(2)}) async-start(), calls=%async_computation.6 | async-start | bytes 8257536 | tf_op jit(solution)/shard_map/all_gather | solution.py:1741
  66.1 36.4 %copy-start.12 = (bf16[256,3456]{1,0:T(8,128)(2,1)S(1)}, bf16[256,3456]{1,0:T(8,128)(2,1)}, u32[]{:S(2)}) copy-start(bf16[256,3456]{1,0:T(8,128)(2,1)} %param.21) | copy-start | bytes 5308420
  102.5 2.4 copy-start.13
  108.3 168.2 %all-gather.8.cloned.1.call-start = ((), (), s32[]{:S(2)}) async-start(), calls=%async_computation.7 | async-start | bytes 4128768 | tf_op jit(solution)/shard_map/all_gather | solution.py:1741
  109.2 6.4 %copy-start.8 = (f32[1,2048]{1,0:T(1,128)}, f32[1,2048]{1,0:T(1,128)S(1)}, u32[]{:S(2)}) copy-start(f32[1,2048]{1,0:T(1,128)S(1)} %get-tuple-element.119.gain_ref) | copy-start | bytes 24580
  109.2 2.2 copy-start.3
  115.6 2.0 copy-start.2
  117.5 2.0 copy-start.5
  188.7 173.5 %reduce-scatter.6.cloned.1.call-start = ((), (), s32[]{:S(2)}) async-start(), calls=%async_computation.8 | async-start | bytes 4128768 | tf_op jit(solution)/shard_map/reduce_scatter | solution.py:1744
  276.4 126.9 %reduce-scatter.8.cloned.1.call-start = ((), (), s32[]{:S(2)}) async-start(), calls=%async_computation.9 | async-start | bytes 8257536 | tf_op jit(solution)/shard_map/reduce_scatter | solution.py:1744
  326.0 197.5 %reduce-scatter.14.cloned.1.call-start = ((), (), s32[]{:S(2)}) async-start(), calls=%async_computation.12 | async-start | bytes 4128768 | tf_op jit(solution)/shard_map/reduce_scatter | solution.py:1744
  401.4 142.1 %reduce-scatter.12.cloned.1.call-start = ((), (), s32[]{:S(2)}) async-start(), calls=%async_computation.11 | async-start | bytes 8847360 | tf_op jit(solution)/shard_map/reduce_scatter | solution.py:1744
  444.4 136.3 %reduce-scatter.10.cloned.1.call-start = ((), (), s32[]{:S(2)}) async-start(), calls=%async_computation.10 | async-start | bytes 4128768 | tf_op jit(solution)/shard_map/reduce_scatter | solution.py:1744
  511.4 1.6 copy-start.10
  511.5 2.7 copy-start.7
  514.1 2.1 copy-start.6
  516.2 6.2 %copy-start.11 = (f32[256,2048]{1,0:T(8,128)S(1)}, f32[256,2048]{1,0:T(8,128)}, u32[]{:S(2)}) copy-start(f32[256,2048]{1,0:T(8,128)} %get-tuple-element.98) | copy-start | bytes 6291460
  575.0 2.2 copy-start.4
  577.2 23.3 %copy-start.1 = (bf16[432,2048]{1,0:T(8,128)(2,1)S(1)}, bf16[432,2048]{1,0:T(8,128)(2,1)}, u32[]{:S(2)}) copy-start(bf16[432,2048]{1,0:T(8,128)(2,1)} %param.18) | copy-start | bytes 5308420
Sparse Core Ops, SparseCore 0:
  14.7 140.8 all-gather.3
  157.8 71.6 all-gather.5
  231.7 41.1 all-gather.7
  276.6 42.4 reduce-scatter.5
  326.2 77.1 reduce-scatter.7
  405.5 43.4 reduce-scatter.13
  451.2 82.9 reduce-scatter.11
  536.6 43.4 reduce-scatter.9

commit v6 on v5

--- a/solution.py
+++ b/solution.py
@@ -464,6 +464,44 @@
     )(values)
 
 
+def gather_two_kernel(a_ref, b_ref, a_out, b_out, sends, recvs, locals_):
+    me = lax.axis_index("seq")
+    greet((me ^ 1, me ^ 2))
+    moves = Moves(locals_)
+    moves.store(a_ref, a_out.at[me])
+    moves.store(b_ref, b_out.at[me])
+    both = [
+        square_pass(ref, out, sends, recvs, first, half_rows(ref.shape[0]))
+        for ref, out, first in ((a_ref, a_out, 0), (b_ref, b_out, 6))
+    ]
+    for copies in both:
+        for copy in copies[:4]:
+            copy.start()
+    for copies in both:
+        pass_on(copies)
+    for copies in both:
+        for copy in copies[2:]:
+            copy.wait_recv()
+    moves.close()
+    for copies in both:
+        for copy in copies:
+            copy.wait_send()
+
+
+def gather_two(a, b, call):
+    return comm_call(
+        gather_two_kernel,
+        [(a, False), (b, False)],
+        [((4,) + a.shape, BF, False), ((4,) + b.shape, BF, False)],
+        [],
+        12,
+        2,
+        call,
+        a.size + b.size,
+        "gather_two",
+    )
+
+
 def exchange_kernel(count, x_ref, o_ref, sends, recvs, local):
     me = lax.axis_index("seq")
     peers = [lax.rem(me + step, count) for step in range(1, count)]
@@ -810,6 +848,55 @@
     )(*inputs)
 
 
+def core_sum(moves, make, send_ref, twin_ref, out_ref, targets, sends, recvs, first):
+    shard = lax.axis_index("fsdp")
+    core = lax.rem(shard, 2)
+    count = out_ref.shape[0]
+
+    def copy(t):
+        return pltpu.make_async_remote_copy(
+            src_ref=send_ref.at[t],
+            dst_ref=twin_ref.at[t],
+            send_sem=sends.at[first + t],
+            recv_sem=recvs.at[first + t],
+            device_id={"fsdp": shard ^ 1},
+            device_id_type=MESH,
+        )
+
+    stores = Series(moves, count, lambda t: (out_ref.at[t], targets(t)))
+
+    @pl.loop(0, count)
+    def _(t):
+        send_ref[t] = make(2 * t + 1 - core).astype(BF)
+        copy(t).start()
+
+    @pl.loop(0, count)
+    def _(t):
+        own = make(2 * t + core)
+        copy(t).wait_recv()
+        out_ref[t] = (own + twin_ref[t].astype(F32)).astype(BF)
+        stores.copy(t).start()
+
+    def finish():
+        stores.wait_all()
+        for t in range(count):
+            copy(t).wait_send()
+
+    return finish
+
+
+def greet_near(me, shard):
+    barrier = pltpu.get_barrier_semaphore()
+    for k in (1, 2):
+        pl.semaphore_signal(barrier, inc=1, device_id={"seq": me ^ k}, device_id_type=MESH)
+    pl.semaphore_signal(barrier, inc=1, device_id={"fsdp": shard ^ 1}, device_id_type=MESH)
+    pl.semaphore_wait(barrier, 3)
+
+
+def core_scratch(rows, width):
+    return [pltpu.VMEM((rows // (2 * BLOCK), BLOCK, width), BF)] * 3
+
+
 def comm_call(body, inputs, outputs, scratch, remotes, moves, call, cost, name):
     return pl.pallas_call(
         body,
@@ -1012,8 +1099,12 @@
         here = block_rows(k, rows)
         both = product(full[me ^ k], w_ref[...])
         gate, up = both[:, :ff], both[:, ff:]
-        both_ref[here, :] = both
-        hidden = (gate * (0.5 + 0.5 * lax.erf(gate * math.sqrt(0.5))) * up).astype(BF)
+        bell = 0.5 + 0.5 * lax.erf(gate * math.sqrt(0.5))
+        passed = gate * bell
+        slope = bell + gate * (math.sqrt(0.5 / math.pi) * jnp.exp(-0.5 * gate * gate))
+        both_ref[here, :ff] = (up * slope).astype(BF)
+        both_ref[here, ff:] = passed.astype(BF)
+        hidden = (passed * up).astype(BF)
         hidden_ref[here, :] = hidden
         for store in stores:
             store.copy(me ^ k).start()
@@ -1035,7 +1126,7 @@
         functools.partial(feed_forward_gather_kernel, ff),
         [(own, False), (weight, False), (cotangent, False)],
         [
-            ((length, 2 * ff), F32, False),
+            ((length, 2 * ff), BF, False),
             ((length, ff), BF, False),
             ((ff, width), BF, False),
             ((4, rows, width), BF, False),
@@ -1044,7 +1135,7 @@
             pltpu.VMEM((4, rows, width), BF),
             pltpu.VMEM(weight.shape, BF),
             pltpu.VMEM(cotangent.shape, BF),
-            pltpu.VMEM((length, 2 * ff), F32),
+            pltpu.VMEM((length, 2 * ff), BF),
             pltpu.VMEM((length, ff), BF),
             pltpu.VMEM((ff, width), F32),
             pltpu.VMEM((ff, width), BF),
@@ -1069,7 +1160,7 @@
 def feed_back_scatter_kernel(
     ff, c_any, both_any, w_any, down_any, x_any, m_ref, own_c_ref, gain_ref,
     grad_ref, term_ref, branch_ref, dw_any,
-    c_ref, both_ref, w_ref, down_ref, x_ref, low, dw_ref,
+    c_ref, both_ref, w_ref, down_ref, x_ref, low, dw_send, dw_twin, dw_ref,
     parts, inbox_x, inbox_y, via_x, via_y, out_x, out_y, sends, recvs, locals_,
 ):
     me = lax.axis_index("seq")
@@ -1086,7 +1177,7 @@
         load_c.copy(me ^ k).start()
         load_both.copy(me ^ k).start()
     load_x = moves.start(x_any, x_ref)
-    greet((me ^ 1, me ^ 2))
+    greet_near(me, lax.axis_index("fsdp"))
     boxes = (inbox_x, inbox_y, via_x, via_y, out_x, out_y)
     copies, _, total = square_parts(parts, boxes, sends, recvs, 0)
 
@@ -1094,26 +1185,19 @@
         here = block_rows(k, rows)
         load_c.copy(me ^ k).wait()
         load_both.copy(me ^ k).wait()
-        gate, up = both_ref[here, :ff], both_ref[here, ff:]
         hidden_grad = times_transposed(c_ref[here, :], down_ref[...])
-        bell = 0.5 + 0.5 * lax.erf(gate * math.sqrt(0.5))
-        slope = bell + gate * (math.sqrt(0.5 / math.pi) * jnp.exp(-0.5 * gate * gate))
-        low[here, :ff] = (hidden_grad * up * slope).astype(BF)
-        low[here, ff:] = (hidden_grad * (gate * bell)).astype(BF)
+        low[here, :ff] = (hidden_grad * both_ref[here, :ff].astype(F32)).astype(BF)
+        low[here, ff:] = (hidden_grad * both_ref[here, ff:].astype(F32)).astype(BF)
         pl.when(k == 3)(load_w.wait)
         parts[k] = times_transposed(low[here, :], w_ref[...]).astype(BF)
 
     load_down.wait()
     send_parts(part, copies, lambda: forward_sums(copies, parts, boxes))
     load_x.wait()
-    stores = by_block(moves, x_ref.shape[1] // BLOCK, dw_ref, dw_any)
-
-    @pl.loop(0, stores.count)
-    def _(b):
-        lanes = rows_of(b)
-        dw_ref[lanes, :] = transposed_times(x_ref[:, lanes], low[...]).astype(BF)
-        stores.copy(b).start()
-
+    finish = core_sum(
+        moves, lambda b: transposed_times(x_ref[:, rows_of(b)], low[...]), dw_send, dw_twin, dw_ref,
+        lambda t: dw_any.at[rows_of(t)], sends, recvs, 6,
+    )
     for copy in copies[2:]:
         copy.wait_recv()
 
@@ -1126,7 +1210,7 @@
         return term
 
     term_ref[...] = column_of([back_half(i) for i in range(2)])
-    stores.wait_all()
+    finish()
     for copy in copies:
         copy.wait_send()
 
@@ -1150,20 +1234,20 @@
             ((rows, width), F32, True),
             ((width, 128), F32, True),
             ((rows, width), BF, True),
-            ((width, 2 * ff), BF, False),
+            ((width // 2, 2 * ff), BF, False),
         ],
         [
             pltpu.VMEM(cotangent.shape, BF),
-            pltpu.VMEM(both.shape, F32),
+            pltpu.VMEM(both.shape, BF),
             pltpu.VMEM(weight.shape, BF),
             pltpu.VMEM(down.shape, BF),
             pltpu.VMEM(x.shape, BF),
             pltpu.VMEM((length, 2 * ff), BF),
-            pltpu.VMEM((width, 2 * ff), BF),
         ]
+        + core_scratch(width, 2 * ff)
         + square_scratch(rows, width),
-        6,
-        11 + width // BLOCK,
+        6 + width // (2 * BLOCK),
+        11 + width // (2 * BLOCK),
         call,
         own_cotangent.size,
         "feed_back_scatter",
@@ -1224,7 +1308,7 @@
     heads, cut, branch_any, w_any, swish_any, retained_any, column_any, hidden_any, down_any,
     mixed_any, gated_any, m_any, dswish_any, dret_any, dws_any, dwo_any, out_ref,
     branch_ref, w_ref, swish_ref, retained_ref, column_ref, hidden_ref, down_ref, mixed_ref,
-    gated_ref, m_ref, dswish_ref, dret_ref, dws_ref, dwo_ref,
+    gated_ref, m_ref, dswish_ref, dret_ref, dws_send, dws_twin, dws_ref, dwo_ref,
     parts, inbox_x, inbox_y, via_x, via_y, out_x, out_y, sends, recvs, locals_,
 ):
     me = lax.axis_index("seq")
@@ -1243,7 +1327,7 @@
     load_column = moves.start(column_any, column_ref)
     load_gated = moves.start(gated_any, gated_ref)
     load_m = moves.start(m_any, m_ref)
-    greet((me ^ 1, me ^ 2))
+    greet_near(me, lax.axis_index("fsdp"))
     boxes = (inbox_x, inbox_y, via_x, via_y, out_x, out_y)
     copies, _, total = square_parts(parts, boxes, sends, recvs, 0)
 
@@ -1270,15 +1354,18 @@
     forward_sums(copies, parts, boxes)
     load_mixed.wait()
     load_column.wait()
-    stores = by_block(moves, dws_ref.shape[0] // BLOCK, dws_ref, dws_any)
-
-    @pl.loop(0, stores.count)
-    def _(b):
+    last = dswish_ref.shape[1] - 128
+    spare = lax.broadcasted_iota(jnp.int32, (BLOCK, 128), 1) == heads * VAL_HEAD - last
+
+    def make(b):
         here = rows_of(b)
-        dws_ref[here, :] = product(mixed_ref[here, :], dswish_ref[...]).astype(BF)
-        put_column(dws_ref, here, heads * VAL_HEAD, column_ref[here, :])
-        stores.copy(b).start()
-
+        term = product(mixed_ref[here, :], dswish_ref[...])
+        column = jnp.where(spare, column_ref[here, :], term[:, last:])
+        return jnp.concatenate([term[:, :last], column], axis=1)
+
+    finish = core_sum(
+        moves, make, dws_send, dws_twin, dws_ref, lambda t: dws_any.at[rows_of(t)], sends, recvs, 6
+    )
     load_gated.wait()
     step, tile, lane = 2 * BLOCK, 16, 128
     for h in range(heads):
@@ -1302,7 +1389,7 @@
     for copy in copies[2:]:
         copy.wait_recv()
     out_ref[...] = m_ref[...] + total(slice(0, rows))
-    stores.wait_all()
+    finish()
     moves.close()
     for copy in copies:
         copy.wait_send()
@@ -1319,7 +1406,7 @@
     outputs = [
         ((length, padded), BF, False),
         ((heads, length, VAL_HEAD), BF, False),
-        ((width, padded), BF, False),
+        ((width // 2, padded), BF, False),
         (dwo, BF, False),
         ((rows, width), F32, True),
     ]
@@ -1328,10 +1415,12 @@
         [(value, False) for value in inputs],
         outputs,
         [pltpu.VMEM(v.shape, v.dtype) for v in inputs]
-        + [pltpu.VMEM(shape, kind) for shape, kind, _ in outputs[:4]]
+        + [pltpu.VMEM(shape, kind) for shape, kind, _ in outputs[:2]]
+        + core_scratch(width, padded)
+        + [pltpu.VMEM(dwo, BF)]
         + square_scratch(rows, width),
-        6,
-        20 + 3 * length // BLOCK + width // BLOCK,
+        6 + width // (2 * BLOCK),
+        20 + 3 * length // BLOCK + width // (2 * BLOCK),
         call,
         middle.size,
         "gate_back_scatter",
@@ -1341,8 +1430,8 @@
 def retention_back_exchange_kernel(
     heads, q_any, k_any, v_any, dret_any, table_ref, cos_ref, sin_ref, mixed_any, send_any, share_any,
     dqk_any, dv_any, merged_any, full_any,
-    q_ref, k_ref, v_ref, dret_ref, mixed_ref, send_ref, dqk_ref, dv_ref, dwqk_ref, twin_ref, sum_ref,
-    zero_ref, dv_heads, dq_sum, sends, recvs, locals_,
+    q_ref, k_ref, v_ref, dret_ref, mixed_ref, send_ref, dqk_ref, dv_ref, dw_send, dw_twin, dw_ref,
+    twin_ref, sum_ref, via_x, via_y, dv_heads, dq_sum, sends, recvs, locals_,
 ):
     me = lax.axis_index("seq")
     shard = lax.axis_index("fsdp")
@@ -1361,8 +1450,8 @@
     twin = pltpu.make_async_remote_copy(
         src_ref=send_ref.at[1 - core],
         dst_ref=twin_ref,
-        send_sem=sends.at[9],
-        recv_sem=recvs.at[9],
+        send_sem=sends.at[12],
+        recv_sem=recvs.at[12],
         device_id={"fsdp": shard ^ 1},
         device_id_type=MESH,
     )
@@ -1372,21 +1461,25 @@
         copy.start()
     moves.store(share_any, full_any.at[me])
     step, wide = sum_ref.shape[1:]
+    half = step // 2
     at = dqk_ref.shape[1]
-
-    def place(column, parity):
-        return merged_any.at[
-            pl.ds(pl.multiple_of((2 * column + parity) * step, step), step), pl.ds(at, wide)
-        ]
-
-    zero_ref[...] = jnp.zeros_like(zero_ref)
-    for column in range(4):
-        moves.store(zero_ref, place(column, 1 - core))
+    across, along, corner = me ^ 1, me ^ 2, me ^ 3
+
+    def place(column, start, rows):
+        here = pl.ds(pl.multiple_of(column * step + start, half), rows)
+        return merged_any.at[here, slice(at, at + wide)]
+
+    low, high = slice(0, half), slice(half, step)
+    swaps = [
+        remote(sum_ref.at[corner, low], via_x, sends, recvs, 6, across),
+        remote(sum_ref.at[corner, high], via_y, sends, recvs, 7, along),
+        remote(sum_ref.at[across], place(me, 0, step), sends, recvs, 8, across),
+        remote(sum_ref.at[along], place(me, 0, step), sends, recvs, 9, along),
+        remote(via_x, place(across, 0, half), sends, recvs, 10, along),
+        remote(via_y, place(along, half, half), sends, recvs, 11, across),
+    ]
     for load in loads:
         load.wait()
-    swaps = [
-        remote(sum_ref.at[me ^ k], place(me, core), sends, recvs, 5 + k, me ^ k) for k in (3, 1, 2)
-    ]
     for h in range(heads):
         retention_back_head(
             h, heads, q_ref, k_ref, v_ref, dret_ref, table_ref, cos_ref, sin_ref, dqk_ref,
@@ -1399,29 +1492,22 @@
             def _(k):
                 sum_ref[k] = (send_ref[core, k].astype(F32) + twin_ref[k].astype(F32)).astype(BF)
 
-            for copy in swaps:
+            for copy in swaps[:4]:
                 copy.start()
-            moves.store(sum_ref.at[me], place(me, core))
+            moves.store(sum_ref.at[me], place(me, 0, step))
             pass_on(passed)
+    pass_on(swaps)
     dv_ref[...] = pad_lanes([dv_heads[h] for h in range(heads)], dv_ref.shape[1])
     moves.store(dv_ref, dv_any)
     moves.store(dqk_ref, dqk_any)
     load_mixed.wait()
-    stores = Series(
-        moves,
-        mixed_ref.shape[0] // BLOCK,
-        lambda b: (dwqk_ref.at[rows_of(b)], merged_any.at[rows_of(b), slice(0, at)]),
-    )
-
-    @pl.loop(0, stores.count)
-    def _(b):
-        here = rows_of(b)
-        dwqk_ref[here, :] = product(mixed_ref[here, :], dqk_ref[...]).astype(BF)
-        stores.copy(b).start()
-
-    for copy in passed[2:] + swaps:
+    finish = core_sum(
+        moves, lambda b: product(mixed_ref[rows_of(b), :], dqk_ref[...]), dw_send, dw_twin, dw_ref,
+        lambda t: merged_any.at[rows_of(t), slice(0, at)], sends, recvs, 13,
+    )
+    for copy in passed[2:] + swaps[2:]:
         copy.wait_recv()
-    stores.wait_all()
+    finish()
     moves.close()
     for copy in passed + swaps + [twin]:
         copy.wait_send()
@@ -1438,28 +1524,32 @@
     )
     staged = (q, k, v, dret, mixed_t, send)
     block = send.shape[1:]
+    kept = width // 2
     return comm_call(
         functools.partial(retention_back_exchange_kernel, heads),
         inputs,
         [
             ((length, 2 * qk), BF, False),
             ((length, padded), BF, False),
-            ((width, 2 * qk + block[2]), BF, False),
+            ((kept, 2 * qk + block[2]), BF, False),
             ((4,) + share.shape, BF, False),
         ],
         [pltpu.VMEM(value.shape, BF) for value in staged]
         + [
             pltpu.VMEM((length, 2 * qk), BF),
             pltpu.VMEM((length, padded), BF),
-            pltpu.VMEM((width, 2 * qk), BF),
+        ]
+        + core_scratch(width, 2 * qk)
+        + [
             pltpu.VMEM(block, BF),
             pltpu.VMEM(block, BF),
-            pltpu.VMEM(block[1:], BF),
+            pltpu.VMEM((block[1] // 2, block[2]), BF),
+            pltpu.VMEM((block[1] // 2, block[2]), BF),
             pltpu.VMEM((heads, length, VAL_HEAD), BF),
             pltpu.VMEM((length, KEY_HEAD), F32),
         ],
-        10,
-        16 + width // BLOCK,
+        13 + kept // BLOCK,
+        12 + kept // BLOCK,
         call,
         send.size // 4,
         "retention_back_exchange",
@@ -1590,9 +1680,49 @@
             jax.ShapeDtypeStruct((rows, count * width), F32),
             jax.ShapeDtypeStruct((1, rows), F32),
         ],
+        cost_estimate=pl.CostEstimate(flops=0, bytes_accessed=gathered.size * 4, transcendentals=0),
         name="unpack_columns",
     )(gathered)
     return out, gain[0]
+
+
+def unpack_related_kernel(width, own_ref, across_ref, along_ref, corner_ref, out_ref, gain_ref):
+    me = lax.axis_index("seq")
+    pieces = [ref[...].astype(F32) for ref in (own_ref, across_ref, along_ref, corner_ref)]
+    last = own_ref.shape[1] - 128
+    tile = sum(piece[:, last:] for piece in pieces)
+    gain_ref[...] = tile.T[width - last : width - last + 1, :]
+    pieces = [piece[:, :width] for piece in pieces]
+    low = [jnp.where(me % 2 == k, pieces[0], pieces[1]) for k in range(2)]
+    high = [jnp.where(me % 2 == k, pieces[2], pieces[3]) for k in range(2)]
+    order = [jnp.where(me < 2, low[k], high[k]) for k in range(2)]
+    order += [jnp.where(me < 2, high[k], low[k]) for k in range(2)]
+    out_ref[...] = join(order)
+
+
+def unpack_related(pieces, width):
+    rows, whole = pieces[0].shape
+    block = min(rows, 128)
+    out, gain = pl.pallas_call(
+        functools.partial(unpack_related_kernel, width),
+        grid=(rows // block,),
+        in_specs=[pl.BlockSpec((block, whole), lambda i: (i, 0))] * 4,
+        out_specs=[
+            pl.BlockSpec((block, 4 * width), lambda i: (i, 0)),
+            pl.BlockSpec((1, block), lambda i: (0, i)),
+        ],
+        out_shape=[
+            jax.ShapeDtypeStruct((rows, 4 * width), F32),
+            jax.ShapeDtypeStruct((1, rows), F32),
+        ],
+        compiler_params=pltpu.CompilerParams(vmem_limit_bytes=40 * 1024 * 1024),
+        name="unpack_related",
+    )(*pieces)
+    return out, gain[0]
+
+
+def swap(values, step):
+    return lax.ppermute(values, "seq", [(k, k ^ step) for k in range(4)])
 
 
 def unpack_feed_kernel(cut, shards, in_ref, down_ref, gate_ref, up_ref, out_ref):
@@ -1640,6 +1770,7 @@
             jax.ShapeDtypeStruct((cut.rows, width), F32),
         ],
         compiler_params=pltpu.CompilerParams(vmem_limit_bytes=40 * 1024 * 1024),
+        cost_estimate=pl.CostEstimate(flops=0, bytes_accessed=gathered.size * 4, transcendentals=0),
         name="unpack_feed",
     )(gathered, down)
 
@@ -1669,6 +1800,7 @@
             jax.ShapeDtypeStruct((cut.rows, width), F32),
         ),
         compiler_params=pltpu.CompilerParams(vmem_limit_bytes=40 * 1024 * 1024),
+        cost_estimate=pl.CostEstimate(flops=0, bytes_accessed=gathered.size * 4, transcendentals=0),
         name="unpack_merged",
     )(gathered)
 
@@ -1743,6 +1875,12 @@
     def scatter_rows(values):
         return lax.psum_scatter(values.astype(BF), "fsdp", scatter_dimension=0, tiled=True)
 
+    def scatter_parity(values):
+        groups = [list(range(parity, shards, 2)) for parity in range(2)]
+        return lax.psum_scatter(
+            values, "fsdp", scatter_dimension=0, tiled=True, axis_index_groups=groups
+        )
+
     output_piece = lax.dynamic_slice_in_dim(output_weight, cut.start(me), cut.width, axis=0)
     attention_pieces = [
         columns_of(query_weight, me, qk, qk),
@@ -1826,7 +1964,7 @@
             after(upstream_full, down_term), both_pre, feed_weight, down_full, channel_full,
             middle, upstream, channel_scale, 6,
         )
-        feed_share = scatter_rows(feed_term)
+        feed_share = scatter_parity(feed_term)
         branch_full = whole(branch_own, 7)
     else:
         middle = inputs + scatter_seq(product(gated_low, output_full).astype(BF), 3)
@@ -1851,12 +1989,12 @@
             channel_term, hidden_low, down_full, mixed_turned, gated_low, middle,
             per_device, vd_pad, cut, 5,
         )
-        swish_share = scatter_rows(swish_term)
+        swish_share = scatter_parity(swish_term)
         key_grad, value_grad, merged_term, down_all = retention_backward_exchange(
             query_low, key_low, value_low, after(retained_grad, feed_share), table_back, cosine, sine,
             mixed_turned, output_send, down_share, per_device, vd_pad, 8,
         )
-        merged_share = scatter_rows(merged_term)
+        merged_share = scatter_parity(merged_term)
         input_gradient, value_term, feed_all = input_backward(
             key_grad, value_grad, swish_grad, attention_weight, local_input, middle_grad,
             mixed_turned, mixer_scale, feed_share, (at_value, at_swish), vd, 9,
@@ -1902,23 +2040,35 @@
 
     layer_output = layer_output.astype(BF).reshape(groups, local_length, width)
     if square:
+        swish_all, merged_all = gather_two(
+            after(swish_share, layer_output, input_gradient), merged_share, 13
+        )
+        value_share = after(value_share, swish_all)
+        half = value_share.shape[0] // 2
+        across, along = swap(value_share, 1), swap(value_share, 2)
         gelu_gradient, linear_gradient, down_gradient = unpack_feed(
-            after(feed_all, value_term), down_all, cut, shards
-        )
-        swish_all = gather_seq(
-            after(swish_share, gelu_gradient, layer_output, input_gradient), 13
+            after(feed_all, swish_all), down_all, cut, shards
         )
         swish_gradient, channel_own_gradient = unpack_columns(swish_all, vd)
-        merged_all = gather_seq(after(merged_share, swish_gradient), 15)
+        across, along, gelu_gradient, swish_gradient = after(
+            across, along, gelu_gradient, swish_gradient, all_of=True
+        )
+        corner_low, corner_high = swap(across[:half], 2), swap(along[half:], 1)
         query_gradient, key_gradient, output_gradient = unpack_merged(merged_all, qk, cut, width)
-        value_share = after(value_share, query_gradient)
+        corner_low, corner_high, query_gradient = after(
+            corner_low, corner_high, query_gradient, all_of=True
+        )
+        corner = jnp.concatenate([corner_low, corner_high], axis=0)
+        value_gradient, mixer_own_gradient = unpack_related(
+            (value_share, across, along, corner), vd
+        )
     else:
         down_all = gather_seq(down_share, 10)
         feed_all = gather_seq(after(feed_share, down_all), 11)
         swish_all = gather_seq(after(swish_share, feed_all), 13)
         output_all = gather_seq(after(output_share, swish_all), 12)
         key_all = gather_seq(after(key_share, output_all), 15)
-        value_share = after(value_share, key_all)
+        value_all = gather_seq(after(value_share, key_all), 14)
         swish_gradient, channel_own_gradient = unpack_columns(swish_all, vd)
         output_gradient = cut.assemble([output_all[k] for k in range(seq_count)], 0).astype(F32)
         gelu_gradient, linear_gradient, down_gradient = unpack_feed(
@@ -1930,8 +2080,7 @@
             ).astype(F32)
             for at in (0, qk)
         )
-    value_all = gather_seq(value_share, 14)
-    value_gradient, mixer_own_gradient = unpack_columns(value_all, vd)
+        value_gradient, mixer_own_gradient = unpack_columns(value_all, vd)
     return (
         layer_output,
         input_gradient,

time: 616 us -> 599 us (0.972)
  Pallas kernels: 512 us -> 496 us
    pallas_call x6 -> x3, Pallas kernels: 175 us -> 110 us  [gather_seq(): pl.pallas_call(body, out_shape=jax.ShapeDtypeStruct((count,) + values.sha...]
    pallas_call x7 -> x8, Pallas kernels: 317 us -> 366 us  [comm_call(): pl.pallas_call(body, out_shape=tuple((jax.ShapeDtypeStruct(shape, kind) f...]
    unnamed x38 -> x40, local copies, waits for them, and re-layouts: 16.9 us -> 14.8 us
  transfers between devices with their start and end apart: 8 -> 12, of which waited for: 2 -> 3; matrix products, arithmetic and copies ran while one was open for 3% -> 3% of each run, Pallas kernels for 81% -> 83%
where the time goes in v6:
time: 599 us; the launch traced here: 593 us
  Pallas kernels  496 us (83%)
  waiting for transfers between devices  26.1 us (4%)
  local copies, waits for them, and re-layouts  17 us (3%)
  other arithmetic  15 us (3%)
  between operations  14.9 us (2%)
  blocking collectives  13.5 us (2%)
    pallas_call x8, Pallas kernels, comm_call(): pl.pallas_call(body, out_shape=tuple((jax.ShapeDtypeStruct(shape, kind) f...  366 us
    pallas_call x3, Pallas kernels, gather_seq(): pl.pallas_call(body, out_shape=jax.ShapeDtypeStruct((count,) + values.sha...  110 us
    all_gather x3, waiting for transfers between devices, gather_rows(): return lax.all_gather(values, 'fsdp', axis=0, tiled=True)  24.8 us
    unnamed x40, local copies, waits for them, and re-layouts  14.8 us
    all_gather x1, blocking collectives, on_device(): lax.all_gather(jnp.stack([mixer_gain, channel_gain]), 'fsdp', axis=1, til...  13.5 us
  transfers between devices with their start and end apart: 12, of which 3 were waited for; matrix products, arithmetic and copies ran while one was open for 3% of the time, Pallas kernels for 83%

profile of v6, /device:TPU:0, one launch (start us, length us, event | category | flops | bytes accessed | tf_op | source)
XLA Modules:
  0.0 593.0 jit_solution(9857659861075359253)
XLA Ops:
  7.2 0.0 all-gather.4.cloned.1.call-start
  7.2 1.4 copy-done
  8.7 0.1 dynamic-slice_bitcast_fusion
  8.8 0.1 copy.31
  8.9 0.3 copy.26
  9.3 1.0 dynamic-slice_dynamic-update-slice_fusion.1
  10.2 1.0 dynamic-slice_dynamic-update-slice_fusion
  11.2 1.8 constant_dynamic-slice_fusion
  13.0 0.1 pad_dynamic-update-slice_fusion.1
  13.1 0.1 pad_dynamic-update-slice_fusion
  13.2 0.1 bitcast_dynamic-update-slice_fusion
  13.3 1.2 copy-done.10
  14.6 0.0 all-gather.6.cloned.1.call-start
  14.7 13.5 %all_gather.12 = bf16[2,2048]{1,0:T(2,128)(2,1)S(1)} all-gather(bf16[2,256]{1,0:T(2,128)(2,1)S(1)} %pad_maximum_fusion.2), channel_id=1, replica_groups=mesh['seq'=4,'fsdp'=8] {'fsdp'}, dimensions={1}, use_global_device_ids=true | all-gather | bytes 9216 | tf_op jit(solution)/shard_map/all_gather | solution.py:1905
  28.1 38.0 %gather_seq_0.1 = bf16[4,256,2048]{2,1,0:T(8,128)(2,1)} custom-call(bf16[256,2048]{1,0:T(8,128)(2,1)} %bitcast.34), custom_call_target="tpu_custom_call" | custom-call | bytes 125829120 | tf_op jit(solution)/shard_map/gather_seq_0/pallas_call | solution.py:451
  66.1 36.3 %gather_seq_1.1 = bf16[4,256,2048]{2,1,0:T(8,128)(2,1)} custom-call(bf16[256,2048]{1,0:T(8,128)(2,1)} %bitcast.37), custom_call_target="tpu_custom_call" | custom-call | bytes 125829120 | tf_op jit(solution)/shard_map/gather_seq_1/pallas_call | solution.py:451
  102.5 2.4 fusion.3
  104.9 2.4 fusion.2
  107.3 1.0 pad_maximum_fusion
  108.3 0.3 all-gather.8.cloned.1.call-start
  108.7 0.6 slice_convert_fusion
  109.3 2.2 copy-done.3
  111.5 4.1 norm_and_turn.1
  115.7 2.0 copy-done.2
  117.7 1.9 copy-done.4
  119.7 2.8 fusion.4
  122.5 2.0 dynamic-slice_select_fusion
  124.5 0.4 fusion.1
  124.9 0.4 fusion
  125.2 0.3 maximum_convert_fusion.1
  125.5 0.3 maximum_convert_fusion
  125.9 2.4 exponential_select_fusion.table_ref
  128.3 2.5 exponential_select_fusion.1.table_ref
  130.8 24.8 %all-gather.4.cloned.1.call-done.w_any = bf16[2048,3712]{1,0:T(8,128)(2,1)} async-done(((bf16[256,3712]{1,0:T(8,128)(2,1)}), bf16[2048,3712]{1,0:T(8,128)(2,1)}) %all-gather.4.cloned.1.call-update) | async-done | bytes 15204368 | tf_op jit(solution)/shard_map/all_gather | solution.py:1873
  155.6 33.1 %retention_exchange.1 = (bf16[1024,512]{1,0:T(8,128)(2,1)}, bf16[1024,512]{1,0:T(8,128)(2,1)}, bf16[2,1024,432]{2,1,0:T(8,128)(2,1)}, f32[1024,864]{1,0:T(8,128)...) custom-call(bf16[1024,2048]{1,0:T(8,128)(2,1)} %copy-done.4, ...), custom_call_target="tpu_custom_call" | custom-call | bytes 251658240 | tf_op jit(solution)/shard_map/retention_exchange/pallas_call | solution.py:901
  188.7 0.6 reduce-scatter.6.cloned.1.call-start
  189.3 44.6 %project_and_norm.1 = (f32[256,2048]{1,0:T(8,128)}, bf16[256,2048]{1,0:T(8,128)(2,1)}) custom-call(bf16[1024,864]{1,0:T(8,128)(2,1)} %get-tuple-element.78.g_any.gated_any, bf16[864,2048]{1,0:T(8,128)(2,1)} %get-tuple-element.79.w_any, bf16[256,2048]{1,0:T(8,128)(2,1)} %bitcast.35, f32[1,2048]{1,0:T(1,128)} %get-tuple-element.134.gain_ref), custom_call_target="tpu_custom_call" | custom-call | bytes 125829120 | tf_op jit(solution)/shard_map/project_and_norm/pallas_call | solution.py:901
  233.9 42.6 %feed_forward_gather.1 = (bf16[1024,1792]{1,0:T(8,128)(2,1)}, bf16[1024,896]{1,0:T(8,128)(2,1)}, bf16[896,2048]{1,0:T(8,128)(2,1)}, bf16[4,256,2048]{2,1,0:T(8,128)(2,1)}) custom-call(bf16[256,2048]{1,0:T(8,128)(2,1)} %get-tuple-element.80.x_any, bf16[2048,1792]{1,0:T(8,128)(2,1)} %all-gather.6.cloned.1.call-done.w_any, bf16[1024,2048]{1,0:T(8,128)(2,1)} %bitcast.31), custom_call_target="tpu_custom_call" | custom-call | bytes 125829120 | tf_op jit(solution)/shard_map/feed_forward_gather/pallas_call | solution.py:901
  276.5 0.2 reduce-scatter.8.cloned.1.call-start
  276.8 49.3 %feed_back_scatter.1 = (f32[256,2048]{1,0:T(8,128)}, f32[2048,128]{1,0:T(8,128)}, bf16[256,2048]{1,0:T(8,128)(2,1)}, bf16[1024,1792]{1,0:T(8,128)(2,1)}) custom-call(bf16[1024,2048]{1,0:T(8,128)(2,1)} %bitcast.32, bf16[1024,1792]{1,0:T(8,128)(2,1)} %get-tuple-element.84.both_any, bf16[2048,1792]{1,0:T(8,128)(2,1)} %all-gather.6.cloned.1.call-done.w_any, ...), custom_call_target="tpu_custom_call" | custom-call | bytes 125829120 | tf_op jit(solution)/shard_map/feed_back_scatter/pallas_call | solution.py:901
  326.2 0.3 reduce-scatter.12.cloned.1.call-start
  326.4 35.9 %gather_seq_7.1 = bf16[4,256,2048]{2,1,0:T(8,128)(2,1)} custom-call(bf16[256,2048]{1,0:T(8,128)(2,1)} %get-tuple-element.88.x_ref), custom_call_target="tpu_custom_call" | custom-call | bytes 125829120 | tf_op jit(solution)/shard_map/gather_seq_7/pallas_call | solution.py:451
  362.4 0.0 reduce-scatter.6.cloned.1.call-done.share_any
  362.4 39.1 %gate_back_scatter.1 = (bf16[1024,896]{1,0:T(8,128)(2,1)}, bf16[2,1024,432]{2,1,0:T(8,128)(2,1)}, bf16[1024,896]{1,0:T(8,128)(2,1)}, bf16[2,4,256,896]{3,2,1,0:T(8,128)(2,1)}, f32[256,2048]{1,0:T(8,128)}) custom-call(bf16[1024,2048]{1,0:T(8,128)(2,1)} %bitcast.33, bf16[864,2048]{1,0:T(8,128)(2,1)} %get-tuple-element.79.w_any, ...), custom_call_target="tpu_custom_call" | custom-call | bytes 125829120 | tf_op jit(solution)/shard_map/gate_back_scatter/pallas_call | solution.py:901
  401.6 0.0 reduce-scatter.14.cloned.1.call-start
  401.7 41.5 %retention_back_exchange.1 = (bf16[1024,1024]{1,0:T(8,128)(2,1)}, bf16[1024,896]{1,0:T(8,128)(2,1)}, bf16[1024,1920]{1,0:T(8,128)(2,1)}, bf16[4,112,2048]{2,1,0:T(8,128)(2,1)}) custom-call(bf16[1024,512]{1,0:T(8,128)(2,1)} %get-tuple-element.95.q_any, bf16[1024,512]{1,0:T(8,128)(2,1)} %get-tuple-element.96.k_any, ...), custom_call_target="tpu_custom_call" | custom-call | bytes 110100480 | tf_op jit(solution)/shard_map/retention_back_exchange/pallas_call | solution.py:901
  443.2 0.3 reduce-scatter.10.cloned.1.call-start
  443.5 66.5 %input_backward.1 = (f32[256,2048]{1,0:T(8,128)}, bf16[2048,896]{1,0:T(8,128)(2,1)}, bf16[4,256,1792]{2,1,0:T(8,128)(2,1)}) custom-call(bf16[1024,1024]{1,0:T(8,128)(2,1)} %get-tuple-element.102.dqk_any, bf16[1024,896]{1,0:T(8,128)(2,1)} %get-tuple-element.103.dv_any, bf16[1024,896]{1,0:T(8,128)(2,1)} %get-tuple-element.104.ds_any, ...), custom_call_target="tpu_custom_call" | custom-call | bytes 235929600 | tf_op jit(solution)/shard_map/input_backward/pallas_call | solution.py:901
  510.0 1.5 copy-done.11
  511.5 1.1 convert_bitcast_fusion.1
  512.7 1.1 convert_bitcast_fusion
  513.8 49.5 %gather_two.1 = (bf16[4,256,896]{2,1,0:T(8,128)(2,1)}, bf16[4,256,1920]{2,1,0:T(8,128)(2,1)}) custom-call(bf16[256,896]{1,0:T(8,128)(2,1)} %reduce-scatter.12.cloned.1.call-done.a_ref, bf16[256,1920]{1,0:T(8,128)(2,1)} %reduce-scatter.14.cloned.1.call-done.b_ref), custom_call_target="tpu_custom_call" | custom-call | bytes 173015040 | tf_op jit(solution)/shard_map/gather_two/pallas_call | solution.py:901
  563.3 0.0 reduce-scatter.10.cloned.1.call-done.own_ref
  563.3 0.6 collective-permute-start.1
  563.9 1.5 collective-permute-start
  565.4 3.2 unpack_columns.1
  568.6 2.0 copy-done.6
  570.7 6.2 %unpack_feed.1 = (f32[256,3456]{1,0:T(8,128)}, f32[256,3456]{1,0:T(8,128)}, f32[432,2048]{1,0:T(8,128)}) custom-call(bf16[4,256,1792]{2,1,0:T(8,128)(2,1)S(1)} %copy-done.6, bf16[4,112,2048]{2,1,0:T(8,128)(2,1)S(1)} %copy-done.7), custom_call_target="tpu_custom_call" | custom-call | bytes 7340032 | tf_op jit(solution)/shard_map/unpack_feed/pallas_call | solution.py:1755
  576.9 0.6 collective-permute-start.3
  577.5 1.5 collective-permute-start.2
  579.0 3.5 unpack_merged.1
  582.4 0.5 collective-permute-done.3
  583.0 0.6 collective-permute-done.2
  583.6 2.3 unpack_related.1
  (57 shorter events, 0.5 us)
Async XLA Ops:
  7.2 1.5 copy-start
  7.2 148.4 %all-gather.4.cloned.1.call-start = ((), (), s32[]{:S(2)}) async-start(), calls=%async_computation.5 | async-start | bytes 17104896 | tf_op jit(solution)/shard_map/all_gather | solution.py:1873
  13.1 1.5 copy-start.15
  13.1 1.5 copy-start.16
  13.3 1.3 copy-start.10
  14.6 219.4 %all-gather.6.cloned.1.call-start = ((), (), s32[]{:S(2)}) async-start(), calls=%async_computation.6 | async-start | bytes 8257536 | tf_op jit(solution)/shard_map/all_gather | solution.py:1873
  66.1 36.4 %copy-start.13 = (bf16[256,3456]{1,0:T(8,128)(2,1)S(1)}, bf16[256,3456]{1,0:T(8,128)(2,1)}, u32[]{:S(2)}) copy-start(bf16[256,3456]{1,0:T(8,128)(2,1)} %param.21) | copy-start | bytes 5308420
  102.5 2.4 copy-start.14
  108.3 168.5 %all-gather.8.cloned.1.call-start = ((), (), s32[]{:S(2)}) async-start(), calls=%async_computation.7 | async-start | bytes 4128768 | tf_op jit(solution)/shard_map/all_gather | solution.py:1873
  109.3 6.4 %copy-start.9 = (f32[1,2048]{1,0:T(1,128)}, f32[1,2048]{1,0:T(1,128)S(1)}, u32[]{:S(2)}) copy-start(f32[1,2048]{1,0:T(1,128)S(1)} %get-tuple-element.135.gain_ref) | copy-start | bytes 24580
  109.3 2.2 copy-start.3
  115.7 2.0 copy-start.2
  117.7 1.9 copy-start.4
  188.7 173.7 %reduce-scatter.6.cloned.1.call-start = ((), (), s32[]{:S(2)}) async-start(), calls=%async_computation.8 | async-start | bytes 4128768 | tf_op jit(solution)/shard_map/reduce_scatter | solution.py:1876
  276.5 125.1 %reduce-scatter.8.cloned.1.call-start = ((), (), s32[]{:S(2)}) async-start(), calls=%async_computation.9 | async-start | bytes 4587520 | tf_op jit(solution)/shard_map/reduce_scatter | solution.py:1880
  326.2 187.6 %reduce-scatter.12.cloned.1.call-start = ((), (), s32[]{:S(2)}) async-start(), calls=%async_computation.11 | async-start | bytes 2293760 | tf_op jit(solution)/shard_map/reduce_scatter | solution.py:1880
  401.6 112.2 %reduce-scatter.14.cloned.1.call-start = ((), (), s32[]{:S(2)}) async-start(), calls=%async_computation.12 | async-start | bytes 4915200 | tf_op jit(solution)/shard_map/reduce_scatter | solution.py:1880
  443.2 120.1 %reduce-scatter.10.cloned.1.call-start = ((), (), s32[]{:S(2)}) async-start(), calls=%async_computation.10 | async-start | bytes 4128768 | tf_op jit(solution)/shard_map/reduce_scatter | solution.py:1876
  509.9 1.6 copy-start.11
  510.0 2.7 copy-start.12
  513.8 54.8 %copy-start.7 = (bf16[4,112,2048]{2,1,0:T(8,128)(2,1)S(1)}, bf16[4,112,2048]{2,1,0:T(8,128)(2,1)}, u32[]{:S(2)}) copy-start(bf16[4,112,2048]{2,1,0:T(8,128)(2,1)} %get-tuple-element.115.down_ref) | copy-start | bytes 5505028
  563.3 13.5 %collective-permute-start.1 = (bf16[256,896]{1,0:T(8,128)(2,1)}, bf16[256,896]{1,0:T(8,128)(2,1)S(1)}, u32[]{:S(2)}, u32[]{:S(2)}) collective-permute-start(bf16[256,896]{1,0:T(8,128)(2,1)} %reduce-scatter.10.cloned.1.call-done.own_ref), channel_id=1, source_target_pairs={{0,16},{8,24},{16,0},{24,8},{1,17},{9,25},{17,1},{25,9},{2,18},{10... | collective-permute-start | bytes 1376264 | tf_op jit(solution)/shard_map/ppermute | solution.py:1725
  563.9 12.9 %collective-permute-start = (bf16[256,896]{1,0:T(8,128)(2,1)}, bf16[256,896]{1,0:T(8,128)(2,1)S(1)}, u32[]{:S(2)}, u32[]{:S(2)}) collective-permute-start(bf16[256,896]{1,0:T(8,128)(2,1)} %reduce-scatter.10.cloned.1.call-done.own_ref), channel_id=1, source_target_pairs={{0,8},{8,0},{16,24},{24,16},{1,9},{9,1},{17,25},{25,17},{2,10},{10... | collective-permute-start | bytes 1376264 | tf_op jit(solution)/shard_map/ppermute | solution.py:1725
  568.6 2.0 copy-start.6
  570.7 8.3 %copy-start.5 = (bf16[4,256,1920]{2,1,0:T(8,128)(2,1)S(1)}, bf16[4,256,1920]{2,1,0:T(8,128)(2,1)}, u32[]{:S(2)}) copy-start(bf16[4,256,1920]{2,1,0:T(8,128)(2,1)} %get-tuple-element.120.in_ref) | copy-start | bytes 11796484
  576.9 6.1 %collective-permute-start.3 = (bf16[128,896]{1,0:T(8,128)(2,1)S(1)}, bf16[128,896]{1,0:T(8,128)(2,1)S(1)}, u32[]{:S(2)}, u32[]{:S(2)}) collective-permute-start(bf16[128,896]{1,0:T(8,128)(2,1)S(1)} %slice.15), channel_id=1, source_target_pairs={{0,8},{8,0},{16,24},{24,16},{1,9},{9,1},{17,25},{25,17},{2,10},{10... | collective-permute-start | bytes 688136 | tf_op jit(solution)/shard_map/ppermute | solution.py:1725
  577.5 6.0 %collective-permute-start.2 = (bf16[128,896]{1,0:T(8,128)(2,1)S(1)}, bf16[128,896]{1,0:T(8,128)(2,1)S(1)}, u32[]{:S(2)}, u32[]{:S(2)}) collective-permute-start(bf16[128,896]{1,0:T(8,128)(2,1)S(1)} %slice.14), channel_id=1, source_target_pairs={{0,16},{8,24},{16,0},{24,8},{1,17},{9,25},{17,1},{25,9},{2,18},{10... | collective-permute-start | bytes 688136 | tf_op jit(solution)/shard_map/ppermute | solution.py:1725
  579.0 4.6 copy-start.8
  579.0 6.9 %copy-start.1 = (bf16[432,2048]{1,0:T(8,128)(2,1)S(1)}, bf16[432,2048]{1,0:T(8,128)(2,1)}, u32[]{:S(2)}) copy-start(bf16[432,2048]{1,0:T(8,128)(2,1)} %param.18) | copy-start | bytes 5308420
Sparse Core Ops, SparseCore 0:
  14.7 140.8 all-gather.3
  157.8 71.6 all-gather.5
  231.7 41.2 all-gather.7
  276.7 42.3 reduce-scatter.5
  326.3 65.7 reduce-scatter.7
  401.7 37.1 reduce-scatter.11
  443.3 70.0 reduce-scatter.13
  515.6 45.3 reduce-scatter.9

commit v7 on v6

--- a/solution.py
+++ b/solution.py
@@ -1831,6 +1831,74 @@
             if self.skip(k) < self.width:
                 kept.append(lax.slice_in_dim(piece, self.skip(k), self.width, axis=axis))
         return jnp.concatenate(kept, axis=axis)
+
+
+def pack_kernel(
+    cut, qk, vd, padded, q_any, k_any, v_any, s_any, o_any, out_any,
+    qk_ref, v_ref, s_ref, o_ref, values_ref, tiles_ref, sems,
+):
+    me = lax.axis_index("seq")
+    moves = Moves(sems)
+    total, wide = v_any.shape[1], v_ref.shape[1]
+    base = jnp.minimum((me * vd) // 128 * 128, total - wide)
+    window = pl.ds(pl.multiple_of(base, 128), wide)
+    loads = [
+        moves.start(v_any.at[:, window], v_ref),
+        moves.start(s_any.at[:, window], s_ref),
+        moves.start(o_any.at[pl.ds(pl.multiple_of(cut.start(me), 16), cut.width)], o_ref),
+    ]
+    own = pl.ds(pl.multiple_of(me * qk, 128), qk)
+    loads += [
+        moves.start(q_any.at[:, own], qk_ref.at[:, slice(0, qk)]),
+        moves.start(k_any.at[:, own], qk_ref.at[:, slice(qk, 2 * qk)]),
+    ]
+    tile, lane = 16, 128
+    loads[2].wait()
+    for r in range(cut.width // tile):
+        for c in range(o_ref.shape[1] // lane):
+            tiles_ref[c * tile : (c + 1) * tile, head_lanes(r, lane)] = o_ref[
+                r * tile : (r + 1) * tile, head_lanes(c, lane)
+            ]
+    at = 2 * qk + 2 * padded
+    moves.store(tiles_ref, out_any.at[:, slice(at, at + tiles_ref.shape[1])])
+    loads[0].wait()
+    loads[1].wait()
+    for k in range(4):
+        shift = k * vd - min(k * vd // 128 * 128, total - wide)
+
+        @pl.when(me == k)
+        def _():
+            for n, ref in enumerate((v_ref, s_ref)):
+                values_ref[:, head_lanes(n, padded)] = pad_lanes([ref[:, shift : shift + vd]], padded)
+
+    moves.store(values_ref, out_any.at[:, slice(2 * qk, at)])
+    loads[3].wait()
+    loads[4].wait()
+    moves.store(qk_ref, out_any.at[:, slice(0, 2 * qk)])
+    moves.close()
+
+
+def pack(query, key, value, swish, output, cut, qk, vd, padded):
+    rows, width = query.shape
+    wide = min(padded + 128, value.shape[1])
+    tiles = cut.width * width // rows
+    return pl.pallas_call(
+        functools.partial(pack_kernel, cut, qk, vd, padded),
+        out_shape=jax.ShapeDtypeStruct((rows, 2 * qk + 2 * padded + tiles), BF),
+        in_specs=[ANYWHERE] * 5,
+        out_specs=ANYWHERE,
+        scratch_shapes=[
+            pltpu.VMEM((rows, 2 * qk), BF),
+            pltpu.VMEM((rows, wide), BF),
+            pltpu.VMEM((rows, wide), BF),
+            pltpu.VMEM((cut.width, width), BF),
+            pltpu.VMEM((rows, 2 * padded), BF),
+            pltpu.VMEM((rows, tiles), BF),
+            pltpu.SemaphoreType.DMA((8,)),
+        ],
+        compiler_params=pltpu.CompilerParams(vmem_limit_bytes=60 * 1024 * 1024),
+        name="pack",
+    )(query, key, value, swish, output)
 
 
 def columns_of(weight, index, width, padded):
@@ -1881,19 +1949,24 @@
             values, "fsdp", scatter_dimension=0, tiled=True, axis_index_groups=groups
         )
 
-    output_piece = lax.dynamic_slice_in_dim(output_weight, cut.start(me), cut.width, axis=0)
-    attention_pieces = [
-        columns_of(query_weight, me, qk, qk),
-        columns_of(key_weight, me, qk, qk),
-        columns_of(value_weight, me, vd, vd_pad),
-        columns_of(swish_weight, me, vd, vd_pad),
-    ]
     if square:
-        tiles = output_piece.reshape(cut.width // 16, 16, width // 128, 128)
-        attention_pieces.append(tiles.transpose(2, 1, 0, 3).reshape(width // 8, cut.width * 8))
+        attention_piece = pack(
+            query_weight, key_weight, value_weight, swish_weight, output_weight, cut, qk, vd, vd_pad
+        )
     else:
-        output_pieces = gather_rows(output_piece)
-    attention_weight = gather_rows(jnp.concatenate(attention_pieces, axis=1))
+        output_pieces = gather_rows(
+            lax.dynamic_slice_in_dim(output_weight, cut.start(me), cut.width, axis=0)
+        )
+        attention_piece = jnp.concatenate(
+            [
+                columns_of(query_weight, me, qk, qk),
+                columns_of(key_weight, me, qk, qk),
+                columns_of(value_weight, me, vd, vd_pad),
+                columns_of(swish_weight, me, vd, vd_pad),
+            ],
+            axis=1,
+        )
+    attention_weight = gather_rows(attention_piece)
     column = lax.broadcasted_iota(jnp.int32, (hidden_units, ff), 0)
     slot = lax.broadcasted_iota(jnp.int32, (hidden_units, ff), 1)
     chosen = (slot // cut.width) * own_rows + cut.start(me) + slot % cut.width

time: 599 us -> 594 us (level)
  local copies, waits for them, and re-layouts: 17 us -> 9.85 us
    unnamed x40 -> x30, local copies, waits for them, and re-layouts: 14.8 us -> 9.8 us
  transfers between devices with their start and end apart: 12 -> 12, of which waited for: 3 -> 3; matrix products, arithmetic and copies ran while one was open for 3% -> 3% of each run, Pallas kernels for 83% -> 84%
where the time goes in v7:
time: 594 us; the launch traced here: 589 us
  Pallas kernels  499 us (84%)
  waiting for transfers between devices  26.1 us (4%)
  other arithmetic  15 us (3%)
  between operations  14.8 us (2%)
  blocking collectives  13.5 us (2%)
  local copies, waits for them, and re-layouts  9.85 us (2%)
  starting transfers between devices  5.97 us (1%)
    pallas_call x8, Pallas kernels, comm_call(): pl.pallas_call(body, out_shape=tuple((jax.ShapeDtypeStruct(shape, kind) f...  366 us
    pallas_call x3, Pallas kernels, gather_seq(): pl.pallas_call(body, out_shape=jax.ShapeDtypeStruct((count,) + values.sha...  110 us
    all_gather x3, waiting for transfers between devices, gather_rows(): return lax.all_gather(values, 'fsdp', axis=0, tiled=True)  24.8 us
    all_gather x1, blocking collectives, on_device(): lax.all_gather(jnp.stack([mixer_gain, channel_gain]), 'fsdp', axis=1, til...  13.5 us
  transfers between devices with their start and end apart: 12, of which 3 were waited for; matrix products, arithmetic and copies ran while one was open for 3% of the time, Pallas kernels for 84%

profile of v7, /device:TPU:0, one launch (start us, length us, event | category | flops | bytes accessed | tf_op | source)
XLA Modules:
  0.0 588.7 jit_solution(16174502634254046287)
XLA Ops:
  7.2 0.0 all-gather.4.cloned.1.call-start
  7.3 2.9 pack.1
  10.1 0.0 all-gather.4.cloned.1.call-update
  10.2 0.0 all-gather.6.cloned.1.call-start
  10.3 13.5 %all_gather.12 = bf16[2,2048]{1,0:T(2,128)(2,1)S(1)} all-gather(bf16[2,256]{1,0:T(2,128)(2,1)S(1)} %pad_maximum_fusion.2), channel_id=1, replica_groups=mesh['seq'=4,'fsdp'=8] {'fsdp'}, dimensions={1}, use_global_device_ids=true | all-gather | bytes 9216 | tf_op jit(solution)/shard_map/all_gather | solution.py:1978
  23.7 38.2 %gather_seq_0.1 = bf16[4,256,2048]{2,1,0:T(8,128)(2,1)} custom-call(bf16[256,2048]{1,0:T(8,128)(2,1)} %bitcast.22), custom_call_target="tpu_custom_call" | custom-call | bytes 125829120 | tf_op jit(solution)/shard_map/gather_seq_0/pallas_call | solution.py:451
  61.9 36.3 %gather_seq_1.1 = bf16[4,256,2048]{2,1,0:T(8,128)(2,1)} custom-call(bf16[256,2048]{1,0:T(8,128)(2,1)} %bitcast.25), custom_call_target="tpu_custom_call" | custom-call | bytes 125829120 | tf_op jit(solution)/shard_map/gather_seq_1/pallas_call | solution.py:451
  98.3 2.4 fusion.3
  100.7 2.4 fusion.2
  103.1 1.0 pad_maximum_fusion
  104.2 0.3 all-gather.8.cloned.1.call-start
  104.5 0.6 slice_convert_fusion
  105.1 2.2 copy-done.3
  107.3 4.1 norm_and_turn.1
  111.5 2.0 copy-done.2
  113.5 1.9 copy-done.4
  115.5 2.8 fusion.4
  118.3 2.0 dynamic-slice_select_fusion
  120.3 0.4 fusion.1
  120.7 0.4 fusion
  121.1 0.3 maximum_convert_fusion.1
  121.4 0.3 maximum_convert_fusion
  121.7 2.5 exponential_select_fusion.table_ref
  124.1 2.5 exponential_select_fusion.1.table_ref
  126.6 24.8 %all-gather.4.cloned.1.call-done.w_any = bf16[2048,3712]{1,0:T(8,128)(2,1)} async-done(((bf16[256,3712]{1,0:T(8,128)(2,1)}), bf16[2048,3712]{1,0:T(8,128)(2,1)}) %all-gather.4.cloned.1.call-update) | async-done | bytes 15204368 | tf_op jit(solution)/shard_map/all_gather | solution.py:1941
  151.4 33.1 %retention_exchange.1 = (bf16[1024,512]{1,0:T(8,128)(2,1)}, bf16[1024,512]{1,0:T(8,128)(2,1)}, bf16[2,1024,432]{2,1,0:T(8,128)(2,1)}, f32[1024,864]{1,0:T(8,128)...) custom-call(bf16[1024,2048]{1,0:T(8,128)(2,1)} %copy-done.4, ...), custom_call_target="tpu_custom_call" | custom-call | bytes 251658240 | tf_op jit(solution)/shard_map/retention_exchange/pallas_call | solution.py:901
  184.5 0.0 all-gather.8.cloned.1.call-update
  184.5 0.6 reduce-scatter.6.cloned.1.call-start
  185.1 44.6 %project_and_norm.1 = (f32[256,2048]{1,0:T(8,128)}, bf16[256,2048]{1,0:T(8,128)(2,1)}) custom-call(bf16[1024,864]{1,0:T(8,128)(2,1)} %get-tuple-element.78.g_any.gated_any, bf16[864,2048]{1,0:T(8,128)(2,1)} %get-tuple-element.79.w_any, bf16[256,2048]{1,0:T(8,128)(2,1)} %bitcast.23, f32[1,2048]{1,0:T(1,128)} %get-tuple-element.134.gain_ref), custom_call_target="tpu_custom_call" | custom-call | bytes 125829120 | tf_op jit(solution)/shard_map/project_and_norm/pallas_call | solution.py:901
  229.6 0.0 all-gather.6.cloned.1.call-done.w_any
  229.7 42.6 %feed_forward_gather.1 = (bf16[1024,1792]{1,0:T(8,128)(2,1)}, bf16[1024,896]{1,0:T(8,128)(2,1)}, bf16[896,2048]{1,0:T(8,128)(2,1)}, bf16[4,256,2048]{2,1,0:T(8,128)(2,1)}) custom-call(bf16[256,2048]{1,0:T(8,128)(2,1)} %get-tuple-element.80.x_any, bf16[2048,1792]{1,0:T(8,128)(2,1)} %all-gather.6.cloned.1.call-done.w_any, bf16[1024,2048]{1,0:T(8,128)(2,1)} %bitcast.19), custom_call_target="tpu_custom_call" | custom-call | bytes 125829120 | tf_op jit(solution)/shard_map/feed_forward_gather/pallas_call | solution.py:901
  272.2 0.0 reduce-scatter.6.cloned.1.call-update
  272.3 0.2 reduce-scatter.8.cloned.1.call-start
  272.5 0.0 all-gather.8.cloned.1.call-done.down_any
  272.5 49.3 %feed_back_scatter.1 = (f32[256,2048]{1,0:T(8,128)}, f32[2048,128]{1,0:T(8,128)}, bf16[256,2048]{1,0:T(8,128)(2,1)}, bf16[1024,1792]{1,0:T(8,128)(2,1)}) custom-call(bf16[1024,2048]{1,0:T(8,128)(2,1)} %bitcast.20, bf16[1024,1792]{1,0:T(8,128)(2,1)} %get-tuple-element.84.both_any, bf16[2048,1792]{1,0:T(8,128)(2,1)} %all-gather.6.cloned.1.call-done.w_any, ...), custom_call_target="tpu_custom_call" | custom-call | bytes 125829120 | tf_op jit(solution)/shard_map/feed_back_scatter/pallas_call | solution.py:901
  321.9 0.0 reduce-scatter.8.cloned.1.call-update
  321.9 0.3 reduce-scatter.12.cloned.1.call-start
  322.2 35.9 %gather_seq_7.1 = bf16[4,256,2048]{2,1,0:T(8,128)(2,1)} custom-call(bf16[256,2048]{1,0:T(8,128)(2,1)} %get-tuple-element.88.x_ref), custom_call_target="tpu_custom_call" | custom-call | bytes 125829120 | tf_op jit(solution)/shard_map/gather_seq_7/pallas_call | solution.py:451
  358.1 0.0 reduce-scatter.6.cloned.1.call-done.share_any
  358.1 39.2 %gate_back_scatter.1 = (bf16[1024,896]{1,0:T(8,128)(2,1)}, bf16[2,1024,432]{2,1,0:T(8,128)(2,1)}, bf16[1024,896]{1,0:T(8,128)(2,1)}, bf16[2,4,256,896]{3,2,1,0:T(8,128)(2,1)}, f32[256,2048]{1,0:T(8,128)}) custom-call(bf16[1024,2048]{1,0:T(8,128)(2,1)} %bitcast.21, bf16[864,2048]{1,0:T(8,128)(2,1)} %get-tuple-element.79.w_any, ...), custom_call_target="tpu_custom_call" | custom-call | bytes 125829120 | tf_op jit(solution)/shard_map/gate_back_scatter/pallas_call | solution.py:901
  397.3 0.0 reduce-scatter.12.cloned.1.call-update
  397.3 0.0 reduce-scatter.14.cloned.1.call-start
  397.3 0.0 reduce-scatter.8.cloned.1.call-done.share_any
  397.4 41.5 %retention_back_exchange.1 = (bf16[1024,1024]{1,0:T(8,128)(2,1)}, bf16[1024,896]{1,0:T(8,128)(2,1)}, bf16[1024,1920]{1,0:T(8,128)(2,1)}, bf16[4,112,2048]{2,1,0:T(8,128)(2,1)}) custom-call(bf16[1024,512]{1,0:T(8,128)(2,1)} %get-tuple-element.95.q_any, bf16[1024,512]{1,0:T(8,128)(2,1)} %get-tuple-element.96.k_any, ...), custom_call_target="tpu_custom_call" | custom-call | bytes 110100480 | tf_op jit(solution)/shard_map/retention_back_exchange/pallas_call | solution.py:901
  438.9 0.0 reduce-scatter.14.cloned.1.call-update
  438.9 0.3 reduce-scatter.10.cloned.1.call-start
  439.2 66.5 %input_backward.1 = (f32[256,2048]{1,0:T(8,128)}, bf16[2048,896]{1,0:T(8,128)(2,1)}, bf16[4,256,1792]{2,1,0:T(8,128)(2,1)}) custom-call(bf16[1024,1024]{1,0:T(8,128)(2,1)} %get-tuple-element.102.dqk_any, bf16[1024,896]{1,0:T(8,128)(2,1)} %get-tuple-element.103.dv_any, bf16[1024,896]{1,0:T(8,128)(2,1)} %get-tuple-element.104.ds_any, ...), custom_call_target="tpu_custom_call" | custom-call | bytes 235929600 | tf_op jit(solution)/shard_map/input_backward/pallas_call | solution.py:901
  505.7 0.0 reduce-scatter.10.cloned.1.call-update
  505.7 1.5 copy-done.10
  507.3 1.1 convert_bitcast_fusion.1
  508.4 1.1 convert_bitcast_fusion
  509.5 49.5 %gather_two.1 = (bf16[4,256,896]{2,1,0:T(8,128)(2,1)}, bf16[4,256,1920]{2,1,0:T(8,128)(2,1)}) custom-call(bf16[256,896]{1,0:T(8,128)(2,1)} %reduce-scatter.12.cloned.1.call-done.a_ref, bf16[256,1920]{1,0:T(8,128)(2,1)} %reduce-scatter.14.cloned.1.call-done.b_ref), custom_call_target="tpu_custom_call" | custom-call | bytes 173015040 | tf_op jit(solution)/shard_map/gather_two/pallas_call | solution.py:901
  559.0 0.0 reduce-scatter.10.cloned.1.call-done.own_ref
  559.0 0.6 collective-permute-start.1
  559.7 1.5 collective-permute-start
  561.1 3.2 unpack_columns.1
  564.4 2.0 copy-done.6
  566.4 6.2 %unpack_feed.1 = (f32[256,3456]{1,0:T(8,128)}, f32[256,3456]{1,0:T(8,128)}, f32[432,2048]{1,0:T(8,128)}) custom-call(bf16[4,256,1792]{2,1,0:T(8,128)(2,1)S(1)} %copy-done.6, bf16[4,112,2048]{2,1,0:T(8,128)(2,1)S(1)} %copy-done.7), custom_call_target="tpu_custom_call" | custom-call | bytes 7340032 | tf_op jit(solution)/shard_map/unpack_feed/pallas_call | solution.py:1755
  572.6 0.6 collective-permute-start.3
  573.3 1.5 collective-permute-start.2
  574.7 3.5 unpack_merged.1
  578.2 0.5 collective-permute-done.3
  578.7 0.5 collective-permute-done.2
  579.3 2.3 unpack_related.1
  (44 shorter events, 0.2 us)
Async XLA Ops:
  7.2 91.1 %copy-start = (bf16[256,3456]{1,0:T(8,128)(2,1)S(1)}, bf16[256,3456]{1,0:T(8,128)(2,1)}, u32[]{:S(2)}) copy-start(bf16[256,3456]{1,0:T(8,128)(2,1)} %param.21) | copy-start | bytes 5308420
  7.2 3.0 copy-start.13
  7.2 3.0 copy-start.14
  7.2 144.2 %all-gather.4.cloned.1.call-start = ((), (), s32[]{:S(2)}) async-start(), calls=%async_computation.5 | async-start | bytes 17104896 | tf_op jit(solution)/shard_map/all_gather | solution.py:1941
  10.2 219.5 %all-gather.6.cloned.1.call-start = ((), (), s32[]{:S(2)}) async-start(), calls=%async_computation.6 | async-start | bytes 8257536 | tf_op jit(solution)/shard_map/all_gather | solution.py:1941
  98.3 2.4 copy-start.12
  104.2 168.4 %all-gather.8.cloned.1.call-start = ((), (), s32[]{:S(2)}) async-start(), calls=%async_computation.7 | async-start | bytes 4128768 | tf_op jit(solution)/shard_map/all_gather | solution.py:1941
  105.1 15.2 %copy-start.9 = (f32[1,2048]{1,0:T(1,128)}, f32[1,2048]{1,0:T(1,128)S(1)}, u32[]{:S(2)}) copy-start(f32[1,2048]{1,0:T(1,128)S(1)} %get-tuple-element.135.gain_ref) | copy-start | bytes 24580
  105.1 2.2 copy-start.3
  111.5 2.0 copy-start.2
  113.5 1.9 copy-start.4
  184.5 173.6 %reduce-scatter.6.cloned.1.call-start = ((), (), s32[]{:S(2)}) async-start(), calls=%async_computation.8 | async-start | bytes 4128768 | tf_op jit(solution)/shard_map/reduce_scatter | solution.py:1944
  272.3 125.1 %reduce-scatter.8.cloned.1.call-start = ((), (), s32[]{:S(2)}) async-start(), calls=%async_computation.9 | async-start | bytes 4587520 | tf_op jit(solution)/shard_map/reduce_scatter | solution.py:1948
  321.9 187.6 %reduce-scatter.12.cloned.1.call-start = ((), (), s32[]{:S(2)}) async-start(), calls=%async_computation.11 | async-start | bytes 2293760 | tf_op jit(solution)/shard_map/reduce_scatter | solution.py:1948
  397.3 112.2 %reduce-scatter.14.cloned.1.call-start = ((), (), s32[]{:S(2)}) async-start(), calls=%async_computation.12 | async-start | bytes 4915200 | tf_op jit(solution)/shard_map/reduce_scatter | solution.py:1948
  438.9 120.1 %reduce-scatter.10.cloned.1.call-start = ((), (), s32[]{:S(2)}) async-start(), calls=%async_computation.10 | async-start | bytes 4128768 | tf_op jit(solution)/shard_map/reduce_scatter | solution.py:1944
  505.7 1.6 copy-start.10
  505.7 2.7 copy-start.11
  508.4 56.0 %copy-start.7 = (bf16[4,112,2048]{2,1,0:T(8,128)(2,1)S(1)}, bf16[4,112,2048]{2,1,0:T(8,128)(2,1)}, u32[]{:S(2)}) copy-start(bf16[4,112,2048]{2,1,0:T(8,128)(2,1)} %get-tuple-element.115.down_ref) | copy-start | bytes 5505028
  559.0 13.5 %collective-permute-start.1 = (bf16[256,896]{1,0:T(8,128)(2,1)}, bf16[256,896]{1,0:T(8,128)(2,1)S(1)}, u32[]{:S(2)}, u32[]{:S(2)}) collective-permute-start(bf16[256,896]{1,0:T(8,128)(2,1)} %reduce-scatter.10.cloned.1.call-done.own_ref), channel_id=1, source_target_pairs={{0,16},{8,24},{16,0},{24,8},{1,17},{9,25},{17,1},{25,9},{2,18},{10... | collective-permute-start | bytes 1376264 | tf_op jit(solution)/shard_map/ppermute | solution.py:1725
  559.7 12.9 %collective-permute-start = (bf16[256,896]{1,0:T(8,128)(2,1)}, bf16[256,896]{1,0:T(8,128)(2,1)S(1)}, u32[]{:S(2)}, u32[]{:S(2)}) collective-permute-start(bf16[256,896]{1,0:T(8,128)(2,1)} %reduce-scatter.10.cloned.1.call-done.own_ref), channel_id=1, source_target_pairs={{0,8},{8,0},{16,24},{24,16},{1,9},{9,1},{17,25},{25,17},{2,10},{10... | collective-permute-start | bytes 1376264 | tf_op jit(solution)/shard_map/ppermute | solution.py:1725
  564.4 2.0 copy-start.6
  566.4 8.3 %copy-start.5 = (bf16[4,256,1920]{2,1,0:T(8,128)(2,1)S(1)}, bf16[4,256,1920]{2,1,0:T(8,128)(2,1)}, u32[]{:S(2)}) copy-start(bf16[4,256,1920]{2,1,0:T(8,128)(2,1)} %get-tuple-element.120.in_ref) | copy-start | bytes 11796484
  572.6 6.7 %copy-start.8 = (bf16[256,896]{1,0:T(8,128)(2,1)S(1)}, bf16[256,896]{1,0:T(8,128)(2,1)}, u32[]{:S(2)}) copy-start(bf16[256,896]{1,0:T(8,128)(2,1)} %reduce-scatter.10.cloned.1.call-done.own_ref) | copy-start | bytes 1376260
  572.6 6.1 %collective-permute-start.3 = (bf16[128,896]{1,0:T(8,128)(2,1)S(1)}, bf16[128,896]{1,0:T(8,128)(2,1)S(1)}, u32[]{:S(2)}, u32[]{:S(2)}) collective-permute-start(bf16[128,896]{1,0:T(8,128)(2,1)S(1)} %slice.15), channel_id=1, source_target_pairs={{0,8},{8,0},{16,24},{24,16},{1,9},{9,1},{17,25},{25,17},{2,10},{10... | collective-permute-start | bytes 688136 | tf_op jit(solution)/shard_map/ppermute | solution.py:1725
  573.3 6.0 %collective-permute-start.2 = (bf16[128,896]{1,0:T(8,128)(2,1)S(1)}, bf16[128,896]{1,0:T(8,128)(2,1)S(1)}, u32[]{:S(2)}, u32[]{:S(2)}) collective-permute-start(bf16[128,896]{1,0:T(8,128)(2,1)S(1)} %slice.14), channel_id=1, source_target_pairs={{0,16},{8,24},{16,0},{24,8},{1,17},{9,25},{17,1},{25,9},{2,18},{10... | collective-permute-start | bytes 688136 | tf_op jit(solution)/shard_map/ppermute | solution.py:1725
  574.7 6.9 %copy-start.1 = (bf16[256,3456]{1,0:T(8,128)(2,1)S(1)}, bf16[256,3456]{1,0:T(8,128)(2,1)}, u32[]{:S(2)}) copy-start(bf16[256,3456]{1,0:T(8,128)(2,1)} %param.21) | copy-start | bytes 5308420
Sparse Core Ops, SparseCore 0:
  10.3 141.0 all-gather.3
  153.6 71.6 all-gather.5
  227.5 41.1 all-gather.7
  272.4 42.3 reduce-scatter.5
  322.0 65.7 reduce-scatter.7
  397.4 37.1 reduce-scatter.11
  439.0 70.0 reduce-scatter.13
  511.4 45.3 reduce-scatter.9

commit v8 on v7

--- a/solution.py
+++ b/solution.py
@@ -1686,18 +1686,20 @@
     return out, gain[0]
 
 
+def in_order(pieces):
+    me = lax.axis_index("seq")
+    low = [jnp.where(me % 2 == k, pieces[0], pieces[1]) for k in range(2)]
+    high = [jnp.where(me % 2 == k, pieces[2], pieces[3]) for k in range(2)]
+    order = [jnp.where(me < 2, low[k], high[k]) for k in range(2)]
+    return order + [jnp.where(me < 2, high[k], low[k]) for k in range(2)]
+
+
 def unpack_related_kernel(width, own_ref, across_ref, along_ref, corner_ref, out_ref, gain_ref):
-    me = lax.axis_index("seq")
     pieces = [ref[...].astype(F32) for ref in (own_ref, across_ref, along_ref, corner_ref)]
     last = own_ref.shape[1] - 128
     tile = sum(piece[:, last:] for piece in pieces)
     gain_ref[...] = tile.T[width - last : width - last + 1, :]
-    pieces = [piece[:, :width] for piece in pieces]
-    low = [jnp.where(me % 2 == k, pieces[0], pieces[1]) for k in range(2)]
-    high = [jnp.where(me % 2 == k, pieces[2], pieces[3]) for k in range(2)]
-    order = [jnp.where(me < 2, low[k], high[k]) for k in range(2)]
-    order += [jnp.where(me < 2, high[k], low[k]) for k in range(2)]
-    out_ref[...] = join(order)
+    out_ref[...] = join(in_order([piece[:, :width] for piece in pieces]))
 
 
 def unpack_related(pieces, width):
@@ -1716,6 +1718,9 @@
             jax.ShapeDtypeStruct((1, rows), F32),
         ],
         compiler_params=pltpu.CompilerParams(vmem_limit_bytes=40 * 1024 * 1024),
+        cost_estimate=pl.CostEstimate(
+            flops=0, bytes_accessed=pieces[0].size * 16, transcendentals=0
+        ),
         name="unpack_related",
     )(*pieces)
     return out, gain[0]
@@ -1775,34 +1780,47 @@
     )(gathered, down)
 
 
-def unpack_merged_kernel(cut, in_ref, query_ref, key_ref, out_ref):
-    tile, lane, count = 16, 128, in_ref.shape[0]
+def unpack_merged_kernel(
+    cut, own_ref, across_ref, along_ref, corner_ref, query_ref, key_ref, out_ref, ordered
+):
+    tile, lane, count = 16, 128, 4
     wide = query_ref.shape[1] // count
+    rows = own_ref.shape[0] // 4
+
+    @pl.loop(0, 4)
+    def _(i):
+        here = pl.ds(pl.multiple_of(i * rows, rows), rows)
+        refs = (own_ref, across_ref, along_ref, corner_ref)
+        for k, piece in enumerate(in_order([ref[here, :] for ref in refs])):
+            query_ref[here, head_lanes(k, wide)] = piece[:, :wide].astype(F32)
+            key_ref[here, head_lanes(k, wide)] = piece[:, wide : 2 * wide].astype(F32)
+            ordered[k, here, :] = piece[:, 2 * wide :]
+
     for k in range(count):
-        query_ref[:, head_lanes(k, wide)] = in_ref[k, :, :wide].astype(F32)
-        key_ref[:, head_lanes(k, wide)] = in_ref[k, :, wide : 2 * wide].astype(F32)
         for r in range(cut.skip(k) // tile, cut.width // tile):
             at = cut.start(k) + r * tile
-            lanes = slice(2 * wide + r * lane, 2 * wide + (r + 1) * lane)
             for c in range(out_ref.shape[1] // lane):
-                out_ref[at : at + tile, head_lanes(c, lane)] = in_ref[
-                    k, c * tile : (c + 1) * tile, lanes
+                out_ref[at : at + tile, head_lanes(c, lane)] = ordered[
+                    k, c * tile : (c + 1) * tile, head_lanes(r, lane)
                 ].astype(F32)
 
 
-def unpack_merged(gathered, wide, cut, width):
-    count, rows, _ = gathered.shape
+def unpack_merged(pieces, wide, cut, width):
+    rows, whole = pieces[0].shape
     return pl.pallas_call(
         functools.partial(unpack_merged_kernel, cut),
         out_shape=(
-            jax.ShapeDtypeStruct((rows, count * wide), F32),
-            jax.ShapeDtypeStruct((rows, count * wide), F32),
+            jax.ShapeDtypeStruct((rows, 4 * wide), F32),
+            jax.ShapeDtypeStruct((rows, 4 * wide), F32),
             jax.ShapeDtypeStruct((cut.rows, width), F32),
         ),
+        scratch_shapes=[pltpu.VMEM((4, rows, whole - 2 * wide), BF)],
         compiler_params=pltpu.CompilerParams(vmem_limit_bytes=40 * 1024 * 1024),
-        cost_estimate=pl.CostEstimate(flops=0, bytes_accessed=gathered.size * 4, transcendentals=0),
+        cost_estimate=pl.CostEstimate(
+            flops=0, bytes_accessed=pieces[0].size * 16, transcendentals=0
+        ),
         name="unpack_merged",
-    )(gathered)
+    )(*pieces)
 
 
 def after(values, *others, all_of=False):
@@ -2113,27 +2131,33 @@
 
     layer_output = layer_output.astype(BF).reshape(groups, local_length, width)
     if square:
-        swish_all, merged_all = gather_two(
-            after(swish_share, layer_output, input_gradient), merged_share, 13
-        )
-        value_share = after(value_share, swish_all)
-        half = value_share.shape[0] // 2
-        across, along = swap(value_share, 1), swap(value_share, 2)
+        swish_all = gather_seq(swish_share, 13)
+        merged_share = after(merged_share, swish_all)
+        second = (swap(merged_share, 1), swap(merged_share, 2))
         gelu_gradient, linear_gradient, down_gradient = unpack_feed(
-            after(feed_all, swish_all), down_all, cut, shards
+            after(feed_all, swish_all, layer_output, input_gradient), down_all, cut, shards
         )
         swish_gradient, channel_own_gradient = unpack_columns(swish_all, vd)
-        across, along, gelu_gradient, swish_gradient = after(
-            across, along, gelu_gradient, swish_gradient, all_of=True
-        )
-        corner_low, corner_high = swap(across[:half], 2), swap(along[half:], 1)
-        query_gradient, key_gradient, output_gradient = unpack_merged(merged_all, qk, cut, width)
-        corner_low, corner_high, query_gradient = after(
-            corner_low, corner_high, query_gradient, all_of=True
-        )
-        corner = jnp.concatenate([corner_low, corner_high], axis=0)
+        second, gelu_gradient, swish_gradient = after(
+            second, gelu_gradient, swish_gradient, all_of=True
+        )
+
+        def corners(pair):
+            half = pair[0].shape[0] // 2
+            return swap(pair[0][:half], 2), swap(pair[1][half:], 1)
+
+        def pieces(own, pair, halves):
+            return (own,) + tuple(pair) + (jnp.concatenate(halves, axis=0),)
+
+        second_corner = corners(second)
+        second_corner, value_share = after(second_corner, value_share, all_of=True)
+        third = (swap(value_share, 1), swap(value_share, 2))
+        query_gradient, key_gradient, output_gradient = unpack_merged(
+            pieces(merged_share, second, second_corner), qk, cut, width
+        )
+        third, query_gradient = after(third, query_gradient, all_of=True)
         value_gradient, mixer_own_gradient = unpack_related(
-            (value_share, across, along, corner), vd
+            pieces(value_share, third, corners(third)), vd
         )
     else:
         down_all = gather_seq(down_share, 10)

time: 594 us -> 592 us (level)
  Pallas kernels: 499 us -> 465 us
  waiting for transfers between devices: 26.1 us -> 46.3 us
    pallas_call x8 -> x7, Pallas kernels: 366 us -> 317 us  [comm_call(): pl.pallas_call(body, out_shape=tuple((jax.ShapeDtypeStruct(shape, kind) f...]
    pallas_call x3 -> x4, Pallas kernels: 110 us -> 126 us  [gather_seq(): pl.pallas_call(body, out_shape=jax.ShapeDtypeStruct((count,) + values.sha...]
    reduce_scatter x2, waiting for transfers between devices: 0.04 us -> 10.7 us  [scatter_rows(): lax.psum_scatter(values.astype(BF), 'fsdp', scatter_dimension=0, tiled=True)]
    ppermute x4 -> x8, waiting for transfers between devices: 1.09 us -> 10.5 us  [swap(): return lax.ppermute(values, 'seq', [(k, k ^ step) for k in range(4)])]
  transfers between devices with their start and end apart: 12 -> 16, of which waited for: 3 -> 7; matrix products, arithmetic and copies ran while one was open for 3% -> 4% of each run, Pallas kernels for 84% -> 78%
where the time goes in v8:
time: 592 us; the launch traced here: 586 us
  Pallas kernels  465 us (79%)
  waiting for transfers between devices  46.3 us (8%)
  other arithmetic  19.8 us (3%)
  between operations  14.8 us (2%)
  blocking collectives  13.5 us (2%)
  starting transfers between devices  11 us (2%)
  local copies, waits for them, and re-layouts  10.8 us (2%)
    pallas_call x7, Pallas kernels, comm_call(): pl.pallas_call(body, out_shape=tuple((jax.ShapeDtypeStruct(shape, kind) f...  317 us
    pallas_call x4, Pallas kernels, gather_seq(): pl.pallas_call(body, out_shape=jax.ShapeDtypeStruct((count,) + values.sha...  126 us
    all_gather x3, waiting for transfers between devices, gather_rows(): return lax.all_gather(values, 'fsdp', axis=0, tiled=True)  24.8 us
    all_gather x1, blocking collectives, on_device(): lax.all_gather(jnp.stack([mixer_gain, channel_gain]), 'fsdp', axis=1, til...  13.5 us
  transfers between devices with their start and end apart: 16, of which 7 were waited for; matrix products, arithmetic and copies ran while one was open for 4% of the time, Pallas kernels for 78%

profile of v8, /device:TPU:0, one launch (start us, length us, event | category | flops | bytes accessed | tf_op | source)
XLA Modules:
  0.0 586.2 jit_solution(14003244424108159775)
XLA Ops:
  7.2 0.0 all-gather.4.cloned.1.call-start
  7.3 2.9 pack.1
  10.2 0.0 all-gather.6.cloned.1.call-start
  10.3 13.5 %all_gather.12 = bf16[2,2048]{1,0:T(2,128)(2,1)S(1)} all-gather(bf16[2,256]{1,0:T(2,128)(2,1)S(1)} %pad_maximum_fusion.3), channel_id=1, replica_groups=mesh['seq'=4,'fsdp'=8] {'fsdp'}, dimensions={1}, use_global_device_ids=true | all-gather | bytes 9216 | tf_op jit(solution)/shard_map/all_gather | solution.py:1996
  23.7 38.2 %gather_seq_0.1 = bf16[4,256,2048]{2,1,0:T(8,128)(2,1)} custom-call(bf16[256,2048]{1,0:T(8,128)(2,1)} %bitcast.22), custom_call_target="tpu_custom_call" | custom-call | bytes 125829120 | tf_op jit(solution)/shard_map/gather_seq_0/pallas_call | solution.py:451
  61.9 36.3 %gather_seq_1.1 = bf16[4,256,2048]{2,1,0:T(8,128)(2,1)} custom-call(bf16[256,2048]{1,0:T(8,128)(2,1)} %bitcast.25), custom_call_target="tpu_custom_call" | custom-call | bytes 125829120 | tf_op jit(solution)/shard_map/gather_seq_1/pallas_call | solution.py:451
  98.3 2.4 fusion.3
  100.7 2.4 fusion.2
  103.1 1.0 pad_maximum_fusion.1
  104.2 0.3 all-gather.8.cloned.1.call-start
  104.5 0.6 slice_convert_fusion
  105.1 2.2 copy-done.3
  107.3 4.1 norm_and_turn.1
  111.5 2.0 copy-done.2
  113.5 1.9 copy-done.4
  115.5 2.8 fusion.4
  118.3 2.0 dynamic-slice_select_fusion
  120.3 0.4 fusion.1
  120.7 0.4 fusion
  121.1 0.3 maximum_convert_fusion.1
  121.4 0.3 maximum_convert_fusion
  121.7 2.5 exponential_select_fusion.table_ref
  124.1 2.5 exponential_select_fusion.1.table_ref
  126.6 24.8 %all-gather.4.cloned.1.call-done.w_any = bf16[2048,3712]{1,0:T(8,128)(2,1)} async-done(((bf16[256,3712]{1,0:T(8,128)(2,1)}), bf16[2048,3712]{1,0:T(8,128)(2,1)}) %all-gather.4.cloned.1.call-update) | async-done | bytes 15204368 | tf_op jit(solution)/shard_map/all_gather | solution.py:1959
  151.4 33.1 %retention_exchange.1 = (bf16[1024,512]{1,0:T(8,128)(2,1)}, bf16[1024,512]{1,0:T(8,128)(2,1)}, bf16[2,1024,432]{2,1,0:T(8,128)(2,1)}, f32[1024,864]{1,0:T(8,128)...) custom-call(bf16[1024,2048]{1,0:T(8,128)(2,1)} %copy-done.4, ...), custom_call_target="tpu_custom_call" | custom-call | bytes 251658240 | tf_op jit(solution)/shard_map/retention_exchange/pallas_call | solution.py:901
  184.5 0.6 reduce-scatter.6.cloned.1.call-start
  185.1 44.6 %project_and_norm.1 = (f32[256,2048]{1,0:T(8,128)}, bf16[256,2048]{1,0:T(8,128)(2,1)}) custom-call(bf16[1024,864]{1,0:T(8,128)(2,1)} %get-tuple-element.78.g_any.gated_any, bf16[864,2048]{1,0:T(8,128)(2,1)} %get-tuple-element.79.w_any, bf16[256,2048]{1,0:T(8,128)(2,1)} %bitcast.23, f32[1,2048]{1,0:T(1,128)} %get-tuple-element.134.gain_ref), custom_call_target="tpu_custom_call" | custom-call | bytes 125829120 | tf_op jit(solution)/shard_map/project_and_norm/pallas_call | solution.py:901
  229.7 0.0 all-gather.6.cloned.1.call-done.w_any
  229.8 42.6 %feed_forward_gather.1 = (bf16[1024,1792]{1,0:T(8,128)(2,1)}, bf16[1024,896]{1,0:T(8,128)(2,1)}, bf16[896,2048]{1,0:T(8,128)(2,1)}, bf16[4,256,2048]{2,1,0:T(8,128)(2,1)}) custom-call(bf16[256,2048]{1,0:T(8,128)(2,1)} %get-tuple-element.80.x_any, bf16[2048,1792]{1,0:T(8,128)(2,1)} %all-gather.6.cloned.1.call-done.w_any, bf16[1024,2048]{1,0:T(8,128)(2,1)} %bitcast.19), custom_call_target="tpu_custom_call" | custom-call | bytes 125829120 | tf_op jit(solution)/shard_map/feed_forward_gather/pallas_call | solution.py:901
  272.4 0.2 reduce-scatter.8.cloned.1.call-start
  272.6 49.3 %feed_back_scatter.1 = (f32[256,2048]{1,0:T(8,128)}, f32[2048,128]{1,0:T(8,128)}, bf16[256,2048]{1,0:T(8,128)(2,1)}, bf16[1024,1792]{1,0:T(8,128)(2,1)}) custom-call(bf16[1024,2048]{1,0:T(8,128)(2,1)} %bitcast.20, bf16[1024,1792]{1,0:T(8,128)(2,1)} %get-tuple-element.84.both_any, bf16[2048,1792]{1,0:T(8,128)(2,1)} %all-gather.6.cloned.1.call-done.w_any, ...), custom_call_target="tpu_custom_call" | custom-call | bytes 125829120 | tf_op jit(solution)/shard_map/feed_back_scatter/pallas_call | solution.py:901
  322.0 0.3 reduce-scatter.12.cloned.1.call-start
  322.3 35.9 %gather_seq_7.1 = bf16[4,256,2048]{2,1,0:T(8,128)(2,1)} custom-call(bf16[256,2048]{1,0:T(8,128)(2,1)} %get-tuple-element.88.x_ref), custom_call_target="tpu_custom_call" | custom-call | bytes 125829120 | tf_op jit(solution)/shard_map/gather_seq_7/pallas_call | solution.py:451
  358.2 0.0 reduce-scatter.6.cloned.1.call-done.share_any
  358.2 39.1 %gate_back_scatter.1 = (bf16[1024,896]{1,0:T(8,128)(2,1)}, bf16[2,1024,432]{2,1,0:T(8,128)(2,1)}, bf16[1024,896]{1,0:T(8,128)(2,1)}, bf16[2,4,256,896]{3,2,1,0:T(8,128)(2,1)}, f32[256,2048]{1,0:T(8,128)}) custom-call(bf16[1024,2048]{1,0:T(8,128)(2,1)} %bitcast.21, bf16[864,2048]{1,0:T(8,128)(2,1)} %get-tuple-element.79.w_any, ...), custom_call_target="tpu_custom_call" | custom-call | bytes 125829120 | tf_op jit(solution)/shard_map/gate_back_scatter/pallas_call | solution.py:901
  397.4 0.0 reduce-scatter.10.cloned.1.call-start
  397.5 41.5 %retention_back_exchange.1 = (bf16[1024,1024]{1,0:T(8,128)(2,1)}, bf16[1024,896]{1,0:T(8,128)(2,1)}, bf16[1024,1920]{1,0:T(8,128)(2,1)}, bf16[4,112,2048]{2,1,0:T(8,128)(2,1)}) custom-call(bf16[1024,512]{1,0:T(8,128)(2,1)} %get-tuple-element.95.q_any, bf16[1024,512]{1,0:T(8,128)(2,1)} %get-tuple-element.96.k_any, ...), custom_call_target="tpu_custom_call" | custom-call | bytes 110100480 | tf_op jit(solution)/shard_map/retention_back_exchange/pallas_call | solution.py:901
  439.0 0.3 reduce-scatter.14.cloned.1.call-start
  439.3 66.5 %input_backward.1 = (f32[256,2048]{1,0:T(8,128)}, bf16[2048,896]{1,0:T(8,128)(2,1)}, bf16[4,256,1792]{2,1,0:T(8,128)(2,1)}) custom-call(bf16[1024,1024]{1,0:T(8,128)(2,1)} %get-tuple-element.102.dqk_any, bf16[1024,896]{1,0:T(8,128)(2,1)} %get-tuple-element.103.dv_any, bf16[1024,896]{1,0:T(8,128)(2,1)} %get-tuple-element.104.ds_any, ...), custom_call_target="tpu_custom_call" | custom-call | bytes 235929600 | tf_op jit(solution)/shard_map/input_backward/pallas_call | solution.py:901
  505.8 15.4 %gather_seq_13.1.in_ref = bf16[4,256,896]{2,1,0:T(8,128)(2,1)} custom-call(bf16[256,896]{1,0:T(8,128)(2,1)} %reduce-scatter.12.cloned.1.call-done.x_ref), custom_call_target="tpu_custom_call" | custom-call | bytes 55050240 | tf_op jit(solution)/shard_map/gather_seq_13/pallas_call | solution.py:451
  521.3 1.8 collective-permute-start.1
  523.1 0.3 collective-permute-start
  523.4 2.7 convert_bitcast_fusion.1
  526.1 3.2 unpack_columns.1
  529.4 2.9 convert_bitcast_fusion
  532.2 2.1 copy-done.5
  534.3 6.2 %unpack_feed.1 = (f32[256,3456]{1,0:T(8,128)}, f32[256,3456]{1,0:T(8,128)}, f32[432,2048]{1,0:T(8,128)}) custom-call(bf16[4,256,1792]{2,1,0:T(8,128)(2,1)S(1)} %copy-done.5, bf16[4,112,2048]{2,1,0:T(8,128)(2,1)S(1)} %copy-done.8), custom_call_target="tpu_custom_call" | custom-call | bytes 7340032 | tf_op jit(solution)/shard_map/unpack_feed/pallas_call | solution.py:1760
  540.5 2.6 collective-permute-done.1.along_ref
  543.1 0.9 collective-permute-done.across_ref
  544.1 1.3 collective-permute-start.3
  545.4 0.8 collective-permute-start.2
  546.2 10.7 %reduce-scatter.14.cloned.1.call-done.own_ref = bf16[256,896]{1,0:T(8,128)(2,1)} async-done(((bf16[2048,896]{1,0:T(8,128)(2,1)}), bf16[256,896]{1,0:T(8,128)(2,1)}) %reduce-scatter.14.cloned.1.call-update) | async-done | bytes 458768 | tf_op jit(solution)/shard_map/reduce_scatter | solution.py:1962
  556.9 1.5 collective-permute-start.5
  558.4 1.5 collective-permute-start.4
  559.9 1.4 pad_maximum_fusion.corner_ref
  561.3 1.2 copy-done.7
  562.5 1.2 copy-done.9
  563.7 4.0 unpack_merged.1
  567.7 1.5 collective-permute-done.4.across_ref
  569.2 1.5 collective-permute-start.7
  570.8 0.5 collective-permute-start.6
  571.3 4.0 collective-permute-done.7
  575.3 1.5 collective-permute-done.6
  576.8 2.3 unpack_related.1
  (55 shorter events, 0.5 us)
Async XLA Ops:
  7.2 91.1 %copy-start = (bf16[256,3456]{1,0:T(8,128)(2,1)S(1)}, bf16[256,3456]{1,0:T(8,128)(2,1)}, u32[]{:S(2)}) copy-start(bf16[256,3456]{1,0:T(8,128)(2,1)} %param.21) | copy-start | bytes 5308420
  7.2 3.0 copy-start.13
  7.2 3.0 copy-start.14
  7.2 144.2 %all-gather.4.cloned.1.call-start = ((), (), s32[]{:S(2)}) async-start(), calls=%async_computation.5 | async-start | bytes 17104896 | tf_op jit(solution)/shard_map/all_gather | solution.py:1959
  10.2 219.6 %all-gather.6.cloned.1.call-start = ((), (), s32[]{:S(2)}) async-start(), calls=%async_computation.6 | async-start | bytes 8257536 | tf_op jit(solution)/shard_map/all_gather | solution.py:1959
  98.3 2.4 copy-start.12
  104.2 168.5 %all-gather.8.cloned.1.call-start = ((), (), s32[]{:S(2)}) async-start(), calls=%async_computation.7 | async-start | bytes 4128768 | tf_op jit(solution)/shard_map/all_gather | solution.py:1959
  105.1 15.2 %copy-start.11 = (f32[1,2048]{1,0:T(1,128)}, f32[1,2048]{1,0:T(1,128)S(1)}, u32[]{:S(2)}) copy-start(f32[1,2048]{1,0:T(1,128)S(1)} %get-tuple-element.135.gain_ref) | copy-start | bytes 24580
  105.1 2.2 copy-start.3
  111.5 2.0 copy-start.2
  113.5 1.9 copy-start.4
  184.5 173.7 %reduce-scatter.6.cloned.1.call-start = ((), (), s32[]{:S(2)}) async-start(), calls=%async_computation.8 | async-start | bytes 4128768 | tf_op jit(solution)/shard_map/reduce_scatter | solution.py:1962
  272.4 125.1 %reduce-scatter.8.cloned.1.call-start = ((), (), s32[]{:S(2)}) async-start(), calls=%async_computation.9 | async-start | bytes 4587520 | tf_op jit(solution)/shard_map/reduce_scatter | solution.py:1966
  322.0 183.8 %reduce-scatter.12.cloned.1.call-start = ((), (), s32[]{:S(2)}) async-start(), calls=%async_computation.11 | async-start | bytes 2293760 | tf_op jit(solution)/shard_map/reduce_scatter | solution.py:1966
  397.4 123.9 %reduce-scatter.10.cloned.1.call-start = ((), (), s32[]{:S(2)}) async-start(), calls=%async_computation.10 | async-start | bytes 4915200 | tf_op jit(solution)/shard_map/reduce_scatter | solution.py:1966
  439.0 117.9 %reduce-scatter.14.cloned.1.call-start = ((), (), s32[]{:S(2)}) async-start(), calls=%async_computation.12 | async-start | bytes 4128768 | tf_op jit(solution)/shard_map/reduce_scatter | solution.py:1962
  521.3 21.8 %collective-permute-start.1 = (bf16[256,1920]{1,0:T(8,128)(2,1)}, bf16[256,1920]{1,0:T(8,128)(2,1)S(1)}, u32[]{:S(2)}, u32[]{:S(2)}) collective-permute-start(bf16[256,1920]{1,0:T(8,128)(2,1)} %reduce-scatter.10.cloned.1.call-done.own_ref), channel_id=1, source_target_pairs={{0,16},{8,24},{16,0},{24,8},{1,17},{9,25},{17,1},{25,9},{2,18},{10... | collective-permute-start | bytes 2949128 | tf_op jit(solution)/shard_map/ppermute | solution.py:1730
  523.1 20.9 %collective-permute-start = (bf16[256,1920]{1,0:T(8,128)(2,1)}, bf16[256,1920]{1,0:T(8,128)(2,1)S(1)}, u32[]{:S(2)}, u32[]{:S(2)}) collective-permute-start(bf16[256,1920]{1,0:T(8,128)(2,1)} %reduce-scatter.10.cloned.1.call-done.own_ref), channel_id=1, source_target_pairs={{0,8},{8,0},{16,24},{24,16},{1,9},{9,1},{17,25},{25,17},{2,10},{10... | collective-permute-start | bytes 2949128 | tf_op jit(solution)/shard_map/ppermute | solution.py:1730
  529.4 2.9 copy-start.8
  532.2 2.1 copy-start.5
  544.0 14.4 %copy-start.6 = (bf16[256,1920]{1,0:T(8,128)(2,1)}, bf16[256,1920]{1,0:T(8,128)(2,1)S(1)}, u32[]{:S(2)}) copy-start(bf16[256,1920]{1,0:T(8,128)(2,1)S(1)} %collective-permute-done.across_ref) | copy-start | bytes 2949124
  544.1 12.8 %collective-permute-start.3 = (bf16[128,1920]{1,0:T(8,128)(2,1)S(1)}, bf16[128,1920]{1,0:T(8,128)(2,1)}, u32[]{:S(2)}, u32[]{:S(2)}) collective-permute-start(bf16[128,1920]{1,0:T(8,128)(2,1)S(1)} %slice.21), channel_id=1, source_target_pairs={{0,8},{8,0},{16,24},{24,16},{1,9},{9,1},{17,25},{25,17},{2,10},{10... | collective-permute-start | bytes 1474568 | tf_op jit(solution)/shard_map/ppermute | solution.py:1730
  545.4 11.5 %collective-permute-start.2 = (bf16[128,1920]{1,0:T(8,128)(2,1)S(1)}, bf16[128,1920]{1,0:T(8,128)(2,1)}, u32[]{:S(2)}, u32[]{:S(2)}) collective-permute-start(bf16[128,1920]{1,0:T(8,128)(2,1)S(1)} %slice.20), channel_id=1, source_target_pairs={{0,16},{8,24},{16,0},{24,8},{1,17},{9,25},{17,1},{25,9},{2,18},{10... | collective-permute-start | bytes 1474568 | tf_op jit(solution)/shard_map/ppermute | solution.py:1730
  556.9 10.8 %collective-permute-start.5 = (bf16[256,896]{1,0:T(8,128)(2,1)}, bf16[256,896]{1,0:T(8,128)(2,1)S(1)}, u32[]{:S(2)}, u32[]{:S(2)}) collective-permute-start(bf16[256,896]{1,0:T(8,128)(2,1)} %reduce-scatter.14.cloned.1.call-done.own_ref), channel_id=1, source_target_pairs={{0,16},{8,24},{16,0},{24,8},{1,17},{9,25},{17,1},{25,9},{2,18},{10... | collective-permute-start | bytes 1376264 | tf_op jit(solution)/shard_map/ppermute | solution.py:1730
  558.4 10.8 %collective-permute-start.4 = (bf16[256,896]{1,0:T(8,128)(2,1)}, bf16[256,896]{1,0:T(8,128)(2,1)S(1)}, u32[]{:S(2)}, u32[]{:S(2)}) collective-permute-start(bf16[256,896]{1,0:T(8,128)(2,1)} %reduce-scatter.14.cloned.1.call-done.own_ref), channel_id=1, source_target_pairs={{0,8},{8,0},{16,24},{24,16},{1,9},{9,1},{17,25},{25,17},{2,10},{10... | collective-permute-start | bytes 1376264 | tf_op jit(solution)/shard_map/ppermute | solution.py:1730
  559.9 19.2 %copy-start.1 = (bf16[256,3456]{1,0:T(8,128)(2,1)S(1)}, bf16[256,3456]{1,0:T(8,128)(2,1)}, u32[]{:S(2)}) copy-start(bf16[256,3456]{1,0:T(8,128)(2,1)} %param.21) | copy-start | bytes 5308420
  561.3 1.2 copy-start.7
  562.5 1.2 copy-start.9
  563.7 13.2 %copy-start.10 = (bf16[256,896]{1,0:T(8,128)(2,1)S(1)}, bf16[256,896]{1,0:T(8,128)(2,1)}, u32[]{:S(2)}) copy-start(bf16[256,896]{1,0:T(8,128)(2,1)} %reduce-scatter.14.cloned.1.call-done.own_ref) | copy-start | bytes 1376260
  569.2 6.1 %collective-permute-start.7 = (bf16[128,896]{1,0:T(8,128)(2,1)S(1)}, bf16[128,896]{1,0:T(8,128)(2,1)S(1)}, u32[]{:S(2)}, u32[]{:S(2)}) collective-permute-start(bf16[128,896]{1,0:T(8,128)(2,1)S(1)} %slice.23), channel_id=1, source_target_pairs={{0,8},{8,0},{16,24},{24,16},{1,9},{9,1},{17,25},{25,17},{2,10},{10... | collective-permute-start | bytes 688136 | tf_op jit(solution)/shard_map/ppermute | solution.py:1730
  570.8 6.0 %collective-permute-start.6 = (bf16[128,896]{1,0:T(8,128)(2,1)S(1)}, bf16[128,896]{1,0:T(8,128)(2,1)S(1)}, u32[]{:S(2)}, u32[]{:S(2)}) collective-permute-start(bf16[128,896]{1,0:T(8,128)(2,1)S(1)} %slice.22), channel_id=1, source_target_pairs={{0,16},{8,24},{16,0},{24,8},{1,17},{9,25},{17,1},{25,9},{2,18},{10... | collective-permute-start | bytes 688136 | tf_op jit(solution)/shard_map/ppermute | solution.py:1730
Sparse Core Ops, SparseCore 0:
  10.3 141.0 all-gather.3
  153.6 71.6 all-gather.5
  227.5 41.1 all-gather.7
  272.5 42.3 reduce-scatter.5
  322.1 65.7 reduce-scatter.7
  397.5 37.1 reduce-scatter.11
  439.1 70.0 reduce-scatter.9
  511.5 45.3 reduce-scatter.13

commit v9 on v8

--- a/solution.py
+++ b/solution.py
@@ -790,8 +790,8 @@
 
 
 def project_kernel(
-    g_any, w_any, x_ref, gain_ref, middle_ref, own_ref,
-    g_ref, w_ref, parts, inbox_x, inbox_y, via_x, via_y, out_x, out_y, sends, recvs, locals_,
+    g_any, w_any, x_ref, gain_ref, middle_any, own_any,
+    middle_ref, own_ref, g_ref, w_ref, parts, inbox_x, inbox_y, via_x, via_y, out_x, out_y, sends, recvs, locals_,
 ):
     me = lax.axis_index("seq")
     rows = x_ref.shape[0]
@@ -810,13 +810,22 @@
     send_parts(part, copies)
     finish()
 
+    stores = [
+        by_block(moves, 2, middle_ref, middle_any, half),
+        by_block(moves, 2, own_ref, own_any, half),
+    ]
+
     @pl.loop(0, 2)
     def _(i):
         here = pl.ds(pl.multiple_of(i * half, half), half)
         middle = x_ref[here, :].astype(F32) + total(here)
         middle_ref[here, :] = middle
         own_ref[here, :] = normalize(middle, gain_ref[...]).astype(BF)
-
+        for store in stores:
+            store.copy(i).start()
+
+    for store in stores:
+        store.wait_all()
     for copy in copies:
         copy.wait_send()
 
@@ -1043,10 +1052,12 @@
     return comm_call(
         project_kernel,
         [(gated, False), (weight, False), (x, True), (gain[None, :], True)],
-        [((rows, width), F32, True), ((rows, width), BF, True)],
-        [pltpu.VMEM(gated.shape, BF), pltpu.VMEM(weight.shape, BF)] + square_scratch(rows, width),
+        [((rows, width), F32, False), ((rows, width), BF, False)],
+        [pltpu.VMEM((rows, width), F32), pltpu.VMEM((rows, width), BF)]
+        + [pltpu.VMEM(gated.shape, BF), pltpu.VMEM(weight.shape, BF)]
+        + square_scratch(rows, width),
         6,
-        2,
+        6,
         call,
         x.size,
         "project_and_norm",
@@ -1110,9 +1121,16 @@
             store.copy(me ^ k).start()
         total[...] += transposed_times(hidden, c_ref[here, :])
 
-    down_ref[...] = total[...].astype(BF)
-    moves.store(down_ref, down_any)
-    for store in stores:
+    piece = ff // 4
+    downs = by_block(moves, 4, down_ref, down_any, piece)
+
+    @pl.loop(0, 4)
+    def _(n):
+        here = pl.ds(pl.multiple_of(n * piece, piece), piece)
+        down_ref[here, :] = total[here, :].astype(BF)
+        downs.copy(n).start()
+
+    for store in stores + [downs]:
         store.wait_all()
     moves.close()
     for copy in copies:
@@ -1141,7 +1159,7 @@
             pltpu.VMEM((ff, width), BF),
         ],
         6,
-        16,
+        19,
         call,
         own.size,
         "feed_forward_gather",
@@ -1159,8 +1177,8 @@
 
 def feed_back_scatter_kernel(
     ff, c_any, both_any, w_any, down_any, x_any, m_ref, own_c_ref, gain_ref,
-    grad_ref, term_ref, branch_ref, dw_any,
-    c_ref, both_ref, w_ref, down_ref, x_ref, low, dw_send, dw_twin, dw_ref,
+    grad_any, term_ref, branch_any, dw_any,
+    grad_ref, branch_ref, c_ref, both_ref, w_ref, down_ref, x_ref, low, dw_send, dw_twin, dw_ref,
     parts, inbox_x, inbox_y, via_x, via_y, out_x, out_y, sends, recvs, locals_,
 ):
     me = lax.axis_index("seq")
@@ -1207,10 +1225,13 @@
         grad = own_c_ref[here, :].astype(F32) + back
         grad_ref[here, :] = grad
         branch_ref[here, :] = grad.astype(BF)
+        moves.store(grad_ref.at[here], grad_any.at[here])
+        moves.store(branch_ref.at[here], branch_any.at[here])
         return term
 
     term_ref[...] = column_of([back_half(i) for i in range(2)])
     finish()
+    moves.close()
     for copy in copies:
         copy.wait_send()
 
@@ -1231,12 +1252,14 @@
             (gain[None, :], True),
         ],
         [
-            ((rows, width), F32, True),
+            ((rows, width), F32, False),
             ((width, 128), F32, True),
-            ((rows, width), BF, True),
+            ((rows, width), BF, False),
             ((width // 2, 2 * ff), BF, False),
         ],
         [
+            pltpu.VMEM((rows, width), F32),
+            pltpu.VMEM((rows, width), BF),
             pltpu.VMEM(cotangent.shape, BF),
             pltpu.VMEM(both.shape, BF),
             pltpu.VMEM(weight.shape, BF),
@@ -1247,7 +1270,7 @@
         + core_scratch(width, 2 * ff)
         + square_scratch(rows, width),
         6 + width // (2 * BLOCK),
-        11 + width // (2 * BLOCK),
+        15 + width // (2 * BLOCK),
         call,
         own_cotangent.size,
         "feed_back_scatter",

time: 592 us -> 591 us (level)
  transfers between devices with their start and end apart: 16 -> 16, of which waited for: 7 -> 7; matrix products, arithmetic and copies ran while one was open for 4% -> 4% of each run, Pallas kernels for 78% -> 79%
where the time goes in v9:
time: 591 us; the launch traced here: 586 us
  Pallas kernels  465 us (79%)
  waiting for transfers between devices  46.2 us (8%)
  other arithmetic  19.8 us (3%)
  between operations  14.8 us (3%)
  blocking collectives  13.5 us (2%)
  starting transfers between devices  11 us (2%)
  local copies, waits for them, and re-layouts  10.8 us (2%)
    pallas_call x7, Pallas kernels, comm_call(): pl.pallas_call(body, out_shape=tuple((jax.ShapeDtypeStruct(shape, kind) f...  316 us
    pallas_call x4, Pallas kernels, gather_seq(): pl.pallas_call(body, out_shape=jax.ShapeDtypeStruct((count,) + values.sha...  126 us
    all_gather x3, waiting for transfers between devices, gather_rows(): return lax.all_gather(values, 'fsdp', axis=0, tiled=True)  24.8 us
    all_gather x1, blocking collectives, on_device(): lax.all_gather(jnp.stack([mixer_gain, channel_gain]), 'fsdp', axis=1, til...  13.5 us
  transfers between devices with their start and end apart: 16, of which 7 were waited for; matrix products, arithmetic and copies ran while one was open for 4% of the time, Pallas kernels for 79%

profile of v9, /device:TPU:0, one launch (start us, length us, event | category | flops | bytes accessed | tf_op | source)
XLA Modules:
  0.0 585.6 jit_solution(16202931153253081693)
XLA Ops:
  7.2 0.0 all-gather.4.cloned.1.call-start
  7.3 2.9 pack.1
  10.2 0.0 all-gather.6.cloned.1.call-start
  10.3 13.5 %all_gather.12 = bf16[2,2048]{1,0:T(2,128)(2,1)S(1)} all-gather(bf16[2,256]{1,0:T(2,128)(2,1)S(1)} %pad_maximum_fusion.3), channel_id=1, replica_groups=mesh['seq'=4,'fsdp'=8] {'fsdp'}, dimensions={1}, use_global_device_ids=true | all-gather | bytes 9216 | tf_op jit(solution)/shard_map/all_gather | solution.py:2019
  23.7 38.2 %gather_seq_0.1 = bf16[4,256,2048]{2,1,0:T(8,128)(2,1)} custom-call(bf16[256,2048]{1,0:T(8,128)(2,1)} %bitcast.22), custom_call_target="tpu_custom_call" | custom-call | bytes 125829120 | tf_op jit(solution)/shard_map/gather_seq_0/pallas_call | solution.py:451
  61.9 36.3 %gather_seq_1.1 = bf16[4,256,2048]{2,1,0:T(8,128)(2,1)} custom-call(bf16[256,2048]{1,0:T(8,128)(2,1)} %bitcast.25), custom_call_target="tpu_custom_call" | custom-call | bytes 125829120 | tf_op jit(solution)/shard_map/gather_seq_1/pallas_call | solution.py:451
  98.3 2.4 fusion.3
  100.7 2.4 fusion.2
  103.1 1.0 pad_maximum_fusion.1
  104.2 0.3 all-gather.8.cloned.1.call-start
  104.5 0.6 slice_convert_fusion
  105.1 2.2 copy-done.3
  107.3 4.1 norm_and_turn.1
  111.5 2.0 copy-done.2
  113.5 1.9 copy-done.4
  115.5 2.8 fusion.4
  118.3 2.0 dynamic-slice_select_fusion
  120.3 0.4 fusion.1
  120.7 0.4 fusion
  121.1 0.3 maximum_convert_fusion.1
  121.4 0.3 maximum_convert_fusion
  121.7 2.5 exponential_select_fusion.table_ref
  124.1 2.5 exponential_select_fusion.1.table_ref
  126.6 24.8 %all-gather.4.cloned.1.call-done.w_any = bf16[2048,3712]{1,0:T(8,128)(2,1)} async-done(((bf16[256,3712]{1,0:T(8,128)(2,1)}), bf16[2048,3712]{1,0:T(8,128)(2,1)}) %all-gather.4.cloned.1.call-update) | async-done | bytes 15204368 | tf_op jit(solution)/shard_map/all_gather | solution.py:1982
  151.4 33.1 %retention_exchange.1 = (bf16[1024,512]{1,0:T(8,128)(2,1)}, bf16[1024,512]{1,0:T(8,128)(2,1)}, bf16[2,1024,432]{2,1,0:T(8,128)(2,1)}, f32[1024,864]{1,0:T(8,128)...) custom-call(bf16[1024,2048]{1,0:T(8,128)(2,1)} %copy-done.4, ...), custom_call_target="tpu_custom_call" | custom-call | bytes 251658240 | tf_op jit(solution)/shard_map/retention_exchange/pallas_call | solution.py:910
  184.5 0.6 reduce-scatter.6.cloned.1.call-start
  185.1 44.0 %project_and_norm.1 = (f32[256,2048]{1,0:T(8,128)}, bf16[256,2048]{1,0:T(8,128)(2,1)}) custom-call(bf16[1024,864]{1,0:T(8,128)(2,1)} %get-tuple-element.78.g_any.gated_any, bf16[864,2048]{1,0:T(8,128)(2,1)} %get-tuple-element.79.w_any, bf16[256,2048]{1,0:T(8,128)(2,1)} %bitcast.23, f32[1,2048]{1,0:T(1,128)} %get-tuple-element.134.gain_ref), custom_call_target="tpu_custom_call" | custom-call | bytes 125829120 | tf_op jit(solution)/shard_map/project_and_norm/pallas_call | solution.py:910
  229.1 0.0 all-gather.6.cloned.1.call-done.w_any
  229.1 42.3 %feed_forward_gather.1 = (bf16[1024,1792]{1,0:T(8,128)(2,1)}, bf16[1024,896]{1,0:T(8,128)(2,1)}, bf16[896,2048]{1,0:T(8,128)(2,1)}, bf16[4,256,2048]{2,1,0:T(8,128)(2,1)}) custom-call(bf16[256,2048]{1,0:T(8,128)(2,1)} %get-tuple-element.80.x_any, bf16[2048,1792]{1,0:T(8,128)(2,1)} %all-gather.6.cloned.1.call-done.w_any, bf16[1024,2048]{1,0:T(8,128)(2,1)} %bitcast.19), custom_call_target="tpu_custom_call" | custom-call | bytes 125829120 | tf_op jit(solution)/shard_map/feed_forward_gather/pallas_call | solution.py:910
  271.5 0.2 reduce-scatter.8.cloned.1.call-start
  271.7 49.8 %feed_back_scatter.1 = (f32[256,2048]{1,0:T(8,128)}, f32[2048,128]{1,0:T(8,128)}, bf16[256,2048]{1,0:T(8,128)(2,1)}, bf16[1024,1792]{1,0:T(8,128)(2,1)}) custom-call(bf16[1024,2048]{1,0:T(8,128)(2,1)} %bitcast.20, bf16[1024,1792]{1,0:T(8,128)(2,1)} %get-tuple-element.84.both_any, bf16[2048,1792]{1,0:T(8,128)(2,1)} %all-gather.6.cloned.1.call-done.w_any, ...), custom_call_target="tpu_custom_call" | custom-call | bytes 125829120 | tf_op jit(solution)/shard_map/feed_back_scatter/pallas_call | solution.py:910
  321.5 0.3 reduce-scatter.12.cloned.1.call-start
  321.8 35.9 %gather_seq_7.1 = bf16[4,256,2048]{2,1,0:T(8,128)(2,1)} custom-call(bf16[256,2048]{1,0:T(8,128)(2,1)} %get-tuple-element.88.x_ref), custom_call_target="tpu_custom_call" | custom-call | bytes 125829120 | tf_op jit(solution)/shard_map/gather_seq_7/pallas_call | solution.py:451
  357.7 0.0 reduce-scatter.6.cloned.1.call-done.share_any
  357.8 39.1 %gate_back_scatter.1 = (bf16[1024,896]{1,0:T(8,128)(2,1)}, bf16[2,1024,432]{2,1,0:T(8,128)(2,1)}, bf16[1024,896]{1,0:T(8,128)(2,1)}, bf16[2,4,256,896]{3,2,1,0:T(8,128)(2,1)}, f32[256,2048]{1,0:T(8,128)}) custom-call(bf16[1024,2048]{1,0:T(8,128)(2,1)} %bitcast.21, bf16[864,2048]{1,0:T(8,128)(2,1)} %get-tuple-element.79.w_any, ...), custom_call_target="tpu_custom_call" | custom-call | bytes 125829120 | tf_op jit(solution)/shard_map/gate_back_scatter/pallas_call | solution.py:910
  396.9 0.0 reduce-scatter.10.cloned.1.call-start
  397.0 41.5 %retention_back_exchange.1 = (bf16[1024,1024]{1,0:T(8,128)(2,1)}, bf16[1024,896]{1,0:T(8,128)(2,1)}, bf16[1024,1920]{1,0:T(8,128)(2,1)}, bf16[4,112,2048]{2,1,0:T(8,128)(2,1)}) custom-call(bf16[1024,512]{1,0:T(8,128)(2,1)} %get-tuple-element.95.q_any, bf16[1024,512]{1,0:T(8,128)(2,1)} %get-tuple-element.96.k_any, ...), custom_call_target="tpu_custom_call" | custom-call | bytes 110100480 | tf_op jit(solution)/shard_map/retention_back_exchange/pallas_call | solution.py:910
  438.5 0.3 reduce-scatter.14.cloned.1.call-start
  438.8 66.5 %input_backward.1 = (f32[256,2048]{1,0:T(8,128)}, bf16[2048,896]{1,0:T(8,128)(2,1)}, bf16[4,256,1792]{2,1,0:T(8,128)(2,1)}) custom-call(bf16[1024,1024]{1,0:T(8,128)(2,1)} %get-tuple-element.102.dqk_any, bf16[1024,896]{1,0:T(8,128)(2,1)} %get-tuple-element.103.dv_any, bf16[1024,896]{1,0:T(8,128)(2,1)} %get-tuple-element.104.ds_any, ...), custom_call_target="tpu_custom_call" | custom-call | bytes 235929600 | tf_op jit(solution)/shard_map/input_backward/pallas_call | solution.py:910
  505.4 15.4 %gather_seq_13.1.in_ref = bf16[4,256,896]{2,1,0:T(8,128)(2,1)} custom-call(bf16[256,896]{1,0:T(8,128)(2,1)} %reduce-scatter.12.cloned.1.call-done.x_ref), custom_call_target="tpu_custom_call" | custom-call | bytes 55050240 | tf_op jit(solution)/shard_map/gather_seq_13/pallas_call | solution.py:451
  520.8 1.8 collective-permute-start.1
  522.6 0.3 collective-permute-start
  522.9 2.7 convert_bitcast_fusion.1
  525.7 3.2 unpack_columns.1
  528.9 2.9 convert_bitcast_fusion
  531.8 2.1 copy-done.5
  533.8 6.2 %unpack_feed.1 = (f32[256,3456]{1,0:T(8,128)}, f32[256,3456]{1,0:T(8,128)}, f32[432,2048]{1,0:T(8,128)}) custom-call(bf16[4,256,1792]{2,1,0:T(8,128)(2,1)S(1)} %copy-done.5, bf16[4,112,2048]{2,1,0:T(8,128)(2,1)S(1)} %copy-done.8), custom_call_target="tpu_custom_call" | custom-call | bytes 7340032 | tf_op jit(solution)/shard_map/unpack_feed/pallas_call | solution.py:1783
  540.0 2.6 collective-permute-done.1.along_ref
  542.6 1.0 collective-permute-done.across_ref
  543.7 1.3 collective-permute-start.3
  545.0 0.8 collective-permute-start.2
  545.8 10.5 %reduce-scatter.14.cloned.1.call-done.own_ref = bf16[256,896]{1,0:T(8,128)(2,1)} async-done(((bf16[2048,896]{1,0:T(8,128)(2,1)}), bf16[256,896]{1,0:T(8,128)(2,1)}) %reduce-scatter.14.cloned.1.call-update) | async-done | bytes 458768 | tf_op jit(solution)/shard_map/reduce_scatter | solution.py:1985
  556.3 1.5 collective-permute-start.5
  557.8 1.5 collective-permute-start.4
  559.3 1.4 pad_maximum_fusion.corner_ref
  560.7 1.2 copy-done.7
  561.9 1.2 copy-done.9
  563.1 4.0 unpack_merged.1
  567.1 1.5 collective-permute-done.4.across_ref
  568.6 1.5 collective-permute-start.7
  570.2 0.5 collective-permute-start.6
  570.7 4.0 collective-permute-done.7
  574.7 1.5 collective-permute-done.6
  576.2 2.3 unpack_related.1
  (55 shorter events, 0.5 us)
Async XLA Ops:
  7.2 91.1 %copy-start = (bf16[256,3456]{1,0:T(8,128)(2,1)S(1)}, bf16[256,3456]{1,0:T(8,128)(2,1)}, u32[]{:S(2)}) copy-start(bf16[256,3456]{1,0:T(8,128)(2,1)} %param.21) | copy-start | bytes 5308420
  7.2 3.0 copy-start.13
  7.2 3.0 copy-start.14
  7.2 144.2 %all-gather.4.cloned.1.call-start = ((), (), s32[]{:S(2)}) async-start(), calls=%async_computation.5 | async-start | bytes 17104896 | tf_op jit(solution)/shard_map/all_gather | solution.py:1982
  10.2 219.0 %all-gather.6.cloned.1.call-start = ((), (), s32[]{:S(2)}) async-start(), calls=%async_computation.6 | async-start | bytes 8257536 | tf_op jit(solution)/shard_map/all_gather | solution.py:1982
  98.3 2.4 copy-start.12
  104.2 167.6 %all-gather.8.cloned.1.call-start = ((), (), s32[]{:S(2)}) async-start(), calls=%async_computation.7 | async-start | bytes 4128768 | tf_op jit(solution)/shard_map/all_gather | solution.py:1982
  105.1 15.2 %copy-start.11 = (f32[1,2048]{1,0:T(1,128)}, f32[1,2048]{1,0:T(1,128)S(1)}, u32[]{:S(2)}) copy-start(f32[1,2048]{1,0:T(1,128)S(1)} %get-tuple-element.135.gain_ref) | copy-start | bytes 24580
  105.1 2.2 copy-start.3
  111.5 2.0 copy-start.2
  113.5 1.9 copy-start.4
  184.5 173.2 %reduce-scatter.6.cloned.1.call-start = ((), (), s32[]{:S(2)}) async-start(), calls=%async_computation.8 | async-start | bytes 4128768 | tf_op jit(solution)/shard_map/reduce_scatter | solution.py:1985
  271.5 125.5 %reduce-scatter.8.cloned.1.call-start = ((), (), s32[]{:S(2)}) async-start(), calls=%async_computation.9 | async-start | bytes 4587520 | tf_op jit(solution)/shard_map/reduce_scatter | solution.py:1989
  321.5 183.8 %reduce-scatter.12.cloned.1.call-start = ((), (), s32[]{:S(2)}) async-start(), calls=%async_computation.11 | async-start | bytes 2293760 | tf_op jit(solution)/shard_map/reduce_scatter | solution.py:1989
  396.9 123.9 %reduce-scatter.10.cloned.1.call-start = ((), (), s32[]{:S(2)}) async-start(), calls=%async_computation.10 | async-start | bytes 4915200 | tf_op jit(solution)/shard_map/reduce_scatter | solution.py:1989
  438.5 117.8 %reduce-scatter.14.cloned.1.call-start = ((), (), s32[]{:S(2)}) async-start(), calls=%async_computation.12 | async-start | bytes 4128768 | tf_op jit(solution)/shard_map/reduce_scatter | solution.py:1985
  520.8 21.8 %collective-permute-start.1 = (bf16[256,1920]{1,0:T(8,128)(2,1)}, bf16[256,1920]{1,0:T(8,128)(2,1)S(1)}, u32[]{:S(2)}, u32[]{:S(2)}) collective-permute-start(bf16[256,1920]{1,0:T(8,128)(2,1)} %reduce-scatter.10.cloned.1.call-done.own_ref), channel_id=1, source_target_pairs={{0,16},{8,24},{16,0},{24,8},{1,17},{9,25},{17,1},{25,9},{2,18},{10... | collective-permute-start | bytes 2949128 | tf_op jit(solution)/shard_map/ppermute | solution.py:1753
  522.6 21.0 %collective-permute-start = (bf16[256,1920]{1,0:T(8,128)(2,1)}, bf16[256,1920]{1,0:T(8,128)(2,1)S(1)}, u32[]{:S(2)}, u32[]{:S(2)}) collective-permute-start(bf16[256,1920]{1,0:T(8,128)(2,1)} %reduce-scatter.10.cloned.1.call-done.own_ref), channel_id=1, source_target_pairs={{0,8},{8,0},{16,24},{24,16},{1,9},{9,1},{17,25},{25,17},{2,10},{10... | collective-permute-start | bytes 2949128 | tf_op jit(solution)/shard_map/ppermute | solution.py:1753
  528.9 2.9 copy-start.8
  531.8 2.1 copy-start.5
  543.6 14.2 %copy-start.6 = (bf16[256,1920]{1,0:T(8,128)(2,1)}, bf16[256,1920]{1,0:T(8,128)(2,1)S(1)}, u32[]{:S(2)}) copy-start(bf16[256,1920]{1,0:T(8,128)(2,1)S(1)} %collective-permute-done.across_ref) | copy-start | bytes 2949124
  543.7 12.6 %collective-permute-start.3 = (bf16[128,1920]{1,0:T(8,128)(2,1)S(1)}, bf16[128,1920]{1,0:T(8,128)(2,1)}, u32[]{:S(2)}, u32[]{:S(2)}) collective-permute-start(bf16[128,1920]{1,0:T(8,128)(2,1)S(1)} %slice.21), channel_id=1, source_target_pairs={{0,8},{8,0},{16,24},{24,16},{1,9},{9,1},{17,25},{25,17},{2,10},{10... | collective-permute-start | bytes 1474568 | tf_op jit(solution)/shard_map/ppermute | solution.py:1753
  545.0 11.4 %collective-permute-start.2 = (bf16[128,1920]{1,0:T(8,128)(2,1)S(1)}, bf16[128,1920]{1,0:T(8,128)(2,1)}, u32[]{:S(2)}, u32[]{:S(2)}) collective-permute-start(bf16[128,1920]{1,0:T(8,128)(2,1)S(1)} %slice.20), channel_id=1, source_target_pairs={{0,16},{8,24},{16,0},{24,8},{1,17},{9,25},{17,1},{25,9},{2,18},{10... | collective-permute-start | bytes 1474568 | tf_op jit(solution)/shard_map/ppermute | solution.py:1753
  556.3 10.7 %collective-permute-start.5 = (bf16[256,896]{1,0:T(8,128)(2,1)}, bf16[256,896]{1,0:T(8,128)(2,1)S(1)}, u32[]{:S(2)}, u32[]{:S(2)}) collective-permute-start(bf16[256,896]{1,0:T(8,128)(2,1)} %reduce-scatter.14.cloned.1.call-done.own_ref), channel_id=1, source_target_pairs={{0,16},{8,24},{16,0},{24,8},{1,17},{9,25},{17,1},{25,9},{2,18},{10... | collective-permute-start | bytes 1376264 | tf_op jit(solution)/shard_map/ppermute | solution.py:1753
  557.8 10.8 %collective-permute-start.4 = (bf16[256,896]{1,0:T(8,128)(2,1)}, bf16[256,896]{1,0:T(8,128)(2,1)S(1)}, u32[]{:S(2)}, u32[]{:S(2)}) collective-permute-start(bf16[256,896]{1,0:T(8,128)(2,1)} %reduce-scatter.14.cloned.1.call-done.own_ref), channel_id=1, source_target_pairs={{0,8},{8,0},{16,24},{24,16},{1,9},{9,1},{17,25},{25,17},{2,10},{10... | collective-permute-start | bytes 1376264 | tf_op jit(solution)/shard_map/ppermute | solution.py:1753
  559.3 19.2 %copy-start.1 = (bf16[256,3456]{1,0:T(8,128)(2,1)S(1)}, bf16[256,3456]{1,0:T(8,128)(2,1)}, u32[]{:S(2)}) copy-start(bf16[256,3456]{1,0:T(8,128)(2,1)} %param.21) | copy-start | bytes 5308420
  560.7 1.2 copy-start.7
  561.9 1.2 copy-start.9
  563.1 13.2 %copy-start.10 = (bf16[256,896]{1,0:T(8,128)(2,1)S(1)}, bf16[256,896]{1,0:T(8,128)(2,1)}, u32[]{:S(2)}) copy-start(bf16[256,896]{1,0:T(8,128)(2,1)} %reduce-scatter.14.cloned.1.call-done.own_ref) | copy-start | bytes 1376260
  568.6 6.1 %collective-permute-start.7 = (bf16[128,896]{1,0:T(8,128)(2,1)S(1)}, bf16[128,896]{1,0:T(8,128)(2,1)S(1)}, u32[]{:S(2)}, u32[]{:S(2)}) collective-permute-start(bf16[128,896]{1,0:T(8,128)(2,1)S(1)} %slice.23), channel_id=1, source_target_pairs={{0,8},{8,0},{16,24},{24,16},{1,9},{9,1},{17,25},{25,17},{2,10},{10... | collective-permute-start | bytes 688136 | tf_op jit(solution)/shard_map/ppermute | solution.py:1753
  570.2 6.0 %collective-permute-start.6 = (bf16[128,896]{1,0:T(8,128)(2,1)S(1)}, bf16[128,896]{1,0:T(8,128)(2,1)S(1)}, u32[]{:S(2)}, u32[]{:S(2)}) collective-permute-start(bf16[128,896]{1,0:T(8,128)(2,1)S(1)} %slice.22), channel_id=1, source_target_pairs={{0,16},{8,24},{16,0},{24,8},{1,17},{9,25},{17,1},{25,9},{2,18},{10... | collective-permute-start | bytes 688136 | tf_op jit(solution)/shard_map/ppermute | solution.py:1753
Sparse Core Ops, SparseCore 0:
  10.3 141.0 all-gather.3
  153.6 71.6 all-gather.5
  227.5 41.1 all-gather.7
  271.6 43.1 reduce-scatter.5
  321.7 65.6 reduce-scatter.7
  397.1 37.0 reduce-scatter.11
  438.6 69.9 reduce-scatter.9
  510.9 45.3 reduce-scatter.13
